TPU v7x, 32 devices: a whole 2x2x4 slice. The times are simulated.
32 devices in a mesh: wide: 8 (over z, y), narrow: 4 (over x, core).
Axes of the slice: x: 2, y: 2, z: 4, core: 2. Of those that a mesh axis runs over, the one named last changes fastest.
Arguments:
- units: bfloat16 [16384, 1024], P('wide'), may hold values from -6 to 6
- text: bfloat16 [4096, 1024], P('wide'), may hold values from -6 to 6
- out_grad: bfloat16 [16384, 1024], P('wide'), may hold values from -6 to 6
- unit_lengths: int32 [16], P('wide'), may hold values from 512 to 1024, as said below
- text_lengths: int32 [16], P('wide'), may hold values from 128 to 256
- bucket_counts: int32 [8], P('wide'), may hold values from 1 to 2
- norm_gain: float32 [3, 1024], replicated, may hold values from 0.25 to 1.75
- norm_shift: float32 [3, 1024], replicated, may hold values from -2 to 2
- self_qkv: bfloat16 [1024, 3, 1024], P(None, None, 'narrow'), may hold values from -0.1875 to 0.1875
- self_bias: float32 [2, 1024], P(None, 'narrow'), may hold values from -3 to 3
- self_out: bfloat16 [1024, 1024], P('narrow'), may hold values from -0.75 to 0.75
- cross_q: bfloat16 [1024, 1024], P(None, 'narrow'), may hold values from -0.1875 to 0.1875
- cross_kv: bfloat16 [1024, 2, 1024], P(None, None, 'narrow'), may hold values from -0.1875 to 0.1875
- cross_bias: float32 [2, 1024], P(None, 'narrow'), may hold values from -3 to 3
- cross_out: bfloat16 [1024, 1024], P('narrow'), may hold values from -0.75 to 0.75
- ffn_in: bfloat16 [1024, 8192], P(None, 'narrow'), may hold values from -0.1875 to 0.1875
- ffn_in_bias: float32 [8192], P('narrow'), may hold values from -3 to 3
- ffn_out: bfloat16 [8192, 1024], P('narrow'), may hold values from -0.0625 to 0.0625
- out_bias: float32 [3, 1024], replicated, may hold values from -3 to 3
Outputs:
- output: bfloat16 [16384, 1024], P(('wide', 'narrow'))
- units_grad: float32 [16384, 1024], P(('wide', 'narrow'))
- text_grad: float32 [4096, 1024], P(('wide', 'narrow'))
- norm_gain_grad: float32 [3, 1024], replicated
- norm_shift_grad: float32 [3, 1024], replicated
- self_qkv_grad: float32 [1024, 3, 1024], P(None, None, 'narrow')
- self_bias_grad: float32 [2, 1024], P(None, 'narrow')
- self_out_grad: float32 [1024, 1024], P('narrow')
- cross_q_grad: float32 [1024, 1024], P(None, 'narrow')
- cross_kv_grad: float32 [1024, 2, 1024], P(None, None, 'narrow')
- cross_bias_grad: float32 [2, 1024], P(None, 'narrow')
- cross_out_grad: float32 [1024, 1024], P('narrow')
- ffn_in_grad: float32 [1024, 8192], P(None, 'narrow')
- ffn_in_bias_grad: float32 [8192], P('narrow')
- ffn_out_grad: float32 [8192, 1024], P('narrow')
- out_bias_grad: float32 [3, 1024], replicated
Inputs may be any that keep to these rules, and one draw needn't show every extreme that they name: `unit_lengths`: A multiple of 256; slots at or past their bucket's count hold no sequence.
All inputs are finite; a program needn't handle non-finite values.
Results may differ from a plain program's by a relative error of at most 0.03.
Values may be sent and summed in bfloat16 or wider, within the bound.
A program may use at most 192 MiB of HBM per device.

v0:
```python
import jax
import jax.numpy as jnp
from jax import lax
from jax.sharding import PartitionSpec as P

HEAD_DIM = 64
UNITS = 1024
TEXT = 256


NORM_EPSILON = 1e-05
MASKED_SCORE = -1000000000.0
EXACT = lax.Precision.HIGHEST


def smooth_gate(values):
    return jax.nn.gelu(values, approximate=False)


def norm_forward(values, gain_vec, shift_vec):
    row_mean = jnp.mean(values, axis=-1, keepdims=True)
    centered = values - row_mean
    inv_std = lax.rsqrt(jnp.mean(centered * centered, axis=-1, keepdims=True) + NORM_EPSILON)
    normed = centered * inv_std
    return (normed * gain_vec + shift_vec, normed, inv_std)


def norm_backward(grad_in, normed, inv_std, gain_vec):
    scaled = grad_in * gain_vec
    inner_term = scaled - jnp.mean(scaled, axis=-1, keepdims=True)
    inner_term = inner_term - normed * jnp.mean(scaled * normed, axis=-1, keepdims=True)
    return inner_term * inv_std


def split_heads(values):
    return values.reshape(values.shape[0], -1, HEAD_DIM)


def block_slices(block_index, queries, key_rows, value_rows, key_count, query_block):
    per_slot = UNITS // query_block
    slot_id = block_index // per_slot
    first_row = block_index * query_block
    block_queries = lax.dynamic_slice_in_dim(queries, first_row, query_block, 0)
    block_keys = lax.dynamic_slice_in_dim(key_rows, slot_id * key_count, key_count, 0)
    block_values = lax.dynamic_slice_in_dim(value_rows, slot_id * key_count, key_count, 0)
    return (slot_id, first_row - slot_id * UNITS, block_queries, block_keys, block_values)


def masked_scores(block_queries, block_keys, allowed, score_scale):
    scores = (
        jnp.einsum("qhd,khd->hqk", block_queries, block_keys, preferred_element_type=jnp.float32)
        * score_scale
    )
    return jnp.where(allowed[None], scores, MASKED_SCORE)


def attention_forward(
    queries, key_rows, value_rows, key_count, query_block, score_scale, allowed_fn
):

    def one_block(block_index):
        slot_id, offset, block_queries, block_keys, block_values = block_slices(
            block_index, queries, key_rows, value_rows, key_count, query_block
        )
        scores = masked_scores(block_queries, block_keys, allowed_fn(slot_id, offset), score_scale)
        row_max = jnp.max(scores, axis=-1, keepdims=True)
        exp_scores = jnp.exp(scores - row_max)
        row_total = jnp.sum(exp_scores, axis=-1, keepdims=True)
        weights = (exp_scores / row_total).astype(jnp.bfloat16)
        context = jnp.einsum(
            "hqk,khd->qhd", weights, block_values, preferred_element_type=jnp.float32
        )
        return (context, (row_max + jnp.log(row_total))[:, :, 0])

    block_total = queries.shape[0] // query_block
    context, log_total = lax.map(one_block, jnp.arange(block_total, dtype=jnp.int32))
    return (context.reshape(queries.shape[0], -1), log_total)


def attention_backward(
    queries,
    key_rows,
    value_rows,
    context_grad,
    log_total,
    key_count,
    query_block,
    score_scale,
    allowed_fn,
):

    def one_block(packed):
        block_index, block_log = packed
        slot_id, offset, block_queries, block_keys, block_values = block_slices(
            block_index, queries, key_rows, value_rows, key_count, query_block
        )
        block_grad = lax.dynamic_slice_in_dim(
            context_grad, block_index * query_block, query_block, 0
        )
        scores = masked_scores(block_queries, block_keys, allowed_fn(slot_id, offset), score_scale)
        weights = jnp.exp(scores - block_log[:, :, None])
        value_grad = jnp.einsum(
            "hqk,qhd->khd",
            weights.astype(jnp.bfloat16),
            block_grad,
            preferred_element_type=jnp.float32,
        )
        weight_grad = jnp.einsum(
            "qhd,khd->hqk", block_grad, block_values, preferred_element_type=jnp.float32
        )
        score_grad = weights * (
            weight_grad - jnp.sum(weights * weight_grad, axis=-1, keepdims=True)
        )
        query_grad = (
            jnp.einsum("hqk,khd->qhd", score_grad, block_keys.astype(jnp.float32), precision=EXACT)
            * score_scale
        )
        key_grad = (
            jnp.einsum(
                "hqk,qhd->khd", score_grad, block_queries.astype(jnp.float32), precision=EXACT
            )
            * score_scale
        )
        return (query_grad, key_grad, value_grad)

    row_count = queries.shape[0]
    block_total = row_count // query_block
    per_slot = UNITS // query_block
    slot_count = row_count // UNITS
    query_grad, key_grad, value_grad = lax.map(
        one_block, (jnp.arange(block_total, dtype=jnp.int32), log_total)
    )
    query_grad = query_grad.reshape(row_count, -1)
    key_grad = jnp.sum(key_grad.reshape(slot_count, per_slot, key_count, -1), axis=1).reshape(
        slot_count * key_count, -1
    )
    value_grad = jnp.sum(value_grad.reshape(slot_count, per_slot, key_count, -1), axis=1).reshape(
        slot_count * key_count, -1
    )
    return (query_grad, key_grad, value_grad)


def local(
    units,
    text,
    out_grad,
    unit_lengths,
    text_lengths,
    bucket_counts,
    norm_gain,
    norm_shift,
    self_qkv,
    self_bias,
    self_out,
    cross_q,
    cross_kv,
    cross_bias,
    cross_out,
    ffn_in,
    ffn_in_bias,
    ffn_out,
    out_bias,
):
    narrow_size = lax.axis_size("narrow")
    narrow_index = lax.axis_index("narrow")
    group_rows = units.shape[0]
    own_rows = group_rows // narrow_size
    first_own = narrow_index * own_rows
    slot_count = unit_lengths.shape[0]
    score_scale = HEAD_DIM ** (-0.5)
    query_block = min(512, UNITS)
    slot_live = jnp.arange(slot_count, dtype=jnp.int32) < bucket_counts[0]
    lengths = jnp.where(slot_live, unit_lengths, 0)
    positions = jnp.arange(group_rows, dtype=jnp.int32)
    slot_match = (positions // UNITS)[:, None] == jnp.arange(slot_count, dtype=jnp.int32)[None, :]
    row_limit = jnp.sum(jnp.where(slot_match, lengths[None, :], 0), axis=1)
    row_valid = positions % UNITS < row_limit
    valid_own = lax.dynamic_slice_in_dim(row_valid, first_own, own_rows, 0)
    unit_pos = jnp.arange(UNITS, dtype=jnp.int32)
    text_pos = jnp.arange(TEXT, dtype=jnp.int32)

    def self_allowed(slot_id, offset):
        rows_here = offset + jnp.arange(query_block, dtype=jnp.int32)
        length = lax.dynamic_index_in_dim(lengths, slot_id, keepdims=False)
        before = unit_pos[None, :] <= rows_here[:, None]
        return before & ((unit_pos[None, :] < length) | (unit_pos[None, :] == rows_here[:, None]))

    def cross_allowed(slot_id, offset):
        length = lax.dynamic_index_in_dim(text_lengths, slot_id, keepdims=False)
        return jnp.broadcast_to(text_pos[None, :] < length, (query_block, TEXT))

    resid_all = units.astype(jnp.float32)
    norm_one, normed_all, inv_all = norm_forward(resid_all, norm_gain[0], norm_shift[0])
    normed_one = lax.dynamic_slice_in_dim(normed_all, first_own, own_rows, 0)
    inv_one = lax.dynamic_slice_in_dim(inv_all, first_own, own_rows, 0)
    first_in = norm_one.astype(jnp.bfloat16)
    projected = jnp.einsum("rd,dcn->rcn", first_in, self_qkv, preferred_element_type=jnp.float32)
    queries = (projected[:, 0] + self_bias[0]).astype(jnp.bfloat16)
    key_rows = projected[:, 1].astype(jnp.bfloat16)
    value_rows = (projected[:, 2] + self_bias[1]).astype(jnp.bfloat16)
    self_context, self_log = attention_forward(
        split_heads(queries),
        split_heads(key_rows),
        split_heads(value_rows),
        UNITS,
        query_block,
        score_scale,
        self_allowed,
    )
    self_context = self_context.astype(jnp.bfloat16)
    self_sum = lax.psum_scatter(
        jnp.dot(self_context, self_out, preferred_element_type=jnp.float32).astype(jnp.bfloat16),
        "narrow",
        scatter_dimension=0,
        tiled=True,
    ).astype(jnp.float32)
    resid_one = lax.dynamic_slice_in_dim(resid_all, first_own, own_rows, 0) + self_sum + out_bias[0]
    norm_two, normed_two, inv_two = norm_forward(resid_one, norm_gain[1], norm_shift[1])
    second_all = lax.all_gather(norm_two.astype(jnp.bfloat16), "narrow", axis=0, tiled=True)
    cross_queries = (
        jnp.dot(second_all, cross_q, preferred_element_type=jnp.float32) + cross_bias[0]
    ).astype(jnp.bfloat16)
    text_proj = jnp.einsum("td,dcn->tcn", text, cross_kv, preferred_element_type=jnp.float32)
    text_keys = text_proj[:, 0].astype(jnp.bfloat16)
    text_values = (text_proj[:, 1] + cross_bias[1]).astype(jnp.bfloat16)
    cross_context, cross_log = attention_forward(
        split_heads(cross_queries),
        split_heads(text_keys),
        split_heads(text_values),
        TEXT,
        query_block,
        score_scale,
        cross_allowed,
    )
    cross_context = cross_context.astype(jnp.bfloat16)
    cross_sum = lax.psum_scatter(
        jnp.dot(cross_context, cross_out, preferred_element_type=jnp.float32).astype(jnp.bfloat16),
        "narrow",
        scatter_dimension=0,
        tiled=True,
    ).astype(jnp.float32)
    resid_two = resid_one + cross_sum + out_bias[1]
    norm_three, normed_three, inv_three = norm_forward(resid_two, norm_gain[2], norm_shift[2])
    third_all = lax.all_gather(norm_three.astype(jnp.bfloat16), "narrow", axis=0, tiled=True)
    hidden_pre = jnp.dot(third_all, ffn_in, preferred_element_type=jnp.float32) + ffn_in_bias
    hidden_full, gate_pullback = jax.vjp(smooth_gate, hidden_pre)
    hidden = hidden_full.astype(jnp.bfloat16)
    ffn_sum = lax.psum_scatter(
        jnp.dot(hidden, ffn_out, preferred_element_type=jnp.float32).astype(jnp.bfloat16),
        "narrow",
        scatter_dimension=0,
        tiled=True,
    ).astype(jnp.float32)
    output = jnp.where(valid_own[:, None], resid_two + ffn_sum + out_bias[2], 0.0).astype(
        jnp.bfloat16
    )
    grad_all = jnp.where(row_valid[:, None], out_grad, jnp.zeros_like(out_grad))
    grad_two = lax.dynamic_slice_in_dim(grad_all, first_own, own_rows, 0).astype(jnp.float32)
    ffn_out_grad = jnp.einsum("rf,rd->fd", hidden, grad_all, preferred_element_type=jnp.float32)
    hidden_grad = jnp.einsum("rd,fd->rf", grad_all, ffn_out, preferred_element_type=jnp.float32)
    pre_grad = gate_pullback(hidden_grad)[0].astype(jnp.bfloat16)
    ffn_in_bias_grad = jnp.sum(pre_grad, axis=0, dtype=jnp.float32)
    ffn_in_grad = jnp.einsum("rd,rf->df", third_all, pre_grad, preferred_element_type=jnp.float32)
    third_part = jnp.einsum("rf,df->rd", pre_grad, ffn_in, preferred_element_type=jnp.float32)
    third_grad = lax.psum_scatter(
        third_part.astype(jnp.bfloat16), "narrow", scatter_dimension=0, tiled=True
    ).astype(jnp.float32)
    gain_three = jnp.sum(third_grad * normed_three, axis=0)
    shift_three = jnp.sum(third_grad, axis=0)
    resid_two_grad = grad_two + norm_backward(third_grad, normed_three, inv_three, norm_gain[2])
    bias_two_grad = jnp.sum(grad_two, axis=0)
    cross_out_all = lax.all_gather(
        resid_two_grad.astype(jnp.bfloat16), "narrow", axis=0, tiled=True
    )
    cross_out_grad = jnp.einsum(
        "rn,rd->nd", cross_context, cross_out_all, preferred_element_type=jnp.float32
    )
    cross_context_grad = jnp.einsum(
        "rd,nd->rn", cross_out_all, cross_out, preferred_element_type=jnp.float32
    ).astype(jnp.bfloat16)
    cross_query_grad, text_key_grad, text_value_grad = attention_backward(
        split_heads(cross_queries),
        split_heads(text_keys),
        split_heads(text_values),
        split_heads(cross_context_grad),
        cross_log,
        TEXT,
        query_block,
        score_scale,
        cross_allowed,
    )
    cross_query_grad = cross_query_grad.astype(jnp.bfloat16)
    text_kv_grad = jnp.stack([text_key_grad, text_value_grad], axis=1).astype(jnp.bfloat16)
    cross_q_grad = jnp.einsum(
        "rd,rn->dn", second_all, cross_query_grad, preferred_element_type=jnp.float32
    )
    cross_kv_grad = jnp.einsum(
        "td,tcn->dcn", text, text_kv_grad, preferred_element_type=jnp.float32
    )
    cross_bias_grad = jnp.stack(
        [
            jnp.sum(cross_query_grad, axis=0, dtype=jnp.float32),
            jnp.sum(text_kv_grad[:, 1], axis=0, dtype=jnp.float32),
        ]
    )
    second_part = jnp.einsum(
        "rn,dn->rd", cross_query_grad, cross_q, preferred_element_type=jnp.float32
    )
    text_part = jnp.einsum(
        "tcn,dcn->td", text_kv_grad, cross_kv, preferred_element_type=jnp.float32
    )
    second_grad, text_grad = (
        lax.psum_scatter(
            second_part.astype(jnp.bfloat16), "narrow", scatter_dimension=0, tiled=True
        ).astype(jnp.float32),
        lax.psum_scatter(
            text_part.astype(jnp.bfloat16), "narrow", scatter_dimension=0, tiled=True
        ).astype(jnp.float32),
    )
    gain_two = jnp.sum(second_grad * normed_two, axis=0)
    shift_two = jnp.sum(second_grad, axis=0)
    resid_one_grad = resid_two_grad + norm_backward(second_grad, normed_two, inv_two, norm_gain[1])
    bias_one_grad = jnp.sum(resid_two_grad, axis=0)
    self_out_all = lax.all_gather(resid_one_grad.astype(jnp.bfloat16), "narrow", axis=0, tiled=True)
    self_out_grad = jnp.einsum(
        "rn,rd->nd", self_context, self_out_all, preferred_element_type=jnp.float32
    )
    self_context_grad = jnp.einsum(
        "rd,nd->rn", self_out_all, self_out, preferred_element_type=jnp.float32
    ).astype(jnp.bfloat16)
    query_grad, key_grad, value_grad = attention_backward(
        split_heads(queries),
        split_heads(key_rows),
        split_heads(value_rows),
        split_heads(self_context_grad),
        self_log,
        UNITS,
        query_block,
        score_scale,
        self_allowed,
    )
    qkv_grad = jnp.stack([query_grad, key_grad, value_grad], axis=1).astype(jnp.bfloat16)
    self_qkv_grad = jnp.einsum(
        "rd,rcn->dcn", first_in, qkv_grad, preferred_element_type=jnp.float32
    )
    self_bias_grad = jnp.stack(
        [
            jnp.sum(qkv_grad[:, 0], axis=0, dtype=jnp.float32),
            jnp.sum(qkv_grad[:, 2], axis=0, dtype=jnp.float32),
        ]
    )
    first_part = jnp.einsum("rcn,dcn->rd", qkv_grad, self_qkv, preferred_element_type=jnp.float32)
    first_grad = lax.psum_scatter(
        first_part.astype(jnp.bfloat16), "narrow", scatter_dimension=0, tiled=True
    ).astype(jnp.float32)
    gain_one = jnp.sum(first_grad * normed_one, axis=0)
    shift_one = jnp.sum(first_grad, axis=0)
    units_grad = resid_one_grad + norm_backward(first_grad, normed_one, inv_one, norm_gain[0])
    bias_zero_grad = jnp.sum(resid_one_grad, axis=0)
    small_sums = lax.psum(
        jnp.stack(
            [
                gain_one,
                gain_two,
                gain_three,
                shift_one,
                shift_two,
                shift_three,
                bias_zero_grad,
                bias_one_grad,
                bias_two_grad,
            ]
        ),
        ("wide", "narrow"),
    )
    (
        self_qkv_grad,
        self_bias_grad,
        self_out_grad,
        cross_q_grad,
        cross_kv_grad,
        cross_bias_grad,
        cross_out_grad,
        ffn_in_grad,
        ffn_in_bias_grad,
        ffn_out_grad,
    ) = lax.psum(
        (
            self_qkv_grad,
            self_bias_grad,
            self_out_grad,
            cross_q_grad,
            cross_kv_grad,
            cross_bias_grad,
            cross_out_grad,
            ffn_in_grad,
            ffn_in_bias_grad,
            ffn_out_grad,
        ),
        "wide",
    )
    return (
        output,
        units_grad,
        text_grad,
        small_sums[0:3],
        small_sums[3:6],
        self_qkv_grad,
        self_bias_grad,
        self_out_grad,
        cross_q_grad,
        cross_kv_grad,
        cross_bias_grad,
        cross_out_grad,
        ffn_in_grad,
        ffn_in_bias_grad,
        ffn_out_grad,
        small_sums[6:9],
    )


def solution(mesh):
    placed = (
        P("wide", None),
        P("wide", None),
        P("wide", None),
        P("wide"),
        P("wide"),
        P("wide"),
        P(),
        P(),
        P(None, None, "narrow"),
        P(None, "narrow"),
        P("narrow", None),
        P(None, "narrow"),
        P(None, None, "narrow"),
        P(None, "narrow"),
        P("narrow", None),
        P(None, "narrow"),
        P("narrow"),
        P("narrow", None),
        P(),
    )
    return jax.shard_map(
        local,
        mesh=mesh,
        in_specs=placed,
        out_specs=(
            P(("wide", "narrow"), None),
            P(("wide", "narrow"), None),
            P(("wide", "narrow"), None),
            P(),
            P(),
            P(None, None, "narrow"),
            P(None, "narrow"),
            P("narrow", None),
            P(None, "narrow"),
            P(None, None, "narrow"),
            P(None, "narrow"),
            P("narrow", None),
            P(None, "narrow"),
            P("narrow"),
            P("narrow", None),
            P(),
        ),
        check_vma=False,
    )
```

profile of v0, /device:TPU:0, one launch (start us, length us, event | category | flops | bytes accessed | tf_op | source)
XLA Modules:
  0.0 1713.9 jit_solution(4811554516095660484)
XLA Ops:
  13.6 4.3 fusion.131
  26.6 57.6 %while.68 = (s32[]{:T(128)}, bf16[4,512,4,64]{1,3,2,0:T(8,128)(2,1)}, f32[4,4,512]{2,1,0:T(4,128)S(1)}, s32[4]{0:T(128)S(1)}, bf16[2048,4,64]{0,2,1:T(8,128)(2,1...) while((s32[]{:T(128)}, ...), condition=%wide.region_6.7_spmd.clone.clone, body=%wide.region_3.6_spmd.clone.clone.sunk | while | flops 564133376 | bytes 41753148 | solution.py:76
  87.9 3.3 convolution_convert_fusion.4
  91.3 6.6 convert_element_type.171
  98.5 40.1 %reduce-scatter.8.cloned.1.call-done = bf16[512,1024]{1,0:T(8,128)(2,1)} async-done(((bf16[2048,1024]{1,0:T(8,128)(2,1)}), bf16[512,1024]{1,0:T(8,128)(2,1)}) %reduce-scatter.8.cloned.1.call-update) | async-done | bytes 1048592 | tf_op jit(solution)/shard_map/reduce_scatter | solution.py:211
  145.9 32.3 %all-gather.5.cloned.1.call-done = bf16[2048,1024]{1,0:T(8,128)(2,1)} async-done(((bf16[512,1024]{1,0:T(8,128)(2,1)}), bf16[2048,1024]{1,0:T(8,128)(2,1)}) %all-gather.5.cloned.1.call-update) | async-done | bytes 4194320 | tf_op jit(solution)/shard_map/all_gather | solution.py:219
  178.2 3.6 fusion.109
  182.9 32.0 %while.66 = (s32[]{:T(128)}, bf16[4,512,4,64]{1,3,2,0:T(8,128)(2,1)}, f32[4,4,512]{2,1,0:T(4,128)S(1)}, s32[4]{0:T(128)S(1)}, bf16[512,4,64]{0,2,1:T(8,128)(2,1)...) while((s32[]{:T(128)}, ...), condition=%wide.region_13.14_spmd.clone, body=%wide.region_10.13_spmd.clone.sunk | while | flops 140507424 | bytes 15796241 | solution.py:76
  218.9 3.3 convolution_convert_fusion.3
  222.3 44.6 %reduce-scatter.10.cloned.1.call-done = bf16[512,1024]{1,0:T(8,128)(2,1)} async-done(((bf16[2048,1024]{1,0:T(8,128)(2,1)}), bf16[512,1024]{1,0:T(8,128)(2,1)}) %reduce-scatter.10.cloned.1.call-update) | async-done | bytes 1048592 | tf_op jit(solution)/shard_map/reduce_scatter | solution.py:236
  272.6 4.1 broadcast_select_fusion
  276.7 29.7 %all-gather.7.cloned.1.call-done = bf16[2048,1024]{1,0:T(8,128)(2,1)} async-done(((bf16[512,1024]{1,0:T(8,128)(2,1)}), bf16[2048,1024]{1,0:T(8,128)(2,1)}) %all-gather.7.cloned.1.call-update) | async-done | bytes 4194320 | tf_op jit(solution)/shard_map/all_gather | solution.py:244
  306.5 49.3 %multiply_convert_fusion = (bf16[2048,2048]{1,0:T(8,128)(2,1)}, f32[2048,2048]{1,0:T(8,128)}, f32[2048,2048]{1,0:T(8,128)}) fusion(f32[2048]{0:T(1024)S(1)} %copy-done.96, bf16[2048,1024]{1,0:T(8,128)(2,1)} %all-gather.7.cloned.1.call-done, bf16[1024,2048]{1,0:T(8,128)(2,1)} %param.42), kind=kOutput, calls=%fused_computation.120 | convolution fusion | flops 8866758656 | bytes 50339840 | tf_op jit(solution)/shard_map/dot_general | solution.py:245
  355.8 22.8 %convert_reduce_fusion = (f32[2048]{0:T(1024)}, bf16[2048,2048]{1,0:T(8,128)(2,1)}) fusion(f32[2048,2048]{1,0:T(8,128)} %get-tuple-element.877, bf16[2048,1024]{1,0:T(8,128)(2,1)S(1)} %copy-done.27, bf16[2048,1024]{1,0:T(8,128)(2,1)} %param.44, f32[2048,2048]{1,0:T(8,128)} %get-tuple-element.908, f32[2048]{0:T(1024)S(1)} %copy-done.96), kind=kOutput, calls=%fused_computation.118 | convolution fusion | flops 8661235712 | bytes 50348032 | tf_op jit(solution)/shard_map/rd,fd->rf/dot_general | solution.py:260
  378.6 14.1 convolution_convert_fusion.1
  392.7 13.8 convolution_convert_fusion.2
  407.4 30.0 %reduce-scatter.14.cloned.1.call-done = bf16[512,1024]{1,0:T(8,128)(2,1)} async-done(((bf16[2048,1024]{1,0:T(8,128)(2,1)}), bf16[512,1024]{1,0:T(8,128)(2,1)}) %reduce-scatter.14.cloned.1.call-update) | async-done | bytes 1048592 | tf_op jit(solution)/shard_map/reduce_scatter | solution.py:265
  437.4 3.4 fusion.121
  440.8 43.6 %reduce-scatter.12.cloned.1.call-done = bf16[512,1024]{1,0:T(8,128)(2,1)} async-done(((bf16[2048,1024]{1,0:T(8,128)(2,1)}), bf16[512,1024]{1,0:T(8,128)(2,1)}) %reduce-scatter.12.cloned.1.call-update) | async-done | bytes 1048592 | tf_op jit(solution)/shard_map/reduce_scatter | solution.py:248
  484.5 4.6 fusion.144
  491.6 34.5 %all-gather.9.cloned.1.call-done = bf16[2048,1024]{1,0:T(8,128)(2,1)} async-done(((bf16[512,1024]{1,0:T(8,128)(2,1)}), bf16[2048,1024]{1,0:T(8,128)(2,1)}) %all-gather.9.cloned.1.call-update) | async-done | bytes 4194320 | tf_op jit(solution)/shard_map/all_gather | solution.py:272
  526.1 4.6 convolution_convert_fusion.6
  531.8 66.2 %while.67 = (s32[]{:T(128)}, bf16[4,512,4,64]{1,3,2,0:T(8,128)(2,1)}, f32[4,256,4,64]{1,3,2,0:T(8,128)}, f32[4,256,4,64]{1,3,2,0:T(8,128)}, s32[4]{0:T(128)S(1)}...) while((s32[]{:T(128)}, ...), condition=%wide.region_23.24_spmd.clone, body=%wide.region_21.23_spmd.clone.sunk | while | flops 1012070656 | bytes 36095324 | solution.py:130
  601.4 3.3 convolution_convert_fusion
  604.8 44.6 %reduce-scatter.16.cloned.1.call-done = bf16[512,1024]{1,0:T(8,128)(2,1)} async-done(((bf16[2048,1024]{1,0:T(8,128)(2,1)}), bf16[512,1024]{1,0:T(8,128)(2,1)}) %reduce-scatter.16.cloned.1.call-update) | async-done | bytes 1048592 | tf_op jit(solution)/shard_map/reduce_scatter | solution.py:313
  649.4 3.6 fusion.122
  653.0 3.2 fusion.145
  663.7 29.7 %all-gather.11.cloned.1.call-done = bf16[2048,1024]{1,0:T(8,128)(2,1)} async-done(((bf16[512,1024]{1,0:T(8,128)(2,1)}), bf16[2048,1024]{1,0:T(8,128)(2,1)}) %all-gather.11.cloned.1.call-update) | async-done | bytes 4194320 | tf_op jit(solution)/shard_map/all_gather | solution.py:324
  693.4 4.4 convolution_convert_fusion.5
  698.9 155.0 %while.69 = (s32[]{:T(128)}, bf16[4,512,4,64]{1,3,2,0:T(8,128)(2,1)}, f32[4,1024,4,64]{1,3,2,0:T(8,128)}, f32[4,1024,4,64]{1,3,2,0:T(8,128)}, s32[4]{0:T(128)S(1...) while((s32[]{:T(128)}, ...), condition=%wide.region_29.30_spmd.clone.clone, body=%wide.region_27.29_spmd.clone.clone.sunk | while | flops 4068867584 | bytes 108608128 | solution.py:130
  703.2 5.5 fusion.248
  711.3 7.2 multiply_reduce_fusion.8
  718.6 7.0 fusion.250
  725.6 8.2 fusion.251
  733.8 4.4 fusion.252
  742.0 5.5 fusion.248
  750.1 7.0 multiply_reduce_fusion.8
  757.2 7.0 fusion.250
  764.2 8.1 fusion.251
  772.4 4.4 fusion.252
  780.6 5.5 fusion.248
  788.6 7.0 multiply_reduce_fusion.8
  795.7 7.0 fusion.250
  802.7 8.1 fusion.251
  810.9 4.4 fusion.252
  819.1 5.5 fusion.248
  827.1 7.0 multiply_reduce_fusion.8
  834.2 7.0 fusion.250
  841.2 8.1 fusion.251
  849.4 4.3 fusion.252
  857.9 3.9 reduce_sum.338
  869.1 6.9 bitcast_convert_fusion
  876.1 14.7 fusion.160
  890.9 14.0 fusion.159
  916.3 5.8 fusion.124
  922.2 5.6 subtract_multiply_fusion.6
  931.9 39.0 %all-reduce = (f32[2,256]{1,0:T(2,128)}, f32[2,256]{1,0:T(2,128)}, f32[2048]{0:T(1024)}) all-reduce(f32[2,256]{1,0:T(2,128)S(1)} %pad_maximum_fusion.6, f32[2,256]{1,0:T(2,128)S(1)} %pad_maximum_fusion.7, f32[2048]{0:T(1024)S(1)} %copy-done.85), channel_id=1, replica_groups=mesh['wide'=8,'narrow'=4] {'wide'}, use_global_device_ids=true, to_apply=%region_51.52 | all-reduce | flops 3072 | bytes 24576 | tf_op jit(solution)/shard_map/psum | solution.py:387
  973.8 41.8 %psum.77 = f32[9,1024]{1,0:T(8,128)S(1)} all-reduce(f32[9,1024]{1,0:T(8,128)S(1)} %stack.67), channel_id=1, replica_groups=mesh['wide'=8,'narrow'=4] {'wide','narrow'}, use_global_device_ids=true, to_apply=%region_47.48 | all-reduce | flops 9216 | bytes 73728 | tf_op jit(solution)/shard_map/psum | solution.py:360
  1016.3 4.1 fusion.112
  1020.4 666.0 %all-reduce.4.cloned.1.call-done = (f32[1024,3,256]{2,0,1:T(8,128)}, f32[256,1024]{1,0:T(8,128)}, f32[1024,256]{1,0:T(8,128)}, f32[1024,2,256]{0,2,1:T(8,128)}, ...) async-done(((f32[1024,3,256]{2,0,1:T(8,128)}, f32[256,1024]{1,0:T(8,128)}, f32[1024,256]{1,0:T(8,128)}, f32[1024,2,256]{0,2,1:T(8,128)}, ...) | async-done | bytes 25165840 | tf_op jit(solution)/shard_map/psum | solution.py:387
  1686.4 4.2 copy.98
  1690.6 3.9 copy.178
  1697.4 4.3 copy.182
  1703.3 3.4 copy.183
  (527 shorter events, 215.8 us)
Async XLA Ops:
  7.2 131.4 %reduce-scatter.8.cloned.1.call-start = ((), (), s32[]{:S(2)}) async-start(), calls=%async_computation.7 | async-start | bytes 5242880 | tf_op jit(solution)/shard_map/reduce_scatter | solution.py:211
  9.3 132.0 %copy-start.59 = (f32[1,1024]{1,0:T(1,128)}, f32[1,1024]{1,0:T(1,128)S(1)}, u32[]{:S(2)}) copy-start(f32[1,1024]{1,0:T(1,128)S(1)} %get-tuple-element.902) | copy-start | bytes 12292
  9.3 260.2 %copy-start.61 = (f32[1,1024]{1,0:T(1,128)}, f32[1,1024]{1,0:T(1,128)S(1)}, u32[]{:S(2)}) copy-start(f32[1,1024]{1,0:T(1,128)S(1)} %get-tuple-element.900) | copy-start | bytes 12292
  84.1 187.7 %copy-start.90 = (s32[2]{0:T(128)}, s32[2]{0:T(128)S(1)}, u32[]{:S(2)}) copy-start(s32[2]{0:T(128)S(1)} %get-tuple-element.1451) | copy-start | bytes 28
  91.2 87.0 %all-gather.5.cloned.1.call-start = ((), (), s32[]{:S(2)}) async-start(), calls=%async_computation.8 | async-start | bytes 5242880 | tf_op jit(solution)/shard_map/all_gather | solution.py:219
  143.6 123.3 %reduce-scatter.10.cloned.1.call-start = ((), (), s32[]{:S(2)}) async-start(), calls=%async_computation.9 | async-start | bytes 5242880 | tf_op jit(solution)/shard_map/reduce_scatter | solution.py:236
  215.0 7.2 copy-start.9
  215.0 7.2 copy-start.13
  215.0 7.2 copy-start.37
  215.0 7.2 copy-start.56
  222.2 84.2 %all-gather.7.cloned.1.call-start = ((), (), s32[]{:S(2)}) async-start(), calls=%async_computation.10 | async-start | bytes 5242880 | tf_op jit(solution)/shard_map/all_gather | solution.py:244
  271.8 165.5 %reduce-scatter.14.cloned.1.call-start = ((), (), s32[]{:S(2)}) async-start(), calls=%async_computation.12 | async-start | bytes 5242880 | tf_op jit(solution)/shard_map/reduce_scatter | solution.py:265
  272.6 33.9 %copy-start.96 = (f32[2048]{0:T(1024)S(1)}, f32[2048]{0:T(1024)}, u32[]{:S(2)}) copy-start(f32[2048]{0:T(1024)} %param.43) | copy-start | bytes 24580
  306.5 49.3 %copy-start.27 = (bf16[2048,1024]{1,0:T(8,128)(2,1)S(1)}, bf16[2048,1024]{1,0:T(8,128)(2,1)}, u32[]{:S(2)}) copy-start(bf16[2048,1024]{1,0:T(8,128)(2,1)} %broadcast_select_fusion) | copy-start | bytes 12582916
  392.7 91.8 %reduce-scatter.12.cloned.1.call-start = ((), (), s32[]{:S(2)}) async-start(), calls=%async_computation.11 | async-start | bytes 5242880 | tf_op jit(solution)/shard_map/reduce_scatter | solution.py:248
  406.5 30.9 %copy-start.62 = (f32[1,1024]{1,0:T(1,128)S(1)}, f32[1,1024]{1,0:T(1,128)}, u32[]{:S(2)}) copy-start(f32[1,1024]{1,0:T(1,128)} %copy-done.61) | copy-start | bytes 12292
  406.5 30.9 %copy-start.66 = (f32[512]{0:T(512)S(1)}, f32[512]{0:T(512)}, u32[]{:S(2)}) copy-start(f32[512]{0:T(512)} %copy-done.65) | copy-start | bytes 6148
  406.5 30.9 %copy-start.74 = (f32[512]{0:T(512)S(1)}, f32[512]{0:T(512)}, u32[]{:S(2)}) copy-start(f32[512]{0:T(512)} %copy-done.73) | copy-start | bytes 6148
  406.5 78.0 %copy-start.78 = (f32[1,1024]{1,0:T(1,128)S(1)}, f32[1,1024]{1,0:T(1,128)}, u32[]{:S(2)}) copy-start(f32[1,1024]{1,0:T(1,128)} %get-tuple-element.897) | copy-start | bytes 12292
  406.5 119.6 %all-gather.9.cloned.1.call-start = ((), (), s32[]{:S(2)}) async-start(), calls=%async_computation.13 | async-start | bytes 5242880 | tf_op jit(solution)/shard_map/all_gather | solution.py:272
  491.5 157.9 %reduce-scatter.16.cloned.1.call-start = ((), (), s32[]{:S(2)}) async-start(), calls=%async_computation.14 | async-start | bytes 5242880 | tf_op jit(solution)/shard_map/reduce_scatter | solution.py:313
  491.6 40.2 %copy-start.10 = (bf16[512,4,64]{0,2,1:T(8,128)(2,1)S(1)}, bf16[512,4,64]{0,2,1:T(8,128)(2,1)}, u32[]{:S(2)}) copy-start(bf16[512,4,64]{0,2,1:T(8,128)(2,1)} %copy-done.9) | copy-start | bytes 786436
  491.6 40.2 %copy-start.14 = (bf16[2048,4,64]{0,2,1:T(8,128)(2,1)S(1)}, bf16[2048,4,64]{0,2,1:T(8,128)(2,1)}, u32[]{:S(2)}) copy-start(bf16[2048,4,64]{0,2,1:T(8,128)(2,1)} %copy-done.13) | copy-start | bytes 3145732
  491.6 40.2 %copy-start.38 = (bf16[512,4,64]{0,2,1:T(8,128)(2,1)S(1)}, bf16[512,4,64]{0,2,1:T(8,128)(2,1)}, u32[]{:S(2)}) copy-start(bf16[512,4,64]{0,2,1:T(8,128)(2,1)} %copy-done.37) | copy-start | bytes 786436
  491.6 40.2 %copy-start.99 = (s32[2]{0:T(128)S(1)}, s32[2]{0:T(128)}, u32[]{:S(2)}) copy-start(s32[2]{0:T(128)} %param.31) | copy-start | bytes 28
  604.7 44.7 %copy-start.60 = (f32[1,1024]{1,0:T(1,128)S(1)}, f32[1,1024]{1,0:T(1,128)}, u32[]{:S(2)}) copy-start(f32[1,1024]{1,0:T(1,128)} %copy-done.59) | copy-start | bytes 12292
  604.7 44.7 %copy-start.64 = (f32[512]{0:T(512)S(1)}, f32[512]{0:T(512)}, u32[]{:S(2)}) copy-start(f32[512]{0:T(512)} %copy-done.63) | copy-start | bytes 6148
  604.7 44.7 %copy-start.72 = (f32[512]{0:T(512)S(1)}, f32[512]{0:T(512)}, u32[]{:S(2)}) copy-start(f32[512]{0:T(512)} %copy-done.71) | copy-start | bytes 6148
  604.8 88.6 %all-gather.11.cloned.1.call-start = ((), (), s32[]{:S(2)}) async-start(), calls=%async_computation.15 | async-start | bytes 5242880 | tf_op jit(solution)/shard_map/all_gather | solution.py:324
  658.7 269.6 %reduce-scatter.20.cloned.1.call-start = ((), (), s32[]{:S(2)}) async-start(), calls=%async_computation.17 | async-start | bytes 1310720 | tf_op jit(solution)/shard_map/reduce_scatter | solution.py:316
  660.3 33.0 %copy-start.54 = (bf16[256,1024]{1,0:T(8,128)(2,1)S(1)}, bf16[256,1024]{1,0:T(8,128)(2,1)}, u32[]{:S(2)}) copy-start(bf16[256,1024]{1,0:T(8,128)(2,1)} %param.37) | copy-start | bytes 1572868
  663.6 35.3 %copy-start.3 = (bf16[2048,4,64]{0,2,1:T(8,128)(2,1)S(1)}, bf16[2048,4,64]{0,2,1:T(8,128)(2,1)}, u32[]{:S(2)}) copy-start(bf16[2048,4,64]{0,2,1:T(8,128)(2,1)} %copy-done.2) | copy-start | bytes 3145732
  663.6 35.3 %copy-start.91 = (s32[2]{0:T(128)S(1)}, s32[2]{0:T(128)}, u32[]{:S(2)}) copy-start(s32[2]{0:T(128)} %copy-done.90) | copy-start | bytes 28
  663.6 307.3 %reduce-scatter.18.cloned.1.call-start = ((), (), s32[]{:S(2)}) async-start(), calls=%async_computation.16 | async-start | bytes 5242880 | tf_op jit(solution)/shard_map/reduce_scatter | solution.py:353
  710.6 7.9 slice-start
  711.3 7.3 slice-start.1
  711.3 7.3 copy-start.30
  725.6 8.2 copy-start.31
  749.5 7.7 slice-start
  764.2 8.2 copy-start.31
  788.0 7.7 slice-start
  788.6 7.1 slice-start.1
  788.6 7.1 copy-start.30
  802.7 8.1 copy-start.31
  826.5 7.7 slice-start
  827.1 7.1 slice-start.1
  827.1 7.1 copy-start.30
  841.2 8.2 copy-start.31
  876.0 810.3 %all-reduce.4.cloned.1.call-start = ((), (), s32[]{:S(2)}) async-start(), calls=%async_computation.18 | async-start | bytes 50331648 | tf_op jit(solution)/shard_map/psum | solution.py:387
  876.1 14.8 copy-start.93
  890.8 14.0 copy-start.40
  890.8 14.0 copy-start.42
  890.8 14.0 copy-start.44
  890.8 16.1 copy-start.26
  890.9 16.1 copy-start.92
  927.8 45.9 %copy-start.75 = (f32[1024]{0:T(1024)S(1)}, f32[1024]{0:T(1024)}, u32[]{:S(2)}) copy-start(f32[1024]{0:T(1024)} %get-tuple-element.872) | copy-start | bytes 12292
  927.8 45.9 %copy-start.76 = (f32[1024]{0:T(1024)S(1)}, f32[1024]{0:T(1024)}, u32[]{:S(2)}) copy-start(f32[1024]{0:T(1024)} %get-tuple-element.892) | copy-start | bytes 12292
  927.8 45.9 %copy-start.77 = (f32[1024]{0:T(1024)S(1)}, f32[1024]{0:T(1024)}, u32[]{:S(2)}) copy-start(f32[1024]{0:T(1024)} %get-tuple-element.874) | copy-start | bytes 12292
  927.8 45.9 %copy-start.79 = (f32[1024]{0:T(1024)S(1)}, f32[1024]{0:T(1024)}, u32[]{:S(2)}) copy-start(f32[1024]{0:T(1024)} %get-tuple-element.774) | copy-start | bytes 12292
  927.9 45.9 %copy-start.80 = (f32[1024]{0:T(1024)S(1)}, f32[1024]{0:T(1024)}, u32[]{:S(2)}) copy-start(f32[1024]{0:T(1024)} %get-tuple-element.781) | copy-start | bytes 12292
  927.9 45.9 %copy-start.81 = (f32[1024]{0:T(1024)S(1)}, f32[1024]{0:T(1024)}, u32[]{:S(2)}) copy-start(f32[1024]{0:T(1024)} %get-tuple-element.776) | copy-start | bytes 12292
  927.9 45.9 %copy-start.82 = (f32[1024]{0:T(1024)S(1)}, f32[1024]{0:T(1024)}, u32[]{:S(2)}) copy-start(f32[1024]{0:T(1024)} %get-tuple-element.782) | copy-start | bytes 12292
  970.9 45.4 %copy-start.28 = (bf16[512,1024]{1,0:T(8,128)(2,1)S(1)}, bf16[512,1024]{1,0:T(8,128)(2,1)}, u32[]{:S(2)}) copy-start(bf16[512,1024]{1,0:T(8,128)(2,1)} %reduce-scatter.18.cloned.1.call-done) | copy-start | bytes 3145732
  1686.4 9.1 copy-start.47
  (88 other events, 291.0 us)
Sparse Core Ops, SparseCore 0:
  91.3 47.2 reduce-scatter.7
  143.7 34.4 all-gather.4
  222.3 44.5 reduce-scatter.9
  272.0 34.4 all-gather.6
  392.8 44.5 reduce-scatter.13
  439.9 44.5 reduce-scatter.11
  491.6 34.4 all-gather.8
  604.9 44.4 reduce-scatter.15
  658.8 34.4 all-gather.10
  695.9 24.8 reduce-scatter.19
  876.1 44.4 reduce-scatter.17
  928.5 757.7 all-reduce.3
where the time goes:
time: 1720 us; the launch traced here: 1710 us
  waiting for transfers between devices  995 us (58%)
  matrix products  378 us (22%)
  other arithmetic  96.6 us (6%)
  local copies, waits for them, and re-layouts  92.1 us (5%)
  blocking collectives  80.8 us (5%)
  loops' own time  54.3 us (3%)
    psum x1, waiting for transfers between devices, local(): lax.psum((self_qkv_grad, self_bias_grad, self_out_grad, cross_q_grad, cro...  666 us
    dot_general x1, matrix products, local(): jnp.dot(third_all, ffn_in, preferred_element_type=jnp.float32) + ffn_in_bias  49.3 us
    reduce_scatter x1, waiting for transfers between devices, local(): lax.psum_scatter(jnp.dot(cross_context, cross_out, preferred_element_type...  44.6 us
    reduce_scatter x1, waiting for transfers between devices, local(): lax.psum_scatter(second_part.astype(jnp.bfloat16), 'narrow', scatter_dime...  44.6 us
    dot_general x16, matrix products, masked_scores(): jnp.einsum('qhd,khd->hqk', block_queries, block_keys, preferred_element_t...  44.2 us
    reduce_scatter x1, waiting for transfers between devices, local(): lax.psum_scatter(jnp.dot(hidden, ffn_out, preferred_element_type=jnp.floa...  43.6 us
    psum x1, blocking collectives, local(): lax.psum(jnp.stack([gain_one, gain_two, gain_three, shift_one, shift_two,...  41.8 us
    dot_general x8, matrix products, one_block(): jnp.einsum('hqk,qhd->khd', score_grad, block_queries.astype(jnp.float32),...  40.8 us
  transfers between devices with their start and end apart: 12, of which 10 were waited for; matrix products, arithmetic and copies ran while one was open for 15% of the time, Pallas kernels for 0%

commit v1 on v0

--- a/solution.py
+++ b/solution.py
@@ -1,6 +1,8 @@
 import jax
 import jax.numpy as jnp
 from jax import lax
+from jax.experimental import pallas as pl
+from jax.experimental.pallas import tpu as pltpu
 from jax.sharding import PartitionSpec as P
 
 HEAD_DIM = 64
@@ -138,6 +140,156 @@
         slot_count * key_count, -1
     )
     return (query_grad, key_grad, value_grad)
+
+
+BLOCK = 256
+MIB = 1 << 20
+
+
+def head_mask(shape, head):
+    lane = lax.broadcasted_iota(jnp.int32, shape, len(shape) - 1)
+    return (lane >= head * HEAD_DIM) & (lane < (head + 1) * HEAD_DIM)
+
+
+def pick_head(values, head):
+    return jnp.where(head_mask(values.shape, head), values, jnp.zeros_like(values))
+
+
+def dot_nt(a, b):
+    return lax.dot_general(a, b, (((1,), (1,)), ((), ())), preferred_element_type=jnp.float32)
+
+
+def dot_nn(a, b):
+    return jnp.dot(a, b, preferred_element_type=jnp.float32)
+
+
+def dot_tn(a, b):
+    return lax.dot_general(a, b, (((0,), (0,)), ((), ())), preferred_element_type=jnp.float32)
+
+
+def front_kernel(lens, x_ref, g_ref, s_ref, w_ref, qb_ref, vb_ref, h_ref, q_ref, k_ref, v_ref, c_ref):
+    length = lens[pl.program_id(0)]
+    width = q_ref.shape[1]
+    for i in range(x_ref.shape[0] // BLOCK):
+        rows = pl.ds(i * BLOCK, BLOCK)
+
+        @pl.when(i * BLOCK < length)
+        def _():
+            normed, _, _ = norm_forward(x_ref[rows, :].astype(jnp.float32), g_ref[...], s_ref[...])
+            h1 = normed.astype(jnp.bfloat16)
+            h_ref[rows, :] = h1
+            qkv = dot_nn(h1, w_ref[...])
+            queries = (qkv[:, :width] + qb_ref[...]).astype(jnp.bfloat16)
+            q_ref[rows, :] = queries
+            k_ref[rows, :] = qkv[:, width : 2 * width].astype(jnp.bfloat16)
+            v_ref[rows, :] = (qkv[:, 2 * width :] + vb_ref[...]).astype(jnp.bfloat16)
+            count = (i + 1) * BLOCK
+            keys, values = k_ref[:count, :], v_ref[:count, :]
+            scaled = queries * jnp.bfloat16(HEAD_DIM**-0.5)
+            row = lax.broadcasted_iota(jnp.int32, (BLOCK, count), 0) + i * BLOCK
+            allowed = lax.broadcasted_iota(jnp.int32, (BLOCK, count), 1) <= row
+            total = jnp.zeros((BLOCK, width), jnp.float32)
+            for head in range(width // HEAD_DIM):
+                scores = jnp.where(allowed, dot_nt(pick_head(scaled, head), keys), MASKED_SCORE)
+                weights = jnp.exp(scores - jnp.max(scores, axis=1, keepdims=True))
+                weights = weights * (1.0 / jnp.sum(weights, axis=1, keepdims=True))
+                total += dot_nn(weights.astype(jnp.bfloat16), pick_head(values, head))
+            c_ref[rows, :] = total.astype(jnp.bfloat16)
+
+        @pl.when(i * BLOCK >= length)
+        def _():
+            for ref in (h_ref, q_ref, k_ref, v_ref, c_ref):
+                ref[rows, :] = jnp.zeros((BLOCK, ref.shape[1]), ref.dtype)
+
+
+def front(lengths, units, gain_vec, shift_vec, weights, q_bias, v_bias):
+    rows, width = units.shape
+    slots = lengths.shape[0]
+    slot_rows = rows // slots
+    cols = weights.shape[1] // 3
+    whole = lambda a: pl.BlockSpec(a.shape, lambda s, *_: (0,) * a.ndim)
+    slot = lambda w: pl.BlockSpec((slot_rows, w), lambda s, *_: (s, 0))
+    small = [a.reshape(1, -1) for a in (gain_vec, shift_vec, q_bias, v_bias)]
+    shape = lambda w: jax.ShapeDtypeStruct((rows, w), jnp.bfloat16)
+    return pl.pallas_call(
+        front_kernel,
+        grid_spec=pltpu.PrefetchScalarGridSpec(
+            num_scalar_prefetch=1,
+            grid=(slots,),
+            in_specs=[slot(width), whole(small[0]), whole(small[1]), whole(weights), whole(small[2]), whole(small[3])],
+            out_specs=[slot(width), slot(cols), slot(cols), slot(cols), slot(cols)],
+        ),
+        out_shape=[shape(width), shape(cols), shape(cols), shape(cols), shape(cols)],
+        compiler_params=pltpu.CompilerParams(vmem_limit_bytes=48 * MIB),
+        cost_estimate=pl.CostEstimate(flops=20 * 10**9, bytes_accessed=16 * MIB, transcendentals=8 * MIB),
+        name="front",
+    )(lengths, units, small[0], small[1], weights, small[2], small[3])
+
+
+def back_kernel(lens, q_ref, k_ref, v_ref, dc_ref, o_ref, dk_acc, dv_acc):
+    length = lens[pl.program_id(0)]
+    slot_rows, width = q_ref.shape
+    dk_acc[...] = jnp.zeros_like(dk_acc)
+    dv_acc[...] = jnp.zeros_like(dv_acc)
+    for i in range(slot_rows // BLOCK):
+        rows = pl.ds(i * BLOCK, BLOCK)
+
+        @pl.when(i * BLOCK < length)
+        def _():
+            count = (i + 1) * BLOCK
+            keys, values = k_ref[:count, :], v_ref[:count, :]
+            scaled = q_ref[rows, :] * jnp.bfloat16(HEAD_DIM**-0.5)
+            grads = dc_ref[rows, :]
+            col = lax.broadcasted_iota(jnp.int32, (count, BLOCK), 1) + i * BLOCK
+            allowed = lax.broadcasted_iota(jnp.int32, (count, BLOCK), 0) <= col
+            total = jnp.zeros((BLOCK, width), jnp.float32)
+            for head in range(width // HEAD_DIM):
+                q_head, g_head = pick_head(scaled, head), pick_head(grads, head)
+                scores = jnp.where(allowed, dot_nt(keys, q_head), MASKED_SCORE)
+                weights = jnp.exp(scores - jnp.max(scores, axis=0, keepdims=True))
+                weights = weights * (1.0 / jnp.sum(weights, axis=0, keepdims=True))
+                dv_acc[:count, :] += dot_nn(weights.astype(jnp.bfloat16), g_head)
+                weight_grad = dot_nt(values, g_head)
+                inner = jnp.sum(weights * weight_grad, axis=0, keepdims=True)
+                score_grad = (weights * (weight_grad - inner)).astype(jnp.bfloat16)
+                dk_acc[:count, :] += dot_nn(score_grad, q_head)
+                total += dot_tn(score_grad, pick_head(keys, head))
+            o_ref[rows, :width] = (total * HEAD_DIM**-0.5).astype(jnp.bfloat16)
+
+        @pl.when(i * BLOCK >= length)
+        def _():
+            o_ref[rows, :width] = jnp.zeros((BLOCK, width), jnp.bfloat16)
+
+    o_ref[:, width : 2 * width] = dk_acc[...].astype(jnp.bfloat16)
+    o_ref[:, 2 * width :] = dv_acc[...].astype(jnp.bfloat16)
+
+
+def back(lengths, queries, keys, values, grads):
+    rows, width = queries.shape
+    slots = lengths.shape[0]
+    slot_rows = rows // slots
+    slot = lambda w: pl.BlockSpec((slot_rows, w), lambda s, *_: (s, 0))
+    return pl.pallas_call(
+        back_kernel,
+        grid_spec=pltpu.PrefetchScalarGridSpec(
+            num_scalar_prefetch=1,
+            grid=(slots,),
+            in_specs=[slot(width)] * 4,
+            out_specs=slot(3 * width),
+            scratch_shapes=[pltpu.VMEM((slot_rows, width), jnp.float32)] * 2,
+        ),
+        out_shape=jax.ShapeDtypeStruct((rows, 3 * width), jnp.bfloat16),
+        compiler_params=pltpu.CompilerParams(vmem_limit_bytes=48 * MIB),
+        cost_estimate=pl.CostEstimate(flops=30 * 10**9, bytes_accessed=8 * MIB, transcendentals=8 * MIB),
+        name="back",
+    )(lengths, queries, keys, values, grads)
+
+
+def wide_sum(arrays, after=None):
+    parts = tuple(a.astype(jnp.bfloat16) for a in arrays)
+    if after is not None:
+        parts, after = lax.optimization_barrier((parts, after))
+    return lax.psum(parts, "wide"), after
 
 
 def local(
@@ -189,32 +341,19 @@
         length = lax.dynamic_index_in_dim(text_lengths, slot_id, keepdims=False)
         return jnp.broadcast_to(text_pos[None, :] < length, (query_block, TEXT))
 
-    resid_all = units.astype(jnp.float32)
-    norm_one, normed_all, inv_all = norm_forward(resid_all, norm_gain[0], norm_shift[0])
-    normed_one = lax.dynamic_slice_in_dim(normed_all, first_own, own_rows, 0)
-    inv_one = lax.dynamic_slice_in_dim(inv_all, first_own, own_rows, 0)
-    first_in = norm_one.astype(jnp.bfloat16)
-    projected = jnp.einsum("rd,dcn->rcn", first_in, self_qkv, preferred_element_type=jnp.float32)
-    queries = (projected[:, 0] + self_bias[0]).astype(jnp.bfloat16)
-    key_rows = projected[:, 1].astype(jnp.bfloat16)
-    value_rows = (projected[:, 2] + self_bias[1]).astype(jnp.bfloat16)
-    self_context, self_log = attention_forward(
-        split_heads(queries),
-        split_heads(key_rows),
-        split_heads(value_rows),
-        UNITS,
-        query_block,
-        score_scale,
-        self_allowed,
-    )
-    self_context = self_context.astype(jnp.bfloat16)
+    qkv_weights = self_qkv.reshape(self_qkv.shape[0], -1)
+    first_in, queries, key_rows, value_rows, self_context = front(
+        lengths, units, norm_gain[0], norm_shift[0], qkv_weights, self_bias[0], self_bias[1]
+    )
+    own_units = lax.dynamic_slice_in_dim(units, first_own, own_rows, 0).astype(jnp.float32)
+    _, normed_one, inv_one = norm_forward(own_units, norm_gain[0], norm_shift[0])
     self_sum = lax.psum_scatter(
         jnp.dot(self_context, self_out, preferred_element_type=jnp.float32).astype(jnp.bfloat16),
         "narrow",
         scatter_dimension=0,
         tiled=True,
     ).astype(jnp.float32)
-    resid_one = lax.dynamic_slice_in_dim(resid_all, first_own, own_rows, 0) + self_sum + out_bias[0]
+    resid_one = own_units + self_sum + out_bias[0]
     norm_two, normed_two, inv_two = norm_forward(resid_one, norm_gain[1], norm_shift[1])
     second_all = lax.all_gather(norm_two.astype(jnp.bfloat16), "narrow", axis=0, tiled=True)
     cross_queries = (
@@ -328,28 +467,16 @@
     self_context_grad = jnp.einsum(
         "rd,nd->rn", self_out_all, self_out, preferred_element_type=jnp.float32
     ).astype(jnp.bfloat16)
-    query_grad, key_grad, value_grad = attention_backward(
-        split_heads(queries),
-        split_heads(key_rows),
-        split_heads(value_rows),
-        split_heads(self_context_grad),
-        self_log,
-        UNITS,
-        query_block,
-        score_scale,
-        self_allowed,
-    )
-    qkv_grad = jnp.stack([query_grad, key_grad, value_grad], axis=1).astype(jnp.bfloat16)
-    self_qkv_grad = jnp.einsum(
-        "rd,rcn->dcn", first_in, qkv_grad, preferred_element_type=jnp.float32
-    )
+    qkv_grad = back(lengths, queries, key_rows, value_rows, self_context_grad)
+    self_qkv_grad = dot_tn(first_in, qkv_grad).reshape(self_qkv.shape)
+    cols = queries.shape[1]
     self_bias_grad = jnp.stack(
         [
-            jnp.sum(qkv_grad[:, 0], axis=0, dtype=jnp.float32),
-            jnp.sum(qkv_grad[:, 2], axis=0, dtype=jnp.float32),
+            jnp.sum(qkv_grad[:, :cols], axis=0, dtype=jnp.float32),
+            jnp.sum(qkv_grad[:, 2 * cols :], axis=0, dtype=jnp.float32),
         ]
     )
-    first_part = jnp.einsum("rcn,dcn->rd", qkv_grad, self_qkv, preferred_element_type=jnp.float32)
+    first_part = dot_nt(qkv_grad, qkv_weights)
     first_grad = lax.psum_scatter(
         first_part.astype(jnp.bfloat16), "narrow", scatter_dimension=0, tiled=True
     ).astype(jnp.float32)
@@ -373,31 +500,33 @@
         ),
         ("wide", "narrow"),
     )
+    (ffn_in_grad, ffn_out_grad), _ = wide_sum((ffn_in_grad, ffn_out_grad))
+    (cross_q_grad, cross_kv_grad, cross_out_grad), ffn_in_grad = wide_sum(
+        (cross_q_grad, cross_kv_grad, cross_out_grad), ffn_in_grad
+    )
+    (self_qkv_grad, self_out_grad), cross_q_grad = wide_sum((self_qkv_grad, self_out_grad), cross_q_grad)
+    self_bias_grad, cross_bias_grad, ffn_in_bias_grad = lax.psum(
+        (self_bias_grad, cross_bias_grad, ffn_in_bias_grad), "wide"
+    )
     (
         self_qkv_grad,
-        self_bias_grad,
         self_out_grad,
         cross_q_grad,
         cross_kv_grad,
-        cross_bias_grad,
         cross_out_grad,
         ffn_in_grad,
-        ffn_in_bias_grad,
         ffn_out_grad,
-    ) = lax.psum(
-        (
+    ) = (
+        a.astype(jnp.float32)
+        for a in (
             self_qkv_grad,
-            self_bias_grad,
             self_out_grad,
             cross_q_grad,
             cross_kv_grad,
-            cross_bias_grad,
             cross_out_grad,
             ffn_in_grad,
-            ffn_in_bias_grad,
             ffn_out_grad,
-        ),
-        "wide",
+        )
     )
     return (
         output,

time: 1720 us -> 1270 us (0.74)
  waiting for transfers between devices: 995 us -> 767 us
  matrix products: 378 us -> 224 us
  local copies, waits for them, and re-layouts: 92.1 us -> 45.1 us
  Pallas kernels: 0 us -> 30.6 us
  loops' own time: 54.3 us -> 26.7 us
  other arithmetic: 96.6 us -> 74.8 us
    psum x1 -> x3, waiting for transfers between devices: 666 us -> 407 us  [wide_sum(): return (lax.psum(parts, 'wide'), after)]
    dot_general x16 -> x8, matrix products: 44.2 us -> 9.22 us  [masked_scores(): jnp.einsum('qhd,khd->hqk', block_queries, block_keys, preferred_element_t...]
    dot_general x8 -> x4, matrix products: 39.4 us -> 5.88 us  [one_block(): jnp.einsum('qhd,khd->hqk', block_grad, block_values, preferred_element_ty...]
    reduce_scatter x1, waiting for transfers between devices: 0.01 us -> 30.8 us  [local(): lax.psum_scatter(first_part.astype(jnp.bfloat16), 'narrow', scatter_dimen...]
    pallas_call x0 -> x2, Pallas kernels: none -> 30.6 us  [the longest x1 16.7 us: back(): pl.pallas_call(back_kernel, grid_spec=pltpu.PrefetchScalarGridSpec(num_sc...]
    dot_general x8 -> x4, matrix products: 40.8 us -> 12.1 us  [one_block(): jnp.einsum('hqk,qhd->khd', score_grad, block_queries.astype(jnp.float32),...]
    dot_general x8 -> x4, matrix products: 32.2 us -> 7.1 us  [one_block(): jnp.einsum('hqk,khd->qhd', score_grad, block_keys.astype(jnp.float32), pr...]
    dot_general x8 -> x4, matrix products: 25.9 us -> 8.39 us  [one_block(): jnp.einsum('hqk,qhd->khd', weights.astype(jnp.bfloat16), block_grad, pref...]
  transfers between devices with their start and end apart: 12 -> 14, of which waited for: 10 -> 14; matrix products, arithmetic and copies ran while one was open for 15% -> 10% of each run, Pallas kernels for 0% -> 1%
where the time goes in v1:
time: 1270 us; the launch traced here: 1260 us
  waiting for transfers between devices  767 us (60%)
  matrix products  224 us (18%)
  blocking collectives  78.5 us (6%)
  other arithmetic  74.8 us (6%)
  local copies, waits for them, and re-layouts  45.1 us (4%)
  Pallas kernels  30.6 us (2%)
  loops' own time  26.7 us (2%)
  between operations  15.6 us (1%)
    psum x3, waiting for transfers between devices, wide_sum(): return (lax.psum(parts, 'wide'), after)  407 us
    reduce_scatter x1, waiting for transfers between devices, local(): lax.psum_scatter(jnp.dot(self_context, self_out, preferred_element_type=j...  55.1 us
    dot_general x1, matrix products, local(): jnp.dot(third_all, ffn_in, preferred_element_type=jnp.float32) + ffn_in_bias  49.3 us
    reduce_scatter x1, waiting for transfers between devices, local(): lax.psum_scatter(jnp.dot(hidden, ffn_out, preferred_element_type=jnp.floa...  44.9 us
    reduce_scatter x1, waiting for transfers between devices, local(): lax.psum_scatter(jnp.dot(cross_context, cross_out, preferred_element_type...  44.6 us
    psum x1, blocking collectives, local(): lax.psum(jnp.stack([gain_one, gain_two, gain_three, shift_one, shift_two,...  39.7 us
    psum x1, blocking collectives, local(): lax.psum((self_bias_grad, cross_bias_grad, ffn_in_bias_grad), 'wide')  38.8 us
    all_gather x1, waiting for transfers between devices, local(): lax.all_gather(resid_two_grad.astype(jnp.bfloat16), 'narrow', axis=0, til...  34.5 us
  transfers between devices with their start and end apart: 14, of which 14 were waited for; matrix products, arithmetic and copies ran while one was open for 10% of the time, Pallas kernels for 1%

profile of v1, /device:TPU:0, one launch (start us, length us, event | category | flops | bytes accessed | tf_op | source)
XLA Modules:
  0.0 1264.5 jit_solution(13364142219115033621)
XLA Ops:
  8.0 2.6 copy.77
  12.5 13.9 %front.1 = (bf16[2048,1024]{1,0:T(8,128)(2,1)}, bf16[2048,256]{1,0:T(8,128)(2,1)S(1)}, bf16[2048,256]{1,0:T(8,128)(2,1)S(1)}, bf16[2048,256]{1,0:T(8,128)(2,1)S(1)}, bf16[2048,256]{1,0:T(8,128)(2,1)S(1)}) custom-call(s32[2]{0:T(128)S(1)} %compare_select_fusion.1.lens, bf16[2048,1024]{1,0:T(8,128)(2,1)} %x_ref.1, f32[1,1024]{1,0:T(1,128)S(1)} %get-tuple-element.502.g_ref, ...), custom_call_target="tpu_custom_call" | custom-call | flops 20000000000 | bytes 16777216 | tf_op jit(solution)/shard_map/front/pallas_call | solution.py:214
  30.3 3.3 convolution_convert_fusion.5
  34.9 55.1 %reduce-scatter.8.cloned.1.call-done = bf16[512,1024]{1,0:T(8,128)(2,1)} async-done(((bf16[2048,1024]{1,0:T(8,128)(2,1)}), bf16[512,1024]{1,0:T(8,128)(2,1)}) %reduce-scatter.8.cloned.1.call-update) | async-done | bytes 1048592 | tf_op jit(solution)/shard_map/reduce_scatter | solution.py:350
  90.0 2.0 fusion.79
  92.0 2.8 convert_reduce_fusion.4
  94.8 2.8 add_convert_fusion.2
  100.8 31.5 %all-gather.5.cloned.1.call-done = bf16[2048,1024]{1,0:T(8,128)(2,1)} async-done(((bf16[512,1024]{1,0:T(8,128)(2,1)}), bf16[2048,1024]{1,0:T(8,128)(2,1)}) %all-gather.5.cloned.1.call-update) | async-done | bytes 4194320 | tf_op jit(solution)/shard_map/all_gather | solution.py:358
  132.3 3.6 fusion.53
  137.0 32.7 %while.32 = (s32[]{:T(128)}, bf16[4,512,4,64]{1,3,2,0:T(8,128)(2,1)}, f32[4,4,512]{2,1,0:T(4,128)}, s32[4]{0:T(128)S(1)}, bf16[512,4,64]{0,2,1:T(8,128)(2,1)}, /...) while((s32[]{:T(128)}, ...), condition=%wide.region_7.8_spmd.clone, body=%wide.region_4.7_spmd.clone.sunk | while | flops 140507424 | bytes 8457189 | solution.py:78
  169.7 2.5 copy.80
  173.5 3.3 convolution_convert_fusion.4
  176.9 44.6 %reduce-scatter.10.cloned.1.call-done = bf16[512,1024]{1,0:T(8,128)(2,1)} async-done(((bf16[2048,1024]{1,0:T(8,128)(2,1)}), bf16[512,1024]{1,0:T(8,128)(2,1)}) %reduce-scatter.10.cloned.1.call-update) | async-done | bytes 1048592 | tf_op jit(solution)/shard_map/reduce_scatter | solution.py:375
  221.5 2.2 fusion.93
  227.3 3.7 broadcast_select_fusion
  231.1 30.0 %all-gather.7.cloned.1.call-done = bf16[2048,1024]{1,0:T(8,128)(2,1)} async-done(((bf16[512,1024]{1,0:T(8,128)(2,1)}), bf16[2048,1024]{1,0:T(8,128)(2,1)}) %all-gather.7.cloned.1.call-update) | async-done | bytes 4194320 | tf_op jit(solution)/shard_map/all_gather | solution.py:383
  261.1 49.3 %multiply_convert_fusion = (bf16[2048,2048]{1,0:T(8,128)(2,1)}, f32[2048,2048]{1,0:T(8,128)}, f32[2048,2048]{1,0:T(8,128)}) fusion(f32[2048]{0:T(1024)S(1)} %copy-done.64, bf16[2048,1024]{1,0:T(8,128)(2,1)} %all-gather.7.cloned.1.call-done, bf16[1024,2048]{1,0:T(8,128)(2,1)} %param.38), kind=kOutput, calls=%fused_computation.54 | convolution fusion | flops 8866758656 | bytes 50339840 | tf_op jit(solution)/shard_map/dot_general | solution.py:384
  310.4 22.8 %convert_reduce_fusion = (f32[2048]{0:T(1024)}, bf16[2048,2048]{1,0:T(8,128)(2,1)}) fusion(f32[2048,2048]{1,0:T(8,128)} %get-tuple-element.486, bf16[2048,1024]{1,0:T(8,128)(2,1)S(1)} %copy-done.24, bf16[2048,1024]{1,0:T(8,128)(2,1)} %param.40, f32[2048,2048]{1,0:T(8,128)} %get-tuple-element.511, f32[2048]{0:T(1024)S(1)} %copy-done.64), kind=kOutput, calls=%fused_computation.52 | convolution fusion | flops 8661235712 | bytes 50348032 | tf_op jit(solution)/shard_map/rd,fd->rf/dot_general | solution.py:399
  333.1 14.0 %convolution_convert_fusion.2 = bf16[2048,1024]{1,0:T(8,128)(2,1)} fusion(bf16[2048,2048]{1,0:T(8,128)(2,1)} %get-tuple-element.513, bf16[1024,2048]{1,0:T(8,128)(2,1)} %param.38), kind=kOutput, calls=%fused_computation.71 | convolution fusion | flops 8592031744 | bytes 16777216 | tf_op jit(solution)/shard_map/rf,df->rd/dot_general | solution.py:403
  347.2 13.8 %convolution_convert_fusion.3 = bf16[2048,1024]{1,0:T(8,128)(2,1)} fusion(bf16[2048,2048]{1,0:T(8,128)(2,1)} %get-tuple-element.485, bf16[2048,1024]{1,0:T(8,128)(2,1)} %param.40), kind=kOutput, calls=%fused_computation.72 | convolution fusion | flops 8592031744 | bytes 16777216 | tf_op jit(solution)/shard_map/dot_general | solution.py:388
  362.0 29.8 %reduce-scatter.14.cloned.1.call-done = bf16[512,1024]{1,0:T(8,128)(2,1)} async-done(((bf16[2048,1024]{1,0:T(8,128)(2,1)}), bf16[512,1024]{1,0:T(8,128)(2,1)}) %reduce-scatter.14.cloned.1.call-update) | async-done | bytes 1048592 | tf_op jit(solution)/shard_map/reduce_scatter | solution.py:404
  391.9 2.2 fusion.70
  394.1 44.9 %reduce-scatter.12.cloned.1.call-done = bf16[512,1024]{1,0:T(8,128)(2,1)} async-done(((bf16[2048,1024]{1,0:T(8,128)(2,1)}), bf16[512,1024]{1,0:T(8,128)(2,1)}) %reduce-scatter.12.cloned.1.call-update) | async-done | bytes 1048592 | tf_op jit(solution)/shard_map/reduce_scatter | solution.py:387
  439.0 3.7 fusion.89
  445.2 34.5 %all-gather.9.cloned.1.call-done = bf16[2048,1024]{1,0:T(8,128)(2,1)} async-done(((bf16[512,1024]{1,0:T(8,128)(2,1)}), bf16[2048,1024]{1,0:T(8,128)(2,1)}) %all-gather.9.cloned.1.call-update) | async-done | bytes 4194320 | tf_op jit(solution)/shard_map/all_gather | solution.py:411
  479.7 4.4 convolution_convert_fusion.9
  485.3 64.2 %while.33 = (s32[]{:T(128)}, bf16[4,512,4,64]{1,3,2,0:T(8,128)(2,1)}, f32[4,256,4,64]{1,3,2,0:T(8,128)}, f32[4,256,4,64]{1,3,2,0:T(8,128)}, s32[4]{0:T(128)S(1)}...) while((s32[]{:T(128)}, ...), condition=%wide.region_17.18_spmd.clone, body=%wide.region_15.17_spmd.clone.sunk | while | flops 1012070656 | bytes 19319540 | solution.py:132
  494.7 3.0 fusion.160
  497.8 2.1 fusion.161
  510.7 3.0 fusion.160
  513.7 2.1 fusion.161
  526.6 3.0 fusion.160
  529.7 2.1 fusion.161
  542.6 3.0 fusion.160
  545.6 2.1 fusion.161
  549.5 2.1 copy.81
  551.9 3.3 convolution_convert_fusion.1
  555.3 14.0 %convolution_convert_fusion = bf16[1024,2048]{1,0:T(8,128)(2,1)} fusion(bf16[2048,1024]{1,0:T(8,128)(2,1)} %all-gather.7.cloned.1.call-done, bf16[2048,2048]{1,0:T(8,128)(2,1)} %get-tuple-element.513), kind=kOutput, calls=%fused_computation.69 | convolution fusion | flops 8592031744 | bytes 16777216 | tf_op jit(solution)/shard_map/rd,rf->df/dot_general | solution.py:402
  570.0 29.9 %reduce-scatter.16.cloned.1.call-done = bf16[512,1024]{1,0:T(8,128)(2,1)} async-done(((bf16[2048,1024]{1,0:T(8,128)(2,1)}), bf16[512,1024]{1,0:T(8,128)(2,1)}) %reduce-scatter.16.cloned.1.call-update) | async-done | bytes 1048592 | tf_op jit(solution)/shard_map/reduce_scatter | solution.py:452
  599.9 3.4 fusion.71
  603.3 2.3 fusion.90
  613.0 4.4 convolution_convert_fusion.13
  617.4 4.3 convolution_convert_fusion.12
  621.7 138.6 %all-reduce.6.cloned.1.call-done = bf16[1024,2048]{1,0:T(8,128)(2,1)} async-done(((bf16[1024,2048]{1,0:T(8,128)(2,1)}), bf16[1024,2048]{1,0:T(8,128)(2,1)}) %all-reduce.6.cloned.1.call-update) | async-done | bytes 4194320 | tf_op jit(solution)/shard_map/psum | solution.py:292
  760.5 14.0 %convolution_convert_fusion.7 = bf16[2048,1024]{1,0:T(8,128)(2,1)} fusion(bf16[2048,2048]{1,0:T(8,128)(2,1)} %get-tuple-element.485, bf16[2048,1024]{1,0:T(8,128)(2,1)} %broadcast_select_fusion), kind=kOutput, calls=%fused_computation.76 | convolution fusion | flops 8592031744 | bytes 16777216 | tf_op jit(solution)/shard_map/rf,rd->fd/dot_general | solution.py:398
  776.3 19.6 %all-gather.11.cloned.1.call-done = bf16[2048,1024]{1,0:T(8,128)(2,1)} async-done(((bf16[512,1024]{1,0:T(8,128)(2,1)}), bf16[2048,1024]{1,0:T(8,128)(2,1)}) %all-gather.11.cloned.1.call-update) | async-done | bytes 4194320 | tf_op jit(solution)/shard_map/all_gather | solution.py:463
  796.0 3.5 convolution_convert_fusion.8.dc_ref
  801.9 16.7 %back.1 = bf16[2048,768]{1,0:T(8,128)(2,1)} custom-call(s32[2]{0:T(128)S(1)} %compare_select_fusion.1.lens, bf16[2048,256]{1,0:T(8,128)(2,1)S(1)} %copy-done.6, bf16[2048,256]{1,0:T(8,128)(2,1)S(1)} %copy-done.8, bf16[2048,256]{1,0:T(8,128)(2,1)S(1)} %copy-done.10, bf16[2048,256]{1,0:T(8,128)(2,1)S(1)} %convolution_convert_fusion.8.dc_ref), custom_call_target="tpu_custom_call" | custom-call | flops 30000001024 | bytes 8388608 | tf_op jit(solution)/shard_map/back/pallas_call | solution.py:272
  818.7 2.1 convolution_convert_fusion.14
  822.0 3.5 convolution_convert_fusion.10
  825.6 47.2 %all-reduce.8.cloned.1.call-done = bf16[1024,256]{1,0:T(8,128)(2,1)} async-done(((bf16[1024,256]{1,0:T(8,128)(2,1)}), bf16[1024,256]{1,0:T(8,128)(2,1)}) %all-reduce.8.cloned.1.call-update) | async-done | bytes 524304 | tf_op jit(solution)/shard_map/psum | solution.py:292
  875.8 6.9 convolution_convert_fusion.6
  884.2 6.7 convert_element_type.229
  891.1 8.9 reduce-scatter.20.cloned.1.call-done
  904.7 38.8 %all-reduce = (f32[2,256]{1,0:T(2,128)}, f32[2,256]{1,0:T(2,128)}, f32[2048]{0:T(1024)}) all-reduce(f32[2,256]{1,0:T(2,128)S(1)} %pad_maximum_fusion.3, f32[2,256]{1,0:T(2,128)S(1)} %pad_maximum_fusion.4, f32[2048]{0:T(1024)S(1)} %copy-done.58), channel_id=1, replica_groups=mesh['wide'=8,'narrow'=4] {'wide'}, use_global_device_ids=true, to_apply=%region_44.45 | all-reduce | flops 3072 | bytes 24576 | tf_op jit(solution)/shard_map/psum | solution.py:508
  943.5 221.6 %all-reduce.10.cloned.1.call-done = (bf16[1024,2,256]{0,2,1:T(8,128)(2,1)}, bf16[1024,3,256]{2,0,1:T(8,128)(2,1)}, bf16[256,1024]{1,0:T(8,128)(2,1)}, bf16[256,1024]{1,0:T(8,128)(2,1)}, bf16[2048,1024]{1,0:T(8,128)(2,1)}) async-done(((bf16[1024,2,256]{0,2,1:T(8,128)(2,1)}, bf16[1024,3,256]{2,0,1:T(8,128)(2,1)}, bf16[256,1024]{1,0:T(8,128)(2,1)}, bf16[256,1024]{1,0:T(8,128)(2,1)}, ...) | async-done | bytes 7864336 | tf_op jit(solution)/shard_map/psum | solution.py:292
  1165.1 6.8 convert_element_type.232
  1173.8 2.2 copy.87
  1176.0 2.3 convert_element_type.223
  1178.3 2.1 convert_element_type.228
  1180.4 30.8 %reduce-scatter.18.cloned.1.call-done = bf16[512,1024]{1,0:T(8,128)(2,1)} async-done(((bf16[2048,1024]{1,0:T(8,128)(2,1)}), bf16[512,1024]{1,0:T(8,128)(2,1)}) %reduce-scatter.18.cloned.1.call-update) | async-done | bytes 1048592 | tf_op jit(solution)/shard_map/reduce_scatter | solution.py:480
  1211.2 2.5 fusion.72
  1213.8 39.7 %psum.77 = f32[9,1024]{1,0:T(8,128)S(1)} all-reduce(f32[9,1024]{1,0:T(8,128)S(1)} %stack.62), channel_id=1, replica_groups=mesh['wide'=8,'narrow'=4] {'wide','narrow'}, use_global_device_ids=true, to_apply=%region_38.39 | all-reduce | flops 9216 | bytes 73728 | tf_op jit(solution)/shard_map/psum | solution.py:487
  1254.1 3.6 fusion.59
  (286 shorter events, 96.2 us)
Async XLA Ops:
  7.2 90.6 %copy-start = (bf16[512,1024]{1,0:T(8,128)(2,1)S(1)}, bf16[512,1024]{1,0:T(8,128)(2,1)}, u32[]{:S(2)}) copy-start(bf16[512,1024]{1,0:T(8,128)(2,1)} %param.24) | copy-start | bytes 3145732
  7.2 82.8 %reduce-scatter.8.cloned.1.call-start = ((), (), s32[]{:S(2)}) async-start(), calls=%async_computation.7 | async-start | bytes 5242880 | tf_op jit(solution)/shard_map/reduce_scatter | solution.py:350
  8.0 4.4 copy-start.60
  8.0 4.4 copy-start.55
  8.0 4.4 copy-start.56
  8.0 4.4 copy-start.65
  12.4 13.9 %copy-start.3 = (f32[1,1024]{1,0:T(1,128)}, f32[1,1024]{1,0:T(1,128)S(1)}, u32[]{:S(2)}) copy-start(f32[1,1024]{1,0:T(1,128)S(1)} %get-tuple-element.502.g_ref) | copy-start | bytes 12292
  12.4 82.4 %copy-start.41 = (f32[1,1024]{1,0:T(1,128)}, f32[1,1024]{1,0:T(1,128)S(1)}, u32[]{:S(2)}) copy-start(f32[1,1024]{1,0:T(1,128)S(1)} %get-tuple-element.503) | copy-start | bytes 12292
  12.4 211.7 %copy-start.43 = (f32[1,1024]{1,0:T(1,128)}, f32[1,1024]{1,0:T(1,128)S(1)}, u32[]{:S(2)}) copy-start(f32[1,1024]{1,0:T(1,128)S(1)} %get-tuple-element.501) | copy-start | bytes 12292
  12.5 17.8 %copy-start.34 = (bf16[256,1024]{1,0:T(8,128)(2,1)S(1)}, bf16[256,1024]{1,0:T(8,128)(2,1)}, u32[]{:S(2)}) copy-start(bf16[256,1024]{1,0:T(8,128)(2,1)} %param.33) | copy-start | bytes 1572868
  33.6 98.7 %all-gather.5.cloned.1.call-start = ((), (), s32[]{:S(2)}) async-start(), calls=%async_computation.8 | async-start | bytes 5242880 | tf_op jit(solution)/shard_map/all_gather | solution.py:358
  34.9 186.6 %copy-start.39 = (f32[1,1024]{1,0:T(1,128)}, f32[1,1024]{1,0:T(1,128)S(1)}, u32[]{:S(2)}) copy-start(f32[1,1024]{1,0:T(1,128)S(1)} %get-tuple-element.499) | copy-start | bytes 12292
  90.0 4.9 copy-start.13
  92.0 5.7 copy-start.47
  94.8 4.9 copy-start.51
  97.7 2.2 copy-start.61
  97.7 123.8 %reduce-scatter.10.cloned.1.call-start = ((), (), s32[]{:S(2)}) async-start(), calls=%async_computation.9 | async-start | bytes 5242880 | tf_op jit(solution)/shard_map/reduce_scatter | solution.py:375
  132.3 4.7 copy-start.66
  169.7 7.1 copy-start.15
  169.7 7.1 copy-start.21
  169.7 3.8 copy-start.31
  176.8 84.2 %all-gather.7.cloned.1.call-start = ((), (), s32[]{:S(2)}) async-start(), calls=%async_computation.10 | async-start | bytes 5242880 | tf_op jit(solution)/shard_map/all_gather | solution.py:383
  226.4 165.5 %reduce-scatter.14.cloned.1.call-start = ((), (), s32[]{:S(2)}) async-start(), calls=%async_computation.12 | async-start | bytes 5242880 | tf_op jit(solution)/shard_map/reduce_scatter | solution.py:404
  227.3 33.7 %copy-start.64 = (f32[2048]{0:T(1024)S(1)}, f32[2048]{0:T(1024)}, u32[]{:S(2)}) copy-start(f32[2048]{0:T(1024)} %param.39) | copy-start | bytes 24580
  261.0 49.3 %copy-start.24 = (bf16[2048,1024]{1,0:T(8,128)(2,1)S(1)}, bf16[2048,1024]{1,0:T(8,128)(2,1)}, u32[]{:S(2)}) copy-start(bf16[2048,1024]{1,0:T(8,128)(2,1)} %broadcast_select_fusion) | copy-start | bytes 12582916
  347.2 91.8 %reduce-scatter.12.cloned.1.call-start = ((), (), s32[]{:S(2)}) async-start(), calls=%async_computation.11 | async-start | bytes 5242880 | tf_op jit(solution)/shard_map/reduce_scatter | solution.py:387
  361.0 30.8 %copy-start.12 = (f32[512,1024]{1,0:T(8,128)S(1)}, f32[512,1024]{1,0:T(8,128)}, u32[]{:S(2)}) copy-start(f32[512,1024]{1,0:T(8,128)} %copy-done.11) | copy-start | bytes 6291460
  361.0 30.8 %copy-start.44 = (f32[1,1024]{1,0:T(1,128)S(1)}, f32[1,1024]{1,0:T(1,128)}, u32[]{:S(2)}) copy-start(f32[1,1024]{1,0:T(1,128)} %copy-done.43) | copy-start | bytes 12292
  361.0 30.8 %copy-start.46 = (f32[512]{0:T(512)S(1)}, f32[512]{0:T(512)}, u32[]{:S(2)}) copy-start(f32[512]{0:T(512)} %copy-done.45) | copy-start | bytes 6148
  361.1 30.8 %copy-start.50 = (f32[512]{0:T(512)S(1)}, f32[512]{0:T(512)}, u32[]{:S(2)}) copy-start(f32[512]{0:T(512)} %copy-done.49) | copy-start | bytes 6148
  361.1 77.9 %copy-start.53 = (f32[1,1024]{1,0:T(1,128)S(1)}, f32[1,1024]{1,0:T(1,128)}, u32[]{:S(2)}) copy-start(f32[1,1024]{1,0:T(1,128)} %get-tuple-element.498) | copy-start | bytes 12292
  361.1 118.6 %all-gather.9.cloned.1.call-start = ((), (), s32[]{:S(2)}) async-start(), calls=%async_computation.13 | async-start | bytes 5242880 | tf_op jit(solution)/shard_map/all_gather | solution.py:411
  442.6 37.1 %copy-start.32 = (bf16[256,1024]{1,0:T(8,128)(2,1)S(1)}, bf16[256,1024]{1,0:T(8,128)(2,1)}, u32[]{:S(2)}) copy-start(bf16[256,1024]{1,0:T(8,128)(2,1)} %param.37) | copy-start | bytes 1572868
  445.1 154.8 %reduce-scatter.16.cloned.1.call-start = ((), (), s32[]{:S(2)}) async-start(), calls=%async_computation.14 | async-start | bytes 5242880 | tf_op jit(solution)/shard_map/reduce_scatter | solution.py:452
  445.2 40.1 %copy-start.16 = (bf16[512,4,64]{0,2,1:T(8,128)(2,1)S(1)}, bf16[512,4,64]{0,2,1:T(8,128)(2,1)}, u32[]{:S(2)}) copy-start(bf16[512,4,64]{0,2,1:T(8,128)(2,1)} %copy-done.15) | copy-start | bytes 786436
  445.2 40.1 %copy-start.67 = (s32[2]{0:T(128)S(1)}, s32[2]{0:T(128)}, u32[]{:S(2)}) copy-start(s32[2]{0:T(128)} %param.27) | copy-start | bytes 28
  549.5 2.4 copy-start.33
  555.2 205.2 %all-reduce.6.cloned.1.call-start = ((), (), s32[]{:S(2)}) async-start(), calls=%async_computation.18 | async-start | bytes 8388608 | tf_op jit(solution)/shard_map/psum | solution.py:292
  569.3 30.6 %copy-start.14 = (bf16[512,1024]{1,0:T(8,128)(2,1)S(1)}, bf16[512,1024]{1,0:T(8,128)(2,1)}, u32[]{:S(2)}) copy-start(bf16[512,1024]{1,0:T(8,128)(2,1)} %reduce-scatter.8.cloned.1.call-done) | copy-start | bytes 3145732
  569.3 30.6 %copy-start.40 = (f32[1,1024]{1,0:T(1,128)S(1)}, f32[1,1024]{1,0:T(1,128)}, u32[]{:S(2)}) copy-start(f32[1,1024]{1,0:T(1,128)} %copy-done.39) | copy-start | bytes 12292
  569.3 30.6 %copy-start.42 = (f32[1,1024]{1,0:T(1,128)S(1)}, f32[1,1024]{1,0:T(1,128)}, u32[]{:S(2)}) copy-start(f32[1,1024]{1,0:T(1,128)} %copy-done.41) | copy-start | bytes 12292
  569.3 30.6 %copy-start.48 = (f32[512]{0:T(512)S(1)}, f32[512]{0:T(512)}, u32[]{:S(2)}) copy-start(f32[512]{0:T(512)} %copy-done.47) | copy-start | bytes 6148
  569.3 30.6 %copy-start.52 = (f32[512]{0:T(512)S(1)}, f32[512]{0:T(512)}, u32[]{:S(2)}) copy-start(f32[512]{0:T(512)} %copy-done.51) | copy-start | bytes 6148
  569.4 226.6 %all-gather.11.cloned.1.call-start = ((), (), s32[]{:S(2)}) async-start(), calls=%async_computation.15 | async-start | bytes 5242880 | tf_op jit(solution)/shard_map/all_gather | solution.py:463
  599.9 3.4 copy-start.18
  599.9 3.4 copy-start.26
  608.1 264.7 %all-reduce.8.cloned.1.call-start = ((), (), s32[]{:S(2)}) async-start(), calls=%async_computation.19 | async-start | bytes 1048576 | tf_op jit(solution)/shard_map/psum | solution.py:292
  613.0 4.4 copy-start.23
  760.4 14.1 %copy-start.38 = (bf16[2,256,256]{2,1,0:T(8,128)(2,1)S(1)}, bf16[2,256,256]{2,1,0:T(8,128)(2,1)}, u32[]{:S(2)}) copy-start(bf16[2,256,256]{2,1,0:T(8,128)(2,1)} %copy-done.37) | copy-start | bytes 786436
  760.4 14.1 %copy-start.63 = (bf16[1024,2,256]{2,1,0:T(2,128)(2,1)S(1)}, bf16[1024,2,256]{2,1,0:T(2,128)(2,1)}, u32[]{:S(2)}) copy-start(bf16[1024,2,256]{2,1,0:T(2,128)(2,1)} %param.35) | copy-start | bytes 3145732
  760.4 139.5 %reduce-scatter.20.cloned.1.call-start = ((), (), s32[]{:S(2)}) async-start(), calls=%async_computation.17 | async-start | bytes 1310720 | tf_op jit(solution)/shard_map/reduce_scatter | solution.py:455
  774.5 21.5 %copy-start.35 = (bf16[256,1024]{1,0:T(8,128)(2,1)S(1)}, bf16[256,1024]{1,0:T(8,128)(2,1)}, u32[]{:S(2)}) copy-start(bf16[256,1024]{1,0:T(8,128)(2,1)} %param.33) | copy-start | bytes 1572868
  776.3 23.2 %copy-start.6 = (bf16[2048,256]{1,0:T(8,128)(2,1)S(1)}, bf16[2048,256]{1,0:T(8,128)(2,1)}, u32[]{:S(2)}) copy-start(bf16[2048,256]{1,0:T(8,128)(2,1)} %copy-done.5) | copy-start | bytes 3145732
  776.3 388.8 %all-reduce.10.cloned.1.call-start = ((), (), s32[]{:S(2)}) async-start(), calls=%async_computation.20 | async-start | bytes 15728640 | tf_op jit(solution)/shard_map/psum | solution.py:292
  801.9 16.7 %copy-start.2 = (bf16[2048,256]{1,0:T(8,128)(2,1)S(1)}, bf16[2048,256]{1,0:T(8,128)(2,1)}, u32[]{:S(2)}) copy-start(bf16[2048,256]{1,0:T(8,128)(2,1)} %copy-done.1) | copy-start | bytes 3145732
  801.9 16.7 %copy-start.62 = (bf16[2048,1024]{1,0:T(8,128)(2,1)S(1)}, bf16[2048,1024]{1,0:T(8,128)(2,1)}, u32[]{:S(2)}) copy-start(bf16[2048,1024]{1,0:T(8,128)(2,1)} %all-gather.11.cloned.1.call-done) | copy-start | bytes 12582916
  818.7 2.1 copy-start.29
  818.7 3.3 copy-start.68
  874.4 336.8 %reduce-scatter.18.cloned.1.call-start = ((), (), s32[]{:S(2)}) async-start(), calls=%async_computation.16 | async-start | bytes 5242880 | tf_op jit(solution)/shard_map/reduce_scatter | solution.py:480
  884.2 17.5 %copy-start.36 = (bf16[1024,256]{1,0:T(8,128)(2,1)S(1)}, bf16[1024,256]{1,0:T(8,128)(2,1)}, u32[]{:S(2)}) copy-start(bf16[1024,256]{1,0:T(8,128)(2,1)} %all-reduce.8.cloned.1.call-done) | copy-start | bytes 1572868
  890.9 13.7 %copy-start.58 = (f32[2048]{0:T(1024)S(1)}, f32[2048]{0:T(1024)}, u32[]{:S(2)}) copy-start(f32[2048]{0:T(1024)} %get-tuple-element.512) | copy-start | bytes 24580
  1165.1 6.8 copy-start.28
  1173.8 37.4 %copy-start.4 = (f32[1,1024]{1,0:T(1,128)S(1)}, f32[1,1024]{1,0:T(1,128)}, u32[]{:S(2)}) copy-start(f32[1,1024]{1,0:T(1,128)} %copy-done.3) | copy-start | bytes 12292
  1176.0 78.2 %copy-start.20 = (f32[512,1024]{1,0:T(8,128)S(1)}, f32[512,1024]{1,0:T(8,128)}, u32[]{:S(2)}) copy-start(f32[512,1024]{1,0:T(8,128)} %copy-done.19) | copy-start | bytes 6291460
  (22 other events, 27.2 us)
Sparse Core Ops, SparseCore 0:
  33.7 56.2 reduce-scatter.7
  97.8 34.4 all-gather.4
  176.9 44.5 reduce-scatter.9
  226.5 34.4 all-gather.6
  347.3 44.5 reduce-scatter.13
  394.4 44.5 reduce-scatter.11
  445.2 34.4 all-gather.8
  555.3 44.4 reduce-scatter.15
  604.0 156.3 all-reduce.5
  762.5 33.4 all-gather.10
  800.4 72.3 all-reduce.7
  875.7 24.1 reduce-scatter.19
  906.7 258.4 all-reduce.9
  1167.7 43.5 reduce-scatter.17

commit v2 on v1

--- a/solution.py
+++ b/solution.py
@@ -144,6 +144,9 @@
 
 BLOCK = 256
 MIB = 1 << 20
+NARROW = 4
+STEPS = 8
+MESH = pl.DeviceIdType.MESH
 
 
 def head_mask(shape, head):
@@ -283,6 +286,235 @@
         cost_estimate=pl.CostEstimate(flops=30 * 10**9, bytes_accessed=8 * MIB, transcendentals=8 * MIB),
         name="back",
     )(lengths, queries, keys, values, grads)
+
+
+def place():
+    index = lax.axis_index("narrow")
+    core = index + 1 - 2 * (index % 2)
+    return index, core, (index + 2) % NARROW, (core + 2) % NARROW
+
+
+def greet():
+    _, core, cross, _ = place()
+    barrier = pltpu.get_barrier_semaphore()
+    for peer in (core, cross):
+        pl.semaphore_signal(barrier, inc=1, device_id={"narrow": peer}, device_id_type=MESH)
+    pl.semaphore_wait(barrier, 2)
+
+
+def remote(source, target, sems, kind, step, peer):
+    return pltpu.make_async_remote_copy(
+        src_ref=source,
+        dst_ref=target,
+        send_sem=sems.at[0, kind, step],
+        recv_sem=sems.at[1, kind, step],
+        device_id={"narrow": peer},
+        device_id_type=MESH,
+    )
+
+
+class Hop:
+    KINDS = 6
+
+    def __init__(self, part, from_core, to_cross, from_cross, full, sems, chunk):
+        self.part, self.from_core, self.to_cross, self.from_cross = part, from_core, to_cross, from_cross
+        self.full, self.sems, self.chunk = full, sems, chunk
+        self.own = part.shape[0] // NARROW
+        self.index, self.core, self.cross, self.diagonal = place()
+
+    def rows(self, owner, step):
+        return pl.ds(pl.multiple_of(owner * self.own + step * self.chunk, self.chunk), self.chunk)
+
+    def own_rows(self, step):
+        return pl.ds(pl.multiple_of(step * self.chunk, self.chunk), self.chunk)
+
+    def core_copies(self, step):
+        return [
+            remote(self.part.at[self.rows(owner, step)], self.from_core.at[step, slot], self.sems, slot, step, self.core)
+            for slot, owner in enumerate((self.core, self.diagonal))
+        ]
+
+    def cross_copy(self, step):
+        return remote(self.to_cross.at[step], self.from_cross.at[step], self.sems, 2, step, self.cross)
+
+    def gather_copy(self, step, kind):
+        owner = self.cross if kind == 5 else self.index
+        rows = self.full.at[self.rows(owner, step)]
+        return remote(rows, rows, self.sems, kind, step, self.cross if kind == 3 else self.core)
+
+    def send_core(self, step):
+        for copy in self.core_copies(step):
+            copy.start()
+
+    def send_cross(self, step):
+        for copy in self.core_copies(step):
+            copy.wait_recv()
+        total = self.part[self.rows(self.cross, step), :].astype(jnp.float32)
+        total += self.from_core[step, 1].astype(jnp.float32)
+        self.to_cross[step] = total.astype(jnp.bfloat16)
+        self.cross_copy(step).start()
+
+    def result(self, step):
+        total = self.part[self.rows(self.index, step), :].astype(jnp.float32)
+        total += self.from_core[step, 0].astype(jnp.float32)
+        self.cross_copy(step).wait_recv()
+        return total + self.from_cross[step].astype(jnp.float32)
+
+    def send_gather(self, step, values):
+        self.full[self.rows(self.index, step), :] = values
+        self.gather_copy(step, 3).start()
+        self.gather_copy(step, 4).start()
+
+    def forward(self, step):
+        self.gather_copy(step, 3).wait_recv()
+        self.gather_copy(step, 5).start()
+
+    def gathered(self, step):
+        self.gather_copy(step, 4).wait_recv()
+        self.gather_copy(step, 5).wait_recv()
+
+    def finish(self, step, gather=True):
+        for copy in self.core_copies(step):
+            copy.wait_send()
+        self.cross_copy(step).wait_send()
+        if gather:
+            for kind in (3, 4, 5):
+                self.gather_copy(step, kind).wait_send()
+
+    def take(self, ref, step):
+        return jnp.concatenate([ref[self.rows(owner, step), :] for owner in range(NARROW)], axis=0)
+
+    def put(self, ref, step, values):
+        for owner in range(NARROW):
+            ref[self.rows(owner, step), :] = values[owner * self.chunk : (owner + 1) * self.chunk]
+
+
+def hop_scratch(own, chunk, width):
+    steps = own // chunk
+    return [
+        pltpu.VMEM((steps, 2, chunk, width), jnp.bfloat16),
+        pltpu.VMEM((steps, chunk, width), jnp.bfloat16),
+        pltpu.VMEM((steps, chunk, width), jnp.bfloat16),
+        pltpu.SemaphoreType.DMA((2, Hop.KINDS, steps)),
+    ]
+
+
+def stages(steps, work):
+    def body(tick, carry):
+        for delay, stage in enumerate(work):
+            step = tick - delay
+
+            @pl.when((step >= 0) & (step < steps))
+            def _():
+                stage(step)
+
+        return carry
+
+    lax.fori_loop(0, steps + len(work) - 1, body, 0)
+
+
+def middle_kernel(
+    c1, units, text, vec, bias, keep, so_w, cq_w, kv_w, co_w,
+    h2, h3, q2, c2, kv2, x1, x2,
+    part1, part2, core1, tox1, fromx1, sem1, core2, tox2, fromx2, sem2,
+):
+    steps, chunk, width = tox1.shape
+    cols = q2.shape[1]
+    slots = keep.shape[0]
+    texts = text.shape[0] // slots
+    greet()
+    one = Hop(part1, core1, tox1, fromx1, h2, sem1, chunk)
+    two = Hop(part2, core2, tox2, fromx2, h3, sem2, chunk)
+    scale = jnp.bfloat16(HEAD_DIM**-0.5)
+
+    def project(step):
+        one.put(part1, step, dot_nn(one.take(c1, step), so_w[...]).astype(jnp.bfloat16))
+        one.send_core(step)
+
+        @pl.when(step == 1)
+        def _():
+            both = dot_nn(text[...], kv_w[...])
+            kv2[:, :cols] = both[:, :cols].astype(jnp.bfloat16)
+            kv2[:, cols:] = (both[:, cols:] + bias[1:2, :]).astype(jnp.bfloat16)
+
+    def norm_one(step):
+        rows = one.own_rows(step)
+        resid = units[rows, :].astype(jnp.float32) + one.result(step) + vec[2:3, :]
+        x1[rows, :] = resid
+        one.send_gather(step, norm_forward(resid, vec[0:1, :], vec[1:2, :])[0].astype(jnp.bfloat16))
+
+    def cross(step):
+        one.gathered(step)
+        queries = (dot_nn(one.take(h2, step), cq_w[...]) + bias[0:1, :]).astype(jnp.bfloat16)
+        one.put(q2, step, queries)
+        scaled = queries * scale
+        count = queries.shape[0] // slots
+        context = []
+        for slot in range(slots):
+            mine = scaled[slot * count : (slot + 1) * count]
+            keys = kv2[slot * texts : (slot + 1) * texts, :cols]
+            values = kv2[slot * texts : (slot + 1) * texts, cols:]
+            total = jnp.zeros((count, cols), jnp.float32)
+            for head in range(cols // HEAD_DIM):
+                scores = dot_nt(pick_head(mine, head), keys)
+                scores = jnp.where(keep[slot : slot + 1, :] > 0.5, scores, MASKED_SCORE)
+                weights = jnp.exp(scores - jnp.max(scores, axis=1, keepdims=True))
+                weights = weights * (1.0 / jnp.sum(weights, axis=1, keepdims=True))
+                total += dot_nn(weights.astype(jnp.bfloat16), pick_head(values, head))
+            context.append(total.astype(jnp.bfloat16))
+        context = jnp.concatenate(context, axis=0)
+        one.put(c2, step, context)
+        two.put(part2, step, dot_nn(context, co_w[...]).astype(jnp.bfloat16))
+        two.send_core(step)
+
+    def norm_two(step):
+        rows = one.own_rows(step)
+        resid = x1[rows, :] + two.result(step) + vec[5:6, :]
+        x2[rows, :] = resid
+        two.send_gather(step, norm_forward(resid, vec[3:4, :], vec[4:5, :])[0].astype(jnp.bfloat16))
+
+    stages(
+        steps,
+        [
+            project, one.send_cross, norm_one, one.forward, cross,
+            two.send_cross, norm_two, two.forward, two.gathered,
+        ],
+    )
+
+    def finish(step, carry):
+        one.finish(step)
+        two.finish(step)
+        return carry
+
+    lax.fori_loop(0, steps, finish, 0)
+
+
+def middle(c1, units_own, text, vec, bias, keep, so_w, cq_w, kv_w, co_w):
+    rows, cols = c1.shape
+    own, width = units_own.shape
+    chunk = own // STEPS
+    bf, f32 = jnp.bfloat16, jnp.float32
+    shape = jax.ShapeDtypeStruct
+    vmem = pl.BlockSpec(memory_space=pltpu.VMEM)
+    hop = hop_scratch(own, chunk, width)
+    return pl.pallas_call(
+        middle_kernel,
+        in_specs=[vmem] * 10,
+        out_specs=[vmem] * 7,
+        out_shape=[
+            shape((rows, width), bf),
+            shape((rows, width), bf),
+            shape((rows, cols), bf),
+            shape((rows, cols), bf),
+            shape((text.shape[0], 2 * cols), bf),
+            shape((own, width), f32),
+            shape((own, width), f32),
+        ],
+        scratch_shapes=[pltpu.VMEM((rows, width), bf)] * 2 + hop + hop,
+        compiler_params=pltpu.CompilerParams(collective_id=0, has_side_effects=True, vmem_limit_bytes=58 * MIB),
+        cost_estimate=pl.CostEstimate(flops=100 * 10**9, bytes_accessed=24 * MIB, transcendentals=4 * MIB),
+        name="middle",
+    )(c1, units_own, text, vec, bias, keep, so_w, cq_w, kv_w, co_w)
 
 
 def wide_sum(arrays, after=None):
@@ -347,40 +579,25 @@
     )
     own_units = lax.dynamic_slice_in_dim(units, first_own, own_rows, 0).astype(jnp.float32)
     _, normed_one, inv_one = norm_forward(own_units, norm_gain[0], norm_shift[0])
-    self_sum = lax.psum_scatter(
-        jnp.dot(self_context, self_out, preferred_element_type=jnp.float32).astype(jnp.bfloat16),
-        "narrow",
-        scatter_dimension=0,
-        tiled=True,
-    ).astype(jnp.float32)
-    resid_one = own_units + self_sum + out_bias[0]
-    norm_two, normed_two, inv_two = norm_forward(resid_one, norm_gain[1], norm_shift[1])
-    second_all = lax.all_gather(norm_two.astype(jnp.bfloat16), "narrow", axis=0, tiled=True)
-    cross_queries = (
-        jnp.dot(second_all, cross_q, preferred_element_type=jnp.float32) + cross_bias[0]
-    ).astype(jnp.bfloat16)
-    text_proj = jnp.einsum("td,dcn->tcn", text, cross_kv, preferred_element_type=jnp.float32)
-    text_keys = text_proj[:, 0].astype(jnp.bfloat16)
-    text_values = (text_proj[:, 1] + cross_bias[1]).astype(jnp.bfloat16)
-    cross_context, cross_log = attention_forward(
-        split_heads(cross_queries),
-        split_heads(text_keys),
-        split_heads(text_values),
-        TEXT,
-        query_block,
-        score_scale,
-        cross_allowed,
-    )
-    cross_context = cross_context.astype(jnp.bfloat16)
-    cross_sum = lax.psum_scatter(
-        jnp.dot(cross_context, cross_out, preferred_element_type=jnp.float32).astype(jnp.bfloat16),
-        "narrow",
-        scatter_dimension=0,
-        tiled=True,
-    ).astype(jnp.float32)
-    resid_two = resid_one + cross_sum + out_bias[1]
-    norm_three, normed_three, inv_three = norm_forward(resid_two, norm_gain[2], norm_shift[2])
-    third_all = lax.all_gather(norm_three.astype(jnp.bfloat16), "narrow", axis=0, tiled=True)
+    vec = jnp.stack(
+        [norm_gain[1], norm_shift[1], out_bias[0], norm_gain[2], norm_shift[2], out_bias[1], out_bias[2], out_bias[2]]
+    )
+    keep = (text_pos[None, :] < text_lengths[:, None]).astype(jnp.float32)
+    second_all, third_all, cross_queries, cross_context, text_kv, resid_one, resid_two = middle(
+        self_context,
+        lax.dynamic_slice_in_dim(units, first_own, own_rows, 0),
+        text,
+        vec,
+        cross_bias,
+        keep,
+        self_out,
+        cross_q,
+        cross_kv.reshape(cross_kv.shape[0], -1),
+        cross_out,
+    )
+    text_keys, text_values = jnp.split(text_kv, 2, axis=1)
+    _, normed_two, inv_two = norm_forward(resid_one, norm_gain[1], norm_shift[1])
+    _, normed_three, inv_three = norm_forward(resid_two, norm_gain[2], norm_shift[2])
     hidden_pre = jnp.dot(third_all, ffn_in, preferred_element_type=jnp.float32) + ffn_in_bias
     hidden_full, gate_pullback = jax.vjp(smooth_gate, hidden_pre)
     hidden = hidden_full.astype(jnp.bfloat16)
@@ -417,6 +634,15 @@
     cross_context_grad = jnp.einsum(
         "rd,nd->rn", cross_out_all, cross_out, preferred_element_type=jnp.float32
     ).astype(jnp.bfloat16)
+    _, cross_log = attention_forward(
+        split_heads(cross_queries),
+        split_heads(text_keys),
+        split_heads(text_values),
+        TEXT,
+        query_block,
+        score_scale,
+        cross_allowed,
+    )
     cross_query_grad, text_key_grad, text_value_grad = attention_backward(
         split_heads(cross_queries),
         split_heads(text_keys),

time: 1270 us -> 1030 us (0.81)
  waiting for transfers between devices: 767 us -> 448 us
  Pallas kernels: 30.6 us -> 131 us
    pallas_call x0 -> x1, Pallas kernels: none -> 107 us  [middle(): pl.pallas_call(middle_kernel, in_specs=[vmem] * 10, out_specs=[vmem] * 7,...]
    reduce_scatter x2 -> x0, waiting for transfers between devices: 99.7 us -> none  [the longest x1 55.1 us: local(): lax.psum_scatter(jnp.dot(self_context, self_out, preferred_element_type=j...]
    psum x3, waiting for transfers between devices: 407 us -> 338 us  [wide_sum(): return (lax.psum(parts, 'wide'), after)]
    all_gather x2 -> x0, waiting for transfers between devices: 61.5 us -> none  [the longest x1 31.5 us: local(): lax.all_gather(norm_two.astype(jnp.bfloat16), 'narrow', axis=0, tiled=True)]
    all_gather x1, waiting for transfers between devices: 34.5 us -> 2.75 us  [local(): lax.all_gather(resid_two_grad.astype(jnp.bfloat16), 'narrow', axis=0, til...]
    reduce_scatter x1, waiting for transfers between devices: 30.8 us -> 0.01 us  [local(): lax.psum_scatter(first_part.astype(jnp.bfloat16), 'narrow', scatter_dimen...]
    all_gather x1, waiting for transfers between devices: 19.6 us -> 0.02 us  [local(): lax.all_gather(resid_one_grad.astype(jnp.bfloat16), 'narrow', axis=0, til...]
    dot_general x8 -> x0, matrix products: 17.8 us -> none  [the longest x4 5.64 us: one_block(): jnp.einsum('hqk,khd->qhd', weights, block_values, preferred_element_type=...]
  transfers between devices with their start and end apart: 14 -> 10, of which waited for: 14 -> 7; matrix products, arithmetic and copies ran while one was open for 10% -> 13% of each run, Pallas kernels for 1% -> 1%
where the time goes in v2:
time: 1030 us; the launch traced here: 1020 us
  waiting for transfers between devices  448 us (43%)
  matrix products  213 us (21%)
  Pallas kernels  131 us (13%)
  blocking collectives  76.9 us (7%)
  other arithmetic  64.4 us (6%)
  local copies, waits for them, and re-layouts  44.1 us (4%)
  loops' own time  26.9 us (3%)
  between operations  17.1 us (2%)
    psum x3, waiting for transfers between devices, wide_sum(): return (lax.psum(parts, 'wide'), after)  338 us
    pallas_call x1, Pallas kernels, middle(): pl.pallas_call(middle_kernel, in_specs=[vmem] * 10, out_specs=[vmem] * 7,...  107 us
    dot_general x1, matrix products, local(): jnp.dot(third_all, ffn_in, preferred_element_type=jnp.float32) + ffn_in_bias  49.3 us
    reduce_scatter x1, waiting for transfers between devices, local(): lax.psum_scatter(jnp.dot(hidden, ffn_out, preferred_element_type=jnp.floa...  44.4 us
    psum x1, blocking collectives, local(): lax.psum(jnp.stack([gain_one, gain_two, gain_three, shift_one, shift_two,...  39.4 us
    psum x1, blocking collectives, local(): lax.psum((self_bias_grad, cross_bias_grad, ffn_in_bias_grad), 'wide')  37.4 us
    reduce_scatter x1, waiting for transfers between devices, local(): lax.psum_scatter(third_part.astype(jnp.bfloat16), 'narrow', scatter_dimen...  34.6 us
    reduce_scatter x1, waiting for transfers between devices, local(): lax.psum_scatter(second_part.astype(jnp.bfloat16), 'narrow', scatter_dime...  28.3 us
  transfers between devices with their start and end apart: 10, of which 7 were waited for; matrix products, arithmetic and copies ran while one was open for 13% of the time, Pallas kernels for 1%

profile of v2, /device:TPU:0, one launch (start us, length us, event | category | flops | bytes accessed | tf_op | source)
XLA Modules:
  0.0 1021.9 jit_solution(14647431360477939885)
XLA Ops:
  10.4 2.6 copy.79
  16.8 2.9 convert_reduce_fusion.4
  19.7 3.8 broadcast_select_fusion
  23.4 11.7 %front.1 = (bf16[2048,1024]{1,0:T(8,128)(2,1)}, bf16[2048,256]{1,0:T(8,128)(2,1)S(1)}, bf16[2048,256]{1,0:T(8,128)(2,1)S(1)}, bf16[2048,256]{1,0:T(8,128)(2,1)S(1)}, bf16[2048,256]{1,0:T(8,128)(2,1)S(1)}) custom-call(s32[2]{0:T(128)S(1)} %compare_select_fusion.1.lens, bf16[2048,1024]{1,0:T(8,128)(2,1)} %x_ref.1, f32[1,1024]{1,0:T(1,128)S(1)} %get-tuple-element.508.g_ref, ...), custom_call_target="tpu_custom_call" | custom-call | flops 20000000000 | bytes 16777216 | tf_op jit(solution)/shard_map/front/pallas_call | solution.py:217
  38.7 106.9 %middle.1 = (bf16[2048,1024]{1,0:T(8,128)(2,1)}, bf16[2048,1024]{1,0:T(8,128)(2,1)}, bf16[2048,256]{1,0:T(8,128)(2,1)}, bf16[2048,256]{1,0:T(8,128)(2,1)}, bf16[...) custom-call(bf16[2048,256]{1,0:T(8,128)(2,1)} %copy-done, ...), custom_call_target="tpu_custom_call" | custom-call | flops 99999997952 | bytes 25165824 | tf_op jit(solution)/shard_map/middle/pallas_call | solution.py:500
  145.6 49.3 %multiply_convert_fusion = (bf16[2048,2048]{1,0:T(8,128)(2,1)}, f32[2048,2048]{1,0:T(8,128)}, f32[2048,2048]{1,0:T(8,128)}) fusion(f32[2048]{0:T(1024)S(1)} %copy-done.43, bf16[2048,1024]{1,0:T(8,128)(2,1)} %get-tuple-element.279, bf16[1024,2048]{1,0:T(8,128)(2,1)} %param.38), kind=kOutput, calls=%fused_computation.42 | convolution fusion | flops 8866758656 | bytes 50339840 | tf_op jit(solution)/shard_map/dot_general | solution.py:601
  195.0 22.9 %convert_reduce_fusion = (f32[2048]{0:T(1024)}, bf16[2048,2048]{1,0:T(8,128)(2,1)}) fusion(f32[2048,2048]{1,0:T(8,128)} %get-tuple-element.482, bf16[2048,1024]{1,0:T(8,128)(2,1)S(1)} %copy-done.15, bf16[2048,1024]{1,0:T(8,128)(2,1)} %param.40, f32[2048,2048]{1,0:T(8,128)} %get-tuple-element.504, f32[2048]{0:T(1024)S(1)} %copy-done.43), kind=kOutput, calls=%fused_computation.40 | convolution fusion | flops 8661235712 | bytes 50348032 | tf_op jit(solution)/shard_map/rd,fd->rf/dot_general | solution.py:616
  217.9 13.8 %convolution_convert_fusion.2 = bf16[2048,1024]{1,0:T(8,128)(2,1)} fusion(bf16[2048,2048]{1,0:T(8,128)(2,1)} %get-tuple-element.506, bf16[1024,2048]{1,0:T(8,128)(2,1)} %param.38), kind=kOutput, calls=%fused_computation.59 | convolution fusion | flops 8592031744 | bytes 16777216 | tf_op jit(solution)/shard_map/rf,df->rd/dot_general | solution.py:620
  231.8 13.8 %convolution_convert_fusion.3 = bf16[2048,1024]{1,0:T(8,128)(2,1)} fusion(bf16[2048,2048]{1,0:T(8,128)(2,1)} %get-tuple-element.481, bf16[2048,1024]{1,0:T(8,128)(2,1)} %param.40), kind=kOutput, calls=%fused_computation.60 | convolution fusion | flops 8592031744 | bytes 16777216 | tf_op jit(solution)/shard_map/dot_general | solution.py:605
  248.3 34.6 %reduce-scatter.8.cloned.1.call-done = bf16[512,1024]{1,0:T(8,128)(2,1)} async-done(((bf16[2048,1024]{1,0:T(8,128)(2,1)}), bf16[512,1024]{1,0:T(8,128)(2,1)}) %reduce-scatter.8.cloned.1.call-update) | async-done | bytes 1048592 | tf_op jit(solution)/shard_map/reduce_scatter | solution.py:621
  282.9 2.8 fusion.58
  285.7 44.4 %reduce-scatter.6.cloned.1.call-done = bf16[512,1024]{1,0:T(8,128)(2,1)} async-done(((bf16[2048,1024]{1,0:T(8,128)(2,1)}), bf16[512,1024]{1,0:T(8,128)(2,1)}) %reduce-scatter.6.cloned.1.call-update) | async-done | bytes 1048592 | tf_op jit(solution)/shard_map/reduce_scatter | solution.py:604
  330.1 3.7 fusion.73
  338.8 29.3 %while.30 = (s32[]{:T(128)}, f32[4,4,512]{2,1,0:T(4,128)S(1)}, s32[4]{0:T(128)S(1)}, s32[2]{0:T(128)S(1)}, bf16[2048,4,64]{0,2,1:T(8,128)(2,1)}, /*index=5*/bf16...) while((s32[]{:T(128)}, f32[4,4,512]{2,1,0:T(4,128)S(1)}, ...), condition=%wide.region_10.11_spmd.clone, body=%wide.region_7.10_spmd.clone.sunk | while | flops 70777112 | bytes 4638137 | solution.py:78
  368.1 2.8 all-gather.3.cloned.1.call-done
  370.9 4.5 convolution_convert_fusion.7
  375.4 61.2 %while.31 = (s32[]{:T(128)}, bf16[4,512,4,64]{1,3,2,0:T(8,128)(2,1)}, f32[4,256,4,64]{1,3,2,0:T(8,128)}, f32[4,256,4,64]{1,3,2,0:T(8,128)}, s32[4]{0:T(128)S(1)}...) while((s32[]{:T(128)}, ...), condition=%wide.region_13.14_spmd.clone, body=%wide.region_11.13_spmd.clone.sunk | while | flops 1012070656 | bytes 19319540 | solution.py:132
  382.0 1.8 multiply_reduce_fusion.4
  383.8 3.0 fusion.131
  386.8 2.1 fusion.132
  388.9 1.8 fusion.130
  397.3 1.8 multiply_reduce_fusion.4
  399.1 3.0 fusion.131
  402.1 2.1 fusion.132
  404.2 1.8 fusion.130
  412.6 1.8 multiply_reduce_fusion.4
  414.4 3.0 fusion.131
  417.4 2.1 fusion.132
  419.5 1.8 fusion.130
  427.9 1.8 multiply_reduce_fusion.4
  429.7 3.0 fusion.131
  432.7 2.1 fusion.132
  434.8 1.8 fusion.130
  436.6 2.1 copy.84
  439.9 3.3 convolution_convert_fusion.1
  443.5 14.0 %convolution_convert_fusion = bf16[1024,2048]{1,0:T(8,128)(2,1)} fusion(bf16[2048,1024]{1,0:T(8,128)(2,1)} %get-tuple-element.279, bf16[2048,2048]{1,0:T(8,128)(2,1)} %get-tuple-element.506), kind=kOutput, calls=%fused_computation.57 | convolution fusion | flops 8592031744 | bytes 16777216 | tf_op jit(solution)/shard_map/rd,rf->df/dot_general | solution.py:619
  459.6 28.3 %reduce-scatter.10.cloned.1.call-done = bf16[512,1024]{1,0:T(8,128)(2,1)} async-done(((bf16[2048,1024]{1,0:T(8,128)(2,1)}), bf16[512,1024]{1,0:T(8,128)(2,1)}) %reduce-scatter.10.cloned.1.call-update) | async-done | bytes 1048592 | tf_op jit(solution)/shard_map/reduce_scatter | solution.py:678
  487.9 2.4 fusion.59
  490.3 2.1 fusion.74
  497.9 3.0 fusion.61
  500.8 4.8 convolution_convert_fusion.11
  505.7 4.6 convolution_convert_fusion.10
  510.3 103.4 %all-reduce.6.cloned.1.call-done = bf16[1024,2048]{1,0:T(8,128)(2,1)} async-done(((bf16[1024,2048]{1,0:T(8,128)(2,1)}), bf16[1024,2048]{1,0:T(8,128)(2,1)}) %all-reduce.6.cloned.1.call-update) | async-done | bytes 4194320 | tf_op jit(solution)/shard_map/psum | solution.py:524
  613.8 14.0 %convolution_convert_fusion.5 = bf16[2048,1024]{1,0:T(8,128)(2,1)} fusion(bf16[2048,2048]{1,0:T(8,128)(2,1)} %get-tuple-element.481, bf16[2048,1024]{1,0:T(8,128)(2,1)} %broadcast_select_fusion), kind=kOutput, calls=%fused_computation.62 | convolution fusion | flops 8592031744 | bytes 16777216 | tf_op jit(solution)/shard_map/rf,rd->fd/dot_general | solution.py:615
  627.8 1.7 bitcast_convert_fusion
  629.7 3.7 convolution_convert_fusion.6.dc_ref
  634.7 12.1 %back.1 = bf16[2048,768]{1,0:T(8,128)(2,1)} custom-call(s32[2]{0:T(128)S(1)} %compare_select_fusion.1.lens, bf16[2048,256]{1,0:T(8,128)(2,1)S(1)} %get-tuple-element.285.q_ref, bf16[2048,256]{1,0:T(8,128)(2,1)S(1)} %copy-done.3, bf16[2048,256]{1,0:T(8,128)(2,1)S(1)} %copy-done.5, bf16[2048,256]{1,0:T(8,128)(2,1)S(1)} %convolution_convert_fusion.6.dc_ref), custom_call_target="tpu_custom_call" | custom-call | flops 30000001024 | bytes 8388608 | tf_op jit(solution)/shard_map/back/pallas_call | solution.py:275
  646.9 2.1 convolution_convert_fusion.12
  650.2 3.7 convolution_convert_fusion.8
  653.9 35.2 %all-reduce.8.cloned.1.call-done = bf16[1024,256]{1,0:T(8,128)(2,1)} async-done(((bf16[1024,256]{1,0:T(8,128)(2,1)}), bf16[1024,256]{1,0:T(8,128)(2,1)}) %all-reduce.8.cloned.1.call-update) | async-done | bytes 524304 | tf_op jit(solution)/shard_map/psum | solution.py:524
  692.1 6.9 convolution_convert_fusion.4
  702.4 7.6 convert_element_type.180
  710.2 1.8 convert_element_type.162
  713.0 1.9 convert_reduce_fusion.8
  714.9 37.4 %all-reduce = (f32[2,256]{1,0:T(2,128)}, f32[2,256]{1,0:T(2,128)}, f32[2048]{0:T(1024)}) all-reduce(f32[2,256]{1,0:T(2,128)S(1)} %pad_maximum_fusion.3, f32[2,256]{1,0:T(2,128)S(1)} %pad_maximum_fusion.4, f32[2048]{0:T(1024)S(1)} %copy-done.36), channel_id=1, replica_groups=mesh['wide'=8,'narrow'=4] {'wide'}, use_global_device_ids=true, to_apply=%region_42.43 | all-reduce | flops 3072 | bytes 24576 | tf_op jit(solution)/shard_map/psum | solution.py:734
  752.4 199.2 %all-reduce.10.cloned.1.call-done = (bf16[1024,2,256]{0,2,1:T(8,128)(2,1)}, bf16[1024,3,256]{2,0,1:T(8,128)(2,1)}, bf16[256,1024]{1,0:T(8,128)(2,1)}, bf16[256,1024]{1,0:T(8,128)(2,1)}, bf16[2048,1024]{1,0:T(8,128)(2,1)}) async-done(((bf16[1024,2,256]{0,2,1:T(8,128)(2,1)}, bf16[1024,3,256]{2,0,1:T(8,128)(2,1)}, bf16[256,1024]{1,0:T(8,128)(2,1)}, bf16[256,1024]{1,0:T(8,128)(2,1)}, ...) | async-done | bytes 7864336 | tf_op jit(solution)/shard_map/psum | solution.py:524
  951.6 6.8 convert_element_type.183
  958.3 1.9 convert_element_type.171
  960.2 3.9 copy.90
  964.2 2.1 convert_element_type.174
  966.3 2.1 convert_element_type.179
  968.4 2.2 fusion.60
  970.8 39.4 %psum.77 = f32[9,1024]{1,0:T(8,128)S(1)} all-reduce(f32[9,1024]{1,0:T(8,128)S(1)} %stack.66), channel_id=1, replica_groups=mesh['wide'=8,'narrow'=4] {'wide','narrow'}, use_global_device_ids=true, to_apply=%region_36.37 | all-reduce | flops 9216 | bytes 73728 | tf_op jit(solution)/shard_map/psum | solution.py:713
  1010.8 3.3 fusion.48
  (215 shorter events, 65.5 us)
Async XLA Ops:
  8.0 6.7 copy-start.38
  8.0 6.7 copy-start.19
  8.0 274.8 %reduce-scatter.8.cloned.1.call-start = ((), (), s32[]{:S(2)}) async-start(), calls=%async_computation.6 | async-start | bytes 5242880 | tf_op jit(solution)/shard_map/reduce_scatter | solution.py:621
  8.9 29.1 %copy-start.29 = (f32[1,1024]{1,0:T(1,128)}, f32[1,1024]{1,0:T(1,128)S(1)}, u32[]{:S(2)}) copy-start(f32[1,1024]{1,0:T(1,128)S(1)} %get-tuple-element.494) | copy-start | bytes 12292
  10.3 5.6 copy-start.39
  10.3 6.2 copy-start.44
  10.3 6.3 copy-start.33
  10.3 6.3 copy-start.34
  16.7 6.7 copy-start.35
  16.7 21.3 %copy-start.25 = (f32[1,1024]{1,0:T(1,128)}, f32[1,1024]{1,0:T(1,128)S(1)}, u32[]{:S(2)}) copy-start(f32[1,1024]{1,0:T(1,128)S(1)} %get-tuple-element.507) | copy-start | bytes 12292
  16.7 21.3 %copy-start.27 = (f32[1,1024]{1,0:T(1,128)}, f32[1,1024]{1,0:T(1,128)S(1)}, u32[]{:S(2)}) copy-start(f32[1,1024]{1,0:T(1,128)S(1)} %get-tuple-element.509) | copy-start | bytes 12292
  35.1 1.0 copy-start
  36.1 1.0 copy-start.2
  37.1 1.0 copy-start.4
  38.7 106.9 %copy-start.43 = (f32[2048]{0:T(1024)S(1)}, f32[2048]{0:T(1024)}, u32[]{:S(2)}) copy-start(f32[2048]{0:T(1024)} %param.39) | copy-start | bytes 24580
  145.6 49.3 %copy-start.15 = (bf16[2048,1024]{1,0:T(8,128)(2,1)S(1)}, bf16[2048,1024]{1,0:T(8,128)(2,1)}, u32[]{:S(2)}) copy-start(bf16[2048,1024]{1,0:T(8,128)(2,1)} %broadcast_select_fusion) | copy-start | bytes 12582916
  231.7 98.4 %reduce-scatter.6.cloned.1.call-start = ((), (), s32[]{:S(2)}) async-start(), calls=%async_computation.5 | async-start | bytes 5242880 | tf_op jit(solution)/shard_map/reduce_scatter | solution.py:604
  245.6 2.2 copy-start.7
  245.6 37.3 %copy-start.28 = (f32[1,1024]{1,0:T(1,128)S(1)}, f32[1,1024]{1,0:T(1,128)}, u32[]{:S(2)}) copy-start(f32[1,1024]{1,0:T(1,128)} %copy-done.27) | copy-start | bytes 12292
  245.6 84.5 %copy-start.30 = (f32[1,1024]{1,0:T(1,128)S(1)}, f32[1,1024]{1,0:T(1,128)}, u32[]{:S(2)}) copy-start(f32[1,1024]{1,0:T(1,128)} %copy-done.29) | copy-start | bytes 12292
  245.6 125.3 %all-gather.3.cloned.1.call-start = ((), (), s32[]{:S(2)}) async-start(), calls=%async_computation.7 | async-start | bytes 5242880 | tf_op jit(solution)/shard_map/all_gather | solution.py:628
  333.7 1.3 copy-start.8
  333.7 2.6 copy-start.24
  333.7 2.8 copy-start.21
  335.1 3.7 copy-start.40
  336.2 151.7 %reduce-scatter.10.cloned.1.call-start = ((), (), s32[]{:S(2)}) async-start(), calls=%async_computation.8 | async-start | bytes 5242880 | tf_op jit(solution)/shard_map/reduce_scatter | solution.py:678
  338.8 32.1 %copy-start.42 = (bf16[256,1024]{1,0:T(8,128)(2,1)S(1)}, bf16[256,1024]{1,0:T(8,128)(2,1)}, u32[]{:S(2)}) copy-start(bf16[256,1024]{1,0:T(8,128)(2,1)} %co_w.1) | copy-start | bytes 1572868
  436.6 3.4 copy-start.22
  438.9 1.0 copy-start.13
  443.2 170.5 %all-reduce.6.cloned.1.call-start = ((), (), s32[]{:S(2)}) async-start(), calls=%async_computation.12 | async-start | bytes 8388608 | tf_op jit(solution)/shard_map/psum | solution.py:524
  457.5 1.6 copy-start.6
  457.5 30.4 %copy-start.26 = (f32[1,1024]{1,0:T(1,128)S(1)}, f32[1,1024]{1,0:T(1,128)}, u32[]{:S(2)}) copy-start(f32[1,1024]{1,0:T(1,128)} %copy-done.25) | copy-start | bytes 12292
  457.5 172.1 %all-gather.5.cloned.1.call-start = ((), (), s32[]{:S(2)}) async-start(), calls=%async_computation.9 | async-start | bytes 5242880 | tf_op jit(solution)/shard_map/all_gather | solution.py:689
  487.9 2.4 copy-start.9
  492.4 1.3 copy-start.10
  494.8 6.0 copy-start.14
  494.9 194.3 %all-reduce.8.cloned.1.call-start = ((), (), s32[]{:S(2)}) async-start(), calls=%async_computation.13 | async-start | bytes 1048576 | tf_op jit(solution)/shard_map/psum | solution.py:524
  613.8 14.1 %copy-start.20 = (bf16[1024,2,256]{2,1,0:T(2,128)(2,1)S(1)}, bf16[1024,2,256]{2,1,0:T(2,128)(2,1)}, u32[]{:S(2)}) copy-start(bf16[1024,2,256]{2,1,0:T(2,128)(2,1)} %param.35) | copy-start | bytes 3145732
  613.8 96.4 %reduce-scatter.14.cloned.1.call-start = ((), (), s32[]{:S(2)}) async-start(), calls=%async_computation.11 | async-start | bytes 1310720 | tf_op jit(solution)/shard_map/reduce_scatter | solution.py:681
  629.6 3.8 copy-start.3
  629.6 322.0 %all-reduce.10.cloned.1.call-start = ((), (), s32[]{:S(2)}) async-start(), calls=%async_computation.14 | async-start | bytes 15728640 | tf_op jit(solution)/shard_map/psum | solution.py:524
  633.4 1.3 copy-start.5
  634.7 12.2 %copy-start.1 = (bf16[2048,256]{1,0:T(8,128)(2,1)S(1)}, bf16[2048,256]{1,0:T(8,128)(2,1)}, u32[]{:S(2)}) copy-start(bf16[2048,256]{1,0:T(8,128)(2,1)} %copy-done) | copy-start | bytes 3145732
  634.7 12.2 %copy-start.41 = (bf16[2048,1024]{1,0:T(8,128)(2,1)S(1)}, bf16[2048,1024]{1,0:T(8,128)(2,1)}, u32[]{:S(2)}) copy-start(bf16[2048,1024]{1,0:T(8,128)(2,1)} %all-gather.5.cloned.1.call-done) | copy-start | bytes 12582916
  646.8 2.1 copy-start.18
  646.9 3.4 copy-start.45
  690.7 1.4 copy-start.16
  690.7 277.7 %reduce-scatter.12.cloned.1.call-start = ((), (), s32[]{:S(2)}) async-start(), calls=%async_computation.10 | async-start | bytes 5242880 | tf_op jit(solution)/shard_map/reduce_scatter | solution.py:706
  699.0 0.7 copy-start.37
  699.0 1.5 copy-start.12
  702.4 9.6 copy-start.23
  710.0 4.9 copy-start.36
  951.5 6.8 copy-start.17
  960.2 10.4 %copy-start.31 = (f32[1024]{0:T(1024)S(1)}, f32[1024]{0:T(1024)}, u32[]{:S(2)}) copy-start(f32[1024]{0:T(1024)} %get-tuple-element.419) | copy-start | bytes 12292
  960.2 10.4 %copy-start.32 = (f32[1024]{0:T(1024)S(1)}, f32[1024]{0:T(1024)}, u32[]{:S(2)}) copy-start(f32[1024]{0:T(1024)} %get-tuple-element.430) | copy-start | bytes 12292
  960.2 50.6 %copy-start.11 = (f32[512,1024]{1,0:T(8,128)S(1)}, f32[512,1024]{1,0:T(8,128)}, u32[]{:S(2)}) copy-start(f32[512,1024]{1,0:T(8,128)} %copy-done.10) | copy-start | bytes 6291460
Sparse Core Ops, SparseCore 0:
  231.8 50.9 reduce-scatter.7
  285.6 44.4 reduce-scatter.5
  336.3 34.4 all-gather.2
  443.4 44.5 reduce-scatter.9
  495.0 34.4 all-gather.4
  629.7 23.9 reduce-scatter.13
  699.1 43.5 reduce-scatter.11
Sparse Core Ops, SparseCore 1:
  457.6 156.1 all-reduce.5
  618.0 71.1 all-reduce.7
  694.4 257.1 all-reduce.9

commit v3 on v2

--- a/solution.py
+++ b/solution.py
@@ -15,10 +15,6 @@
 EXACT = lax.Precision.HIGHEST
 
 
-def smooth_gate(values):
-    return jax.nn.gelu(values, approximate=False)
-
-
 def norm_forward(values, gain_vec, shift_vec):
     row_mean = jnp.mean(values, axis=-1, keepdims=True)
     centered = values - row_mean
@@ -34,118 +30,11 @@
     return inner_term * inv_std
 
 
-def split_heads(values):
-    return values.reshape(values.shape[0], -1, HEAD_DIM)
-
-
-def block_slices(block_index, queries, key_rows, value_rows, key_count, query_block):
-    per_slot = UNITS // query_block
-    slot_id = block_index // per_slot
-    first_row = block_index * query_block
-    block_queries = lax.dynamic_slice_in_dim(queries, first_row, query_block, 0)
-    block_keys = lax.dynamic_slice_in_dim(key_rows, slot_id * key_count, key_count, 0)
-    block_values = lax.dynamic_slice_in_dim(value_rows, slot_id * key_count, key_count, 0)
-    return (slot_id, first_row - slot_id * UNITS, block_queries, block_keys, block_values)
-
-
-def masked_scores(block_queries, block_keys, allowed, score_scale):
-    scores = (
-        jnp.einsum("qhd,khd->hqk", block_queries, block_keys, preferred_element_type=jnp.float32)
-        * score_scale
-    )
-    return jnp.where(allowed[None], scores, MASKED_SCORE)
-
-
-def attention_forward(
-    queries, key_rows, value_rows, key_count, query_block, score_scale, allowed_fn
-):
-
-    def one_block(block_index):
-        slot_id, offset, block_queries, block_keys, block_values = block_slices(
-            block_index, queries, key_rows, value_rows, key_count, query_block
-        )
-        scores = masked_scores(block_queries, block_keys, allowed_fn(slot_id, offset), score_scale)
-        row_max = jnp.max(scores, axis=-1, keepdims=True)
-        exp_scores = jnp.exp(scores - row_max)
-        row_total = jnp.sum(exp_scores, axis=-1, keepdims=True)
-        weights = (exp_scores / row_total).astype(jnp.bfloat16)
-        context = jnp.einsum(
-            "hqk,khd->qhd", weights, block_values, preferred_element_type=jnp.float32
-        )
-        return (context, (row_max + jnp.log(row_total))[:, :, 0])
-
-    block_total = queries.shape[0] // query_block
-    context, log_total = lax.map(one_block, jnp.arange(block_total, dtype=jnp.int32))
-    return (context.reshape(queries.shape[0], -1), log_total)
-
-
-def attention_backward(
-    queries,
-    key_rows,
-    value_rows,
-    context_grad,
-    log_total,
-    key_count,
-    query_block,
-    score_scale,
-    allowed_fn,
-):
-
-    def one_block(packed):
-        block_index, block_log = packed
-        slot_id, offset, block_queries, block_keys, block_values = block_slices(
-            block_index, queries, key_rows, value_rows, key_count, query_block
-        )
-        block_grad = lax.dynamic_slice_in_dim(
-            context_grad, block_index * query_block, query_block, 0
-        )
-        scores = masked_scores(block_queries, block_keys, allowed_fn(slot_id, offset), score_scale)
-        weights = jnp.exp(scores - block_log[:, :, None])
-        value_grad = jnp.einsum(
-            "hqk,qhd->khd",
-            weights.astype(jnp.bfloat16),
-            block_grad,
-            preferred_element_type=jnp.float32,
-        )
-        weight_grad = jnp.einsum(
-            "qhd,khd->hqk", block_grad, block_values, preferred_element_type=jnp.float32
-        )
-        score_grad = weights * (
-            weight_grad - jnp.sum(weights * weight_grad, axis=-1, keepdims=True)
-        )
-        query_grad = (
-            jnp.einsum("hqk,khd->qhd", score_grad, block_keys.astype(jnp.float32), precision=EXACT)
-            * score_scale
-        )
-        key_grad = (
-            jnp.einsum(
-                "hqk,qhd->khd", score_grad, block_queries.astype(jnp.float32), precision=EXACT
-            )
-            * score_scale
-        )
-        return (query_grad, key_grad, value_grad)
-
-    row_count = queries.shape[0]
-    block_total = row_count // query_block
-    per_slot = UNITS // query_block
-    slot_count = row_count // UNITS
-    query_grad, key_grad, value_grad = lax.map(
-        one_block, (jnp.arange(block_total, dtype=jnp.int32), log_total)
-    )
-    query_grad = query_grad.reshape(row_count, -1)
-    key_grad = jnp.sum(key_grad.reshape(slot_count, per_slot, key_count, -1), axis=1).reshape(
-        slot_count * key_count, -1
-    )
-    value_grad = jnp.sum(value_grad.reshape(slot_count, per_slot, key_count, -1), axis=1).reshape(
-        slot_count * key_count, -1
-    )
-    return (query_grad, key_grad, value_grad)
-
-
 BLOCK = 256
 MIB = 1 << 20
 NARROW = 4
 STEPS = 8
+HIDDEN = 512
 MESH = pl.DeviceIdType.MESH
 
 
@@ -517,6 +406,358 @@
     )(c1, units_own, text, vec, bias, keep, so_w, cq_w, kv_w, co_w)
 
 
+def ffn_kernel(lens, h_ref, e_ref, wi_ref, b_ref, wo_ref, a_ref, d_ref, gi_ref, go_ref, gb_ref, gi_acc, go_acc):
+    block = pl.program_id(0)
+    per_slot = pl.num_programs(0) // lens.shape[0]
+    length = lens[block // per_slot]
+
+    @pl.when(block == 0)
+    def _():
+        gi_acc[...] = jnp.zeros_like(gi_acc)
+        go_acc[...] = jnp.zeros_like(go_acc)
+        gb_ref[...] = jnp.zeros_like(gb_ref)
+
+    live = (block % per_slot) * BLOCK < length
+
+    @pl.when(live)
+    def _():
+        rows, grads = h_ref[...], e_ref[...]
+        out = jnp.zeros(a_ref.shape, jnp.float32)
+        back_out = jnp.zeros(d_ref.shape, jnp.float32)
+        hidden_count = wo_ref.shape[0]
+        for first in range(0, hidden_count, HIDDEN):
+            part = slice(first, first + HIDDEN)
+            pre = dot_nn(rows, wi_ref[:, part]) + b_ref[:, part]
+            cdf = 0.5 + 0.5 * lax.erf(pre * (0.5**0.5))
+            pdf = jnp.exp(-0.5 * pre * pre) * 0.3989422804014327
+            hidden = (pre * cdf).astype(jnp.bfloat16)
+            slope = cdf + pre * pdf
+            pre_grad = slope * dot_nt(grads, wo_ref[part, :])
+            pre_low = pre_grad.astype(jnp.bfloat16)
+            gb_ref[:, part] += jnp.sum(pre_low.astype(jnp.float32), axis=0, keepdims=True)
+            out += dot_nn(hidden, wo_ref[part, :])
+            back_out += dot_nt(pre_low, wi_ref[:, part])
+            go_acc[part, :] += dot_tn(hidden, grads)
+            gi_acc[:, part] += dot_tn(rows, pre_low)
+        a_ref[...] = out.astype(jnp.bfloat16)
+        d_ref[...] = back_out.astype(jnp.bfloat16)
+
+    @pl.when(jnp.logical_not(live))
+    def _():
+        a_ref[...] = jnp.zeros_like(a_ref)
+        d_ref[...] = jnp.zeros_like(d_ref)
+
+    @pl.when(block == pl.num_programs(0) - 1)
+    def _():
+        gi_ref[...] = gi_acc[...].astype(jnp.bfloat16)
+        go_ref[...] = go_acc[...].astype(jnp.bfloat16)
+
+
+def ffn(lengths, rows_in, grads, w_in, b_in, w_out):
+    rows, width = rows_in.shape
+    count = w_out.shape[0]
+    bf, f32 = jnp.bfloat16, jnp.float32
+    shape = jax.ShapeDtypeStruct
+    block = pl.BlockSpec((BLOCK, width), lambda i, *_: (i, 0))
+    whole = lambda a, b: pl.BlockSpec((a, b), lambda i, *_: (0, 0), pipeline_mode=pl.Buffered(1))
+    return pl.pallas_call(
+        ffn_kernel,
+        grid_spec=pltpu.PrefetchScalarGridSpec(
+            num_scalar_prefetch=1,
+            grid=(rows // BLOCK,),
+            in_specs=[block, block, whole(width, count), whole(1, count), whole(count, width)],
+            out_specs=[block, block, whole(width, count), whole(count, width), whole(1, count)],
+            scratch_shapes=[pltpu.VMEM((width, count), f32), pltpu.VMEM((count, width), f32)],
+        ),
+        out_shape=[
+            shape((rows, width), bf),
+            shape((rows, width), bf),
+            shape((width, count), bf),
+            shape((count, width), bf),
+            shape((1, count), f32),
+        ],
+        compiler_params=pltpu.CompilerParams(vmem_limit_bytes=58 * MIB),
+        cost_estimate=pl.CostEstimate(flops=60 * 10**9, bytes_accessed=32 * MIB, transcendentals=8 * MIB),
+        name="ffn",
+    )(lengths, rows_in, grads, w_in, b_in.reshape(1, -1), w_out)
+
+
+class FarHop(Hop):
+    def fetch(self, mine, theirs, sems):
+        self.mine, self.theirs = mine, theirs
+        rows = lambda owner: pl.ds(pl.multiple_of(owner * self.own, self.own), self.own)
+        self.fetches = [
+            pltpu.make_async_copy(self.part.at[rows(owner)], ref, sems.at[slot])
+            for slot, (owner, ref) in enumerate(((self.index, mine), (self.cross, theirs)))
+        ]
+        for copy in self.fetches:
+            copy.start()
+
+    def fetched(self):
+        for copy in self.fetches:
+            copy.wait()
+
+    def cross_copy(self, step):
+        return remote(
+            self.theirs.at[self.own_rows(step)], self.from_cross.at[step], self.sems, 2, step, self.cross
+        )
+
+    def send_cross(self, step):
+        for copy in self.core_copies(step):
+            copy.wait_recv()
+        total = self.theirs[self.own_rows(step), :].astype(jnp.float32)
+        total += self.from_core[step, 1].astype(jnp.float32)
+        self.theirs[self.own_rows(step), :] = total.astype(jnp.bfloat16)
+        self.cross_copy(step).start()
+
+    def result(self, step):
+        total = self.mine[self.own_rows(step), :].astype(jnp.float32)
+        total += self.from_core[step, 0].astype(jnp.float32)
+        self.cross_copy(step).wait_recv()
+        return total + self.from_cross[step].astype(jnp.float32)
+
+
+def column_sum(values):
+    return jnp.sum(values, axis=0, keepdims=True)
+
+
+def turn_kernel(
+    third, ffn_part, x1, x2, e_own, valid, h2, q2, c2, kv2, c1, keep, vec, co_w, cq_w, so_w,
+    y, dx1, dc1, dkv, co_g, cq_g, so_g, bias_g, stats,
+    mine3, theirs3, core3, fromx3, sem3, mine4, theirs4, core4, fromx4, sem4,
+    part5, core5, tox5, fromx5, sem5, full3, full5, dx2, co_acc, cq_acc, so_acc, dkv_acc, fetch_sem,
+):
+    steps, chunk, width = tox5.shape
+    cols = q2.shape[1]
+    slots = bias_g.shape[0]
+    texts = kv2.shape[0] // slots
+    greet()
+    three = FarHop(third, core3, None, fromx3, full3, sem3, chunk)
+    four = FarHop(ffn_part, core4, None, fromx4, None, sem4, chunk)
+    five = Hop(part5, core5, tox5, fromx5, full5, sem5, chunk)
+    three.fetch(mine3, theirs3, fetch_sem.at[0])
+    four.fetch(mine4, theirs4, fetch_sem.at[1])
+
+    def start(step, carry):
+        three.send_core(step)
+        return carry
+
+    lax.fori_loop(0, steps, start, 0)
+    for ref in (co_acc, cq_acc, so_acc, dkv_acc, bias_g, stats):
+        ref[...] = jnp.zeros_like(ref)
+    three.fetched()
+    four.fetched()
+    scale = jnp.bfloat16(HEAD_DIM**-0.5)
+
+    def norm_three(step):
+        rows = three.own_rows(step)
+        grad_in = three.result(step)
+        _, normed, inv_std = norm_forward(x2[rows, :], vec[0:1, :], vec[0:1, :])
+        stats[0:1, :] += column_sum(grad_in * normed)
+        stats[1:2, :] += column_sum(grad_in)
+        above = e_own[rows, :].astype(jnp.float32)
+        total = above + norm_backward(grad_in, normed, inv_std, vec[0:1, :])
+        stats[2:3, :] += column_sum(above)
+        stats[3:4, :] += column_sum(total)
+        dx2[rows, :] = total
+        three.send_gather(step, total.astype(jnp.bfloat16))
+        four.send_core(step)
+
+    def cross(step):
+        three.gathered(step)
+        grads = three.take(full3, step)
+        co_acc[...] += dot_tn(three.take(c2, step), grads)
+        context = dot_nt(grads, co_w[...]).astype(jnp.bfloat16)
+        queries = three.take(q2, step) * scale
+        count = queries.shape[0] // slots
+        q_grad = []
+        for slot in range(slots):
+            rows = slice(slot * count, (slot + 1) * count)
+            texts_here = slice(slot * texts, (slot + 1) * texts)
+            keys, values = kv2[texts_here, :cols], kv2[texts_here, cols:]
+            total = jnp.zeros((count, cols), jnp.float32)
+            for head in range(cols // HEAD_DIM):
+                q_head, g_head = pick_head(queries[rows], head), pick_head(context[rows], head)
+                scores = jnp.where(keep[texts_here, :] > 0.5, dot_nt(keys, q_head), MASKED_SCORE)
+                weights = jnp.exp(scores - jnp.max(scores, axis=0, keepdims=True))
+                weights = weights * (1.0 / jnp.sum(weights, axis=0, keepdims=True))
+                dkv_acc[texts_here, cols:] += dot_nn(weights.astype(jnp.bfloat16), g_head)
+                weight_grad = dot_nt(values, g_head)
+                inner = jnp.sum(weights * weight_grad, axis=0, keepdims=True)
+                score_grad = (weights * (weight_grad - inner)).astype(jnp.bfloat16)
+                dkv_acc[texts_here, :cols] += dot_nn(score_grad, q_head)
+                total += dot_tn(score_grad, pick_head(keys, head))
+            q_grad.append((total * HEAD_DIM**-0.5).astype(jnp.bfloat16))
+        q_grad = jnp.concatenate(q_grad, axis=0)
+        five.put(part5, step, dot_nt(q_grad, cq_w[...]).astype(jnp.bfloat16))
+        five.send_core(step)
+        bias_g[0:1, :] += column_sum(q_grad.astype(jnp.float32))
+        cq_acc[...] += dot_tn(five.take(h2, step), q_grad)
+
+    def norm_two(step):
+        rows = five.own_rows(step)
+        grad_in = five.result(step)
+        _, normed, inv_std = norm_forward(x1[rows, :], vec[1:2, :], vec[1:2, :])
+        stats[4:5, :] += column_sum(grad_in * normed)
+        stats[5:6, :] += column_sum(grad_in)
+        total = dx2[rows, :] + norm_backward(grad_in, normed, inv_std, vec[1:2, :])
+        stats[6:7, :] += column_sum(total)
+        dx1[rows, :] = total
+        five.send_gather(step, total.astype(jnp.bfloat16))
+
+    def last(step):
+        five.gathered(step)
+        grads = five.take(full5, step)
+        dc1_rows = dot_nt(grads, so_w[...]).astype(jnp.bfloat16)
+        five.put(dc1, step, dc1_rows)
+        so_acc[...] += dot_tn(five.take(c1, step), grads)
+
+    def output(step):
+        rows = four.own_rows(step)
+        total = x2[rows, :] + four.result(step) + vec[2:3, :]
+        y[rows, :] = jnp.where(valid[rows, :1] > 0.5, total, 0.0).astype(jnp.bfloat16)
+
+    stages(
+        steps,
+        [
+            three.send_cross, norm_three, three.forward, cross,
+            five.send_cross, norm_two, five.forward, last,
+            four.send_cross, output,
+        ],
+    )
+    dkv[...] = dkv_acc[...].astype(jnp.bfloat16)
+    bias_g[1:2, :] = column_sum(dkv[:, cols:].astype(jnp.float32))
+    co_g[...] = co_acc[...].astype(jnp.bfloat16)
+    cq_g[...] = cq_acc[...].astype(jnp.bfloat16)
+    so_g[...] = so_acc[...].astype(jnp.bfloat16)
+
+    def finish(step, carry):
+        three.finish(step)
+        four.finish(step, False)
+        five.finish(step)
+        return carry
+
+    lax.fori_loop(0, steps, finish, 0)
+
+
+def turn(third, ffn_part, x1, x2, e_own, valid, h2, q2, c2, kv2, c1, keep, vec, co_w, cq_w, so_w):
+    rows, cols = c1.shape
+    own, width = x1.shape
+    chunk = own // STEPS
+    bf, f32 = jnp.bfloat16, jnp.float32
+    shape = jax.ShapeDtypeStruct
+    vmem = pl.BlockSpec(memory_space=pltpu.VMEM)
+    hbm = pl.BlockSpec(memory_space=pl.ANY)
+    hop = hop_scratch(own, chunk, width)
+    far = [pltpu.VMEM((own, width), bf)] * 2 + [hop[0], hop[2], hop[3]]
+    return pl.pallas_call(
+        turn_kernel,
+        in_specs=[hbm, hbm] + [vmem] * 14,
+        out_specs=[vmem] * 9,
+        out_shape=[
+            shape((own, width), bf),
+            shape((own, width), f32),
+            shape((rows, cols), bf),
+            shape(kv2.shape, bf),
+            shape((cols, width), bf),
+            shape((width, cols), bf),
+            shape((cols, width), bf),
+            shape((2, cols), f32),
+            shape((8, width), f32),
+        ],
+        scratch_shapes=far
+        + far
+        + [pltpu.VMEM((rows, width), bf)]
+        + hop
+        + [pltpu.VMEM((rows, width), bf)] * 2
+        + [
+            pltpu.VMEM((own, width), f32),
+            pltpu.VMEM((cols, width), f32),
+            pltpu.VMEM((width, cols), f32),
+            pltpu.VMEM((cols, width), f32),
+            pltpu.VMEM(kv2.shape, f32),
+            pltpu.SemaphoreType.DMA((2, 2)),
+        ],
+        compiler_params=pltpu.CompilerParams(collective_id=1, has_side_effects=True, vmem_limit_bytes=60 * MIB),
+        cost_estimate=pl.CostEstimate(flops=100 * 10**9, bytes_accessed=24 * MIB, transcendentals=4 * MIB),
+        name="turn",
+    )(third, ffn_part, x1, x2, e_own, valid, h2, q2, c2, kv2, c1, keep, vec, co_w, cq_w, so_w)
+
+
+def last_kernel(
+    dqkv, dkv, units, dx1, gain, qkv_w, kv_w, units_g, text_g, stats,
+    part6, core6, tox6, fromx6, sem6, part7, core7, tox7, fromx7, sem7,
+):
+    steps, chunk, _ = tox6.shape
+    text_steps = tox7.shape[0]
+    greet()
+    six = Hop(part6, core6, tox6, fromx6, None, sem6, chunk)
+    seven = Hop(part7, core7, tox7, fromx7, None, sem7, chunk)
+    stats[...] = jnp.zeros_like(stats)
+
+    def project(step):
+        six.put(part6, step, dot_nt(six.take(dqkv, step), qkv_w[...]).astype(jnp.bfloat16))
+        six.send_core(step)
+
+    def norm_one(step):
+        rows = six.own_rows(step)
+        grad_in = six.result(step)
+        _, normed, inv_std = norm_forward(units[rows, :].astype(jnp.float32), gain[...], gain[...])
+        stats[0:1, :] += column_sum(grad_in * normed)
+        stats[1:2, :] += column_sum(grad_in)
+        units_g[rows, :] = dx1[rows, :] + norm_backward(grad_in, normed, inv_std, gain[...])
+
+    def text_only(work):
+        def stage(step):
+            @pl.when(step < text_steps)
+            def _():
+                work(step)
+
+        return stage
+
+    def text_project(step):
+        seven.put(part7, step, dot_nt(seven.take(dkv, step), kv_w[...]).astype(jnp.bfloat16))
+        seven.send_core(step)
+
+    def text_result(step):
+        text_g[seven.own_rows(step), :] = seven.result(step)
+
+    stages(
+        steps,
+        [project, six.send_cross, norm_one, text_only(text_project), text_only(seven.send_cross), text_only(text_result)],
+    )
+
+    def finish(step, carry):
+        six.finish(step, False)
+        text_only(lambda s: seven.finish(s, False))(step)
+        return carry
+
+    lax.fori_loop(0, steps, finish, 0)
+
+
+def last(dqkv, dkv, units_own, dx1, gain_vec, qkv_w, kv_w):
+    rows = dqkv.shape[0]
+    own, width = units_own.shape
+    chunk = own // STEPS
+    text_own = dkv.shape[0] // NARROW
+    bf, f32 = jnp.bfloat16, jnp.float32
+    shape = jax.ShapeDtypeStruct
+    vmem = pl.BlockSpec(memory_space=pltpu.VMEM)
+    return pl.pallas_call(
+        last_kernel,
+        in_specs=[vmem] * 7,
+        out_specs=[vmem] * 3,
+        out_shape=[shape((own, width), f32), shape((text_own, width), f32), shape((8, width), f32)],
+        scratch_shapes=[pltpu.VMEM((rows, width), bf)]
+        + hop_scratch(own, chunk, width)
+        + [pltpu.VMEM((dkv.shape[0], width), bf)]
+        + hop_scratch(text_own, chunk, width),
+        compiler_params=pltpu.CompilerParams(collective_id=2, has_side_effects=True, vmem_limit_bytes=58 * MIB),
+        cost_estimate=pl.CostEstimate(flops=30 * 10**9, bytes_accessed=16 * MIB, transcendentals=0),
+        name="last",
+    )(dqkv, dkv, units_own, dx1, gain_vec.reshape(1, -1), qkv_w, kv_w)
+
+
 def wide_sum(arrays, after=None):
     parts = tuple(a.astype(jnp.bfloat16) for a in arrays)
     if after is not None:
@@ -545,156 +786,64 @@
     ffn_out,
     out_bias,
 ):
-    narrow_size = lax.axis_size("narrow")
-    narrow_index = lax.axis_index("narrow")
-    group_rows = units.shape[0]
-    own_rows = group_rows // narrow_size
-    first_own = narrow_index * own_rows
+    own_rows = units.shape[0] // NARROW
+    first_own = lax.axis_index("narrow") * own_rows
     slot_count = unit_lengths.shape[0]
-    score_scale = HEAD_DIM ** (-0.5)
-    query_block = min(512, UNITS)
     slot_live = jnp.arange(slot_count, dtype=jnp.int32) < bucket_counts[0]
     lengths = jnp.where(slot_live, unit_lengths, 0)
-    positions = jnp.arange(group_rows, dtype=jnp.int32)
+    positions = first_own + jnp.arange(own_rows, dtype=jnp.int32)
     slot_match = (positions // UNITS)[:, None] == jnp.arange(slot_count, dtype=jnp.int32)[None, :]
     row_limit = jnp.sum(jnp.where(slot_match, lengths[None, :], 0), axis=1)
-    row_valid = positions % UNITS < row_limit
-    valid_own = lax.dynamic_slice_in_dim(row_valid, first_own, own_rows, 0)
-    unit_pos = jnp.arange(UNITS, dtype=jnp.int32)
+    valid_own = positions % UNITS < row_limit
     text_pos = jnp.arange(TEXT, dtype=jnp.int32)
-
-    def self_allowed(slot_id, offset):
-        rows_here = offset + jnp.arange(query_block, dtype=jnp.int32)
-        length = lax.dynamic_index_in_dim(lengths, slot_id, keepdims=False)
-        before = unit_pos[None, :] <= rows_here[:, None]
-        return before & ((unit_pos[None, :] < length) | (unit_pos[None, :] == rows_here[:, None]))
-
-    def cross_allowed(slot_id, offset):
-        length = lax.dynamic_index_in_dim(text_lengths, slot_id, keepdims=False)
-        return jnp.broadcast_to(text_pos[None, :] < length, (query_block, TEXT))
+    keep = (text_pos[None, :] < text_lengths[:, None]).astype(jnp.float32)
+
+    def own(rows):
+        return lax.dynamic_slice_in_dim(rows, first_own, own_rows, 0)
 
     qkv_weights = self_qkv.reshape(self_qkv.shape[0], -1)
+    kv_weights = cross_kv.reshape(cross_kv.shape[0], -1)
+    own_units = own(units)
     first_in, queries, key_rows, value_rows, self_context = front(
         lengths, units, norm_gain[0], norm_shift[0], qkv_weights, self_bias[0], self_bias[1]
     )
-    own_units = lax.dynamic_slice_in_dim(units, first_own, own_rows, 0).astype(jnp.float32)
-    _, normed_one, inv_one = norm_forward(own_units, norm_gain[0], norm_shift[0])
-    vec = jnp.stack(
-        [norm_gain[1], norm_shift[1], out_bias[0], norm_gain[2], norm_shift[2], out_bias[1], out_bias[2], out_bias[2]]
-    )
-    keep = (text_pos[None, :] < text_lengths[:, None]).astype(jnp.float32)
+    last_bias = jnp.zeros((3,) + out_bias.shape[1:], jnp.float32)
     second_all, third_all, cross_queries, cross_context, text_kv, resid_one, resid_two = middle(
         self_context,
-        lax.dynamic_slice_in_dim(units, first_own, own_rows, 0),
+        own_units,
         text,
-        vec,
+        jnp.concatenate([norm_gain[1:2], norm_shift[1:2], out_bias[0:1], norm_gain[2:3], norm_shift[2:3], out_bias[1:2], last_bias[:2]]),
         cross_bias,
         keep,
         self_out,
         cross_q,
-        cross_kv.reshape(cross_kv.shape[0], -1),
+        kv_weights,
         cross_out,
     )
-    text_keys, text_values = jnp.split(text_kv, 2, axis=1)
-    _, normed_two, inv_two = norm_forward(resid_one, norm_gain[1], norm_shift[1])
-    _, normed_three, inv_three = norm_forward(resid_two, norm_gain[2], norm_shift[2])
-    hidden_pre = jnp.dot(third_all, ffn_in, preferred_element_type=jnp.float32) + ffn_in_bias
-    hidden_full, gate_pullback = jax.vjp(smooth_gate, hidden_pre)
-    hidden = hidden_full.astype(jnp.bfloat16)
-    ffn_sum = lax.psum_scatter(
-        jnp.dot(hidden, ffn_out, preferred_element_type=jnp.float32).astype(jnp.bfloat16),
-        "narrow",
-        scatter_dimension=0,
-        tiled=True,
-    ).astype(jnp.float32)
-    output = jnp.where(valid_own[:, None], resid_two + ffn_sum + out_bias[2], 0.0).astype(
-        jnp.bfloat16
-    )
-    grad_all = jnp.where(row_valid[:, None], out_grad, jnp.zeros_like(out_grad))
-    grad_two = lax.dynamic_slice_in_dim(grad_all, first_own, own_rows, 0).astype(jnp.float32)
-    ffn_out_grad = jnp.einsum("rf,rd->fd", hidden, grad_all, preferred_element_type=jnp.float32)
-    hidden_grad = jnp.einsum("rd,fd->rf", grad_all, ffn_out, preferred_element_type=jnp.float32)
-    pre_grad = gate_pullback(hidden_grad)[0].astype(jnp.bfloat16)
-    ffn_in_bias_grad = jnp.sum(pre_grad, axis=0, dtype=jnp.float32)
-    ffn_in_grad = jnp.einsum("rd,rf->df", third_all, pre_grad, preferred_element_type=jnp.float32)
-    third_part = jnp.einsum("rf,df->rd", pre_grad, ffn_in, preferred_element_type=jnp.float32)
-    third_grad = lax.psum_scatter(
-        third_part.astype(jnp.bfloat16), "narrow", scatter_dimension=0, tiled=True
-    ).astype(jnp.float32)
-    gain_three = jnp.sum(third_grad * normed_three, axis=0)
-    shift_three = jnp.sum(third_grad, axis=0)
-    resid_two_grad = grad_two + norm_backward(third_grad, normed_three, inv_three, norm_gain[2])
-    bias_two_grad = jnp.sum(grad_two, axis=0)
-    cross_out_all = lax.all_gather(
-        resid_two_grad.astype(jnp.bfloat16), "narrow", axis=0, tiled=True
-    )
-    cross_out_grad = jnp.einsum(
-        "rn,rd->nd", cross_context, cross_out_all, preferred_element_type=jnp.float32
-    )
-    cross_context_grad = jnp.einsum(
-        "rd,nd->rn", cross_out_all, cross_out, preferred_element_type=jnp.float32
-    ).astype(jnp.bfloat16)
-    _, cross_log = attention_forward(
-        split_heads(cross_queries),
-        split_heads(text_keys),
-        split_heads(text_values),
-        TEXT,
-        query_block,
-        score_scale,
-        cross_allowed,
-    )
-    cross_query_grad, text_key_grad, text_value_grad = attention_backward(
-        split_heads(cross_queries),
-        split_heads(text_keys),
-        split_heads(text_values),
-        split_heads(cross_context_grad),
-        cross_log,
-        TEXT,
-        query_block,
-        score_scale,
-        cross_allowed,
-    )
-    cross_query_grad = cross_query_grad.astype(jnp.bfloat16)
-    text_kv_grad = jnp.stack([text_key_grad, text_value_grad], axis=1).astype(jnp.bfloat16)
-    cross_q_grad = jnp.einsum(
-        "rd,rn->dn", second_all, cross_query_grad, preferred_element_type=jnp.float32
-    )
-    cross_kv_grad = jnp.einsum(
-        "td,tcn->dcn", text, text_kv_grad, preferred_element_type=jnp.float32
-    )
-    cross_bias_grad = jnp.stack(
-        [
-            jnp.sum(cross_query_grad, axis=0, dtype=jnp.float32),
-            jnp.sum(text_kv_grad[:, 1], axis=0, dtype=jnp.float32),
-        ]
-    )
-    second_part = jnp.einsum(
-        "rn,dn->rd", cross_query_grad, cross_q, preferred_element_type=jnp.float32
-    )
-    text_part = jnp.einsum(
-        "tcn,dcn->td", text_kv_grad, cross_kv, preferred_element_type=jnp.float32
-    )
-    second_grad, text_grad = (
-        lax.psum_scatter(
-            second_part.astype(jnp.bfloat16), "narrow", scatter_dimension=0, tiled=True
-        ).astype(jnp.float32),
-        lax.psum_scatter(
-            text_part.astype(jnp.bfloat16), "narrow", scatter_dimension=0, tiled=True
-        ).astype(jnp.float32),
-    )
-    gain_two = jnp.sum(second_grad * normed_two, axis=0)
-    shift_two = jnp.sum(second_grad, axis=0)
-    resid_one_grad = resid_two_grad + norm_backward(second_grad, normed_two, inv_two, norm_gain[1])
-    bias_one_grad = jnp.sum(resid_two_grad, axis=0)
-    self_out_all = lax.all_gather(resid_one_grad.astype(jnp.bfloat16), "narrow", axis=0, tiled=True)
-    self_out_grad = jnp.einsum(
-        "rn,rd->nd", self_context, self_out_all, preferred_element_type=jnp.float32
-    )
-    self_context_grad = jnp.einsum(
-        "rd,nd->rn", self_out_all, self_out, preferred_element_type=jnp.float32
-    ).astype(jnp.bfloat16)
+    ffn_part, third_part, ffn_in_grad, ffn_out_grad, ffn_in_bias_grad = ffn(
+        lengths, third_all, out_grad, ffn_in, ffn_in_bias, ffn_out
+    )
+    grad_own = jnp.where(valid_own[:, None], own(out_grad), jnp.zeros((), out_grad.dtype))
+    spread = own_rows // STEPS * NARROW // slot_count
+    output, resid_one_grad, self_context_grad, text_kv_grad, cross_out_grad, cross_q_grad, self_out_grad, cross_bias_grad, stats = turn(
+        third_part,
+        ffn_part,
+        resid_one,
+        resid_two,
+        grad_own,
+        jnp.broadcast_to(valid_own[:, None].astype(jnp.float32), (own_rows, 128)),
+        second_all,
+        cross_queries,
+        cross_context,
+        text_kv,
+        self_context,
+        jnp.broadcast_to(keep.reshape(-1, 1), (keep.size, spread)),
+        jnp.concatenate([norm_gain[2:3], norm_gain[1:2], out_bias[2:3]]),
+        cross_out,
+        cross_q,
+        self_out,
+    )
     qkv_grad = back(lengths, queries, key_rows, value_rows, self_context_grad)
-    self_qkv_grad = dot_tn(first_in, qkv_grad).reshape(self_qkv.shape)
     cols = queries.shape[1]
     self_bias_grad = jnp.stack(
         [
@@ -702,26 +851,24 @@
             jnp.sum(qkv_grad[:, 2 * cols :], axis=0, dtype=jnp.float32),
         ]
     )
-    first_part = dot_nt(qkv_grad, qkv_weights)
-    first_grad = lax.psum_scatter(
-        first_part.astype(jnp.bfloat16), "narrow", scatter_dimension=0, tiled=True
-    ).astype(jnp.float32)
-    gain_one = jnp.sum(first_grad * normed_one, axis=0)
-    shift_one = jnp.sum(first_grad, axis=0)
-    units_grad = resid_one_grad + norm_backward(first_grad, normed_one, inv_one, norm_gain[0])
-    bias_zero_grad = jnp.sum(resid_one_grad, axis=0)
+    self_qkv_grad = dot_tn(first_in, qkv_grad).astype(jnp.bfloat16).reshape(self_qkv.shape)
+    cross_kv_grad = dot_tn(text, text_kv_grad).astype(jnp.bfloat16).reshape(cross_kv.shape)
+    units_grad, text_grad, last_stats = last(
+        qkv_grad, text_kv_grad, own_units, resid_one_grad, norm_gain[0], qkv_weights, kv_weights
+    )
+    ffn_in_bias_grad = ffn_in_bias_grad.reshape(ffn_in_bias.shape)
     small_sums = lax.psum(
         jnp.stack(
             [
-                gain_one,
-                gain_two,
-                gain_three,
-                shift_one,
-                shift_two,
-                shift_three,
-                bias_zero_grad,
-                bias_one_grad,
-                bias_two_grad,
+                last_stats[0],
+                stats[4],
+                stats[0],
+                last_stats[1],
+                stats[5],
+                stats[1],
+                stats[6],
+                stats[3],
+                stats[2],
             ]
         ),
         ("wide", "narrow"),

time: 1030 us -> 763 us (0.74)
  Pallas kernels: 131 us -> 369 us
  waiting for transfers between devices: 448 us -> 226 us
  matrix products: 213 us -> 9.8 us
  other arithmetic: 64.4 us -> 25.4 us
  loops' own time: 26.9 us -> 0 us
  local copies, waits for them, and re-layouts: 44.1 us -> 26 us
  starting transfers between devices: 1 us -> 13.1 us
    pallas_call x0 -> x3, Pallas kernels: none -> 224 us  [the longest x1 130 us: turn(): pl.pallas_call(turn_kernel, in_specs=[hbm, hbm] + [vmem] * 14, out_specs=...]
    dot_general x39 -> x0, matrix products: 209 us -> none  [the longest x1 49.3 us: local(): jnp.dot(third_all, ffn_in, preferred_element_type=jnp.float32) + ffn_in_bias]
    psum x3, waiting for transfers between devices: 338 us -> 226 us  [wide_sum(): return (lax.psum(parts, 'wide'), after)]
    reduce_scatter x5 -> x0, waiting for transfers between devices: 107 us -> none  [the longest x1 44.4 us: local(): lax.psum_scatter(jnp.dot(hidden, ffn_out, preferred_element_type=jnp.floa...]
    another operation x2 -> x0, loops' own time: 26.9 us -> none  [the longest x1 13.7 us: attention_forward(): lax.map(one_block, jnp.arange(block_total, dtype=jnp.int32))]
    reduce_sum x19 -> x0, other arithmetic: 23.7 us -> none  [the longest x1 3.66 us: local(): bias_one_grad = jnp.sum(resid_two_grad, axis=0)]
    psum x3, starting transfers between devices: 0.31 us -> 13.1 us  [wide_sum(): return (lax.psum(parts, 'wide'), after)]
    unnamed x96 -> x70, local copies, waits for them, and re-layouts: 21.6 us -> 12.9 us
  transfers between devices with their start and end apart: 10 -> 3, of which waited for: 7 -> 3; matrix products, arithmetic and copies ran while one was open for 13% -> 3% of each run, Pallas kernels for 1% -> 25%
where the time goes in v3:
time: 763 us; the launch traced here: 762 us
  Pallas kernels  369 us (48%)
  waiting for transfers between devices  226 us (30%)
  blocking collectives  77.6 us (10%)
  local copies, waits for them, and re-layouts  26 us (3%)
  other arithmetic  25.4 us (3%)
  between operations  15.3 us (2%)
  starting transfers between devices  13.1 us (2%)
  matrix products  9.8 us (1%)
    psum x3, waiting for transfers between devices, wide_sum(): return (lax.psum(parts, 'wide'), after)  226 us
    pallas_call x1, Pallas kernels, turn(): pl.pallas_call(turn_kernel, in_specs=[hbm, hbm] + [vmem] * 14, out_specs=...  130 us
    pallas_call x1, Pallas kernels, middle(): pl.pallas_call(middle_kernel, in_specs=[vmem] * 10, out_specs=[vmem] * 7,...  107 us
    pallas_call x1, Pallas kernels, ffn(): pl.pallas_call(ffn_kernel, grid_spec=pltpu.PrefetchScalarGridSpec(num_sca...  53.3 us
    pallas_call x1, Pallas kernels, last(): pl.pallas_call(last_kernel, in_specs=[vmem] * 7, out_specs=[vmem] * 3, ou...  41.1 us
    psum x1, blocking collectives, local(): lax.psum(jnp.stack([last_stats[0], stats[4], stats[0], last_stats[1], sta...  40.1 us
    psum x1, blocking collectives, local(): lax.psum((self_bias_grad, cross_bias_grad, ffn_in_bias_grad), 'wide')  37.5 us
    pallas_call x1, Pallas kernels, back(): pl.pallas_call(back_kernel, grid_spec=pltpu.PrefetchScalarGridSpec(num_sc...  20.8 us
  transfers between devices with their start and end apart: 3, of which 3 were waited for; matrix products, arithmetic and copies ran while one was open for 3% of the time, Pallas kernels for 25%

profile of v3, /device:TPU:0, one launch (start us, length us, event | category | flops | bytes accessed | tf_op | source)
XLA Modules:
  0.0 761.6 jit_solution(12066893992497481933)
XLA Ops:
  7.2 0.0 all-reduce.6.cloned.1.call-start
  8.0 0.8 fusion.14
  8.8 1.3 fusion.5
  10.1 1.4 fusion.11
  11.5 2.4 copy.48
  13.9 0.9 copy.43
  14.8 0.7 copy.44.w_ref.qkv_w
  15.5 0.0 copy-start
  15.6 0.0 copy-start.2
  15.6 0.0 copy-start.20
  15.6 0.0 copy-start.22
  15.6 2.7 constant_dynamic-slice_fusion.units
  18.4 17.1 %front.1 = (bf16[2048,1024]{1,0:T(8,128)(2,1)}, bf16[2048,256]{1,0:T(8,128)(2,1)S(1)}, bf16[2048,256]{1,0:T(8,128)(2,1)S(1)}, bf16[2048,256]{1,0:T(8,128)(2,1)S(1)}, bf16[2048,256]{1,0:T(8,128)(2,1)S(1)}) custom-call(s32[2]{0:T(128)S(1)} %compare_select_fusion.1.lens, bf16[2048,1024]{1,0:T(8,128)(2,1)} %x_ref.1, ...), custom_call_target="tpu_custom_call" | custom-call | flops 20000000000 | bytes 16777216 | tf_op jit(solution)/shard_map/front/pallas_call | solution.py:106
  35.5 0.0 copy-start.4
  35.5 1.0 copy-done.4
  36.5 1.0 copy-done.6
  37.5 1.0 copy-done.8
  38.5 0.7 concatenate.6.vec
  39.1 106.7 %middle.1 = (bf16[2048,1024]{1,0:T(8,128)(2,1)}, bf16[2048,1024]{1,0:T(8,128)(2,1)}, bf16[2048,256]{1,0:T(8,128)(2,1)}, bf16[2048,256]{1,0:T(8,128)(2,1)}, bf16[...) custom-call(bf16[2048,256]{1,0:T(8,128)(2,1)} %copy-done.8, ...), custom_call_target="tpu_custom_call" | custom-call | flops 99999997952 | bytes 25165824 | tf_op jit(solution)/shard_map/middle/pallas_call | solution.py:389
  145.8 53.3 %ffn.1 = (bf16[2048,1024]{1,0:T(8,128)(2,1)}, bf16[2048,1024]{1,0:T(8,128)(2,1)}, bf16[1024,2048]{1,0:T(8,128)(2,1)}, bf16[2048,1024]{1,0:T(8,128)(2,1)}, f32[1,2048]{1,0:T(1,128)}) custom-call(s32[2]{0:T(128)} %copy-done.2, bf16[2048,1024]{1,0:T(8,128)(2,1)} %get-tuple-element.53.h_ref, bf16[2048,1024]{1,0:T(8,128)(2,1)} %e_ref.1, ...), custom_call_target="tpu_custom_call" | custom-call | flops 60000002048 | bytes 33554432 | tf_op jit(solution)/shard_map/ffn/pallas_call | solution.py:463
  199.1 0.0 copy-start.3
  199.1 0.0 copy-start.29
  199.1 0.0 copy-start.21
  199.2 0.0 copy-start.23
  199.2 0.0 all-reduce.6.cloned.1.call-update
  199.2 13.0 %all-reduce.8.cloned.1.call-start = ((), (), s32[]{:S(2)}) async-start(), calls=%async_computation.1 | async-start | bytes 1048576 | tf_op jit(solution)/shard_map/psum | solution.py:765
  212.3 0.1 fusion
  212.4 0.6 pad_maximum_fusion.vec
  213.1 2.4 dynamic-slice_select_fusion.e_own
  215.5 0.8 broadcast_in_dim.51.keep
  216.3 0.8 broadcast_in_dim.50.valid
  217.2 129.8 %turn.1 = (bf16[512,1024]{1,0:T(8,128)(2,1)}, f32[512,1024]{1,0:T(8,128)}, bf16[2048,256]{1,0:T(8,128)(2,1)}, bf16[512,512]{1,0:T(8,128)(2,1)}, bf16[256,1024]{1...) custom-call(bf16[2048,1024]{1,0:T(8,128)(2,1)} %get-tuple-element.54, ...), custom_call_target="tpu_custom_call" | custom-call | flops 99999997952 | bytes 25165824 | tf_op jit(solution)/shard_map/turn/pallas_call | solution.py:653
  347.0 3.1 convolution_convert_fusion.1
  350.1 1.2 copy-done.7
  351.3 1.2 copy-done.9
  352.5 20.8 %back.1.dqkv = bf16[2048,768]{1,0:T(8,128)(2,1)} custom-call(s32[2]{0:T(128)S(1)} %copy-done.3, bf16[2048,256]{1,0:T(8,128)(2,1)S(1)} %get-tuple-element.63.q_ref, bf16[2048,256]{1,0:T(8,128)(2,1)S(1)} %copy-done.5, bf16[2048,256]{1,0:T(8,128)(2,1)S(1)} %copy-done.7, bf16[2048,256]{1,0:T(8,128)(2,1)S(1)} %copy-done.9), custom_call_target="tpu_custom_call" | custom-call | flops 30000001024 | bytes 8388608 | tf_op jit(solution)/shard_map/back/pallas_call | solution.py:164
  373.3 0.4 all-reduce.6.cloned.1.call-done
  373.7 0.0 all-reduce.8.cloned.1.call-update
  373.8 0.0 all-reduce.10.cloned.1.call-start
  373.8 0.0 copy-start.17
  373.8 6.7 convolution_convert_fusion
  380.6 2.0 copy.47
  382.6 89.2 %all-reduce.8.cloned.1.call-done = bf16[1024,256]{1,0:T(8,128)(2,1)} async-done(((bf16[1024,256]{1,0:T(8,128)(2,1)}), bf16[1024,256]{1,0:T(8,128)(2,1)}) %all-reduce.8.cloned.1.call-update) | async-done | bytes 524304 | tf_op jit(solution)/shard_map/psum | solution.py:765
  471.8 1.6 copy.46
  473.4 0.0 all-reduce.10.cloned.1.call-update
  473.5 41.1 %last.1 = (f32[512,1024]{1,0:T(8,128)}, f32[128,1024]{1,0:T(8,128)}, f32[8,1024]{1,0:T(8,128)}) custom-call(bf16[2048,768]{1,0:T(8,128)(2,1)} %back.1.dqkv, bf16[512,512]{1,0:T(8,128)(2,1)} %get-tuple-element.67.dkv, bf16[512,1024]{1,0:T(8,128)(2,1)} %constant_dynamic-slice_fusion.units, f32[512,1024]{1,0:T(8,128)} %get-tuple-element.68.dx1, ...), custom_call_target="tpu_custom_call" | custom-call | flops 30000001024 | bytes 16777216 | tf_op jit(solution)/shard_map/last/pallas_call | solution.py:746
  514.6 0.8 fusion.10
  515.4 0.1 stack.12
  515.5 0.3 convert_reduce_fusion.1
  515.9 37.5 %all-reduce = (f32[2,256]{1,0:T(2,128)}, f32[2,256]{1,0:T(2,128)}, f32[2048]{0:T(1024)}) all-reduce(f32[2,256]{1,0:T(2,128)S(1)} %pad_maximum_fusion.1, f32[2,256]{1,0:T(2,128)S(1)} %copy-done.30, f32[2048]{0:T(1024)S(1)} %bitcast.27), channel_id=1, replica_groups=mesh['wide'=8,'narrow'=4] {'wide'}, use_global_device_ids=true, to_apply=%region_7.8 | all-reduce | flops 3072 | bytes 24576 | tf_op jit(solution)/shard_map/psum | solution.py:881
  553.3 40.1 %psum.77 = f32[9,1024]{1,0:T(8,128)S(1)} all-reduce(f32[9,1024]{1,0:T(8,128)S(1)} %stack.12), channel_id=1, replica_groups=mesh['wide'=8,'narrow'=4] {'wide','narrow'}, use_global_device_ids=true, to_apply=%region_1.2 | all-reduce | flops 9216 | bytes 73728 | tf_op jit(solution)/shard_map/psum | solution.py:860
  593.4 0.6 fusion.8
  594.1 6.7 convert_element_type.65
  600.8 1.0 convert_element_type.62
  601.8 135.9 %all-reduce.10.cloned.1.call-done = (bf16[1024,3,256]{2,0,1:T(8,128)(2,1)}, bf16[256,1024]{1,0:T(8,128)(2,1)}, bf16[1024,2,256]{2,1,0:T(2,128)(2,1)}, bf16[256,1024]{1,0:T(8,128)(2,1)}, bf16[2048,1024]{1,0:T(8,128)(2,1)}) async-done(((bf16[1024,3,256]{2,0,1:T(8,128)(2,1)}, bf16[256,1024]{1,0:T(8,128)(2,1)}, bf16[1024,2,256]{2,1,0:T(2,128)(2,1)}, bf16[256,1024]{1,0:T(8,128)(2,1)}, ...) | async-done | bytes 7864336 | tf_op jit(solution)/shard_map/psum | solution.py:765
  737.7 2.2 convert_element_type.61
  739.9 2.2 convert_element_type.64
  742.2 1.9 convert_element_type.58
  744.1 2.0 convert_element_type.63
  746.1 4.4 convert_element_type.66
  750.6 1.0 copy.61
  751.6 1.0 copy-done.11
  752.5 1.3 copy.62
  753.9 0.8 copy.63
  (56 shorter events, 0.2 us)
Async XLA Ops:
  7.2 6.7 copy-start.12
  7.2 366.6 %all-reduce.6.cloned.1.call-start = ((), (), s32[]{:S(2)}) async-start(), calls=%async_computation | async-start | bytes 8388608 | tf_op jit(solution)/shard_map/psum | solution.py:765
  13.9 1.6 copy-start.31
  13.9 1.6 copy-start.26
  13.9 1.6 copy-start.27
  15.5 20.0 %copy-start = (bf16[1024,768]{1,0:T(8,128)(2,1)}, bf16[1024,768]{1,0:T(8,128)(2,1)S(1)}, u32[]{:S(2)}) copy-start(bf16[1024,768]{1,0:T(8,128)(2,1)S(1)} %copy.44.w_ref.qkv_w) | copy-start | bytes 4718596
  15.6 19.9 %copy-start.2 = (s32[2]{0:T(128)}, s32[2]{0:T(128)S(1)}, u32[]{:S(2)}) copy-start(s32[2]{0:T(128)S(1)} %compare_select_fusion.1.lens) | copy-start | bytes 28
  15.6 19.9 %copy-start.1 = (f32[1,1024]{1,0:T(1,128)}, f32[1,1024]{1,0:T(1,128)S(1)}, u32[]{:S(2)}) copy-start(f32[1,1024]{1,0:T(1,128)S(1)} %get-tuple-element.126.g_ref.gain) | copy-start | bytes 12292
  15.6 22.8 %copy-start.20 = (f32[1,1024]{1,0:T(1,128)}, f32[1,1024]{1,0:T(1,128)S(1)}, u32[]{:S(2)}) copy-start(f32[1,1024]{1,0:T(1,128)S(1)} %get-tuple-element.125) | copy-start | bytes 12292
  15.6 22.8 %copy-start.22 = (f32[1,1024]{1,0:T(1,128)}, f32[1,1024]{1,0:T(1,128)S(1)}, u32[]{:S(2)}) copy-start(f32[1,1024]{1,0:T(1,128)S(1)} %get-tuple-element.127) | copy-start | bytes 12292
  35.5 1.0 copy-start.4
  36.5 1.0 copy-start.6
  37.5 1.0 copy-start.8
  199.1 13.1 %copy-start.3 = (s32[2]{0:T(128)S(1)}, s32[2]{0:T(128)}, u32[]{:S(2)}) copy-start(s32[2]{0:T(128)} %copy-done.2) | copy-start | bytes 28
  199.1 13.2 %copy-start.29 = (f32[1,2,2,128]{3,2,1,0:T(2,128)S(1)}, f32[1,2,2,128]{3,2,1,0:T(2,128)}, u32[]{:S(2)}) copy-start(f32[1,2,2,128]{3,2,1,0:T(2,128)} %get-tuple-element.123) | copy-start | bytes 6148
  199.1 13.3 %copy-start.21 = (f32[1,1024]{1,0:T(1,128)S(1)}, f32[1,1024]{1,0:T(1,128)}, u32[]{:S(2)}) copy-start(f32[1,1024]{1,0:T(1,128)} %copy-done.20) | copy-start | bytes 12292
  199.2 13.3 %copy-start.23 = (f32[1,1024]{1,0:T(1,128)S(1)}, f32[1,1024]{1,0:T(1,128)}, u32[]{:S(2)}) copy-start(f32[1,1024]{1,0:T(1,128)} %copy-done.22) | copy-start | bytes 12292
  199.2 13.2 %copy-start.25 = (f32[1,1024]{1,0:T(1,128)S(1)}, f32[1,1024]{1,0:T(1,128)}, u32[]{:S(2)}) copy-start(f32[1,1024]{1,0:T(1,128)} %get-tuple-element.112) | copy-start | bytes 12292
  199.2 272.6 %all-reduce.8.cloned.1.call-start = ((), (), s32[]{:S(2)}) async-start(), calls=%async_computation.1 | async-start | bytes 1048576 | tf_op jit(solution)/shard_map/psum | solution.py:765
  217.2 132.9 %copy-start.5 = (bf16[2048,256]{1,0:T(8,128)(2,1)S(1)}, bf16[2048,256]{1,0:T(8,128)(2,1)}, u32[]{:S(2)}) copy-start(bf16[2048,256]{1,0:T(8,128)(2,1)} %copy-done.4) | copy-start | bytes 3145732
  350.1 1.2 copy-start.7
  351.3 1.2 copy-start.9
  373.8 363.9 %all-reduce.10.cloned.1.call-start = ((), (), s32[]{:S(2)}) async-start(), calls=%async_computation.2 | async-start | bytes 15728640 | tf_op jit(solution)/shard_map/psum | solution.py:765
  373.8 6.7 copy-start.17
  473.4 42.0 %copy-start.24 = (f32[8,1024]{1,0:T(8,128)S(1)}, f32[8,1024]{1,0:T(8,128)}, u32[]{:S(2)}) copy-start(f32[8,1024]{1,0:T(8,128)} %get-tuple-element.72) | copy-start | bytes 98308
  473.4 42.1 %copy-start.14 = (bf16[2048,768]{1,0:T(8,128)(2,1)S(1)}, bf16[2048,768]{1,0:T(8,128)(2,1)}, u32[]{:S(2)}) copy-start(bf16[2048,768]{1,0:T(8,128)(2,1)} %back.1.dqkv) | copy-start | bytes 9437188
  473.4 42.4 %copy-start.28 = (f32[1,2048]{1,0:T(1,128)S(1)}, f32[1,2048]{1,0:T(1,128)}, u32[]{:S(2)}) copy-start(f32[1,2048]{1,0:T(1,128)} %get-tuple-element.86) | copy-start | bytes 24580
  473.5 42.4 %copy-start.30 = (f32[2,256]{1,0:T(2,128)S(1)}, f32[2,256]{1,0:T(2,128)}, u32[]{:S(2)}) copy-start(f32[2,256]{1,0:T(2,128)} %get-tuple-element.83) | copy-start | bytes 6148
  594.1 6.7 copy-start.18
  737.7 4.5 copy-start.13
  739.9 4.2 copy-start.15
  742.2 4.0 copy-start.10
  746.1 4.4 copy-start.16
  750.6 2.0 copy-start.11
  750.6 3.3 copy-start.19
Sparse Core Ops, SparseCore 0:
  199.3 174.3 all-reduce.5
  377.2 94.6 all-reduce.7
  478.6 259.0 all-reduce.9

commit v4 on v3

--- a/solution.py
+++ b/solution.py
@@ -1,3 +1,5 @@
+import functools
+
 import jax
 import jax.numpy as jnp
 from jax import lax
@@ -183,23 +185,136 @@
     return index, core, (index + 2) % NARROW, (core + 2) % NARROW
 
 
-def greet():
+def greet(*wide_peers):
     _, core, cross, _ = place()
     barrier = pltpu.get_barrier_semaphore()
     for peer in (core, cross):
         pl.semaphore_signal(barrier, inc=1, device_id={"narrow": peer}, device_id_type=MESH)
-    pl.semaphore_wait(barrier, 2)
-
-
-def remote(source, target, sems, kind, step, peer):
+    for peer in wide_peers:
+        pl.semaphore_signal(barrier, inc=1, device_id={"wide": peer}, device_id_type=MESH)
+    pl.semaphore_wait(barrier, 2 + len(wide_peers))
+
+
+def remote(source, target, sems, kind, step, peer, axis="narrow"):
     return pltpu.make_async_remote_copy(
         src_ref=source,
         dst_ref=target,
         send_sem=sems.at[0, kind, step],
         recv_sem=sems.at[1, kind, step],
-        device_id={"narrow": peer},
+        device_id={axis: peer},
         device_id_type=MESH,
     )
+
+
+def ring_place(count):
+    wide = lax.axis_index("wide")
+    odd, half = wide % 2, wide // 2
+    spot = odd * (half + 1) + (1 - odd) * ((count - half) % count)
+
+    def at(where):
+        high = ((where + count - 1) % count) // (count // 2)
+        return (1 - high) * (2 * where - 1) + high * ((2 * (count - where)) % (2 * count))
+
+    return spot, at((spot + 1) % count), at((spot + count - 1) % count)
+
+
+class Ring:
+    UNITS = 4
+
+    def __init__(self, count, sources, outs, view, arrived, held, sems, fetch_sems, keep_sems):
+        self.count, self.sources, self.outs, self.view = count, sources, outs, view
+        self.arrived, self.held, self.sems = arrived, held, sems
+        self.fetch_sems, self.keep_sems = fetch_sems, keep_sems
+        spot, following, previous = ring_place(count)
+        self.spots = (spot, (count - spot) % count)
+        self.peers = (following, previous)
+
+    def block(self, refs, unit, back_by):
+        shard = (self.spots[unit // 2] + 2 * self.count - back_by) % self.count
+        return self.view(refs[unit // 2], unit // 2, unit % 2, shard)
+
+    def send(self, source, target, kind, unit, step):
+        return remote(source, target, self.sems, kind * self.UNITS + unit, step, self.peers[unit // 2], "wide")
+
+    def sum_copy(self, unit, step, first=False):
+        source = self.block(self.sources, unit, 0) if first else self.arrived.at[unit, jnp.maximum(step - 1, 0)]
+        return self.send(source, self.arrived.at[unit, step], 0, unit, step)
+
+    def fetch(self, unit, step):
+        slot = step % 2
+        return pltpu.make_async_copy(
+            self.block(self.sources, unit, step + 1), self.held.at[unit, slot], self.fetch_sems.at[unit, slot]
+        )
+
+    def keep(self, unit):
+        return pltpu.make_async_copy(
+            self.arrived.at[unit, self.count - 2], self.block(self.outs, unit, self.count - 1), self.keep_sems.at[unit]
+        )
+
+    def spread_copy(self, unit, step, first=False):
+        target = self.block(self.outs, unit, self.count - 1 + step)
+        source = self.arrived.at[unit, self.count - 2] if first else target
+        return self.send(source, target, 1, unit, step)
+
+    def start(self):
+        for unit in range(self.UNITS):
+            self.sum_copy(unit, 0, True).start()
+            self.fetch(unit, 0).start()
+            self.fetch(unit, 1).start()
+
+    def serve(self, turn, unit):
+        last = self.count - 2
+
+        @pl.when(turn <= last)
+        def _():
+            self.sum_copy(unit, turn).wait_recv()
+            self.fetch(unit, turn).wait()
+            total = self.held[unit, turn % 2].astype(jnp.float32) + self.arrived[unit, turn].astype(jnp.float32)
+            self.arrived[unit, turn] = total.astype(jnp.bfloat16)
+
+            @pl.when(turn < last)
+            def _():
+                self.sum_copy(unit, turn + 1).start()
+
+            @pl.when(turn < last - 1)
+            def _():
+                self.fetch(unit, turn + 2).start()
+
+            @pl.when(turn == last)
+            def _():
+                self.spread_copy(unit, 0, True).start()
+                self.keep(unit).start()
+
+        @pl.when((turn > last) & (turn <= 2 * last + 1))
+        def _():
+            step = turn - last - 1
+            self.spread_copy(unit, step).wait_recv()
+
+            @pl.when(step < last)
+            def _():
+                self.spread_copy(unit, step + 1).start()
+
+    def finish(self):
+        for unit in range(self.UNITS):
+            self.keep(unit).wait()
+
+        def body(step, carry):
+            for unit in range(self.UNITS):
+                self.sum_copy(unit, step).wait_send()
+                self.spread_copy(unit, step).wait_send()
+            return carry
+
+        lax.fori_loop(0, self.count - 1, body, 0)
+
+
+def ring_scratch(count, block):
+    return [
+        pltpu.VMEM((Ring.UNITS, count - 1) + block, jnp.bfloat16),
+        pltpu.VMEM((Ring.UNITS, 2) + block, jnp.bfloat16),
+        pltpu.SemaphoreType.DMA((2, 2 * Ring.UNITS, count - 1)),
+        pltpu.SemaphoreType.DMA((Ring.UNITS, 2)),
+        pltpu.SemaphoreType.DMA((Ring.UNITS,)),
+    ]
 
 
 class Hop:
@@ -288,7 +403,10 @@
     ]
 
 
-def stages(steps, work):
+def stages(steps, work, ring=None, extra=None, ticks=0):
+    ticks = max(ticks, steps + len(work) - 1)
+    per_tick = 0 if ring is None else -(-2 * (ring.count - 1) // ticks)
+
     def body(tick, carry):
         for delay, stage in enumerate(work):
             step = tick - delay
@@ -297,9 +415,17 @@
             def _():
                 stage(step)
 
+            unit = (delay + 1) * Ring.UNITS // len(work) - 1
+            if per_tick and unit != delay * Ring.UNITS // len(work) - 1:
+                if per_tick == 1:
+                    ring.serve(tick, unit)
+                else:
+                    lax.fori_loop(0, per_tick, lambda i, c: (ring.serve(tick * per_tick + i, unit), c)[1], 0)
+        if extra is not None:
+            extra(tick)
         return carry
 
-    lax.fori_loop(0, steps + len(work) - 1, body, 0)
+    lax.fori_loop(0, ticks, body, 0)
 
 
 def middle_kernel(
@@ -522,21 +648,29 @@
 
 
 def turn_kernel(
-    third, ffn_part, x1, x2, e_own, valid, h2, q2, c2, kv2, c1, keep, vec, co_w, cq_w, so_w,
-    y, dx1, dc1, dkv, co_g, cq_g, so_g, bias_g, stats,
-    mine3, theirs3, core3, fromx3, sem3, mine4, theirs4, core4, fromx4, sem4,
+    third, in_g, out_g, x1, x2, e_own, h2, q2, c2, kv2, c1, keep, vec, co_w, cq_w, so_w,
+    in_sum, out_sum, dx1, dc1, dkv, co_g, cq_g, so_g, bias_g, stats,
+    mine3, theirs3, core3, fromx3, sem3,
     part5, core5, tox5, fromx5, sem5, full3, full5, dx2, co_acc, cq_acc, so_acc, dkv_acc, fetch_sem,
+    *ring_refs, count,
 ):
     steps, chunk, width = tox5.shape
     cols = q2.shape[1]
     slots = bias_g.shape[0]
     texts = kv2.shape[0] // slots
-    greet()
+
+    def ring_view(ref, way, half, shard):
+        high = width // count
+        if way == 0:
+            return ref.at[pl.ds(pl.multiple_of(shard * high, high), high), pl.ds(half * width, width)]
+        return ref.at[pl.ds(pl.multiple_of(shard * 2 * high + half * high, high), high), :]
+
+    ring = Ring(count, (in_g, out_g), (in_sum, out_sum), ring_view, *ring_refs)
+    greet(*ring.peers)
+    ring.start()
     three = FarHop(third, core3, None, fromx3, full3, sem3, chunk)
-    four = FarHop(ffn_part, core4, None, fromx4, None, sem4, chunk)
     five = Hop(part5, core5, tox5, fromx5, full5, sem5, chunk)
-    three.fetch(mine3, theirs3, fetch_sem.at[0])
-    four.fetch(mine4, theirs4, fetch_sem.at[1])
+    three.fetch(mine3, theirs3, fetch_sem)
 
     def start(step, carry):
         three.send_core(step)
@@ -546,7 +680,6 @@
     for ref in (co_acc, cq_acc, so_acc, dkv_acc, bias_g, stats):
         ref[...] = jnp.zeros_like(ref)
     three.fetched()
-    four.fetched()
     scale = jnp.bfloat16(HEAD_DIM**-0.5)
 
     def norm_three(step):
@@ -561,7 +694,6 @@
         stats[3:4, :] += column_sum(total)
         dx2[rows, :] = total
         three.send_gather(step, total.astype(jnp.bfloat16))
-        four.send_core(step)
 
     def cross(step):
         three.gathered(step)
@@ -612,18 +744,13 @@
         five.put(dc1, step, dc1_rows)
         so_acc[...] += dot_tn(five.take(c1, step), grads)
 
-    def output(step):
-        rows = four.own_rows(step)
-        total = x2[rows, :] + four.result(step) + vec[2:3, :]
-        y[rows, :] = jnp.where(valid[rows, :1] > 0.5, total, 0.0).astype(jnp.bfloat16)
-
     stages(
         steps,
         [
             three.send_cross, norm_three, three.forward, cross,
             five.send_cross, norm_two, five.forward, last,
-            four.send_cross, output,
         ],
+        ring,
     )
     dkv[...] = dkv_acc[...].astype(jnp.bfloat16)
     bias_g[1:2, :] = column_sum(dkv[:, cols:].astype(jnp.float32))
@@ -633,14 +760,14 @@
 
     def finish(step, carry):
         three.finish(step)
-        four.finish(step, False)
         five.finish(step)
         return carry
 
     lax.fori_loop(0, steps, finish, 0)
-
-
-def turn(third, ffn_part, x1, x2, e_own, valid, h2, q2, c2, kv2, c1, keep, vec, co_w, cq_w, so_w):
+    ring.finish()
+
+
+def turn(count, third, in_g, out_g, x1, x2, e_own, h2, q2, c2, kv2, c1, keep, vec, co_w, cq_w, so_w):
     rows, cols = c1.shape
     own, width = x1.shape
     chunk = own // STEPS
@@ -651,11 +778,12 @@
     hop = hop_scratch(own, chunk, width)
     far = [pltpu.VMEM((own, width), bf)] * 2 + [hop[0], hop[2], hop[3]]
     return pl.pallas_call(
-        turn_kernel,
-        in_specs=[hbm, hbm] + [vmem] * 14,
-        out_specs=[vmem] * 9,
+        functools.partial(turn_kernel, count=count),
+        in_specs=[hbm] * 3 + [vmem] * 13,
+        out_specs=[hbm] * 2 + [vmem] * 8,
         out_shape=[
-            shape((own, width), bf),
+            shape(in_g.shape, bf),
+            shape(out_g.shape, bf),
             shape((own, width), f32),
             shape((rows, cols), bf),
             shape(kv2.shape, bf),
@@ -666,7 +794,6 @@
             shape((8, width), f32),
         ],
         scratch_shapes=far
-        + far
         + [pltpu.VMEM((rows, width), bf)]
         + hop
         + [pltpu.VMEM((rows, width), bf)] * 2
@@ -676,36 +803,116 @@
             pltpu.VMEM((width, cols), f32),
             pltpu.VMEM((cols, width), f32),
             pltpu.VMEM(kv2.shape, f32),
-            pltpu.SemaphoreType.DMA((2, 2)),
-        ],
+            pltpu.SemaphoreType.DMA((2,)),
+        ]
+        + ring_scratch(count, (width // count, width)),
         compiler_params=pltpu.CompilerParams(collective_id=1, has_side_effects=True, vmem_limit_bytes=60 * MIB),
         cost_estimate=pl.CostEstimate(flops=100 * 10**9, bytes_accessed=24 * MIB, transcendentals=4 * MIB),
         name="turn",
-    )(third, ffn_part, x1, x2, e_own, valid, h2, q2, c2, kv2, c1, keep, vec, co_w, cq_w, so_w)
+    )(third, in_g, out_g, x1, x2, e_own, h2, q2, c2, kv2, c1, keep, vec, co_w, cq_w, so_w)
+
+
+SMALL = 16
+NORM_ROWS = 9
+
+
+class Small:
+    def __init__(self, count, block, near, far, sems):
+        self.count, self.mine, self.near, self.far, self.sems = count, block, near, far, sems
+        self.index, self.core, self.cross, _ = place()
+        self.spot, self.following, _ = ring_place(count)
+
+    def near_copy(self, kind):
+        owner = self.cross if kind == 2 else self.index
+        return remote(self.near.at[owner], self.near.at[owner], self.sems, 0, kind, (self.cross, self.core, self.core)[kind])
+
+    def far_copy(self, step):
+        block = self.far.at[(self.spot + self.count - step) % self.count]
+        return remote(block, block, self.sems, 1, step, self.following, "wide")
+
+    def begin(self):
+        self.near[self.index] = self.mine[...]
+        self.near_copy(0).start()
+        self.near_copy(1).start()
+
+    def forward(self):
+        self.near_copy(0).wait_recv()
+        self.near_copy(2).start()
+
+    def launch(self):
+        self.near_copy(1).wait_recv()
+        self.near_copy(2).wait_recv()
+        both = self.near[0]
+        for owner in range(1, NARROW):
+            both += self.near[owner]
+        row = lax.broadcasted_iota(jnp.int32, both.shape, 0)
+        self.far[self.spot] = jnp.where(row < SMALL - NORM_ROWS, self.mine[...], both)
+        self.far_copy(0).start()
+
+    def rotate(self, step):
+        self.far_copy(step).wait_recv()
+
+        @pl.when(step < self.count - 2)
+        def _():
+            self.far_copy(step + 1).start()
+
+    def finish(self, out):
+        for kind in range(3):
+            self.near_copy(kind).wait_send()
+
+        def body(step, carry):
+            self.far_copy(step).wait_send()
+            return carry
+
+        lax.fori_loop(0, self.count - 1, body, 0)
+        out[...] = jnp.zeros_like(out)
+
+        def add(spot, carry):
+            out[...] += self.far[spot]
+            return carry
+
+        lax.fori_loop(0, self.count, add, 0)
 
 
 def last_kernel(
-    dqkv, dkv, units, dx1, gain, qkv_w, kv_w, units_g, text_g, stats,
+    ffn_part, g0, g1, dqkv, dkv, units, dx1, x2, valid, before, stats, vec, qkv_w, kv_w,
+    sum0, sum1, y, units_g, text_g, small_sum,
+    mine4, theirs4, core4, fromx4, sem4,
     part6, core6, tox6, fromx6, sem6, part7, core7, tox7, fromx7, sem7,
+    fetch_sem, block, near, far, small_sem, *ring_refs, count,
 ):
-    steps, chunk, _ = tox6.shape
+    steps, chunk, width = tox6.shape
     text_steps = tox7.shape[0]
-    greet()
+
+    def ring_view(ref, way, half, shard):
+        high = width // count
+        return ref.at[pl.ds(pl.multiple_of(shard * high, high), high), pl.ds(half * (width // 2), width // 2)]
+
+    ring = Ring(count, (g0, g1), (sum0, sum1), ring_view, *ring_refs)
+    small = Small(count, block, near, far, small_sem)
+    greet(*ring.peers)
+    ring.start()
+    four = FarHop(ffn_part, core4, None, fromx4, None, sem4, chunk)
     six = Hop(part6, core6, tox6, fromx6, None, sem6, chunk)
     seven = Hop(part7, core7, tox7, fromx7, None, sem7, chunk)
-    stats[...] = jnp.zeros_like(stats)
+    four.fetch(mine4, theirs4, fetch_sem)
+    four.fetched()
+    block[: SMALL - NORM_ROWS, :] = before[...]
+    block[SMALL - NORM_ROWS :, :] = jnp.concatenate([stats[:7, :], jnp.zeros((2, width), jnp.float32)])
+    gain = vec[0:1, :]
 
     def project(step):
         six.put(part6, step, dot_nt(six.take(dqkv, step), qkv_w[...]).astype(jnp.bfloat16))
         six.send_core(step)
+        four.send_core(step)
 
     def norm_one(step):
         rows = six.own_rows(step)
         grad_in = six.result(step)
-        _, normed, inv_std = norm_forward(units[rows, :].astype(jnp.float32), gain[...], gain[...])
-        stats[0:1, :] += column_sum(grad_in * normed)
-        stats[1:2, :] += column_sum(grad_in)
-        units_g[rows, :] = dx1[rows, :] + norm_backward(grad_in, normed, inv_std, gain[...])
+        _, normed, inv_std = norm_forward(units[rows, :].astype(jnp.float32), gain, gain)
+        block[SMALL - 2 : SMALL - 1, :] += column_sum(grad_in * normed)
+        block[SMALL - 1 : SMALL, :] += column_sum(grad_in)
+        units_g[rows, :] = dx1[rows, :] + norm_backward(grad_in, normed, inv_std, gain)
 
     def text_only(work):
         def stage(step):
@@ -722,20 +929,45 @@
     def text_result(step):
         text_g[seven.own_rows(step), :] = seven.result(step)
 
+    def output(step):
+        rows = four.own_rows(step)
+        total = x2[rows, :] + four.result(step) + vec[1:2, :]
+        y[rows, :] = jnp.where(valid[rows, :1] > 0.5, total, 0.0).astype(jnp.bfloat16)
+
+    ready = steps + 2
+
+    def extra(tick):
+        for when, work in enumerate((small.begin, small.forward, small.launch)):
+            pl.when(tick == ready + when)(work)
+        step = tick - ready - 3
+
+        @pl.when((step >= 0) & (step < count - 1))
+        def _():
+            small.rotate(step)
+
     stages(
         steps,
-        [project, six.send_cross, norm_one, text_only(text_project), text_only(seven.send_cross), text_only(text_result)],
+        [
+            project, six.send_cross, norm_one, four.send_cross, output,
+            text_only(text_project), text_only(seven.send_cross), text_only(text_result),
+        ],
+        ring,
+        extra,
+        ready + 3 + count - 1,
     )
 
     def finish(step, carry):
+        four.finish(step, False)
         six.finish(step, False)
         text_only(lambda s: seven.finish(s, False))(step)
         return carry
 
     lax.fori_loop(0, steps, finish, 0)
-
-
-def last(dqkv, dkv, units_own, dx1, gain_vec, qkv_w, kv_w):
+    ring.finish()
+    small.finish(small_sum)
+
+
+def last(count, ffn_part, g0, g1, dqkv, dkv, units_own, dx1, x2, valid, before, stats, vec, qkv_w, kv_w):
     rows = dqkv.shape[0]
     own, width = units_own.shape
     chunk = own // STEPS
@@ -743,26 +975,38 @@
     bf, f32 = jnp.bfloat16, jnp.float32
     shape = jax.ShapeDtypeStruct
     vmem = pl.BlockSpec(memory_space=pltpu.VMEM)
+    hbm = pl.BlockSpec(memory_space=pl.ANY)
+    hop = hop_scratch(own, chunk, width)
+    far = [pltpu.VMEM((own, width), bf)] * 2 + [hop[0], hop[2], hop[3]]
     return pl.pallas_call(
-        last_kernel,
-        in_specs=[vmem] * 7,
-        out_specs=[vmem] * 3,
-        out_shape=[shape((own, width), f32), shape((text_own, width), f32), shape((8, width), f32)],
-        scratch_shapes=[pltpu.VMEM((rows, width), bf)]
-        + hop_scratch(own, chunk, width)
+        functools.partial(last_kernel, count=count),
+        in_specs=[hbm] * 3 + [vmem] * 11,
+        out_specs=[hbm] * 2 + [vmem] * 4,
+        out_shape=[
+            shape(g0.shape, bf),
+            shape(g1.shape, bf),
+            shape((own, width), bf),
+            shape((own, width), f32),
+            shape((text_own, width), f32),
+            shape((SMALL, width), f32),
+        ],
+        scratch_shapes=far
+        + [pltpu.VMEM((rows, width), bf)]
+        + hop
         + [pltpu.VMEM((dkv.shape[0], width), bf)]
-        + hop_scratch(text_own, chunk, width),
+        + hop_scratch(text_own, chunk, width)
+        + [
+            pltpu.SemaphoreType.DMA((2,)),
+            pltpu.VMEM((SMALL, width), f32),
+            pltpu.VMEM((NARROW, SMALL, width), f32),
+            pltpu.VMEM((count, SMALL, width), f32),
+            pltpu.SemaphoreType.DMA((2, 2, max(count - 1, 3))),
+        ]
+        + ring_scratch(count, (width // count, width // 2)),
         compiler_params=pltpu.CompilerParams(collective_id=2, has_side_effects=True, vmem_limit_bytes=58 * MIB),
         cost_estimate=pl.CostEstimate(flops=30 * 10**9, bytes_accessed=16 * MIB, transcendentals=0),
         name="last",
-    )(dqkv, dkv, units_own, dx1, gain_vec.reshape(1, -1), qkv_w, kv_w)
-
-
-def wide_sum(arrays, after=None):
-    parts = tuple(a.astype(jnp.bfloat16) for a in arrays)
-    if after is not None:
-        parts, after = lax.optimization_barrier((parts, after))
-    return lax.psum(parts, "wide"), after
+    )(ffn_part, g0, g1, dqkv, dkv, units_own, dx1, x2, valid, before, stats, vec, qkv_w, kv_w)
 
 
 def local(
@@ -825,88 +1069,82 @@
     )
     grad_own = jnp.where(valid_own[:, None], own(out_grad), jnp.zeros((), out_grad.dtype))
     spread = own_rows // STEPS * NARROW // slot_count
-    output, resid_one_grad, self_context_grad, text_kv_grad, cross_out_grad, cross_q_grad, self_out_grad, cross_bias_grad, stats = turn(
+    count = lax.axis_size("wide")
+    ffn_in_grad, ffn_out_grad, resid_one_grad, self_context_grad, text_kv_grad, cross_out_grad, cross_q_grad, self_out_grad, cross_bias_grad, stats = turn(
+        count,
         third_part,
-        ffn_part,
+        ffn_in_grad,
+        ffn_out_grad,
         resid_one,
         resid_two,
         grad_own,
-        jnp.broadcast_to(valid_own[:, None].astype(jnp.float32), (own_rows, 128)),
         second_all,
         cross_queries,
         cross_context,
         text_kv,
         self_context,
         jnp.broadcast_to(keep.reshape(-1, 1), (keep.size, spread)),
-        jnp.concatenate([norm_gain[2:3], norm_gain[1:2], out_bias[2:3]]),
+        jnp.concatenate([norm_gain[2:3], norm_gain[1:2]]),
         cross_out,
         cross_q,
         self_out,
     )
     qkv_grad = back(lengths, queries, key_rows, value_rows, self_context_grad)
     cols = queries.shape[1]
-    self_bias_grad = jnp.stack(
+    self_qkv_grad = dot_tn(first_in, qkv_grad).astype(jnp.bfloat16)
+    cross_kv_grad = dot_tn(text, text_kv_grad).astype(jnp.bfloat16)
+    half = cross_kv_grad.shape[0] // 2
+    width = units.shape[1]
+    before = jnp.concatenate(
         [
             jnp.sum(qkv_grad[:, :cols], axis=0, dtype=jnp.float32),
             jnp.sum(qkv_grad[:, 2 * cols :], axis=0, dtype=jnp.float32),
+            cross_bias_grad.reshape(-1),
+            ffn_in_bias_grad.reshape(-1),
         ]
+    ).reshape(-1, width)
+    small_rows = SMALL // 2
+    summed_one, summed_two, output, units_grad, text_grad, small = last(
+        count,
+        ffn_part,
+        jnp.concatenate([self_qkv_grad, cross_q_grad], axis=1),
+        jnp.concatenate(
+            [cross_out_grad, self_out_grad, jnp.concatenate([cross_kv_grad[:half], cross_kv_grad[half:]], axis=1)]
+        ),
+        qkv_grad,
+        text_kv_grad,
+        own_units,
+        resid_one_grad,
+        resid_two,
+        jnp.broadcast_to(valid_own[:, None].astype(jnp.float32), (own_rows, 128)),
+        jnp.concatenate([before, jnp.zeros((SMALL - NORM_ROWS - before.shape[0], width), jnp.float32)]),
+        stats,
+        jnp.concatenate([norm_gain[0:1], out_bias[2:3]]),
+        qkv_weights,
+        kv_weights,
     )
-    self_qkv_grad = dot_tn(first_in, qkv_grad).astype(jnp.bfloat16).reshape(self_qkv.shape)
-    cross_kv_grad = dot_tn(text, text_kv_grad).astype(jnp.bfloat16).reshape(cross_kv.shape)
-    units_grad, text_grad, last_stats = last(
-        qkv_grad, text_kv_grad, own_units, resid_one_grad, norm_gain[0], qkv_weights, kv_weights
-    )
-    ffn_in_bias_grad = ffn_in_bias_grad.reshape(ffn_in_bias.shape)
-    small_sums = lax.psum(
-        jnp.stack(
-            [
-                last_stats[0],
-                stats[4],
-                stats[0],
-                last_stats[1],
-                stats[5],
-                stats[1],
-                stats[6],
-                stats[3],
-                stats[2],
-            ]
-        ),
-        ("wide", "narrow"),
-    )
-    (ffn_in_grad, ffn_out_grad), _ = wide_sum((ffn_in_grad, ffn_out_grad))
-    (cross_q_grad, cross_kv_grad, cross_out_grad), ffn_in_grad = wide_sum(
-        (cross_q_grad, cross_kv_grad, cross_out_grad), ffn_in_grad
-    )
-    (self_qkv_grad, self_out_grad), cross_q_grad = wide_sum((self_qkv_grad, self_out_grad), cross_q_grad)
-    self_bias_grad, cross_bias_grad, ffn_in_bias_grad = lax.psum(
-        (self_bias_grad, cross_bias_grad, ffn_in_bias_grad), "wide"
-    )
-    (
-        self_qkv_grad,
-        self_out_grad,
-        cross_q_grad,
-        cross_kv_grad,
-        cross_out_grad,
-        ffn_in_grad,
-        ffn_out_grad,
-    ) = (
-        a.astype(jnp.float32)
-        for a in (
-            self_qkv_grad,
-            self_out_grad,
-            cross_q_grad,
-            cross_kv_grad,
-            cross_out_grad,
-            ffn_in_grad,
-            ffn_out_grad,
-        )
-    )
+    summed_one, summed_two = summed_one.astype(jnp.float32), summed_two.astype(jnp.float32)
+    self_qkv_grad = summed_one[:, : 3 * cols].reshape(self_qkv.shape)
+    cross_q_grad = summed_one[:, 3 * cols :]
+    cross_out_grad, self_out_grad = summed_two[:cols], summed_two[cols : 2 * cols]
+    cross_kv_grad = jnp.concatenate(
+        [summed_two[2 * cols :, : 2 * cols], summed_two[2 * cols :, 2 * cols :]]
+    ).reshape(cross_kv.shape)
+    ffn_in_grad, ffn_out_grad = ffn_in_grad.astype(jnp.float32), ffn_out_grad.astype(jnp.float32)
+    biases = small[: before.shape[0]].reshape(-1)
+    self_bias_grad = biases[: 2 * cols].reshape(2, cols)
+    cross_bias_grad = biases[2 * cols : 4 * cols].reshape(2, cols)
+    ffn_in_bias_grad = biases[4 * cols :]
+    norms = small[SMALL - NORM_ROWS :]
+    gain_grad = jnp.stack([norms[7], norms[4], norms[0]])
+    shift_grad = jnp.stack([norms[8], norms[5], norms[1]])
+    bias_grad = jnp.stack([norms[6], norms[3], norms[2]])
     return (
         output,
         units_grad,
         text_grad,
-        small_sums[0:3],
-        small_sums[3:6],
+        gain_grad,
+        shift_grad,
         self_qkv_grad,
         self_bias_grad,
         self_out_grad,
@@ -917,7 +1155,7 @@
         ffn_in_grad,
         ffn_in_bias_grad,
         ffn_out_grad,
-        small_sums[6:9],
+        bias_grad,
     )
 
 

time: 763 us -> 582 us (0.76)
  waiting for transfers between devices: 226 us -> 0 us
  Pallas kernels: 369 us -> 515 us
  blocking collectives: 77.6 us -> 0 us
  between operations: 15.3 us -> 2.03 us
  starting transfers between devices: 13.1 us -> 0 us
  local copies, waits for them, and re-layouts: 26 us -> 38.3 us
    psum x3 -> x0, waiting for transfers between devices: 226 us -> none  [wide_sum(): return (lax.psum(parts, 'wide'), after)]
    pallas_call x2, Pallas kernels: 171 us -> 349 us  [the longest x1 217 us: turn(): pl.pallas_call(functools.partial(turn_kernel, count=count), in_specs=[hbm...]
    psum x2 -> x0, blocking collectives: 77.6 us -> none  [the longest x1 40.1 us: local(): lax.psum(jnp.stack([last_stats[0], stats[4], stats[0], last_stats[1], sta...]
    pallas_call x1, Pallas kernels: 53.3 us -> 30.1 us  [ffn(): pl.pallas_call(ffn_kernel, grid_spec=pltpu.PrefetchScalarGridSpec(num_sca...]
    psum x3 -> x0, starting transfers between devices: 13.1 us -> none  [wide_sum(): return (lax.psum(parts, 'wide'), after)]
    pallas_call x1, Pallas kernels: 107 us -> 118 us  [middle(): pl.pallas_call(middle_kernel, in_specs=[vmem] * 10, out_specs=[vmem] * 7,...]
    pallas_call x1, Pallas kernels: 20.8 us -> 9.41 us  [back(): pl.pallas_call(back_kernel, grid_spec=pltpu.PrefetchScalarGridSpec(num_sc...]
    slice x3 -> x11, local copies, waits for them, and re-layouts: 1.49 us -> 12.1 us  [the longest x2 4.28 us: local(): self_qkv_grad = summed_one[:, :3 * cols].reshape(self_qkv.shape)]
  transfers between devices with their start and end apart: 3 -> 0, of which waited for: 3 -> 0; matrix products, arithmetic and copies ran while one was open for 3% -> 0% of each run, Pallas kernels for 25% -> 0%
where the time goes in v4:
time: 582 us; the launch traced here: 587 us
  Pallas kernels  515 us (88%)
  local copies, waits for them, and re-layouts  38.3 us (7%)
  other arithmetic  25.5 us (4%)
    pallas_call x1, Pallas kernels, turn(): pl.pallas_call(functools.partial(turn_kernel, count=count), in_specs=[hbm...  217 us
    pallas_call x1, Pallas kernels, last(): pl.pallas_call(functools.partial(last_kernel, count=count), in_specs=[hbm...  132 us
    pallas_call x1, Pallas kernels, middle(): pl.pallas_call(middle_kernel, in_specs=[vmem] * 10, out_specs=[vmem] * 7,...  118 us
    pallas_call x1, Pallas kernels, ffn(): pl.pallas_call(ffn_kernel, grid_spec=pltpu.PrefetchScalarGridSpec(num_sca...  30.1 us
    unnamed x80, local copies, waits for them, and re-layouts  17.3 us

profile of v4, /device:TPU:0, one launch (start us, length us, event | category | flops | bytes accessed | tf_op | source)
XLA Modules:
  0.0 586.8 jit_solution(15675514114400758915)
XLA Ops:
  1.5 0.7 compare_select_fusion.1.lens
  2.1 0.1 fusion.1
  2.2 0.6 fusion.7
  2.8 3.2 dynamic-slice_select_fusion
  6.0 0.0 copy-start.20
  6.0 0.0 copy-start.22
  6.0 0.0 copy-start.31
  6.0 1.7 copy.46
  7.8 1.7 copy.47.w_ref.qkv_w
  9.5 0.0 copy-start.27
  9.6 0.0 copy-start.33
  9.6 8.2 %front.1 = (bf16[2048,1024]{1,0:T(8,128)(2,1)}, bf16[2048,256]{1,0:T(8,128)(2,1)S(1)}, bf16[2048,256]{1,0:T(8,128)(2,1)S(1)}, bf16[2048,256]{1,0:T(8,128)(2,1)S(1)}, bf16[2048,256]{1,0:T(8,128)(2,1)S(1)}) custom-call(s32[2]{0:T(128)S(1)} %compare_select_fusion.1.lens, bf16[2048,1024]{1,0:T(8,128)(2,1)} %x_ref.1, f32[1,1024]{1,0:T(1,128)S(1)} %get-tuple-element.158.g_ref, ...), custom_call_target="tpu_custom_call" | custom-call | flops 20000000000 | bytes 16777216 | tf_op jit(solution)/shard_map/front/pallas_call | solution.py:108
  17.8 1.0 copy-done.3
  18.8 1.0 copy-done.5
  19.7 1.0 copy-done.7
  20.7 0.6 fusion.14
  21.3 0.7 concatenate.27.vec
  22.0 2.4 copy.55
  24.4 0.7 fusion.6
  25.1 118.3 %middle.1 = (bf16[2048,1024]{1,0:T(8,128)(2,1)}, bf16[2048,1024]{1,0:T(8,128)(2,1)}, bf16[2048,256]{1,0:T(8,128)(2,1)}, bf16[2048,256]{1,0:T(8,128)(2,1)}, bf16[...) custom-call(bf16[2048,256]{1,0:T(8,128)(2,1)} %copy-done.7, ...), custom_call_target="tpu_custom_call" | custom-call | flops 99999997952 | bytes 25165824 | tf_op jit(solution)/shard_map/middle/pallas_call | solution.py:515
  143.4 0.0 copy-start.21
  143.4 0.0 copy-start.23
  143.4 0.0 copy-start.24
  143.4 0.0 copy-start.30
  143.4 30.1 %ffn.1 = (bf16[2048,1024]{1,0:T(8,128)(2,1)}, bf16[2048,1024]{1,0:T(8,128)(2,1)}, bf16[1024,2048]{1,0:T(8,128)(2,1)}, bf16[2048,1024]{1,0:T(8,128)(2,1)}, f32[1,2048]{1,0:T(1,128)}) custom-call(s32[2]{0:T(128)} %copy-done.1, bf16[2048,1024]{1,0:T(8,128)(2,1)} %get-tuple-element.50.h_ref, bf16[2048,1024]{1,0:T(8,128)(2,1)} %e_ref.1, ...), custom_call_target="tpu_custom_call" | custom-call | flops 60000002048 | bytes 33554432 | tf_op jit(solution)/shard_map/ffn/pallas_call | solution.py:589
  173.6 0.6 pad_maximum_fusion.6
  174.2 0.8 broadcast_in_dim.51.keep
  175.1 217.1 %turn.1 = (bf16[1024,2048]{1,0:T(8,128)(2,1)}, bf16[2048,1024]{1,0:T(8,128)(2,1)}, f32[512,1024]{1,0:T(8,128)}, bf16[2048,256]{1,0:T(8,128)(2,1)}, bf16[512,512]...) custom-call(bf16[2048,1024]{1,0:T(8,128)(2,1)} %get-tuple-element.56, ...), custom_call_target="tpu_custom_call" | custom-call | flops 99999997952 | bytes 25165824 | tf_op jit(solution)/shard_map/turn/pallas_call | solution.py:780
  392.2 1.2 copy-done.8
  393.5 9.4 %back.1.dqkv = bf16[2048,768]{1,0:T(8,128)(2,1)} custom-call(s32[2]{0:T(128)S(1)} %copy-done.2, bf16[2048,256]{1,0:T(8,128)(2,1)S(1)} %get-tuple-element.53.q_ref, bf16[2048,256]{1,0:T(8,128)(2,1)S(1)} %copy-done.4, bf16[2048,256]{1,0:T(8,128)(2,1)S(1)} %copy-done.6, bf16[2048,256]{1,0:T(8,128)(2,1)S(1)} %copy-done.8), custom_call_target="tpu_custom_call" | custom-call | flops 30000001024 | bytes 8388608 | tf_op jit(solution)/shard_map/back/pallas_call | solution.py:166
  402.9 2.0 convert_reduce_fusion.1
  404.9 0.6 concatenate.33.before
  405.6 2.3 fusion
  407.8 0.0 copy-start.14
  407.9 0.1 fusion.11
  408.0 1.6 maximum_maximum_fusion.g1
  409.6 1.0 copy-done.14
  410.6 3.5 convolution_convert_fusion
  414.1 0.0 copy-start.28
  414.1 1.6 pad_maximum_fusion.g0
  415.7 0.8 broadcast_in_dim.52.valid
  416.6 131.8 %last.1 = (bf16[1024,1024]{1,0:T(8,128)(2,1)}, bf16[1024,1024]{1,0:T(8,128)(2,1)}, bf16[512,1024]{1,0:T(8,128)(2,1)}, f32[512,1024]{1,0:T(8,128)}, f32[128,1024]{1,0:T(8,128)}, /*index=5*/f32[16,1024]{1,0:T(8,128)}) custom-call(bf16[2048,1024]{1,0:T(8,128)(2,1)} %get-tuple-element.51.ffn_part, bf16[1024,1024]{1,0:T(8,128)(2,1)} %pad_maximum_fusion.g0, ...), custom_call_target="tpu_custom_call" | custom-call | flops 30000001024 | bytes 16777216 | tf_op jit(solution)/shard_map/last/pallas_call | solution.py:981
  548.4 1.1 fusion.12
  549.5 0.6 pad_maximum_fusion.4
  550.1 1.5 fusion.10
  551.6 1.5 pad_maximum_fusion.1
  553.1 3.7 reshape.132
  556.8 1.9 slice.167
  558.7 2.4 copy.51
  561.1 2.4 copy.52
  563.4 0.6 pad_maximum_fusion.3
  564.1 0.6 pad_maximum_fusion.2
  564.7 2.8 fusion.9
  567.4 1.1 slice.170
  568.5 0.8 slice.149
  569.3 0.6 fusion.13
  569.9 0.8 slice_bitcast_fusion
  570.6 0.6 copy.60
  571.2 6.8 %convert_element_type.53 = f32[1024,2048]{1,0:T(8,128)} convert(bf16[1024,2048]{1,0:T(8,128)(2,1)} %get-tuple-element.80) | non-fusion elementwise | flops 2097152 | bytes 12582912 | tf_op jit(solution)/shard_map/convert_element_type | solution.py:1133
  578.1 4.4 convert_element_type.54
  582.5 1.0 copy.65
  583.5 1.0 copy-done.12
  584.5 1.3 copy.66
  585.8 0.8 copy.67
  (63 shorter events, 0.2 us)
Async XLA Ops:
  0.6 5.3 copy-start.25
  0.7 5.3 copy-start.26
  0.7 5.4 copy-start.13
  2.1 7.4 %copy-start.1 = (s32[2]{0:T(128)}, s32[2]{0:T(128)S(1)}, u32[]{:S(2)}) copy-start(s32[2]{0:T(128)S(1)} %compare_select_fusion.1.lens) | copy-start | bytes 28
  6.0 15.3 %copy-start.20 = (f32[1,1024]{1,0:T(1,128)}, f32[1,1024]{1,0:T(1,128)S(1)}, u32[]{:S(2)}) copy-start(f32[1,1024]{1,0:T(1,128)S(1)} %get-tuple-element.157) | copy-start | bytes 12292
  6.0 15.3 %copy-start.22 = (f32[1,1024]{1,0:T(1,128)}, f32[1,1024]{1,0:T(1,128)S(1)}, u32[]{:S(2)}) copy-start(f32[1,1024]{1,0:T(1,128)S(1)} %get-tuple-element.159) | copy-start | bytes 12292
  6.0 3.5 copy-start.31
  9.5 8.3 %copy-start = (bf16[1024,768]{1,0:T(8,128)(2,1)}, bf16[1024,768]{1,0:T(8,128)(2,1)S(1)}, u32[]{:S(2)}) copy-start(bf16[1024,768]{1,0:T(8,128)(2,1)S(1)} %copy.47.w_ref.qkv_w) | copy-start | bytes 4718596
  9.5 11.2 %copy-start.27 = (f32[3,1024]{1,0:T(4,128)S(1)}, f32[3,1024]{1,0:T(4,128)}, u32[]{:S(2)}) copy-start(f32[3,1024]{1,0:T(4,128)} %param.37) | copy-start | bytes 36868
  9.6 14.9 %copy-start.33 = (s32[2]{0:T(128)S(1)}, s32[2]{0:T(128)}, u32[]{:S(2)}) copy-start(s32[2]{0:T(128)} %param.23) | copy-start | bytes 28
  17.8 1.0 copy-start.3
  18.8 1.0 copy-start.5
  19.7 1.0 copy-start.7
  143.4 30.2 %copy-start.21 = (f32[1,1024]{1,0:T(1,128)S(1)}, f32[1,1024]{1,0:T(1,128)}, u32[]{:S(2)}) copy-start(f32[1,1024]{1,0:T(1,128)} %copy-done.20) | copy-start | bytes 12292
  143.4 30.2 %copy-start.23 = (f32[1,1024]{1,0:T(1,128)S(1)}, f32[1,1024]{1,0:T(1,128)}, u32[]{:S(2)}) copy-start(f32[1,1024]{1,0:T(1,128)} %copy-done.22) | copy-start | bytes 12292
  143.4 30.2 %copy-start.24 = (f32[1,1024]{1,0:T(1,128)S(1)}, f32[1,1024]{1,0:T(1,128)}, u32[]{:S(2)}) copy-start(f32[1,1024]{1,0:T(1,128)} %get-tuple-element.151) | copy-start | bytes 12292
  143.4 30.8 %copy-start.30 = (f32[1,2,2,128]{3,2,1,0:T(2,128)S(1)}, f32[1,2,2,128]{3,2,1,0:T(2,128)}, u32[]{:S(2)}) copy-start(f32[1,2,2,128]{3,2,1,0:T(2,128)} %get-tuple-element.162) | copy-start | bytes 6148
  175.1 217.1 %copy-start.2 = (s32[2]{0:T(128)S(1)}, s32[2]{0:T(128)}, u32[]{:S(2)}) copy-start(s32[2]{0:T(128)} %copy-done.1) | copy-start | bytes 28
  175.1 217.1 %copy-start.4 = (bf16[2048,256]{1,0:T(8,128)(2,1)S(1)}, bf16[2048,256]{1,0:T(8,128)(2,1)}, u32[]{:S(2)}) copy-start(bf16[2048,256]{1,0:T(8,128)(2,1)} %copy-done.3) | copy-start | bytes 3145732
  175.1 217.1 %copy-start.6 = (bf16[2048,256]{1,0:T(8,128)(2,1)S(1)}, bf16[2048,256]{1,0:T(8,128)(2,1)}, u32[]{:S(2)}) copy-start(bf16[2048,256]{1,0:T(8,128)(2,1)} %copy-done.5) | copy-start | bytes 3145732
  392.2 1.2 copy-start.8
  393.5 11.4 %copy-start.32 = (f32[2,256]{1,0:T(2,128)S(1)}, f32[2,256]{1,0:T(2,128)}, u32[]{:S(2)}) copy-start(f32[2,256]{1,0:T(2,128)} %get-tuple-element.71) | copy-start | bytes 6148
  393.5 11.4 %copy-start.29 = (f32[1,2048]{1,0:T(1,128)S(1)}, f32[1,2048]{1,0:T(1,128)}, u32[]{:S(2)}) copy-start(f32[1,2048]{1,0:T(1,128)} %get-tuple-element.72) | copy-start | bytes 24580
  402.9 5.0 copy-start.18
  402.9 5.0 copy-start.19
  405.6 4.0 copy-start.34
  407.8 2.7 copy-start.14
  410.6 3.5 copy-start.17
  414.1 1.6 copy-start.28
  553.1 3.7 copy-start.9
  563.4 4.0 copy-start.10
  571.2 6.8 %copy-start.11 = (bf16[2048,1024]{1,0:T(8,128)(2,1)S(1)}, bf16[2048,1024]{1,0:T(8,128)(2,1)}, u32[]{:S(2)}) copy-start(bf16[2048,1024]{1,0:T(8,128)(2,1)} %get-tuple-element.81) | copy-start | bytes 12582916
  578.1 4.4 copy-start.15
  582.5 2.0 copy-start.12
  582.5 3.3 copy-start.16

commit v5 on v4

--- a/solution.py
+++ b/solution.py
@@ -8,8 +8,6 @@
 from jax.sharding import PartitionSpec as P
 
 HEAD_DIM = 64
-UNITS = 1024
-TEXT = 256
 
 
 NORM_EPSILON = 1e-05
@@ -61,7 +59,11 @@
     return lax.dot_general(a, b, (((0,), (0,)), ((), ())), preferred_element_type=jnp.float32)
 
 
-def front_kernel(lens, x_ref, g_ref, s_ref, w_ref, qb_ref, vb_ref, h_ref, q_ref, k_ref, v_ref, c_ref):
+def column_sum(values):
+    return jnp.sum(values, axis=0, keepdims=True)
+
+
+def front_kernel(lens, x_ref, g_ref, s_ref, w_ref, b_ref, h_ref, q_ref, k_ref, v_ref, c_ref):
     length = lens[pl.program_id(0)]
     width = q_ref.shape[1]
     for i in range(x_ref.shape[0] // BLOCK):
@@ -69,14 +71,13 @@
 
         @pl.when(i * BLOCK < length)
         def _():
-            normed, _, _ = norm_forward(x_ref[rows, :].astype(jnp.float32), g_ref[...], s_ref[...])
+            normed, _, _ = norm_forward(x_ref[rows, :].astype(jnp.float32), g_ref[0:1, :], s_ref[0:1, :])
             h1 = normed.astype(jnp.bfloat16)
             h_ref[rows, :] = h1
-            qkv = dot_nn(h1, w_ref[...])
-            queries = (qkv[:, :width] + qb_ref[...]).astype(jnp.bfloat16)
+            queries = (dot_nn(h1, w_ref[0]) + b_ref[0:1, :]).astype(jnp.bfloat16)
             q_ref[rows, :] = queries
-            k_ref[rows, :] = qkv[:, width : 2 * width].astype(jnp.bfloat16)
-            v_ref[rows, :] = (qkv[:, 2 * width :] + vb_ref[...]).astype(jnp.bfloat16)
+            k_ref[rows, :] = dot_nn(h1, w_ref[1]).astype(jnp.bfloat16)
+            v_ref[rows, :] = (dot_nn(h1, w_ref[2]) + b_ref[1:2, :]).astype(jnp.bfloat16)
             count = (i + 1) * BLOCK
             keys, values = k_ref[:count, :], v_ref[:count, :]
             scaled = queries * jnp.bfloat16(HEAD_DIM**-0.5)
@@ -96,31 +97,46 @@
                 ref[rows, :] = jnp.zeros((BLOCK, ref.shape[1]), ref.dtype)
 
 
-def front(lengths, units, gain_vec, shift_vec, weights, q_bias, v_bias):
+def front(lengths, units, gains, shifts, weights, bias):
     rows, width = units.shape
     slots = lengths.shape[0]
     slot_rows = rows // slots
-    cols = weights.shape[1] // 3
+    cols = weights.shape[2]
     whole = lambda a: pl.BlockSpec(a.shape, lambda s, *_: (0,) * a.ndim)
     slot = lambda w: pl.BlockSpec((slot_rows, w), lambda s, *_: (s, 0))
-    small = [a.reshape(1, -1) for a in (gain_vec, shift_vec, q_bias, v_bias)]
     shape = lambda w: jax.ShapeDtypeStruct((rows, w), jnp.bfloat16)
+    far = lambda w: pltpu.HBM((rows, w), jnp.bfloat16)
     return pl.pallas_call(
         front_kernel,
         grid_spec=pltpu.PrefetchScalarGridSpec(
             num_scalar_prefetch=1,
             grid=(slots,),
-            in_specs=[slot(width), whole(small[0]), whole(small[1]), whole(weights), whole(small[2]), whole(small[3])],
+            in_specs=[slot(width)] + [whole(a) for a in (gains, shifts, weights, bias)],
             out_specs=[slot(width), slot(cols), slot(cols), slot(cols), slot(cols)],
         ),
-        out_shape=[shape(width), shape(cols), shape(cols), shape(cols), shape(cols)],
+        out_shape=[far(width), far(cols), far(cols), far(cols), shape(cols)],
         compiler_params=pltpu.CompilerParams(vmem_limit_bytes=48 * MIB),
         cost_estimate=pl.CostEstimate(flops=20 * 10**9, bytes_accessed=16 * MIB, transcendentals=8 * MIB),
         name="front",
-    )(lengths, units, small[0], small[1], weights, small[2], small[3])
-
-
-def back_kernel(lens, q_ref, k_ref, v_ref, dc_ref, o_ref, dk_acc, dv_acc):
+    )(lengths, units, gains, shifts, weights, bias)
+
+
+def back_kernel(
+    lens, q_ref, k_ref, v_ref, dc_ref, h_ref, text_ref, dkv_ref, in_ref, out_ref, _g0, _g1,
+    o_ref, g0_ref, g1_ref, b_ref, in_f32, out_f32, dk_acc, dv_acc, w_acc,
+):
+    in_f32[...] = in_ref[...].astype(jnp.float32)
+    out_f32[...] = out_ref[...].astype(jnp.float32)
+
+    @pl.when(pl.program_id(0) == 0)
+    def _():
+        w_acc[...] = jnp.zeros_like(w_acc)
+        b_ref[...] = jnp.zeros_like(b_ref)
+        kv_grad = dot_tn(text_ref[...], dkv_ref[...]).astype(jnp.bfloat16)
+        half, both = g1_ref.shape[0], dkv_ref.shape[1]
+        g1_ref[:, :both] = kv_grad[:half]
+        g1_ref[:, both:] = kv_grad[half:]
+
     length = lens[pl.program_id(0)]
     slot_rows, width = q_ref.shape
     dk_acc[...] = jnp.zeros_like(dk_acc)
@@ -156,27 +172,62 @@
 
     o_ref[:, width : 2 * width] = dk_acc[...].astype(jnp.bfloat16)
     o_ref[:, 2 * width :] = dv_acc[...].astype(jnp.bfloat16)
-
-
-def back(lengths, queries, keys, values, grads):
-    rows, width = queries.shape
+    for i in range(slot_rows // BLOCK):
+        rows = pl.ds(i * BLOCK, BLOCK)
+
+        @pl.when(i * BLOCK < length)
+        def _():
+            grads = o_ref[rows, :]
+            w_acc[...] += dot_tn(h_ref[rows, :], grads)
+            sums = column_sum(grads.astype(jnp.float32))
+            b_ref[0:1, :] += sums[:, :width]
+            b_ref[1:2, :] += sums[:, 2 * width :]
+
+    @pl.when(pl.program_id(0) == pl.num_programs(0) - 1)
+    def _():
+        g0_ref[...] = w_acc[...].astype(jnp.bfloat16)
+
+
+def back(lengths, queries, keys, values, grads, rows_in, text, dkv, in_sum, out_sum, g0, g1):
+    rows, cols = queries.shape
+    width = rows_in.shape[1]
     slots = lengths.shape[0]
-    slot_rows = rows // slots
-    slot = lambda w: pl.BlockSpec((slot_rows, w), lambda s, *_: (s, 0))
+    bf, f32 = jnp.bfloat16, jnp.float32
+    shape = jax.ShapeDtypeStruct
+    slot = lambda a: pl.BlockSpec((a.shape[0] // slots, a.shape[1]), lambda s, *_: (s, 0))
+    whole = lambda a: pl.BlockSpec(a.shape, lambda s, *_: (0, 0))
+    hbm = pl.BlockSpec(memory_space=pl.ANY)
+    half = text.shape[1] // 2
     return pl.pallas_call(
         back_kernel,
         grid_spec=pltpu.PrefetchScalarGridSpec(
             num_scalar_prefetch=1,
             grid=(slots,),
-            in_specs=[slot(width)] * 4,
-            out_specs=slot(3 * width),
-            scratch_shapes=[pltpu.VMEM((slot_rows, width), jnp.float32)] * 2,
+            in_specs=[slot(queries)] * 4
+            + [slot(rows_in), whole(text), whole(dkv), slot(in_sum), slot(out_sum), hbm, hbm],
+            out_specs=[
+                pl.BlockSpec((rows // slots, 3 * cols), lambda s, *_: (s, 0)),
+                pl.BlockSpec((width, 3 * cols), lambda s, *_: (0, 0)),
+                pl.BlockSpec((half, width), lambda s, *_: (1, 0)),
+                pl.BlockSpec((2, cols), lambda s, *_: (0, 0)),
+                slot(in_sum),
+                slot(out_sum),
+            ],
+            scratch_shapes=[pltpu.VMEM((rows // slots, cols), f32)] * 2 + [pltpu.VMEM((width, 3 * cols), f32)],
         ),
-        out_shape=jax.ShapeDtypeStruct((rows, 3 * width), jnp.bfloat16),
-        compiler_params=pltpu.CompilerParams(vmem_limit_bytes=48 * MIB),
-        cost_estimate=pl.CostEstimate(flops=30 * 10**9, bytes_accessed=8 * MIB, transcendentals=8 * MIB),
+        out_shape=[
+            shape((rows, 3 * cols), bf),
+            pltpu.HBM(g0.shape, bf),
+            pltpu.HBM(g1.shape, bf),
+            shape((2, cols), f32),
+            shape(in_sum.shape, f32),
+            shape(out_sum.shape, f32),
+        ],
+        input_output_aliases={10: 1, 11: 2},
+        compiler_params=pltpu.CompilerParams(vmem_limit_bytes=60 * MIB),
+        cost_estimate=pl.CostEstimate(flops=30 * 10**9, bytes_accessed=40 * MIB, transcendentals=8 * MIB),
         name="back",
-    )(lengths, queries, keys, values, grads)
+    )(lengths, queries, keys, values, grads, rows_in, text, dkv, in_sum, out_sum, g0, g1)
 
 
 def place():
@@ -317,6 +368,12 @@
     ]
 
 
+def own_copy(whole, own, sem):
+    size = own.shape[0]
+    first = pl.multiple_of(lax.axis_index("narrow") * size, size)
+    return pltpu.make_async_copy(whole.at[pl.ds(first, size), :], own, sem)
+
+
 class Hop:
     KINDS = 6
 
@@ -429,18 +486,22 @@
 
 
 def middle_kernel(
-    c1, units, text, vec, bias, keep, so_w, cq_w, kv_w, co_w,
+    all_units, text_lens, c1, text, gains, shifts, biases, bias, so_w, cq_w, kv_w, co_w,
     h2, h3, q2, c2, kv2, x1, x2,
-    part1, part2, core1, tox1, fromx1, sem1, core2, tox2, fromx2, sem2,
+    units, own_sem, part1, part2, core1, tox1, fromx1, sem1, core2, tox2, fromx2, sem2,
 ):
     steps, chunk, width = tox1.shape
     cols = q2.shape[1]
-    slots = keep.shape[0]
+    slots = text_lens.shape[0]
     texts = text.shape[0] // slots
+    fetch = own_copy(all_units, units, own_sem)
+    fetch.start()
     greet()
     one = Hop(part1, core1, tox1, fromx1, h2, sem1, chunk)
     two = Hop(part2, core2, tox2, fromx2, h3, sem2, chunk)
     scale = jnp.bfloat16(HEAD_DIM**-0.5)
+
+    fetch.wait()
 
     def project(step):
         one.put(part1, step, dot_nn(one.take(c1, step), so_w[...]).astype(jnp.bfloat16))
@@ -454,9 +515,9 @@
 
     def norm_one(step):
         rows = one.own_rows(step)
-        resid = units[rows, :].astype(jnp.float32) + one.result(step) + vec[2:3, :]
+        resid = units[rows, :].astype(jnp.float32) + one.result(step) + biases[0:1, :]
         x1[rows, :] = resid
-        one.send_gather(step, norm_forward(resid, vec[0:1, :], vec[1:2, :])[0].astype(jnp.bfloat16))
+        one.send_gather(step, norm_forward(resid, gains[1:2, :], shifts[1:2, :])[0].astype(jnp.bfloat16))
 
     def cross(step):
         one.gathered(step)
@@ -464,6 +525,7 @@
         one.put(q2, step, queries)
         scaled = queries * scale
         count = queries.shape[0] // slots
+        place_of = lax.broadcasted_iota(jnp.int32, (count, texts), 1)
         context = []
         for slot in range(slots):
             mine = scaled[slot * count : (slot + 1) * count]
@@ -472,7 +534,7 @@
             total = jnp.zeros((count, cols), jnp.float32)
             for head in range(cols // HEAD_DIM):
                 scores = dot_nt(pick_head(mine, head), keys)
-                scores = jnp.where(keep[slot : slot + 1, :] > 0.5, scores, MASKED_SCORE)
+                scores = jnp.where(place_of < text_lens[slot], scores, MASKED_SCORE)
                 weights = jnp.exp(scores - jnp.max(scores, axis=1, keepdims=True))
                 weights = weights * (1.0 / jnp.sum(weights, axis=1, keepdims=True))
                 total += dot_nn(weights.astype(jnp.bfloat16), pick_head(values, head))
@@ -484,9 +546,9 @@
 
     def norm_two(step):
         rows = one.own_rows(step)
-        resid = x1[rows, :] + two.result(step) + vec[5:6, :]
+        resid = x1[rows, :] + two.result(step) + biases[1:2, :]
         x2[rows, :] = resid
-        two.send_gather(step, norm_forward(resid, vec[3:4, :], vec[4:5, :])[0].astype(jnp.bfloat16))
+        two.send_gather(step, norm_forward(resid, gains[2:3, :], shifts[2:3, :])[0].astype(jnp.bfloat16))
 
     stages(
         steps,
@@ -504,9 +566,9 @@
     lax.fori_loop(0, steps, finish, 0)
 
 
-def middle(c1, units_own, text, vec, bias, keep, so_w, cq_w, kv_w, co_w):
+def middle(units, text_lens, c1, text, gains, shifts, biases, bias, so_w, cq_w, kv_w, co_w):
     rows, cols = c1.shape
-    own, width = units_own.shape
+    own, width = rows // NARROW, units.shape[1]
     chunk = own // STEPS
     bf, f32 = jnp.bfloat16, jnp.float32
     shape = jax.ShapeDtypeStruct
@@ -514,7 +576,7 @@
     hop = hop_scratch(own, chunk, width)
     return pl.pallas_call(
         middle_kernel,
-        in_specs=[vmem] * 10,
+        in_specs=[pl.BlockSpec(memory_space=pl.ANY), pl.BlockSpec(memory_space=pltpu.SMEM)] + [vmem] * 10,
         out_specs=[vmem] * 7,
         out_shape=[
             shape((rows, width), bf),
@@ -525,11 +587,14 @@
             shape((own, width), f32),
             shape((own, width), f32),
         ],
-        scratch_shapes=[pltpu.VMEM((rows, width), bf)] * 2 + hop + hop,
+        scratch_shapes=[pltpu.VMEM((own, width), bf), pltpu.SemaphoreType.DMA]
+        + [pltpu.VMEM((rows, width), bf)] * 2
+        + hop
+        + hop,
         compiler_params=pltpu.CompilerParams(collective_id=0, has_side_effects=True, vmem_limit_bytes=58 * MIB),
         cost_estimate=pl.CostEstimate(flops=100 * 10**9, bytes_accessed=24 * MIB, transcendentals=4 * MIB),
         name="middle",
-    )(c1, units_own, text, vec, bias, keep, so_w, cq_w, kv_w, co_w)
+    )(units, text_lens, c1, text, gains, shifts, biases, bias, so_w, cq_w, kv_w, co_w)
 
 
 def ffn_kernel(lens, h_ref, e_ref, wi_ref, b_ref, wo_ref, a_ref, d_ref, gi_ref, go_ref, gb_ref, gi_acc, go_acc):
@@ -643,14 +708,20 @@
         return total + self.from_cross[step].astype(jnp.float32)
 
 
-def column_sum(values):
-    return jnp.sum(values, axis=0, keepdims=True)
+def left_here(lens, own, rows):
+    first = lax.axis_index("narrow") * own
+    slot_rows = rows // lens.shape[0]
+    return lens[first // slot_rows] - first % slot_rows
+
+
+def row_of(step, chunk, width):
+    return lax.broadcasted_iota(jnp.int32, (chunk, width), 0) + step * chunk
 
 
 def turn_kernel(
-    third, in_g, out_g, x1, x2, e_own, h2, q2, c2, kv2, c1, keep, vec, co_w, cq_w, so_w,
-    in_sum, out_sum, dx1, dc1, dkv, co_g, cq_g, so_g, bias_g, stats,
-    mine3, theirs3, core3, fromx3, sem3,
+    third, in_g, out_g, out_grad, lens, text_lens, x1, x2, h2, q2, c2, kv2, c1, gains, co_w, cq_w, so_w,
+    in_sum, out_sum, g0, g1, dx1, dc1, dkv, bias_g, stats,
+    co_g, cq_g, so_g, give_sem, e_own, own_sem, mine3, theirs3, core3, fromx3, sem3,
     part5, core5, tox5, fromx5, sem5, full3, full5, dx2, co_acc, cq_acc, so_acc, dkv_acc, fetch_sem,
     *ring_refs, count,
 ):
@@ -666,6 +737,8 @@
         return ref.at[pl.ds(pl.multiple_of(shard * 2 * high + half * high, high), high), :]
 
     ring = Ring(count, (in_g, out_g), (in_sum, out_sum), ring_view, *ring_refs)
+    fetch = own_copy(out_grad, e_own, own_sem)
+    fetch.start()
     greet(*ring.peers)
     ring.start()
     three = FarHop(third, core3, None, fromx3, full3, sem3, chunk)
@@ -680,16 +753,18 @@
     for ref in (co_acc, cq_acc, so_acc, dkv_acc, bias_g, stats):
         ref[...] = jnp.zeros_like(ref)
     three.fetched()
+    fetch.wait()
+    valid_rows = left_here(lens, x1.shape[0], h2.shape[0])
     scale = jnp.bfloat16(HEAD_DIM**-0.5)
 
     def norm_three(step):
         rows = three.own_rows(step)
         grad_in = three.result(step)
-        _, normed, inv_std = norm_forward(x2[rows, :], vec[0:1, :], vec[0:1, :])
+        _, normed, inv_std = norm_forward(x2[rows, :], gains[2:3, :], gains[2:3, :])
         stats[0:1, :] += column_sum(grad_in * normed)
         stats[1:2, :] += column_sum(grad_in)
-        above = e_own[rows, :].astype(jnp.float32)
-        total = above + norm_backward(grad_in, normed, inv_std, vec[0:1, :])
+        above = jnp.where(row_of(step, chunk, width) < valid_rows, e_own[rows, :].astype(jnp.float32), 0.0)
+        total = above + norm_backward(grad_in, normed, inv_std, gains[2:3, :])
         stats[2:3, :] += column_sum(above)
         stats[3:4, :] += column_sum(total)
         dx2[rows, :] = total
@@ -702,6 +777,7 @@
         context = dot_nt(grads, co_w[...]).astype(jnp.bfloat16)
         queries = three.take(q2, step) * scale
         count = queries.shape[0] // slots
+        place_of = lax.broadcasted_iota(jnp.int32, (texts, count), 0)
         q_grad = []
         for slot in range(slots):
             rows = slice(slot * count, (slot + 1) * count)
@@ -710,7 +786,7 @@
             total = jnp.zeros((count, cols), jnp.float32)
             for head in range(cols // HEAD_DIM):
                 q_head, g_head = pick_head(queries[rows], head), pick_head(context[rows], head)
-                scores = jnp.where(keep[texts_here, :] > 0.5, dot_nt(keys, q_head), MASKED_SCORE)
+                scores = jnp.where(place_of < text_lens[slot], dot_nt(keys, q_head), MASKED_SCORE)
                 weights = jnp.exp(scores - jnp.max(scores, axis=0, keepdims=True))
                 weights = weights * (1.0 / jnp.sum(weights, axis=0, keepdims=True))
                 dkv_acc[texts_here, cols:] += dot_nn(weights.astype(jnp.bfloat16), g_head)
@@ -729,10 +805,10 @@
     def norm_two(step):
         rows = five.own_rows(step)
         grad_in = five.result(step)
-        _, normed, inv_std = norm_forward(x1[rows, :], vec[1:2, :], vec[1:2, :])
+        _, normed, inv_std = norm_forward(x1[rows, :], gains[1:2, :], gains[1:2, :])
         stats[4:5, :] += column_sum(grad_in * normed)
         stats[5:6, :] += column_sum(grad_in)
-        total = dx2[rows, :] + norm_backward(grad_in, normed, inv_std, vec[1:2, :])
+        total = dx2[rows, :] + norm_backward(grad_in, normed, inv_std, gains[1:2, :])
         stats[6:7, :] += column_sum(total)
         dx1[rows, :] = total
         five.send_gather(step, total.astype(jnp.bfloat16))
@@ -757,6 +833,13 @@
     co_g[...] = co_acc[...].astype(jnp.bfloat16)
     cq_g[...] = cq_acc[...].astype(jnp.bfloat16)
     so_g[...] = so_acc[...].astype(jnp.bfloat16)
+    gives = [
+        pltpu.make_async_copy(cq_g, g0.at[:, pl.ds(width - cols, cols)], give_sem.at[0]),
+        pltpu.make_async_copy(co_g, g1.at[pl.ds(0, cols), :], give_sem.at[1]),
+        pltpu.make_async_copy(so_g, g1.at[pl.ds(cols, cols), :], give_sem.at[2]),
+    ]
+    for give in gives:
+        give.start()
 
     def finish(step, carry):
         three.finish(step)
@@ -765,9 +848,11 @@
 
     lax.fori_loop(0, steps, finish, 0)
     ring.finish()
-
-
-def turn(count, third, in_g, out_g, x1, x2, e_own, h2, q2, c2, kv2, c1, keep, vec, co_w, cq_w, so_w):
+    for give in gives:
+        give.wait()
+
+
+def turn(count, third, in_g, out_g, out_grad, lens, text_lens, x1, x2, h2, q2, c2, kv2, c1, gains, co_w, cq_w, so_w):
     rows, cols = c1.shape
     own, width = x1.shape
     chunk = own // STEPS
@@ -779,21 +864,28 @@
     far = [pltpu.VMEM((own, width), bf)] * 2 + [hop[0], hop[2], hop[3]]
     return pl.pallas_call(
         functools.partial(turn_kernel, count=count),
-        in_specs=[hbm] * 3 + [vmem] * 13,
-        out_specs=[hbm] * 2 + [vmem] * 8,
+        in_specs=[hbm] * 4 + [pl.BlockSpec(memory_space=pltpu.SMEM)] * 2 + [vmem] * 11,
+        out_specs=[hbm] * 4 + [vmem] * 5,
         out_shape=[
-            shape(in_g.shape, bf),
-            shape(out_g.shape, bf),
+            pltpu.HBM(in_g.shape, bf),
+            pltpu.HBM(out_g.shape, bf),
+            pltpu.HBM((width, width), bf),
+            pltpu.HBM((width, width), bf),
             shape((own, width), f32),
             shape((rows, cols), bf),
             shape(kv2.shape, bf),
-            shape((cols, width), bf),
-            shape((width, cols), bf),
-            shape((cols, width), bf),
             shape((2, cols), f32),
             shape((8, width), f32),
         ],
-        scratch_shapes=far
+        scratch_shapes=[
+            pltpu.VMEM((cols, width), bf),
+            pltpu.VMEM((width, cols), bf),
+            pltpu.VMEM((cols, width), bf),
+            pltpu.SemaphoreType.DMA((3,)),
+            pltpu.VMEM((own, width), bf),
+            pltpu.SemaphoreType.DMA,
+        ]
+        + far
         + [pltpu.VMEM((rows, width), bf)]
         + hop
         + [pltpu.VMEM((rows, width), bf)] * 2
@@ -809,7 +901,7 @@
         compiler_params=pltpu.CompilerParams(collective_id=1, has_side_effects=True, vmem_limit_bytes=60 * MIB),
         cost_estimate=pl.CostEstimate(flops=100 * 10**9, bytes_accessed=24 * MIB, transcendentals=4 * MIB),
         name="turn",
-    )(third, in_g, out_g, x1, x2, e_own, h2, q2, c2, kv2, c1, keep, vec, co_w, cq_w, so_w)
+    )(third, in_g, out_g, out_grad, lens, text_lens, x1, x2, h2, q2, c2, kv2, c1, gains, co_w, cq_w, so_w)
 
 
 SMALL = 16
@@ -820,15 +912,15 @@
     def __init__(self, count, block, near, far, sems):
         self.count, self.mine, self.near, self.far, self.sems = count, block, near, far, sems
         self.index, self.core, self.cross, _ = place()
-        self.spot, self.following, _ = ring_place(count)
+        self.spot, *self.peers = ring_place(count)
 
     def near_copy(self, kind):
         owner = self.cross if kind == 2 else self.index
         return remote(self.near.at[owner], self.near.at[owner], self.sems, 0, kind, (self.cross, self.core, self.core)[kind])
 
-    def far_copy(self, step):
-        block = self.far.at[(self.spot + self.count - step) % self.count]
-        return remote(block, block, self.sems, 1, step, self.following, "wide")
+    def far_copy(self, way, step):
+        block = self.far.at[(self.spot + (2 * way - 1) * step + self.count) % self.count]
+        return remote(block, block, self.sems, 1 + way, step, self.peers[way], "wide")
 
     def begin(self):
         self.near[self.index] = self.mine[...]
@@ -847,24 +939,32 @@
             both += self.near[owner]
         row = lax.broadcasted_iota(jnp.int32, both.shape, 0)
         self.far[self.spot] = jnp.where(row < SMALL - NORM_ROWS, self.mine[...], both)
-        self.far_copy(0).start()
+        self.far_copy(0, 0).start()
+        self.far_copy(1, 0).start()
 
     def rotate(self, step):
-        self.far_copy(step).wait_recv()
-
-        @pl.when(step < self.count - 2)
-        def _():
-            self.far_copy(step + 1).start()
+        for way in range(2):
+            steps = self.count // 2 - way
+
+            @pl.when(step < steps)
+            def _():
+                self.far_copy(way, step).wait_recv()
+
+            @pl.when(step < steps - 1)
+            def _():
+                self.far_copy(way, step + 1).start()
 
     def finish(self, out):
         for kind in range(3):
             self.near_copy(kind).wait_send()
 
-        def body(step, carry):
-            self.far_copy(step).wait_send()
-            return carry
-
-        lax.fori_loop(0, self.count - 1, body, 0)
+        for way in range(2):
+
+            def body(step, carry):
+                self.far_copy(way, step).wait_send()
+                return carry
+
+            lax.fori_loop(0, self.count // 2 - way, body, 0)
         out[...] = jnp.zeros_like(out)
 
         def add(spot, carry):
@@ -875,9 +975,9 @@
 
 
 def last_kernel(
-    ffn_part, g0, g1, dqkv, dkv, units, dx1, x2, valid, before, stats, vec, qkv_w, kv_w,
+    ffn_part, g0, g1, all_units, lens, dqkv, dkv, dx1, x2, self_b, cross_b, ffn_b, stats, gains, biases, qkv_w, kv_w,
     sum0, sum1, y, units_g, text_g, small_sum,
-    mine4, theirs4, core4, fromx4, sem4,
+    units, own_sem, mine4, theirs4, core4, fromx4, sem4,
     part6, core6, tox6, fromx6, sem6, part7, core7, tox7, fromx7, sem7,
     fetch_sem, block, near, far, small_sem, *ring_refs, count,
 ):
@@ -890,6 +990,8 @@
 
     ring = Ring(count, (g0, g1), (sum0, sum1), ring_view, *ring_refs)
     small = Small(count, block, near, far, small_sem)
+    fetch = own_copy(all_units, units, own_sem)
+    fetch.start()
     greet(*ring.peers)
     ring.start()
     four = FarHop(ffn_part, core4, None, fromx4, None, sem4, chunk)
@@ -897,12 +999,21 @@
     seven = Hop(part7, core7, tox7, fromx7, None, sem7, chunk)
     four.fetch(mine4, theirs4, fetch_sem)
     four.fetched()
-    block[: SMALL - NORM_ROWS, :] = before[...]
-    block[SMALL - NORM_ROWS :, :] = jnp.concatenate([stats[:7, :], jnp.zeros((2, width), jnp.float32)])
-    gain = vec[0:1, :]
+    fetch.wait()
+    block[...] = jnp.zeros_like(block)
+    cols = self_b.shape[1]
+    for row in range(2):
+        block[0:1, row * cols : (row + 1) * cols] = self_b[row : row + 1, :]
+        block[0:1, (2 + row) * cols : (3 + row) * cols] = cross_b[row : row + 1, :]
+        block[1 + row : 2 + row, :] = ffn_b[:, row * width : (row + 1) * width]
+    block[SMALL - NORM_ROWS : SMALL - 2, :] = stats[:7, :]
+    valid_rows = left_here(lens, x2.shape[0], dqkv.shape[0])
+    gain = gains[0:1, :]
 
     def project(step):
-        six.put(part6, step, dot_nt(six.take(dqkv, step), qkv_w[...]).astype(jnp.bfloat16))
+        grads = six.take(dqkv, step)
+        total = dot_nt(grads[:, :cols], qkv_w[0]) + dot_nt(grads[:, cols : 2 * cols], qkv_w[1])
+        six.put(part6, step, (total + dot_nt(grads[:, 2 * cols :], qkv_w[2])).astype(jnp.bfloat16))
         six.send_core(step)
         four.send_core(step)
 
@@ -931,17 +1042,17 @@
 
     def output(step):
         rows = four.own_rows(step)
-        total = x2[rows, :] + four.result(step) + vec[1:2, :]
-        y[rows, :] = jnp.where(valid[rows, :1] > 0.5, total, 0.0).astype(jnp.bfloat16)
-
-    ready = steps + 2
+        total = x2[rows, :] + four.result(step) + biases[2:3, :]
+        y[rows, :] = jnp.where(row_of(step, chunk, width) < valid_rows, total, 0.0).astype(jnp.bfloat16)
+
+    ready = steps + 1
 
     def extra(tick):
         for when, work in enumerate((small.begin, small.forward, small.launch)):
             pl.when(tick == ready + when)(work)
         step = tick - ready - 3
 
-        @pl.when((step >= 0) & (step < count - 1))
+        @pl.when((step >= 0) & (step < count // 2))
         def _():
             small.rotate(step)
 
@@ -953,7 +1064,7 @@
         ],
         ring,
         extra,
-        ready + 3 + count - 1,
+        ready + 3 + count // 2,
     )
 
     def finish(step, carry):
@@ -967,9 +1078,9 @@
     small.finish(small_sum)
 
 
-def last(count, ffn_part, g0, g1, dqkv, dkv, units_own, dx1, x2, valid, before, stats, vec, qkv_w, kv_w):
+def last(count, ffn_part, g0, g1, units, lens, dqkv, dkv, dx1, x2, *rest):
     rows = dqkv.shape[0]
-    own, width = units_own.shape
+    own, width = dx1.shape
     chunk = own // STEPS
     text_own = dkv.shape[0] // NARROW
     bf, f32 = jnp.bfloat16, jnp.float32
@@ -980,17 +1091,18 @@
     far = [pltpu.VMEM((own, width), bf)] * 2 + [hop[0], hop[2], hop[3]]
     return pl.pallas_call(
         functools.partial(last_kernel, count=count),
-        in_specs=[hbm] * 3 + [vmem] * 11,
+        in_specs=[hbm] * 4 + [pl.BlockSpec(memory_space=pltpu.SMEM)] + [vmem] * (4 + len(rest)),
         out_specs=[hbm] * 2 + [vmem] * 4,
         out_shape=[
-            shape(g0.shape, bf),
-            shape(g1.shape, bf),
+            pltpu.HBM(g0.shape, bf),
+            pltpu.HBM(g1.shape, bf),
             shape((own, width), bf),
             shape((own, width), f32),
             shape((text_own, width), f32),
             shape((SMALL, width), f32),
         ],
-        scratch_shapes=far
+        scratch_shapes=[pltpu.VMEM((own, width), bf), pltpu.SemaphoreType.DMA]
+        + far
         + [pltpu.VMEM((rows, width), bf)]
         + hop
         + [pltpu.VMEM((dkv.shape[0], width), bf)]
@@ -1000,13 +1112,53 @@
             pltpu.VMEM((SMALL, width), f32),
             pltpu.VMEM((NARROW, SMALL, width), f32),
             pltpu.VMEM((count, SMALL, width), f32),
-            pltpu.SemaphoreType.DMA((2, 2, max(count - 1, 3))),
+            pltpu.SemaphoreType.DMA((2, 3, max(count // 2, 3))),
         ]
         + ring_scratch(count, (width // count, width // 2)),
         compiler_params=pltpu.CompilerParams(collective_id=2, has_side_effects=True, vmem_limit_bytes=58 * MIB),
         cost_estimate=pl.CostEstimate(flops=30 * 10**9, bytes_accessed=16 * MIB, transcendentals=0),
         name="last",
-    )(ffn_part, g0, g1, dqkv, dkv, units_own, dx1, x2, valid, before, stats, vec, qkv_w, kv_w)
+    )(ffn_part, g0, g1, units, lens, dqkv, dkv, dx1, x2, *rest)
+
+
+def unpack_kernel(sum0, sum1, small, qkv_g, cq_g, co_g, so_g, kv_g, gain_g, shift_g, bias_g, self_b, cross_b, ffn_b):
+    cols = cq_g.shape[1]
+    for part in range(3):
+        qkv_g[part] = sum0[:, part * cols : (part + 1) * cols].astype(jnp.float32)
+    cq_g[...] = sum0[:, 3 * cols :].astype(jnp.float32)
+    co_g[...] = sum1[:cols, :].astype(jnp.float32)
+    so_g[...] = sum1[cols : 2 * cols, :].astype(jnp.float32)
+    half = kv_g.shape[1] // 2
+    for side in range(2):
+        for part in range(2):
+            first = (2 * side + part) * cols
+            kv_g[part, side * half : (side + 1) * half, :] = sum1[2 * cols :, first : first + cols].astype(jnp.float32)
+    norms = small[SMALL - NORM_ROWS :, :]
+    for ref, order in ((gain_g, (7, 4, 0)), (shift_g, (8, 5, 1)), (bias_g, (6, 3, 2))):
+        for row, source in enumerate(order):
+            ref[row : row + 1, :] = norms[source : source + 1, :]
+    width = small.shape[1]
+    for row in range(2):
+        self_b[row : row + 1, :] = small[0:1, row * cols : (row + 1) * cols]
+        cross_b[row : row + 1, :] = small[0:1, (2 + row) * cols : (3 + row) * cols]
+        ffn_b[:, row * width : (row + 1) * width] = small[1 + row : 2 + row, :]
+
+
+def unpack(sum0, sum1, small, cols, hidden):
+    width = sum0.shape[0]
+    shape = lambda *dims: jax.ShapeDtypeStruct(dims, jnp.float32)
+    vmem = pl.BlockSpec(memory_space=pltpu.VMEM)
+    return pl.pallas_call(
+        unpack_kernel,
+        in_specs=[vmem] * 3,
+        out_specs=[vmem] * 11,
+        out_shape=[
+            shape(3, width, cols), shape(width, cols), shape(cols, width), shape(cols, width), shape(2, width, cols),
+            shape(3, width), shape(3, width), shape(3, width), shape(2, cols), shape(2, cols), shape(1, hidden),
+        ],
+        compiler_params=pltpu.CompilerParams(vmem_limit_bytes=40 * MIB),
+        name="unpack",
+    )(sum0, sum1, small)
 
 
 def local(
@@ -1030,115 +1182,101 @@
     ffn_out,
     out_bias,
 ):
-    own_rows = units.shape[0] // NARROW
-    first_own = lax.axis_index("narrow") * own_rows
-    slot_count = unit_lengths.shape[0]
-    slot_live = jnp.arange(slot_count, dtype=jnp.int32) < bucket_counts[0]
+    slot_live = jnp.arange(unit_lengths.shape[0], dtype=jnp.int32) < bucket_counts[0]
     lengths = jnp.where(slot_live, unit_lengths, 0)
-    positions = first_own + jnp.arange(own_rows, dtype=jnp.int32)
-    slot_match = (positions // UNITS)[:, None] == jnp.arange(slot_count, dtype=jnp.int32)[None, :]
-    row_limit = jnp.sum(jnp.where(slot_match, lengths[None, :], 0), axis=1)
-    valid_own = positions % UNITS < row_limit
-    text_pos = jnp.arange(TEXT, dtype=jnp.int32)
-    keep = (text_pos[None, :] < text_lengths[:, None]).astype(jnp.float32)
-
-    def own(rows):
-        return lax.dynamic_slice_in_dim(rows, first_own, own_rows, 0)
-
-    qkv_weights = self_qkv.reshape(self_qkv.shape[0], -1)
+    qkv_weights = jnp.transpose(self_qkv, (1, 0, 2))
     kv_weights = cross_kv.reshape(cross_kv.shape[0], -1)
-    own_units = own(units)
+    count = lax.axis_size("wide")
     first_in, queries, key_rows, value_rows, self_context = front(
-        lengths, units, norm_gain[0], norm_shift[0], qkv_weights, self_bias[0], self_bias[1]
+        lengths, units, norm_gain, norm_shift, qkv_weights, self_bias
     )
-    last_bias = jnp.zeros((3,) + out_bias.shape[1:], jnp.float32)
     second_all, third_all, cross_queries, cross_context, text_kv, resid_one, resid_two = middle(
+        units,
+        text_lengths,
         self_context,
-        own_units,
         text,
-        jnp.concatenate([norm_gain[1:2], norm_shift[1:2], out_bias[0:1], norm_gain[2:3], norm_shift[2:3], out_bias[1:2], last_bias[:2]]),
+        norm_gain,
+        norm_shift,
+        out_bias,
         cross_bias,
-        keep,
         self_out,
         cross_q,
         kv_weights,
         cross_out,
     )
-    ffn_part, third_part, ffn_in_grad, ffn_out_grad, ffn_in_bias_grad = ffn(
+    ffn_part, third_part, ffn_in_grad, ffn_out_grad, ffn_bias_sum = ffn(
         lengths, third_all, out_grad, ffn_in, ffn_in_bias, ffn_out
     )
-    grad_own = jnp.where(valid_own[:, None], own(out_grad), jnp.zeros((), out_grad.dtype))
-    spread = own_rows // STEPS * NARROW // slot_count
-    count = lax.axis_size("wide")
-    ffn_in_grad, ffn_out_grad, resid_one_grad, self_context_grad, text_kv_grad, cross_out_grad, cross_q_grad, self_out_grad, cross_bias_grad, stats = turn(
+    in_sum, out_sum, grads_one, grads_two, resid_one_grad, context_grad, text_kv_grad, cross_bias_sum, stats = turn(
         count,
         third_part,
         ffn_in_grad,
         ffn_out_grad,
+        out_grad,
+        lengths,
+        text_lengths,
         resid_one,
         resid_two,
-        grad_own,
         second_all,
         cross_queries,
         cross_context,
         text_kv,
         self_context,
-        jnp.broadcast_to(keep.reshape(-1, 1), (keep.size, spread)),
-        jnp.concatenate([norm_gain[2:3], norm_gain[1:2]]),
+        norm_gain,
         cross_out,
         cross_q,
         self_out,
     )
-    qkv_grad = back(lengths, queries, key_rows, value_rows, self_context_grad)
-    cols = queries.shape[1]
-    self_qkv_grad = dot_tn(first_in, qkv_grad).astype(jnp.bfloat16)
-    cross_kv_grad = dot_tn(text, text_kv_grad).astype(jnp.bfloat16)
-    half = cross_kv_grad.shape[0] // 2
-    width = units.shape[1]
-    before = jnp.concatenate(
-        [
-            jnp.sum(qkv_grad[:, :cols], axis=0, dtype=jnp.float32),
-            jnp.sum(qkv_grad[:, 2 * cols :], axis=0, dtype=jnp.float32),
-            cross_bias_grad.reshape(-1),
-            ffn_in_bias_grad.reshape(-1),
-        ]
-    ).reshape(-1, width)
-    small_rows = SMALL // 2
+    qkv_grad, grads_one, grads_two, self_bias_sum, ffn_in_grad, ffn_out_grad = back(
+        lengths,
+        queries,
+        key_rows,
+        value_rows,
+        context_grad,
+        first_in,
+        text,
+        text_kv_grad,
+        in_sum,
+        out_sum,
+        grads_one,
+        grads_two,
+    )
     summed_one, summed_two, output, units_grad, text_grad, small = last(
         count,
         ffn_part,
-        jnp.concatenate([self_qkv_grad, cross_q_grad], axis=1),
-        jnp.concatenate(
-            [cross_out_grad, self_out_grad, jnp.concatenate([cross_kv_grad[:half], cross_kv_grad[half:]], axis=1)]
-        ),
+        grads_one,
+        grads_two,
+        units,
+        lengths,
         qkv_grad,
         text_kv_grad,
-        own_units,
         resid_one_grad,
         resid_two,
-        jnp.broadcast_to(valid_own[:, None].astype(jnp.float32), (own_rows, 128)),
-        jnp.concatenate([before, jnp.zeros((SMALL - NORM_ROWS - before.shape[0], width), jnp.float32)]),
+        self_bias_sum,
+        cross_bias_sum,
+        ffn_bias_sum,
         stats,
-        jnp.concatenate([norm_gain[0:1], out_bias[2:3]]),
+        norm_gain,
+        out_bias,
         qkv_weights,
         kv_weights,
     )
-    summed_one, summed_two = summed_one.astype(jnp.float32), summed_two.astype(jnp.float32)
-    self_qkv_grad = summed_one[:, : 3 * cols].reshape(self_qkv.shape)
-    cross_q_grad = summed_one[:, 3 * cols :]
-    cross_out_grad, self_out_grad = summed_two[:cols], summed_two[cols : 2 * cols]
-    cross_kv_grad = jnp.concatenate(
-        [summed_two[2 * cols :, : 2 * cols], summed_two[2 * cols :, 2 * cols :]]
-    ).reshape(cross_kv.shape)
-    ffn_in_grad, ffn_out_grad = ffn_in_grad.astype(jnp.float32), ffn_out_grad.astype(jnp.float32)
-    biases = small[: before.shape[0]].reshape(-1)
-    self_bias_grad = biases[: 2 * cols].reshape(2, cols)
-    cross_bias_grad = biases[2 * cols : 4 * cols].reshape(2, cols)
-    ffn_in_bias_grad = biases[4 * cols :]
-    norms = small[SMALL - NORM_ROWS :]
-    gain_grad = jnp.stack([norms[7], norms[4], norms[0]])
-    shift_grad = jnp.stack([norms[8], norms[5], norms[1]])
-    bias_grad = jnp.stack([norms[6], norms[3], norms[2]])
+    (
+        self_qkv_grad,
+        cross_q_grad,
+        cross_out_grad,
+        self_out_grad,
+        cross_kv_grad,
+        gain_grad,
+        shift_grad,
+        bias_grad,
+        self_bias_grad,
+        cross_bias_grad,
+        ffn_in_bias_grad,
+    ) = unpack(summed_one, summed_two, small, queries.shape[1], ffn_in_bias.shape[0])
+    self_qkv_grad = jnp.transpose(self_qkv_grad, (1, 0, 2))
+    cross_kv_grad = jnp.transpose(cross_kv_grad, (1, 0, 2))
+    ffn_in_bias_grad = ffn_in_bias_grad.reshape(-1)
     return (
         output,
         units_grad,

time: 582 us -> 545 us (0.936); the launches traced: 587 us -> 539 us
  other arithmetic: 25.5 us -> 0.66 us
  local copies, waits for them, and re-layouts: 38.3 us -> 17 us
    pallas_call x1, Pallas kernels: 9.41 us -> 32.2 us  [back(): pl.pallas_call(back_kernel, grid_spec=pltpu.PrefetchScalarGridSpec(num_sc...]
    slice x15 -> x0, local copies, waits for them, and re-layouts: 12.7 us -> none  [the longest x2 4.28 us: local(): self_qkv_grad = summed_one[:, :3 * cols].reshape(self_qkv.shape)]
    convert_element_type x3 -> x0, other arithmetic: 11.8 us -> none  [the longest x1 6.8 us: local(): ffn_in_grad.astype(jnp.float32)]
    pallas_call x1, Pallas kernels: 132 us -> 123 us  [last(): pl.pallas_call(functools.partial(last_kernel, count=count), in_specs=[hbm...]
    pallas_call x1 -> x2, Pallas kernels: 118 us -> 110 us  [the longest x1 107 us: middle(): pl.pallas_call(middle_kernel, in_specs=[pl.BlockSpec(memory_space=pl.ANY)...]
    unnamed x80 -> x29, local copies, waits for them, and re-layouts: 17.3 us -> 17 us
where the time goes in v5:
time: 545 us; the launch traced here: 539 us
  Pallas kernels  520 us (95%)
  local copies, waits for them, and re-layouts  17 us (3%)
    pallas_call x1, Pallas kernels, turn(): pl.pallas_call(functools.partial(turn_kernel, count=count), in_specs=[hbm...  214 us
    pallas_call x1, Pallas kernels, last(): pl.pallas_call(functools.partial(last_kernel, count=count), in_specs=[hbm...  123 us
    pallas_call x1, Pallas kernels, middle(): pl.pallas_call(middle_kernel, in_specs=[pl.BlockSpec(memory_space=pl.ANY)...  107 us
    pallas_call x1, Pallas kernels, back(): pl.pallas_call(back_kernel, grid_spec=pltpu.PrefetchScalarGridSpec(num_sc...  32.2 us
    pallas_call x1, Pallas kernels, ffn(): pl.pallas_call(ffn_kernel, grid_spec=pltpu.PrefetchScalarGridSpec(num_sca...  30.3 us
    unnamed x29, local copies, waits for them, and re-layouts  17 us

profile of v5, /device:TPU:0, one launch (start us, length us, event | category | flops | bytes accessed | tf_op | source)
XLA Modules:
  0.0 538.7 jit_solution(15062416721687833066)
XLA Ops:
  1.3 0.7 compare_select_fusion.lens
  2.0 0.0 copy-start.7
  2.0 2.4 copy.38
  4.4 0.0 copy-start.3
  4.4 1.4 copy-done.3
  5.8 0.0 copy-start.4
  5.8 0.7 copy-done.4
  6.5 0.0 copy-start.5
  6.5 0.7 copy-done.5
  7.2 0.0 copy-start.6
  7.2 0.7 copy-done.6
  7.9 9.2 %front.1 = (bf16[2048,1024]{1,0:T(8,128)(2,1)}, bf16[2048,256]{1,0:T(8,128)(2,1)}, bf16[2048,256]{1,0:T(8,128)(2,1)}, bf16[2048,256]{1,0:T(8,128)(2,1)}, bf16[2048,256]{1,0:T(8,128)(2,1)S(1)}) custom-call(s32[2]{0:T(128)S(1)} %compare_select_fusion.lens, bf16[2048,1024]{1,0:T(8,128)(2,1)} %all_units.3, f32[3,1024]{1,0:T(4,128)S(1)} %copy-done.5, ...), custom_call_target="tpu_custom_call" | custom-call | flops 20000000000 | bytes 16777216 | tf_op jit(solution)/shard_map/front/pallas_call | solution.py:109
  17.1 0.0 copy-done.7
  17.1 0.0 copy-start.8
  17.1 1.0 copy-done.8
  18.0 107.2 %middle.1 = (bf16[2048,1024]{1,0:T(8,128)(2,1)}, bf16[2048,1024]{1,0:T(8,128)(2,1)}, bf16[2048,256]{1,0:T(8,128)(2,1)}, bf16[2048,256]{1,0:T(8,128)(2,1)}, bf16[...) custom-call(bf16[2048,1024]{1,0:T(8,128)(2,1)} %all_units.3, s32[2]{0:T(128)} %text_lens.3, ...), custom_call_target="tpu_custom_call" | custom-call | flops 99999997952 | bytes 25165824 | tf_op jit(solution)/shard_map/middle/pallas_call | solution.py:577
  125.2 30.3 %ffn.1 = (bf16[2048,1024]{1,0:T(8,128)(2,1)}, bf16[2048,1024]{1,0:T(8,128)(2,1)}, bf16[1024,2048]{1,0:T(8,128)(2,1)}, bf16[2048,1024]{1,0:T(8,128)(2,1)}, f32[1,2048]{1,0:T(1,128)}) custom-call(s32[2]{0:T(128)} %copy-done.7, bf16[2048,1024]{1,0:T(8,128)(2,1)} %get-tuple-element.66.h_ref, bf16[2048,1024]{1,0:T(8,128)(2,1)} %out_grad.1, ...), custom_call_target="tpu_custom_call" | custom-call | flops 60000002048 | bytes 33554432 | tf_op jit(solution)/shard_map/ffn/pallas_call | solution.py:654
  155.5 214.3 %turn.1 = (bf16[1024,2048]{1,0:T(8,128)(2,1)}, bf16[2048,1024]{1,0:T(8,128)(2,1)}, bf16[1024,1024]{1,0:T(8,128)(2,1)}, bf16[1024,1024]{1,0:T(8,128)(2,1)}, f32[5...) custom-call(bf16[2048,1024]{1,0:T(8,128)(2,1)} %get-tuple-element.71, ...), custom_call_target="tpu_custom_call" | custom-call | flops 99999997952 | bytes 25165824 | tf_op jit(solution)/shard_map/turn/pallas_call | solution.py:865
  369.9 32.2 %back.1 = (bf16[2048,768]{1,0:T(8,128)(2,1)}, bf16[1024,1024]{1,0:T(8,128)(2,1)}, bf16[1024,1024]{1,0:T(8,128)(2,1)}, f32[2,256]{1,0:T(2,128)}, f32[1024,2048]{1,0:T(8,128)}, /*index=5*/f32[2048,1024]{1,0:T(8,128)}) custom-call(s32[2]{0:T(128)} %copy-done.7, ...), custom_call_target="tpu_custom_call", output_to_operand_aliasing={{1}: (10, {}), {2}: (11, {})} | custom-call | flops 30000001024 | bytes 41943040 | tf_op jit(solution)/shard_map/back/pallas_call | solution.py:201
  402.1 123.3 %last.1 = (bf16[1024,1024]{1,0:T(8,128)(2,1)}, bf16[1024,1024]{1,0:T(8,128)(2,1)}, bf16[512,1024]{1,0:T(8,128)(2,1)}, f32[512,1024]{1,0:T(8,128)}, f32[128,1024]{1,0:T(8,128)}, /*index=5*/f32[16,1024]{1,0:T(8,128)}) custom-call(bf16[2048,1024]{1,0:T(8,128)(2,1)} %get-tuple-element.67.ffn_part, bf16[1024,1024]{1,0:T(8,128)(2,1)} %get-tuple-element.87.g0, ...), custom_call_target="tpu_custom_call" | custom-call | flops 30000001024 | bytes 16777216 | tf_op jit(solution)/shard_map/last/pallas_call | solution.py:1092
  525.4 0.0 copy-start
  525.4 1.6 copy-done
  527.0 0.0 copy-start.1
  527.0 1.6 copy-done.1
  528.6 0.0 copy-start.2
  528.6 0.8 copy-done.2
  529.5 3.0 unpack.1
  532.4 0.0 copy-start.10
  532.5 0.0 copy-start.9
  532.5 2.9 copy.37
  535.4 0.0 copy-done.10
  535.4 0.0 copy-start.11
  535.4 1.0 copy.45
  536.4 0.0 copy-done.9
  536.4 1.3 copy.46
  537.7 0.0 copy-done.11
  537.7 0.8 copy.47
Async XLA Ops:
  2.0 15.1 %copy-start.7 = (s32[2]{0:T(128)}, s32[2]{0:T(128)S(1)}, u32[]{:S(2)}) copy-start(s32[2]{0:T(128)S(1)} %compare_select_fusion.lens) | copy-start | bytes 28
  4.4 1.4 copy-start.3
  5.8 0.7 copy-start.4
  6.5 0.7 copy-start.5
  7.2 0.7 copy-start.6
  17.1 1.0 copy-start.8
  525.4 1.6 copy-start
  527.0 1.6 copy-start.1
  528.6 0.8 copy-start.2
  532.4 3.0 copy-start.10
  532.5 3.9 copy-start.9
  535.4 2.3 copy-start.11

commit v6 on v5

--- a/solution.py
+++ b/solution.py
@@ -63,9 +63,14 @@
     return jnp.sum(values, axis=0, keepdims=True)
 
 
-def front_kernel(lens, x_ref, g_ref, s_ref, w_ref, b_ref, h_ref, q_ref, k_ref, v_ref, c_ref):
+def front_kernel(
+    lens, x_ref, t_ref, g_ref, s_ref, w_ref, b_ref, kvw_ref, vb_ref, h_ref, q_ref, k_ref, v_ref, kv_ref, c_ref
+):
     length = lens[pl.program_id(0)]
     width = q_ref.shape[1]
+    both = dot_nn(t_ref[...], kvw_ref[...])
+    kv_ref[:, :width] = both[:, :width].astype(jnp.bfloat16)
+    kv_ref[:, width:] = (both[:, width:] + vb_ref[1:2, :]).astype(jnp.bfloat16)
     for i in range(x_ref.shape[0] // BLOCK):
         rows = pl.ds(i * BLOCK, BLOCK)
 
@@ -97,13 +102,14 @@
                 ref[rows, :] = jnp.zeros((BLOCK, ref.shape[1]), ref.dtype)
 
 
-def front(lengths, units, gains, shifts, weights, bias):
+def front(lengths, units, text, gains, shifts, weights, bias, kv_w, cross_bias):
     rows, width = units.shape
     slots = lengths.shape[0]
     slot_rows = rows // slots
     cols = weights.shape[2]
     whole = lambda a: pl.BlockSpec(a.shape, lambda s, *_: (0,) * a.ndim)
     slot = lambda w: pl.BlockSpec((slot_rows, w), lambda s, *_: (s, 0))
+    texts = lambda w: pl.BlockSpec((text.shape[0] // slots, w), lambda s, *_: (s, 0))
     shape = lambda w: jax.ShapeDtypeStruct((rows, w), jnp.bfloat16)
     far = lambda w: pltpu.HBM((rows, w), jnp.bfloat16)
     return pl.pallas_call(
@@ -111,14 +117,22 @@
         grid_spec=pltpu.PrefetchScalarGridSpec(
             num_scalar_prefetch=1,
             grid=(slots,),
-            in_specs=[slot(width)] + [whole(a) for a in (gains, shifts, weights, bias)],
-            out_specs=[slot(width), slot(cols), slot(cols), slot(cols), slot(cols)],
+            in_specs=[slot(width), texts(width)]
+            + [whole(a) for a in (gains, shifts, weights, bias, kv_w, cross_bias)],
+            out_specs=[slot(width), slot(cols), slot(cols), slot(cols), texts(2 * cols), slot(cols)],
         ),
-        out_shape=[far(width), far(cols), far(cols), far(cols), shape(cols)],
+        out_shape=[
+            far(width),
+            far(cols),
+            far(cols),
+            far(cols),
+            jax.ShapeDtypeStruct((text.shape[0], 2 * cols), jnp.bfloat16),
+            shape(cols),
+        ],
         compiler_params=pltpu.CompilerParams(vmem_limit_bytes=48 * MIB),
         cost_estimate=pl.CostEstimate(flops=20 * 10**9, bytes_accessed=16 * MIB, transcendentals=8 * MIB),
         name="front",
-    )(lengths, units, gains, shifts, weights, bias)
+    )(lengths, units, text, gains, shifts, weights, bias, kv_w, cross_bias)
 
 
 def back_kernel(
@@ -377,8 +391,8 @@
 class Hop:
     KINDS = 6
 
-    def __init__(self, part, from_core, to_cross, from_cross, full, sems, chunk):
-        self.part, self.from_core, self.to_cross, self.from_cross = part, from_core, to_cross, from_cross
+    def __init__(self, part, from_core, from_cross, full, sems, chunk):
+        self.part, self.from_core, self.from_cross = part, from_core, from_cross
         self.full, self.sems, self.chunk = full, sems, chunk
         self.own = part.shape[0] // NARROW
         self.index, self.core, self.cross, self.diagonal = place()
@@ -396,7 +410,9 @@
         ]
 
     def cross_copy(self, step):
-        return remote(self.to_cross.at[step], self.from_cross.at[step], self.sems, 2, step, self.cross)
+        return remote(
+            self.part.at[self.rows(self.cross, step)], self.from_cross.at[step], self.sems, 2, step, self.cross
+        )
 
     def gather_copy(self, step, kind):
         owner = self.cross if kind == 5 else self.index
@@ -412,7 +428,7 @@
             copy.wait_recv()
         total = self.part[self.rows(self.cross, step), :].astype(jnp.float32)
         total += self.from_core[step, 1].astype(jnp.float32)
-        self.to_cross[step] = total.astype(jnp.bfloat16)
+        self.part[self.rows(self.cross, step), :] = total.astype(jnp.bfloat16)
         self.cross_copy(step).start()
 
     def result(self, step):
@@ -434,10 +450,14 @@
         self.gather_copy(step, 4).wait_recv()
         self.gather_copy(step, 5).wait_recv()
 
-    def finish(self, step, gather=True):
+    def sent(self, step):
         for copy in self.core_copies(step):
             copy.wait_send()
         self.cross_copy(step).wait_send()
+
+    def finish(self, step, gather=True, parts=True):
+        if parts:
+            self.sent(step)
         if gather:
             for kind in (3, 4, 5):
                 self.gather_copy(step, kind).wait_send()
@@ -454,7 +474,6 @@
     steps = own // chunk
     return [
         pltpu.VMEM((steps, 2, chunk, width), jnp.bfloat16),
-        pltpu.VMEM((steps, chunk, width), jnp.bfloat16),
         pltpu.VMEM((steps, chunk, width), jnp.bfloat16),
         pltpu.SemaphoreType.DMA((2, Hop.KINDS, steps)),
     ]
@@ -486,34 +505,63 @@
 
 
 def middle_kernel(
-    all_units, text_lens, c1, text, gains, shifts, biases, bias, so_w, cq_w, kv_w, co_w,
-    h2, h3, q2, c2, kv2, x1, x2,
-    units, own_sem, part1, part2, core1, tox1, fromx1, sem1, core2, tox2, fromx2, sem2,
+    all_units, out_grad, far_in, far_out, lens, text_lens, c1, kv2, gains, shifts, biases, bias, so_w, cq_w, co_w, b_in,
+    ffn_part, third, in_g, out_g, h2, q2, c2, x1, x2, in_bias_g,
+    units, own_sem, w_in, w_out, weight_sem, grads_in, grads_sem, give, give_sem, in_acc, out_acc,
+    part, h3, core1, fromx1, sem1, core2, fromx2, sem2,
 ):
-    steps, chunk, width = tox1.shape
+    steps, chunk, width = fromx1.shape
     cols = q2.shape[1]
     slots = text_lens.shape[0]
-    texts = text.shape[0] // slots
-    fetch = own_copy(all_units, units, own_sem)
-    fetch.start()
+    texts = kv2.shape[0] // slots
+    slot_rows = h2.shape[0] // slots
+    hidden_count = w_out.shape[0]
+    fetches = [
+        own_copy(all_units, units, own_sem),
+        pltpu.make_async_copy(far_in, w_in, weight_sem.at[0]),
+        pltpu.make_async_copy(far_out, w_out, weight_sem.at[1]),
+    ]
+    for fetch in fetches:
+        fetch.start()
     greet()
-    one = Hop(part1, core1, tox1, fromx1, h2, sem1, chunk)
-    two = Hop(part2, core2, tox2, fromx2, h3, sem2, chunk)
+    one = Hop(part, core1, fromx1, h2, sem1, chunk)
+    two = Hop(part, core2, fromx2, h3, sem2, chunk)
     scale = jnp.bfloat16(HEAD_DIM**-0.5)
-
-    fetch.wait()
+    in_acc[...] = jnp.zeros_like(in_acc)
+    out_acc[...] = jnp.zeros_like(out_acc)
+    in_bias_g[...] = jnp.zeros_like(in_bias_g)
+
+    def grad_copies(step):
+        slot = step % 2
+        return [
+            pltpu.make_async_copy(
+                out_grad.at[one.rows(owner, step), :],
+                grads_in.at[slot, pl.ds(owner * chunk, chunk), :],
+                grads_sem.at[slot, owner],
+            )
+            for owner in range(NARROW)
+        ]
+
+    def give_copies(step, kind):
+        slot = step % 2
+        return [
+            pltpu.make_async_copy(
+                give.at[kind, slot, pl.ds(owner * chunk, chunk), :],
+                (ffn_part, third)[kind].at[one.rows(owner, step), :],
+                give_sem.at[kind, slot, owner],
+            )
+            for owner in range(NARROW)
+        ]
 
     def project(step):
-        one.put(part1, step, dot_nn(one.take(c1, step), so_w[...]).astype(jnp.bfloat16))
+        one.put(part, step, dot_nn(one.take(c1, step), so_w[...]).astype(jnp.bfloat16))
         one.send_core(step)
 
-        @pl.when(step == 1)
+    def norm_one(step):
+        @pl.when(step == 0)
         def _():
-            both = dot_nn(text[...], kv_w[...])
-            kv2[:, :cols] = both[:, :cols].astype(jnp.bfloat16)
-            kv2[:, cols:] = (both[:, cols:] + bias[1:2, :]).astype(jnp.bfloat16)
-
-    def norm_one(step):
+            fetches[0].wait()
+
         rows = one.own_rows(step)
         resid = units[rows, :].astype(jnp.float32) + one.result(step) + biases[0:1, :]
         x1[rows, :] = resid
@@ -541,7 +589,8 @@
             context.append(total.astype(jnp.bfloat16))
         context = jnp.concatenate(context, axis=0)
         one.put(c2, step, context)
-        two.put(part2, step, dot_nn(context, co_w[...]).astype(jnp.bfloat16))
+        one.sent(step)
+        two.put(part, step, dot_nn(context, co_w[...]).astype(jnp.bfloat16))
         two.send_core(step)
 
     def norm_two(step):
@@ -550,127 +599,135 @@
         x2[rows, :] = resid
         two.send_gather(step, norm_forward(resid, gains[2:3, :], shifts[2:3, :])[0].astype(jnp.bfloat16))
 
+    def forward_two(step):
+        two.forward(step)
+        for copy in grad_copies(step):
+            copy.start()
+
+    def ffn(step):
+        @pl.when(step == 0)
+        def _():
+            fetches[1].wait()
+            fetches[2].wait()
+
+        two.gathered(step)
+        for copy in grad_copies(step):
+            copy.wait()
+        rows = two.take(h3, step)
+        place_in = lax.broadcasted_iota(jnp.int32, (chunk, width), 0) + step * chunk
+        grads = []
+        for owner in range(NARROW):
+            first = owner * two.own
+            valid = place_in < lens[first // slot_rows] - first % slot_rows
+            values = grads_in[step % 2, owner * chunk : (owner + 1) * chunk, :]
+            grads.append(jnp.where(valid, values.astype(jnp.float32), 0.0).astype(jnp.bfloat16))
+        grads = jnp.concatenate(grads, axis=0)
+        out = jnp.zeros(rows.shape, jnp.float32)
+        back_out = jnp.zeros(rows.shape, jnp.float32)
+        for begin in range(0, hidden_count, HIDDEN):
+            some = slice(begin, begin + HIDDEN)
+            pre = dot_nn(rows, w_in[:, some]) + b_in[:, some]
+            cdf = 0.5 + 0.5 * lax.erf(pre * (0.5**0.5))
+            pdf = jnp.exp(-0.5 * pre * pre) * 0.3989422804014327
+            hidden = (pre * cdf).astype(jnp.bfloat16)
+            pre_low = ((cdf + pre * pdf) * dot_nt(grads, w_out[some, :])).astype(jnp.bfloat16)
+            in_bias_g[:, some] += column_sum(pre_low.astype(jnp.float32))
+            out += dot_nn(hidden, w_out[some, :])
+            back_out += dot_nt(pre_low, w_in[:, some])
+            out_acc[some, :] += dot_tn(hidden, grads)
+            side, place_at = divmod(begin, width)
+            in_acc[side * width : (side + 1) * width, place_at : place_at + HIDDEN] += dot_tn(rows, pre_low)
+
+        @pl.when(step >= 2)
+        def _():
+            for kind in range(2):
+                for copy in give_copies(step - 2, kind):
+                    copy.wait()
+
+        give[0, step % 2] = out.astype(jnp.bfloat16)
+        give[1, step % 2] = back_out.astype(jnp.bfloat16)
+        for kind in range(2):
+            for copy in give_copies(step, kind):
+                copy.start()
+
     stages(
         steps,
-        [
-            project, one.send_cross, norm_one, one.forward, cross,
-            two.send_cross, norm_two, two.forward, two.gathered,
-        ],
+        [project, one.send_cross, norm_one, one.forward, cross, two.send_cross, norm_two, forward_two, ffn],
     )
 
     def finish(step, carry):
-        one.finish(step)
+        one.finish(step, True, False)
         two.finish(step)
         return carry
 
     lax.fori_loop(0, steps, finish, 0)
-
-
-def middle(units, text_lens, c1, text, gains, shifts, biases, bias, so_w, cq_w, kv_w, co_w):
+    part[...] = out_acc[...].astype(jnp.bfloat16)
+    results = [pltpu.make_async_copy(part, out_g, weight_sem.at[0])]
+    results[0].start()
+    h3[...] = in_acc[...].astype(jnp.bfloat16)
+    for side in range(hidden_count // width):
+        here = pl.ds(side * width, width)
+        results.append(pltpu.make_async_copy(h3.at[here, :], in_g.at[:, here], weight_sem.at[1 + side]))
+        results[-1].start()
+    for step in (steps - 2, steps - 1):
+        for kind in range(2):
+            for copy in give_copies(step, kind):
+                copy.wait()
+    for copy in results:
+        copy.wait()
+
+
+def middle(units, out_grad, w_in, w_out, lens, text_lens, c1, kv2, gains, shifts, biases, bias, so_w, cq_w, co_w, b_in):
     rows, cols = c1.shape
     own, width = rows // NARROW, units.shape[1]
+    hidden_count = w_out.shape[0]
     chunk = own // STEPS
     bf, f32 = jnp.bfloat16, jnp.float32
     shape = jax.ShapeDtypeStruct
     vmem = pl.BlockSpec(memory_space=pltpu.VMEM)
+    hbm = pl.BlockSpec(memory_space=pl.ANY)
     hop = hop_scratch(own, chunk, width)
+    dma = pltpu.SemaphoreType.DMA
     return pl.pallas_call(
         middle_kernel,
-        in_specs=[pl.BlockSpec(memory_space=pl.ANY), pl.BlockSpec(memory_space=pltpu.SMEM)] + [vmem] * 10,
-        out_specs=[vmem] * 7,
+        in_specs=[hbm] * 4 + [pl.BlockSpec(memory_space=pltpu.SMEM)] * 2 + [vmem] * 10,
+        out_specs=[hbm] * 4 + [vmem] * 6,
         out_shape=[
-            shape((rows, width), bf),
+            pltpu.HBM((rows, width), bf),
+            pltpu.HBM((rows, width), bf),
+            pltpu.HBM((width, hidden_count), bf),
+            pltpu.HBM((hidden_count, width), bf),
             shape((rows, width), bf),
             shape((rows, cols), bf),
             shape((rows, cols), bf),
-            shape((text.shape[0], 2 * cols), bf),
             shape((own, width), f32),
             shape((own, width), f32),
+            shape((1, hidden_count), f32),
         ],
-        scratch_shapes=[pltpu.VMEM((own, width), bf), pltpu.SemaphoreType.DMA]
-        + [pltpu.VMEM((rows, width), bf)] * 2
+        scratch_shapes=[
+            pltpu.VMEM((own, width), bf),
+            dma,
+            pltpu.VMEM((width, hidden_count), bf),
+            pltpu.VMEM((hidden_count, width), bf),
+            dma((1 + hidden_count // width,)),
+            pltpu.VMEM((2, NARROW * chunk, width), bf),
+            dma((2, NARROW)),
+            pltpu.VMEM((2, 2, NARROW * chunk, width), bf),
+            dma((2, 2, NARROW)),
+            pltpu.VMEM((hidden_count, width), f32),
+            pltpu.VMEM((hidden_count, width), f32),
+            pltpu.VMEM((rows, width), bf),
+            pltpu.VMEM((rows, width), bf),
+        ]
         + hop
         + hop,
-        compiler_params=pltpu.CompilerParams(collective_id=0, has_side_effects=True, vmem_limit_bytes=58 * MIB),
-        cost_estimate=pl.CostEstimate(flops=100 * 10**9, bytes_accessed=24 * MIB, transcendentals=4 * MIB),
+        compiler_params=pltpu.CompilerParams(collective_id=0, has_side_effects=True, vmem_limit_bytes=60 * MIB),
+        cost_estimate=pl.CostEstimate(flops=100 * 10**9, bytes_accessed=48 * MIB, transcendentals=8 * MIB),
         name="middle",
-    )(units, text_lens, c1, text, gains, shifts, biases, bias, so_w, cq_w, kv_w, co_w)
-
-
-def ffn_kernel(lens, h_ref, e_ref, wi_ref, b_ref, wo_ref, a_ref, d_ref, gi_ref, go_ref, gb_ref, gi_acc, go_acc):
-    block = pl.program_id(0)
-    per_slot = pl.num_programs(0) // lens.shape[0]
-    length = lens[block // per_slot]
-
-    @pl.when(block == 0)
-    def _():
-        gi_acc[...] = jnp.zeros_like(gi_acc)
-        go_acc[...] = jnp.zeros_like(go_acc)
-        gb_ref[...] = jnp.zeros_like(gb_ref)
-
-    live = (block % per_slot) * BLOCK < length
-
-    @pl.when(live)
-    def _():
-        rows, grads = h_ref[...], e_ref[...]
-        out = jnp.zeros(a_ref.shape, jnp.float32)
-        back_out = jnp.zeros(d_ref.shape, jnp.float32)
-        hidden_count = wo_ref.shape[0]
-        for first in range(0, hidden_count, HIDDEN):
-            part = slice(first, first + HIDDEN)
-            pre = dot_nn(rows, wi_ref[:, part]) + b_ref[:, part]
-            cdf = 0.5 + 0.5 * lax.erf(pre * (0.5**0.5))
-            pdf = jnp.exp(-0.5 * pre * pre) * 0.3989422804014327
-            hidden = (pre * cdf).astype(jnp.bfloat16)
-            slope = cdf + pre * pdf
-            pre_grad = slope * dot_nt(grads, wo_ref[part, :])
-            pre_low = pre_grad.astype(jnp.bfloat16)
-            gb_ref[:, part] += jnp.sum(pre_low.astype(jnp.float32), axis=0, keepdims=True)
-            out += dot_nn(hidden, wo_ref[part, :])
-            back_out += dot_nt(pre_low, wi_ref[:, part])
-            go_acc[part, :] += dot_tn(hidden, grads)
-            gi_acc[:, part] += dot_tn(rows, pre_low)
-        a_ref[...] = out.astype(jnp.bfloat16)
-        d_ref[...] = back_out.astype(jnp.bfloat16)
-
-    @pl.when(jnp.logical_not(live))
-    def _():
-        a_ref[...] = jnp.zeros_like(a_ref)
-        d_ref[...] = jnp.zeros_like(d_ref)
-
-    @pl.when(block == pl.num_programs(0) - 1)
-    def _():
-        gi_ref[...] = gi_acc[...].astype(jnp.bfloat16)
-        go_ref[...] = go_acc[...].astype(jnp.bfloat16)
-
-
-def ffn(lengths, rows_in, grads, w_in, b_in, w_out):
-    rows, width = rows_in.shape
-    count = w_out.shape[0]
-    bf, f32 = jnp.bfloat16, jnp.float32
-    shape = jax.ShapeDtypeStruct
-    block = pl.BlockSpec((BLOCK, width), lambda i, *_: (i, 0))
-    whole = lambda a, b: pl.BlockSpec((a, b), lambda i, *_: (0, 0), pipeline_mode=pl.Buffered(1))
-    return pl.pallas_call(
-        ffn_kernel,
-        grid_spec=pltpu.PrefetchScalarGridSpec(
-            num_scalar_prefetch=1,
-            grid=(rows // BLOCK,),
-            in_specs=[block, block, whole(width, count), whole(1, count), whole(count, width)],
-            out_specs=[block, block, whole(width, count), whole(count, width), whole(1, count)],
-            scratch_shapes=[pltpu.VMEM((width, count), f32), pltpu.VMEM((count, width), f32)],
-        ),
-        out_shape=[
-            shape((rows, width), bf),
-            shape((rows, width), bf),
-            shape((width, count), bf),
-            shape((count, width), bf),
-            shape((1, count), f32),
-        ],
-        compiler_params=pltpu.CompilerParams(vmem_limit_bytes=58 * MIB),
-        cost_estimate=pl.CostEstimate(flops=60 * 10**9, bytes_accessed=32 * MIB, transcendentals=8 * MIB),
-        name="ffn",
-    )(lengths, rows_in, grads, w_in, b_in.reshape(1, -1), w_out)
+    )(
+        units, out_grad, w_in, w_out, lens, text_lens, c1, kv2, gains, shifts, biases, bias, so_w, cq_w, co_w,
+        b_in.reshape(1, -1),
+    )
 
 
 class FarHop(Hop):
@@ -722,10 +779,10 @@
     third, in_g, out_g, out_grad, lens, text_lens, x1, x2, h2, q2, c2, kv2, c1, gains, co_w, cq_w, so_w,
     in_sum, out_sum, g0, g1, dx1, dc1, dkv, bias_g, stats,
     co_g, cq_g, so_g, give_sem, e_own, own_sem, mine3, theirs3, core3, fromx3, sem3,
-    part5, core5, tox5, fromx5, sem5, full3, full5, dx2, co_acc, cq_acc, so_acc, dkv_acc, fetch_sem,
+    part5, core5, fromx5, sem5, full3, full5, dx2, co_acc, cq_acc, so_acc, dkv_acc, fetch_sem,
     *ring_refs, count,
 ):
-    steps, chunk, width = tox5.shape
+    steps, chunk, width = fromx5.shape
     cols = q2.shape[1]
     slots = bias_g.shape[0]
     texts = kv2.shape[0] // slots
@@ -741,8 +798,8 @@
     fetch.start()
     greet(*ring.peers)
     ring.start()
-    three = FarHop(third, core3, None, fromx3, full3, sem3, chunk)
-    five = Hop(part5, core5, tox5, fromx5, full5, sem5, chunk)
+    three = FarHop(third, core3, fromx3, full3, sem3, chunk)
+    five = Hop(part5, core5, fromx5, full5, sem5, chunk)
     three.fetch(mine3, theirs3, fetch_sem)
 
     def start(step, carry):
@@ -861,7 +918,7 @@
     vmem = pl.BlockSpec(memory_space=pltpu.VMEM)
     hbm = pl.BlockSpec(memory_space=pl.ANY)
     hop = hop_scratch(own, chunk, width)
-    far = [pltpu.VMEM((own, width), bf)] * 2 + [hop[0], hop[2], hop[3]]
+    far = [pltpu.VMEM((own, width), bf)] * 2 + hop
     return pl.pallas_call(
         functools.partial(turn_kernel, count=count),
         in_specs=[hbm] * 4 + [pl.BlockSpec(memory_space=pltpu.SMEM)] * 2 + [vmem] * 11,
@@ -978,11 +1035,11 @@
     ffn_part, g0, g1, all_units, lens, dqkv, dkv, dx1, x2, self_b, cross_b, ffn_b, stats, gains, biases, qkv_w, kv_w,
     sum0, sum1, y, units_g, text_g, small_sum,
     units, own_sem, mine4, theirs4, core4, fromx4, sem4,
-    part6, core6, tox6, fromx6, sem6, part7, core7, tox7, fromx7, sem7,
+    part6, core6, fromx6, sem6, part7, core7, fromx7, sem7,
     fetch_sem, block, near, far, small_sem, *ring_refs, count,
 ):
-    steps, chunk, width = tox6.shape
-    text_steps = tox7.shape[0]
+    steps, chunk, width = fromx6.shape
+    text_steps = fromx7.shape[0]
 
     def ring_view(ref, way, half, shard):
         high = width // count
@@ -994,9 +1051,9 @@
     fetch.start()
     greet(*ring.peers)
     ring.start()
-    four = FarHop(ffn_part, core4, None, fromx4, None, sem4, chunk)
-    six = Hop(part6, core6, tox6, fromx6, None, sem6, chunk)
-    seven = Hop(part7, core7, tox7, fromx7, None, sem7, chunk)
+    four = FarHop(ffn_part, core4, fromx4, None, sem4, chunk)
+    six = Hop(part6, core6, fromx6, None, sem6, chunk)
+    seven = Hop(part7, core7, fromx7, None, sem7, chunk)
     four.fetch(mine4, theirs4, fetch_sem)
     four.fetched()
     fetch.wait()
@@ -1088,7 +1145,7 @@
     vmem = pl.BlockSpec(memory_space=pltpu.VMEM)
     hbm = pl.BlockSpec(memory_space=pl.ANY)
     hop = hop_scratch(own, chunk, width)
-    far = [pltpu.VMEM((own, width), bf)] * 2 + [hop[0], hop[2], hop[3]]
+    far = [pltpu.VMEM((own, width), bf)] * 2 + hop
     return pl.pallas_call(
         functools.partial(last_kernel, count=count),
         in_specs=[hbm] * 4 + [pl.BlockSpec(memory_space=pltpu.SMEM)] + [vmem] * (4 + len(rest)),
@@ -1187,25 +1244,37 @@
     qkv_weights = jnp.transpose(self_qkv, (1, 0, 2))
     kv_weights = cross_kv.reshape(cross_kv.shape[0], -1)
     count = lax.axis_size("wide")
-    first_in, queries, key_rows, value_rows, self_context = front(
-        lengths, units, norm_gain, norm_shift, qkv_weights, self_bias
+    first_in, queries, key_rows, value_rows, text_kv, self_context = front(
+        lengths, units, text, norm_gain, norm_shift, qkv_weights, self_bias, kv_weights, cross_bias
     )
-    second_all, third_all, cross_queries, cross_context, text_kv, resid_one, resid_two = middle(
+    (
+        ffn_part,
+        third_part,
+        ffn_in_grad,
+        ffn_out_grad,
+        second_all,
+        cross_queries,
+        cross_context,
+        resid_one,
+        resid_two,
+        ffn_bias_sum,
+    ) = middle(
         units,
+        out_grad,
+        ffn_in,
+        ffn_out,
+        lengths,
         text_lengths,
         self_context,
-        text,
+        text_kv,
         norm_gain,
         norm_shift,
         out_bias,
         cross_bias,
         self_out,
         cross_q,
-        kv_weights,
         cross_out,
-    )
-    ffn_part, third_part, ffn_in_grad, ffn_out_grad, ffn_bias_sum = ffn(
-        lengths, third_all, out_grad, ffn_in, ffn_in_bias, ffn_out
+        ffn_in_bias,
     )
     in_sum, out_sum, grads_one, grads_two, resid_one_grad, context_grad, text_kv_grad, cross_bias_sum, stats = turn(
         count,

time: 545 us -> 518 us (0.950); the launches traced: 539 us -> 519 us
  Pallas kernels: 520 us -> 498 us
    pallas_call x1, Pallas kernels: 214 us -> 183 us  [turn(): pl.pallas_call(functools.partial(turn_kernel, count=count), in_specs=[hbm...]
    pallas_call x1, Pallas kernels: 123 us -> 133 us  [last(): pl.pallas_call(functools.partial(last_kernel, count=count), in_specs=[hbm...]
    unnamed x29 -> x37, local copies, waits for them, and re-layouts: 17 us -> 19.1 us
    pallas_call x2 -> x1, Pallas kernels: 137 us -> 137 us  [middle(): pl.pallas_call(middle_kernel, in_specs=[hbm] * 4 + [pl.BlockSpec(memory_s...]
where the time goes in v6:
time: 518 us; the launch traced here: 519 us
  Pallas kernels  498 us (96%)
  local copies, waits for them, and re-layouts  19.1 us (4%)
    pallas_call x1, Pallas kernels, turn(): pl.pallas_call(functools.partial(turn_kernel, count=count), in_specs=[hbm...  183 us
    pallas_call x1, Pallas kernels, middle(): pl.pallas_call(middle_kernel, in_specs=[hbm] * 4 + [pl.BlockSpec(memory_s...  137 us
    pallas_call x1, Pallas kernels, last(): pl.pallas_call(functools.partial(last_kernel, count=count), in_specs=[hbm...  133 us
    pallas_call x1, Pallas kernels, back(): pl.pallas_call(back_kernel, grid_spec=pltpu.PrefetchScalarGridSpec(num_sc...  32 us
    unnamed x37, local copies, waits for them, and re-layouts  19.1 us

profile of v6, /device:TPU:0, one launch (start us, length us, event | category | flops | bytes accessed | tf_op | source)
XLA Modules:
  0.0 519.2 jit_solution(4213860834843022863)
XLA Ops:
  1.3 0.7 compare_select_fusion.lens
  2.0 0.0 copy-start.10
  2.0 1.4 copy.38
  3.4 0.0 copy-start.2
  3.4 0.0 copy-start.4
  3.4 1.8 copy-done.4
  5.2 0.0 copy-start.5
  5.2 1.2 copy-done.5
  6.4 0.0 copy-start.6
  6.4 0.7 copy-done.6
  7.2 0.0 copy-start.7
  7.2 0.7 copy-done.7
  7.9 0.0 copy-start.8
  7.9 0.7 copy-done.8
  8.6 0.0 copy-start.9
  8.6 0.7 copy-done.9
  9.2 9.6 %front.1 = (bf16[2048,1024]{1,0:T(8,128)(2,1)}, bf16[2048,256]{1,0:T(8,128)(2,1)}, bf16[2048,256]{1,0:T(8,128)(2,1)}, bf16[2048,256]{1,0:T(8,128)(2,1)}, bf16[51...) custom-call(s32[2]{0:T(128)S(1)} %compare_select_fusion.lens, bf16[2048,1024]{1,0:T(8,128)(2,1)} %all_units.3, ...), custom_call_target="tpu_custom_call" | custom-call | flops 20000000000 | bytes 16777216 | tf_op jit(solution)/shard_map/front/pallas_call | solution.py:115
  18.8 0.0 copy-done.10
  18.8 0.0 copy-done.2
  18.8 0.0 copy-start.11
  18.9 1.0 copy-done.11
  19.8 0.0 copy-start.12
  19.8 0.8 copy-done.12
  20.6 136.7 %middle.1 = (bf16[2048,1024]{1,0:T(8,128)(2,1)}, bf16[2048,1024]{1,0:T(8,128)(2,1)}, bf16[1024,2048]{1,0:T(8,128)(2,1)}, bf16[2048,1024]{1,0:T(8,128)(2,1)}, bf1...) custom-call(bf16[2048,1024]{1,0:T(8,128)(2,1)} %all_units.3, ...), custom_call_target="tpu_custom_call" | custom-call | flops 99999997952 | bytes 50331648 | tf_op jit(solution)/shard_map/middle/pallas_call | solution.py:691
  157.3 183.4 %turn.1 = (bf16[1024,2048]{1,0:T(8,128)(2,1)}, bf16[2048,1024]{1,0:T(8,128)(2,1)}, bf16[1024,1024]{1,0:T(8,128)(2,1)}, bf16[1024,1024]{1,0:T(8,128)(2,1)}, f32[5...) custom-call(bf16[2048,1024]{1,0:T(8,128)(2,1)} %get-tuple-element.70, ...), custom_call_target="tpu_custom_call" | custom-call | flops 99999997952 | bytes 25165824 | tf_op jit(solution)/shard_map/turn/pallas_call | solution.py:922
  340.8 32.0 %back.1 = (bf16[2048,768]{1,0:T(8,128)(2,1)}, bf16[1024,1024]{1,0:T(8,128)(2,1)}, bf16[1024,1024]{1,0:T(8,128)(2,1)}, f32[2,256]{1,0:T(2,128)}, f32[1024,2048]{1,0:T(8,128)}, /*index=5*/f32[2048,1024]{1,0:T(8,128)}) custom-call(s32[2]{0:T(128)} %copy-done.10, ...), custom_call_target="tpu_custom_call", output_to_operand_aliasing={{1}: (10, {}), {2}: (11, {})} | custom-call | flops 30000001024 | bytes 41943040 | tf_op jit(solution)/shard_map/back/pallas_call | solution.py:215
  372.8 133.1 %last.1 = (bf16[1024,1024]{1,0:T(8,128)(2,1)}, bf16[1024,1024]{1,0:T(8,128)(2,1)}, bf16[512,1024]{1,0:T(8,128)(2,1)}, f32[512,1024]{1,0:T(8,128)}, f32[128,1024]{1,0:T(8,128)}, /*index=5*/f32[16,1024]{1,0:T(8,128)}) custom-call(bf16[2048,1024]{1,0:T(8,128)(2,1)} %get-tuple-element.66.ffn_part, bf16[1024,1024]{1,0:T(8,128)(2,1)} %get-tuple-element.85.g0, ...), custom_call_target="tpu_custom_call" | custom-call | flops 30000001024 | bytes 16777216 | tf_op jit(solution)/shard_map/last/pallas_call | solution.py:1149
  505.9 0.0 copy-start
  506.0 1.6 copy-done
  507.5 0.0 copy-start.1
  507.5 1.6 copy-done.1
  509.1 0.0 copy-start.3
  509.1 0.8 copy-done.3
  510.0 3.0 unpack.1
  513.0 0.0 copy-start.14
  513.0 0.0 copy-start.13
  513.0 2.9 copy.37
  515.9 0.0 copy-done.14
  515.9 0.0 copy-start.15
  515.9 1.0 copy.45
  516.9 0.0 copy-done.13
  516.9 1.3 copy.46
  518.2 0.0 copy-done.15
  518.2 0.8 copy.47
Async XLA Ops:
  2.0 16.9 %copy-start.10 = (s32[2]{0:T(128)}, s32[2]{0:T(128)S(1)}, u32[]{:S(2)}) copy-start(s32[2]{0:T(128)S(1)} %compare_select_fusion.lens) | copy-start | bytes 28
  3.4 15.4 %copy-start.2 = (bf16[128,8,2,256]{3,1,2,0:T(8,128)(2,1)}, bf16[128,8,2,256]{3,1,2,0:T(8,128)(2,1)S(1)}, u32[]{:S(2)}) copy-start(bf16[128,8,2,256]{3,1,2,0:T(8,128)(2,1)S(1)} %copy.38) | copy-start | bytes 3145732
  3.4 1.8 copy-start.4
  5.2 1.2 copy-start.5
  6.4 0.7 copy-start.6
  7.2 0.7 copy-start.7
  7.9 0.7 copy-start.8
  8.6 0.7 copy-start.9
  18.8 1.0 copy-start.11
  19.8 0.8 copy-start.12
  505.9 1.6 copy-start
  507.5 1.6 copy-start.1
  509.1 0.8 copy-start.3
  513.0 3.0 copy-start.14
  513.0 3.9 copy-start.13
  515.9 2.3 copy-start.15

commit v7 on v6

--- a/solution.py
+++ b/solution.py
@@ -31,6 +31,7 @@
 
 
 BLOCK = 256
+LANES = 128
 MIB = 1 << 20
 NARROW = 4
 STEPS = 8
@@ -63,8 +64,17 @@
     return jnp.sum(values, axis=0, keepdims=True)
 
 
+def mask_diagonal(scores, axis):
+    count = scores.shape[axis]
+    parts = [scores] if count == BLOCK else jnp.split(scores, [count - BLOCK], axis=axis)
+    keys = lax.broadcasted_iota(jnp.int32, (BLOCK, BLOCK), axis)
+    queries = lax.broadcasted_iota(jnp.int32, (BLOCK, BLOCK), 1 - axis)
+    parts[-1] = jnp.where(keys <= queries, parts[-1], MASKED_SCORE)
+    return jnp.concatenate(parts, axis=axis)
+
+
 def front_kernel(
-    lens, x_ref, t_ref, g_ref, s_ref, w_ref, b_ref, kvw_ref, vb_ref, h_ref, q_ref, k_ref, v_ref, kv_ref, c_ref
+    lens, x_ref, t_ref, g_ref, s_ref, w_ref, b_ref, kvw_ref, vb_ref, h_ref, q_ref, k_ref, v_ref, kv_ref, c_ref, log_ref
 ):
     length = lens[pl.program_id(0)]
     width = q_ref.shape[1]
@@ -86,20 +96,24 @@
             count = (i + 1) * BLOCK
             keys, values = k_ref[:count, :], v_ref[:count, :]
             scaled = queries * jnp.bfloat16(HEAD_DIM**-0.5)
-            row = lax.broadcasted_iota(jnp.int32, (BLOCK, count), 0) + i * BLOCK
-            allowed = lax.broadcasted_iota(jnp.int32, (BLOCK, count), 1) <= row
             total = jnp.zeros((BLOCK, width), jnp.float32)
+            logs = jnp.zeros((BLOCK, LANES), jnp.float32)
+            lane = lax.broadcasted_iota(jnp.int32, logs.shape, 1)
             for head in range(width // HEAD_DIM):
-                scores = jnp.where(allowed, dot_nt(pick_head(scaled, head), keys), MASKED_SCORE)
-                weights = jnp.exp(scores - jnp.max(scores, axis=1, keepdims=True))
-                weights = weights * (1.0 / jnp.sum(weights, axis=1, keepdims=True))
-                total += dot_nn(weights.astype(jnp.bfloat16), pick_head(values, head))
+                scores = mask_diagonal(dot_nt(pick_head(scaled, head), keys), 1)
+                top = jnp.max(scores, axis=1, keepdims=True)
+                weights = jnp.exp(scores - top)
+                norm = jnp.sum(weights, axis=1, keepdims=True)
+                total += dot_nn(weights.astype(jnp.bfloat16), pick_head(values, head)) * (1.0 / norm)
+                logs = jnp.where(lane == head, top + jnp.log(norm), logs)
+            log_ref[:, rows] = logs.T[: log_ref.shape[0], :]
             c_ref[rows, :] = total.astype(jnp.bfloat16)
 
         @pl.when(i * BLOCK >= length)
         def _():
             for ref in (h_ref, q_ref, k_ref, v_ref, c_ref):
                 ref[rows, :] = jnp.zeros((BLOCK, ref.shape[1]), ref.dtype)
+            log_ref[:, rows] = jnp.zeros((log_ref.shape[0], BLOCK), jnp.float32)
 
 
 def front(lengths, units, text, gains, shifts, weights, bias, kv_w, cross_bias):
@@ -110,6 +124,7 @@
     whole = lambda a: pl.BlockSpec(a.shape, lambda s, *_: (0,) * a.ndim)
     slot = lambda w: pl.BlockSpec((slot_rows, w), lambda s, *_: (s, 0))
     texts = lambda w: pl.BlockSpec((text.shape[0] // slots, w), lambda s, *_: (s, 0))
+    logs = pl.BlockSpec((8, slot_rows), lambda s, *_: (0, s))
     shape = lambda w: jax.ShapeDtypeStruct((rows, w), jnp.bfloat16)
     far = lambda w: pltpu.HBM((rows, w), jnp.bfloat16)
     return pl.pallas_call(
@@ -119,7 +134,7 @@
             grid=(slots,),
             in_specs=[slot(width), texts(width)]
             + [whole(a) for a in (gains, shifts, weights, bias, kv_w, cross_bias)],
-            out_specs=[slot(width), slot(cols), slot(cols), slot(cols), texts(2 * cols), slot(cols)],
+            out_specs=[slot(width), slot(cols), slot(cols), slot(cols), texts(2 * cols), slot(cols), logs],
         ),
         out_shape=[
             far(width),
@@ -128,6 +143,7 @@
             far(cols),
             jax.ShapeDtypeStruct((text.shape[0], 2 * cols), jnp.bfloat16),
             shape(cols),
+            pltpu.HBM((8, rows), jnp.float32),
         ],
         compiler_params=pltpu.CompilerParams(vmem_limit_bytes=48 * MIB),
         cost_estimate=pl.CostEstimate(flops=20 * 10**9, bytes_accessed=16 * MIB, transcendentals=8 * MIB),
@@ -136,7 +152,7 @@
 
 
 def back_kernel(
-    lens, q_ref, k_ref, v_ref, dc_ref, h_ref, text_ref, dkv_ref, in_ref, out_ref, _g0, _g1,
+    lens, q_ref, k_ref, v_ref, dc_ref, c_ref, log_ref, h_ref, text_ref, dkv_ref, in_ref, out_ref, _g0, _g1,
     o_ref, g0_ref, g1_ref, b_ref, in_f32, out_f32, dk_acc, dv_acc, w_acc,
 ):
     in_f32[...] = in_ref[...].astype(jnp.float32)
@@ -164,18 +180,23 @@
             keys, values = k_ref[:count, :], v_ref[:count, :]
             scaled = q_ref[rows, :] * jnp.bfloat16(HEAD_DIM**-0.5)
             grads = dc_ref[rows, :]
-            col = lax.broadcasted_iota(jnp.int32, (count, BLOCK), 1) + i * BLOCK
-            allowed = lax.broadcasted_iota(jnp.int32, (count, BLOCK), 0) <= col
             total = jnp.zeros((BLOCK, width), jnp.float32)
+            heads = lax.broadcasted_iota(jnp.int32, (8, width), 0)
+            lanes = lax.broadcasted_iota(jnp.int32, (8, width), 1)
+            inner = lax.dot_general(
+                jnp.where((lanes >= heads * HEAD_DIM) & (lanes < (heads + 1) * HEAD_DIM), 1.0, 0.0),
+                grads.astype(jnp.float32) * c_ref[rows, :].astype(jnp.float32),
+                (((1,), (1,)), ((), ())),
+                precision=EXACT,
+                preferred_element_type=jnp.float32,
+            )
             for head in range(width // HEAD_DIM):
                 q_head, g_head = pick_head(scaled, head), pick_head(grads, head)
-                scores = jnp.where(allowed, dot_nt(keys, q_head), MASKED_SCORE)
-                weights = jnp.exp(scores - jnp.max(scores, axis=0, keepdims=True))
-                weights = weights * (1.0 / jnp.sum(weights, axis=0, keepdims=True))
+                scores = mask_diagonal(dot_nt(keys, q_head), 0)
+                weights = jnp.exp(scores - log_ref[head : head + 1, rows])
                 dv_acc[:count, :] += dot_nn(weights.astype(jnp.bfloat16), g_head)
                 weight_grad = dot_nt(values, g_head)
-                inner = jnp.sum(weights * weight_grad, axis=0, keepdims=True)
-                score_grad = (weights * (weight_grad - inner)).astype(jnp.bfloat16)
+                score_grad = (weights * (weight_grad - inner[head : head + 1, :])).astype(jnp.bfloat16)
                 dk_acc[:count, :] += dot_nn(score_grad, q_head)
                 total += dot_tn(score_grad, pick_head(keys, head))
             o_ref[rows, :width] = (total * HEAD_DIM**-0.5).astype(jnp.bfloat16)
@@ -202,7 +223,7 @@
         g0_ref[...] = w_acc[...].astype(jnp.bfloat16)
 
 
-def back(lengths, queries, keys, values, grads, rows_in, text, dkv, in_sum, out_sum, g0, g1):
+def back(lengths, queries, keys, values, grads, context, logs, rows_in, text, dkv, in_sum, out_sum, g0, g1):
     rows, cols = queries.shape
     width = rows_in.shape[1]
     slots = lengths.shape[0]
@@ -217,7 +238,8 @@
         grid_spec=pltpu.PrefetchScalarGridSpec(
             num_scalar_prefetch=1,
             grid=(slots,),
-            in_specs=[slot(queries)] * 4
+            in_specs=[slot(queries)] * 5
+            + [pl.BlockSpec((8, rows // slots), lambda s, *_: (0, s))]
             + [slot(rows_in), whole(text), whole(dkv), slot(in_sum), slot(out_sum), hbm, hbm],
             out_specs=[
                 pl.BlockSpec((rows // slots, 3 * cols), lambda s, *_: (s, 0)),
@@ -237,11 +259,11 @@
             shape(in_sum.shape, f32),
             shape(out_sum.shape, f32),
         ],
-        input_output_aliases={10: 1, 11: 2},
+        input_output_aliases={12: 1, 13: 2},
         compiler_params=pltpu.CompilerParams(vmem_limit_bytes=60 * MIB),
         cost_estimate=pl.CostEstimate(flops=30 * 10**9, bytes_accessed=40 * MIB, transcendentals=8 * MIB),
         name="back",
-    )(lengths, queries, keys, values, grads, rows_in, text, dkv, in_sum, out_sum, g0, g1)
+    )(lengths, queries, keys, values, grads, context, logs, rows_in, text, dkv, in_sum, out_sum, g0, g1)
 
 
 def place():
@@ -480,19 +502,19 @@
 
 
 def stages(steps, work, ring=None, extra=None, ticks=0):
-    ticks = max(ticks, steps + len(work) - 1)
+    ticks = max(ticks, steps + max(delay for delay, _ in work))
     per_tick = 0 if ring is None else -(-2 * (ring.count - 1) // ticks)
 
     def body(tick, carry):
-        for delay, stage in enumerate(work):
+        for number, (delay, stage) in enumerate(work):
             step = tick - delay
 
             @pl.when((step >= 0) & (step < steps))
             def _():
                 stage(step)
 
-            unit = (delay + 1) * Ring.UNITS // len(work) - 1
-            if per_tick and unit != delay * Ring.UNITS // len(work) - 1:
+            unit = (number + 1) * Ring.UNITS // len(work) - 1
+            if per_tick and unit != number * Ring.UNITS // len(work) - 1:
                 if per_tick == 1:
                     ring.serve(tick, unit)
                 else:
@@ -505,9 +527,10 @@
 
 
 def middle_kernel(
-    all_units, out_grad, far_in, far_out, lens, text_lens, c1, kv2, gains, shifts, biases, bias, so_w, cq_w, co_w, b_in,
+    all_units, out_grad, far_in, far_out, far_so, far_cq, far_co, lens, text_lens,
+    c1, kv2, gains, shifts, biases, bias, b_in,
     ffn_part, third, in_g, out_g, h2, q2, c2, x1, x2, in_bias_g,
-    units, own_sem, w_in, w_out, weight_sem, grads_in, grads_sem, give, give_sem, in_acc, out_acc,
+    units, own_sem, so_w, cq_w, co_w, small_sem, w_in, w_out, weight_sem, grads_in, grads_sem, give, give_sem, in_acc, out_acc,
     part, h3, core1, fromx1, sem1, core2, fromx2, sem2,
 ):
     steps, chunk, width = fromx1.shape
@@ -516,6 +539,12 @@
     texts = kv2.shape[0] // slots
     slot_rows = h2.shape[0] // slots
     hidden_count = w_out.shape[0]
+    near = [
+        pltpu.make_async_copy(source, target, small_sem.at[slot])
+        for slot, (source, target) in enumerate(((far_so, so_w), (far_cq, cq_w), (far_co, co_w)))
+    ]
+    for fetch in near:
+        fetch.start()
     fetches = [
         own_copy(all_units, units, own_sem),
         pltpu.make_async_copy(far_in, w_in, weight_sem.at[0]),
@@ -530,6 +559,8 @@
     in_acc[...] = jnp.zeros_like(in_acc)
     out_acc[...] = jnp.zeros_like(out_acc)
     in_bias_g[...] = jnp.zeros_like(in_bias_g)
+    for fetch in near:
+        fetch.wait()
 
     def grad_copies(step):
         slot = step % 2
@@ -652,7 +683,10 @@
 
     stages(
         steps,
-        [project, one.send_cross, norm_one, one.forward, cross, two.send_cross, norm_two, forward_two, ffn],
+        [
+            (0, project), (1, one.send_cross), (2, norm_one), (3, one.forward), (4, cross),
+            (5, two.send_cross), (6, norm_two), (7, forward_two), (8, ffn),
+        ],
     )
 
     def finish(step, carry):
@@ -677,7 +711,7 @@
         copy.wait()
 
 
-def middle(units, out_grad, w_in, w_out, lens, text_lens, c1, kv2, gains, shifts, biases, bias, so_w, cq_w, co_w, b_in):
+def middle(units, out_grad, w_in, w_out, so_w, cq_w, co_w, lens, text_lens, c1, kv2, gains, shifts, biases, bias, b_in):
     rows, cols = c1.shape
     own, width = rows // NARROW, units.shape[1]
     hidden_count = w_out.shape[0]
@@ -690,7 +724,7 @@
     dma = pltpu.SemaphoreType.DMA
     return pl.pallas_call(
         middle_kernel,
-        in_specs=[hbm] * 4 + [pl.BlockSpec(memory_space=pltpu.SMEM)] * 2 + [vmem] * 10,
+        in_specs=[hbm] * 7 + [pl.BlockSpec(memory_space=pltpu.SMEM)] * 2 + [vmem] * 7,
         out_specs=[hbm] * 4 + [vmem] * 6,
         out_shape=[
             pltpu.HBM((rows, width), bf),
@@ -707,6 +741,10 @@
         scratch_shapes=[
             pltpu.VMEM((own, width), bf),
             dma,
+            pltpu.VMEM(so_w.shape, bf),
+            pltpu.VMEM(cq_w.shape, bf),
+            pltpu.VMEM(co_w.shape, bf),
+            dma((3,)),
             pltpu.VMEM((width, hidden_count), bf),
             pltpu.VMEM((hidden_count, width), bf),
             dma((1 + hidden_count // width,)),
@@ -725,7 +763,7 @@
         cost_estimate=pl.CostEstimate(flops=100 * 10**9, bytes_accessed=48 * MIB, transcendentals=8 * MIB),
         name="middle",
     )(
-        units, out_grad, w_in, w_out, lens, text_lens, c1, kv2, gains, shifts, biases, bias, so_w, cq_w, co_w,
+        units, out_grad, w_in, w_out, so_w, cq_w, co_w, lens, text_lens, c1, kv2, gains, shifts, biases, bias,
         b_in.reshape(1, -1),
     )
 
@@ -879,10 +917,14 @@
 
     stages(
         steps,
-        [
-            three.send_cross, norm_three, three.forward, cross,
-            five.send_cross, norm_two, five.forward, last,
-        ],
+        list(
+            enumerate(
+                [
+                    three.send_cross, norm_three, three.forward, cross,
+                    five.send_cross, norm_two, five.forward, last,
+                ]
+            )
+        ),
         ring,
     )
     dkv[...] = dkv_acc[...].astype(jnp.bfloat16)
@@ -1115,10 +1157,14 @@
 
     stages(
         steps,
-        [
-            project, six.send_cross, norm_one, four.send_cross, output,
-            text_only(text_project), text_only(seven.send_cross), text_only(text_result),
-        ],
+        list(
+            enumerate(
+                [
+                    project, six.send_cross, norm_one, four.send_cross, output,
+                    text_only(text_project), text_only(seven.send_cross), text_only(text_result),
+                ]
+            )
+        ),
         ring,
         extra,
         ready + 3 + count // 2,
@@ -1185,11 +1231,11 @@
     cq_g[...] = sum0[:, 3 * cols :].astype(jnp.float32)
     co_g[...] = sum1[:cols, :].astype(jnp.float32)
     so_g[...] = sum1[cols : 2 * cols, :].astype(jnp.float32)
-    half = kv_g.shape[1] // 2
+    half = kv_g.shape[0] // 2
     for side in range(2):
         for part in range(2):
             first = (2 * side + part) * cols
-            kv_g[part, side * half : (side + 1) * half, :] = sum1[2 * cols :, first : first + cols].astype(jnp.float32)
+            kv_g[side * half : (side + 1) * half, part, :] = sum1[2 * cols :, first : first + cols].astype(jnp.float32)
     norms = small[SMALL - NORM_ROWS :, :]
     for ref, order in ((gain_g, (7, 4, 0)), (shift_g, (8, 5, 1)), (bias_g, (6, 3, 2))):
         for row, source in enumerate(order):
@@ -1210,7 +1256,7 @@
         in_specs=[vmem] * 3,
         out_specs=[vmem] * 11,
         out_shape=[
-            shape(3, width, cols), shape(width, cols), shape(cols, width), shape(cols, width), shape(2, width, cols),
+            shape(3, width, cols), shape(width, cols), shape(cols, width), shape(cols, width), shape(width, 2, cols),
             shape(3, width), shape(3, width), shape(3, width), shape(2, cols), shape(2, cols), shape(1, hidden),
         ],
         compiler_params=pltpu.CompilerParams(vmem_limit_bytes=40 * MIB),
@@ -1244,7 +1290,7 @@
     qkv_weights = jnp.transpose(self_qkv, (1, 0, 2))
     kv_weights = cross_kv.reshape(cross_kv.shape[0], -1)
     count = lax.axis_size("wide")
-    first_in, queries, key_rows, value_rows, text_kv, self_context = front(
+    first_in, queries, key_rows, value_rows, text_kv, self_context, self_logs = front(
         lengths, units, text, norm_gain, norm_shift, qkv_weights, self_bias, kv_weights, cross_bias
     )
     (
@@ -1263,6 +1309,9 @@
         out_grad,
         ffn_in,
         ffn_out,
+        self_out,
+        cross_q,
+        cross_out,
         lengths,
         text_lengths,
         self_context,
@@ -1271,9 +1320,6 @@
         norm_shift,
         out_bias,
         cross_bias,
-        self_out,
-        cross_q,
-        cross_out,
         ffn_in_bias,
     )
     in_sum, out_sum, grads_one, grads_two, resid_one_grad, context_grad, text_kv_grad, cross_bias_sum, stats = turn(
@@ -1302,6 +1348,8 @@
         key_rows,
         value_rows,
         context_grad,
+        self_context,
+        self_logs,
         first_in,
         text,
         text_kv_grad,
@@ -1344,7 +1392,6 @@
         ffn_in_bias_grad,
     ) = unpack(summed_one, summed_two, small, queries.shape[1], ffn_in_bias.shape[0])
     self_qkv_grad = jnp.transpose(self_qkv_grad, (1, 0, 2))
-    cross_kv_grad = jnp.transpose(cross_kv_grad, (1, 0, 2))
     ffn_in_bias_grad = ffn_in_bias_grad.reshape(-1)
     return (
         output,

time: 518 us -> 504 us (0.973)
  Pallas kernels: 498 us -> 483 us
    pallas_call x1, Pallas kernels: 133 us -> 119 us  [last(): pl.pallas_call(functools.partial(last_kernel, count=count), in_specs=[hbm...]
    unnamed x37 -> x36, local copies, waits for them, and re-layouts: 19.1 us -> 16.1 us
where the time goes in v7:
time: 504 us; the launch traced here: 501 us
  Pallas kernels  483 us (96%)
  local copies, waits for them, and re-layouts  16.1 us (3%)
    pallas_call x1, Pallas kernels, turn(): pl.pallas_call(functools.partial(turn_kernel, count=count), in_specs=[hbm...  184 us
    pallas_call x1, Pallas kernels, middle(): pl.pallas_call(middle_kernel, in_specs=[hbm] * 7 + [pl.BlockSpec(memory_s...  137 us
    pallas_call x1, Pallas kernels, last(): pl.pallas_call(functools.partial(last_kernel, count=count), in_specs=[hbm...  119 us
    pallas_call x1, Pallas kernels, back(): pl.pallas_call(back_kernel, grid_spec=pltpu.PrefetchScalarGridSpec(num_sc...  29.6 us
    unnamed x36, local copies, waits for them, and re-layouts  16.1 us

profile of v7, /device:TPU:0, one launch (start us, length us, event | category | flops | bytes accessed | tf_op | source)
XLA Modules:
  0.0 501.1 jit_solution(6481522384925771767)
XLA Ops:
  1.3 0.7 compare_select_fusion.lens
  2.0 0.0 copy-start.10
  2.0 1.4 copy.37
  3.4 0.0 copy-start.2
  3.4 0.0 copy-start.4
  3.4 1.8 copy-done.4
  5.2 0.0 copy-start.5
  5.2 1.2 copy-done.5
  6.4 0.0 copy-start.6
  6.4 0.7 copy-done.6
  7.2 0.0 copy-start.7
  7.2 0.7 copy-done.7
  7.9 0.0 copy-start.8
  7.9 0.7 copy-done.8
  8.6 0.0 copy-start.9
  8.6 0.7 copy-done.9
  9.2 9.3 %front.1 = (bf16[2048,1024]{1,0:T(8,128)(2,1)}, bf16[2048,256]{1,0:T(8,128)(2,1)}, bf16[2048,256]{1,0:T(8,128)(2,1)}, bf16[2048,256]{1,0:T(8,128)(2,1)}, bf16[51...) custom-call(s32[2]{0:T(128)S(1)} %compare_select_fusion.lens, ...), custom_call_target="tpu_custom_call" | custom-call | flops 20000000000 | bytes 16777216 | tf_op jit(solution)/shard_map/front/pallas_call | solution.py:130
  18.5 0.0 copy-done.10
  18.5 0.0 copy-done.2
  18.5 0.0 copy-start.11
  18.5 1.0 copy-done.11
  19.5 0.0 copy-start.12
  19.5 0.8 copy-done.12
  20.3 136.8 %middle.1 = (bf16[2048,1024]{1,0:T(8,128)(2,1)}, bf16[2048,1024]{1,0:T(8,128)(2,1)}, bf16[1024,2048]{1,0:T(8,128)(2,1)}, bf16[2048,1024]{1,0:T(8,128)(2,1)}, bf1...) custom-call(bf16[2048,1024]{1,0:T(8,128)(2,1)} %all_units.3, ...), custom_call_target="tpu_custom_call" | custom-call | flops 99999997952 | bytes 50331648 | tf_op jit(solution)/shard_map/middle/pallas_call | solution.py:725
  157.1 184.1 %turn.1 = (bf16[1024,2048]{1,0:T(8,128)(2,1)}, bf16[2048,1024]{1,0:T(8,128)(2,1)}, bf16[1024,1024]{1,0:T(8,128)(2,1)}, bf16[1024,1024]{1,0:T(8,128)(2,1)}, f32[5...) custom-call(bf16[2048,1024]{1,0:T(8,128)(2,1)} %get-tuple-element.71, ...), custom_call_target="tpu_custom_call" | custom-call | flops 99999997952 | bytes 25165824 | tf_op jit(solution)/shard_map/turn/pallas_call | solution.py:964
  341.2 29.6 %back.1 = (bf16[2048,768]{1,0:T(8,128)(2,1)}, bf16[1024,1024]{1,0:T(8,128)(2,1)}, bf16[1024,1024]{1,0:T(8,128)(2,1)}, f32[2,256]{1,0:T(2,128)}, f32[1024,2048]{1,0:T(8,128)}, /*index=5*/f32[2048,1024]{1,0:T(8,128)}) custom-call(s32[2]{0:T(128)} %copy-done.10, ...), custom_call_target="tpu_custom_call", output_to_operand_aliasing={{1}: (12, {}), {2}: (13, {})} | custom-call | flops 30000001024 | bytes 41943040 | tf_op jit(solution)/shard_map/back/pallas_call | solution.py:236
  370.8 119.2 %last.1 = (bf16[1024,1024]{1,0:T(8,128)(2,1)}, bf16[1024,1024]{1,0:T(8,128)(2,1)}, bf16[512,1024]{1,0:T(8,128)(2,1)}, f32[512,1024]{1,0:T(8,128)}, f32[128,1024]{1,0:T(8,128)}, /*index=5*/f32[16,1024]{1,0:T(8,128)}) custom-call(bf16[2048,1024]{1,0:T(8,128)(2,1)} %get-tuple-element.67.ffn_part, bf16[1024,1024]{1,0:T(8,128)(2,1)} %get-tuple-element.87.g0, ...), custom_call_target="tpu_custom_call" | custom-call | flops 30000001024 | bytes 16777216 | tf_op jit(solution)/shard_map/last/pallas_call | solution.py:1195
  490.0 0.0 copy-start
  490.0 1.6 copy-done
  491.6 0.0 copy-start.1
  491.6 1.6 copy-done.1
  493.2 0.0 copy-start.3
  493.2 0.8 copy-done.3
  494.0 0.0 copy-start.14
  494.0 0.0 copy-start.13
  494.0 3.8 unpack.1
  497.8 0.0 copy-done.14
  497.8 0.0 copy-start.15
  497.8 1.0 copy.44
  498.8 0.0 copy-done.13
  498.8 1.3 copy.45
  500.1 0.0 copy-done.15
  500.1 0.8 copy.46
Async XLA Ops:
  2.0 16.6 %copy-start.10 = (s32[2]{0:T(128)}, s32[2]{0:T(128)S(1)}, u32[]{:S(2)}) copy-start(s32[2]{0:T(128)S(1)} %compare_select_fusion.lens) | copy-start | bytes 28
  3.4 15.1 %copy-start.2 = (bf16[128,8,2,256]{3,1,2,0:T(8,128)(2,1)}, bf16[128,8,2,256]{3,1,2,0:T(8,128)(2,1)S(1)}, u32[]{:S(2)}) copy-start(bf16[128,8,2,256]{3,1,2,0:T(8,128)(2,1)S(1)} %copy.37) | copy-start | bytes 3145732
  3.4 1.8 copy-start.4
  5.2 1.2 copy-start.5
  6.4 0.7 copy-start.6
  7.2 0.7 copy-start.7
  7.9 0.7 copy-start.8
  8.6 0.7 copy-start.9
  18.5 1.0 copy-start.11
  19.5 0.8 copy-start.12
  490.0 1.6 copy-start
  491.6 1.6 copy-start.1
  493.2 0.8 copy-start.3
  494.0 3.8 copy-start.14
  494.0 4.8 copy-start.13
  497.8 2.3 copy-start.15

commit v8 on v7

--- a/solution.py
+++ b/solution.py
@@ -145,7 +145,7 @@
             shape(cols),
             pltpu.HBM((8, rows), jnp.float32),
         ],
-        compiler_params=pltpu.CompilerParams(vmem_limit_bytes=48 * MIB),
+        compiler_params=pltpu.CompilerParams(vmem_limit_bytes=60 * MIB),
         cost_estimate=pl.CostEstimate(flops=20 * 10**9, bytes_accessed=16 * MIB, transcendentals=8 * MIB),
         name="front",
     )(lengths, units, text, gains, shifts, weights, bias, kv_w, cross_bias)
@@ -212,11 +212,12 @@
 
         @pl.when(i * BLOCK < length)
         def _():
-            grads = o_ref[rows, :]
-            w_acc[...] += dot_tn(h_ref[rows, :], grads)
-            sums = column_sum(grads.astype(jnp.float32))
+            sums = column_sum(o_ref[rows, :].astype(jnp.float32))
             b_ref[0:1, :] += sums[:, :width]
             b_ref[1:2, :] += sums[:, 2 * width :]
+
+    for first in range(0, h_ref.shape[1], BLOCK):
+        w_acc[first : first + BLOCK, :] += dot_tn(h_ref[:, first : first + BLOCK], o_ref[...])
 
     @pl.when(pl.program_id(0) == pl.num_programs(0) - 1)
     def _():
@@ -410,6 +411,11 @@
     return pltpu.make_async_copy(whole.at[pl.ds(first, size), :], own, sem)
 
 
+def moves(sources, targets, sems):
+    pairs = list(zip(sources, targets, strict=True))
+    return [pltpu.make_async_copy(a, b, sems.at[slot]) for slot, (a, b) in enumerate(pairs)]
+
+
 class Hop:
     KINDS = 6
 
@@ -529,8 +535,8 @@
 def middle_kernel(
     all_units, out_grad, far_in, far_out, far_so, far_cq, far_co, lens, text_lens,
     c1, kv2, gains, shifts, biases, bias, b_in,
-    ffn_part, third, in_g, out_g, h2, q2, c2, x1, x2, in_bias_g,
-    units, own_sem, so_w, cq_w, co_w, small_sem, w_in, w_out, weight_sem, grads_in, grads_sem, give, give_sem, in_acc, out_acc,
+    ffn_part, third, in_g, out_g, far_h2, far_q2, far_c2, far_x1, far_x2, in_bias_g,
+    h2, q2, c2, x1, x2, leave_sem, units, own_sem, so_w, cq_w, co_w, small_sem, w_in, w_out, weight_sem, grads_in, grads_sem, give, give_sem, in_acc, out_acc,
     part, h3, core1, fromx1, sem1, core2, fromx2, sem2,
 ):
     steps, chunk, width = fromx1.shape
@@ -604,19 +610,21 @@
         one.put(q2, step, queries)
         scaled = queries * scale
         count = queries.shape[0] // slots
-        place_of = lax.broadcasted_iota(jnp.int32, (count, texts), 1)
+        place_of = lax.broadcasted_iota(jnp.int32, (count * (cols // HEAD_DIM), texts), 1)
         context = []
         for slot in range(slots):
             mine = scaled[slot * count : (slot + 1) * count]
             keys = kv2[slot * texts : (slot + 1) * texts, :cols]
             values = kv2[slot * texts : (slot + 1) * texts, cols:]
+            heads = range(cols // HEAD_DIM)
+            scores = dot_nt(jnp.concatenate([pick_head(mine, head) for head in heads], axis=0), keys)
+            scores = jnp.where(place_of < text_lens[slot], scores, MASKED_SCORE)
+            weights = jnp.exp(scores - jnp.max(scores, axis=1, keepdims=True))
+            norm = jnp.sum(weights, axis=1, keepdims=True)
+            mixed = dot_nn(weights.astype(jnp.bfloat16), values) * (1.0 / norm)
             total = jnp.zeros((count, cols), jnp.float32)
-            for head in range(cols // HEAD_DIM):
-                scores = dot_nt(pick_head(mine, head), keys)
-                scores = jnp.where(place_of < text_lens[slot], scores, MASKED_SCORE)
-                weights = jnp.exp(scores - jnp.max(scores, axis=1, keepdims=True))
-                weights = weights * (1.0 / jnp.sum(weights, axis=1, keepdims=True))
-                total += dot_nn(weights.astype(jnp.bfloat16), pick_head(values, head))
+            for head in heads:
+                total += pick_head(mixed[head * count : (head + 1) * count], head)
             context.append(total.astype(jnp.bfloat16))
         context = jnp.concatenate(context, axis=0)
         one.put(c2, step, context)
@@ -695,6 +703,9 @@
         return carry
 
     lax.fori_loop(0, steps, finish, 0)
+    leaving = moves((h2, q2, c2, x1, x2), (far_h2, far_q2, far_c2, far_x1, far_x2), leave_sem)
+    for copy in leaving:
+        copy.start()
     part[...] = out_acc[...].astype(jnp.bfloat16)
     results = [pltpu.make_async_copy(part, out_g, weight_sem.at[0])]
     results[0].start()
@@ -707,7 +718,7 @@
         for kind in range(2):
             for copy in give_copies(step, kind):
                 copy.wait()
-    for copy in results:
+    for copy in results + leaving:
         copy.wait()
 
 
@@ -725,20 +736,26 @@
     return pl.pallas_call(
         middle_kernel,
         in_specs=[hbm] * 7 + [pl.BlockSpec(memory_space=pltpu.SMEM)] * 2 + [vmem] * 7,
-        out_specs=[hbm] * 4 + [vmem] * 6,
+        out_specs=[hbm] * 9 + [vmem],
         out_shape=[
             pltpu.HBM((rows, width), bf),
             pltpu.HBM((rows, width), bf),
             pltpu.HBM((width, hidden_count), bf),
             pltpu.HBM((hidden_count, width), bf),
-            shape((rows, width), bf),
-            shape((rows, cols), bf),
-            shape((rows, cols), bf),
-            shape((own, width), f32),
-            shape((own, width), f32),
+            pltpu.HBM((rows, width), bf),
+            pltpu.HBM((rows, cols), bf),
+            pltpu.HBM((rows, cols), bf),
+            pltpu.HBM((own, width), f32),
+            pltpu.HBM((own, width), f32),
             shape((1, hidden_count), f32),
         ],
         scratch_shapes=[
+            pltpu.VMEM((rows, width), bf),
+            pltpu.VMEM((rows, cols), bf),
+            pltpu.VMEM((rows, cols), bf),
+            pltpu.VMEM((own, width), f32),
+            pltpu.VMEM((own, width), f32),
+            dma((5,)),
             pltpu.VMEM((own, width), bf),
             dma,
             pltpu.VMEM(so_w.shape, bf),
@@ -814,10 +831,11 @@
 
 
 def turn_kernel(
-    third, in_g, out_g, out_grad, lens, text_lens, x1, x2, h2, q2, c2, kv2, c1, gains, co_w, cq_w, so_w,
-    in_sum, out_sum, g0, g1, dx1, dc1, dkv, bias_g, stats,
-    co_g, cq_g, so_g, give_sem, e_own, own_sem, mine3, theirs3, core3, fromx3, sem3,
-    part5, core5, fromx5, sem5, full3, full5, dx2, co_acc, cq_acc, so_acc, dkv_acc, fetch_sem,
+    third, ffn_part, in_g, out_g, out_grad, lens, text_lens,
+    far_x1, far_x2, far_h2, far_q2, far_c2, far_kv2, far_c1, gains, biases, far_co, far_cq, far_so,
+    in_sum, out_sum, g0, g1, y, dx1, dc1, dkv, bias_g, stats,
+    x1, x2, h2, q2, c2, kv2, c1, co_w, cq_w, so_w, arrive_sem, cq_g, give_sem, e_own, own_sem, mine3, theirs3, core3, fromx3, sem3, mine4, theirs4, core4, fromx4, sem4,
+    part5, core5, fromx5, sem5, full3, full5, co_acc, cq_acc, so_acc, dkv_acc, fetch_sem,
     *ring_refs, count,
 ):
     steps, chunk, width = fromx5.shape
@@ -837,18 +855,31 @@
     greet(*ring.peers)
     ring.start()
     three = FarHop(third, core3, fromx3, full3, sem3, chunk)
+    four = FarHop(ffn_part, core4, fromx4, None, sem4, chunk)
     five = Hop(part5, core5, fromx5, full5, sem5, chunk)
-    three.fetch(mine3, theirs3, fetch_sem)
+    arriving = moves(
+        (far_x2, far_x1, far_h2, far_q2, far_c2, far_kv2, far_c1, far_co, far_cq, far_so),
+        (x2, x1, h2, q2, c2, kv2, c1, co_w, cq_w, so_w),
+        arrive_sem,
+    )
+    three.fetch(mine3, theirs3, fetch_sem.at[0])
+    for copy in arriving:
+        copy.start()
+    four.fetch(mine4, theirs4, fetch_sem.at[1])
 
     def start(step, carry):
         three.send_core(step)
+        four.send_core(step)
         return carry
 
     lax.fori_loop(0, steps, start, 0)
     for ref in (co_acc, cq_acc, so_acc, dkv_acc, bias_g, stats):
         ref[...] = jnp.zeros_like(ref)
     three.fetched()
+    four.fetched()
     fetch.wait()
+    for copy in arriving:
+        copy.wait()
     valid_rows = left_here(lens, x1.shape[0], h2.shape[0])
     scale = jnp.bfloat16(HEAD_DIM**-0.5)
 
@@ -862,7 +893,7 @@
         total = above + norm_backward(grad_in, normed, inv_std, gains[2:3, :])
         stats[2:3, :] += column_sum(above)
         stats[3:4, :] += column_sum(total)
-        dx2[rows, :] = total
+        dx1[rows, :] = total
         three.send_gather(step, total.astype(jnp.bfloat16))
 
     def cross(step):
@@ -903,7 +934,7 @@
         _, normed, inv_std = norm_forward(x1[rows, :], gains[1:2, :], gains[1:2, :])
         stats[4:5, :] += column_sum(grad_in * normed)
         stats[5:6, :] += column_sum(grad_in)
-        total = dx2[rows, :] + norm_backward(grad_in, normed, inv_std, gains[1:2, :])
+        total = dx1[rows, :] + norm_backward(grad_in, normed, inv_std, gains[1:2, :])
         stats[6:7, :] += column_sum(total)
         dx1[rows, :] = total
         five.send_gather(step, total.astype(jnp.bfloat16))
@@ -914,6 +945,23 @@
         dc1_rows = dot_nt(grads, so_w[...]).astype(jnp.bfloat16)
         five.put(dc1, step, dc1_rows)
         so_acc[...] += dot_tn(five.take(c1, step), grads)
+
+    def output(step):
+        rows = four.own_rows(step)
+        total = x2[rows, :] + four.result(step) + biases[2:3, :]
+        y[rows, :] = jnp.where(row_of(step, chunk, width) < valid_rows, total, 0.0).astype(jnp.bfloat16)
+
+    half = steps // 2
+    late = steps + 2
+
+    def side(tick):
+        for begin, first in ((0, 0), (late, half)):
+            for ahead, work in ((1, output), (0, four.send_cross)):
+                step = tick - begin - ahead
+
+                @pl.when((step >= 0) & (step < half))
+                def _():
+                    work(first + step)
 
     stages(
         steps,
@@ -926,22 +974,24 @@
             )
         ),
         ring,
+        side,
+        late + half + 1,
     )
     dkv[...] = dkv_acc[...].astype(jnp.bfloat16)
     bias_g[1:2, :] = column_sum(dkv[:, cols:].astype(jnp.float32))
-    co_g[...] = co_acc[...].astype(jnp.bfloat16)
+    mine4[:cols, :] = co_acc[...].astype(jnp.bfloat16)
     cq_g[...] = cq_acc[...].astype(jnp.bfloat16)
-    so_g[...] = so_acc[...].astype(jnp.bfloat16)
+    mine4[cols : 2 * cols, :] = so_acc[...].astype(jnp.bfloat16)
     gives = [
         pltpu.make_async_copy(cq_g, g0.at[:, pl.ds(width - cols, cols)], give_sem.at[0]),
-        pltpu.make_async_copy(co_g, g1.at[pl.ds(0, cols), :], give_sem.at[1]),
-        pltpu.make_async_copy(so_g, g1.at[pl.ds(cols, cols), :], give_sem.at[2]),
+        pltpu.make_async_copy(mine4.at[pl.ds(0, 2 * cols), :], g1.at[pl.ds(0, 2 * cols), :], give_sem.at[1]),
     ]
     for give in gives:
         give.start()
 
     def finish(step, carry):
         three.finish(step)
+        four.finish(step, False)
         five.finish(step)
         return carry
 
@@ -951,7 +1001,10 @@
         give.wait()
 
 
-def turn(count, third, in_g, out_g, out_grad, lens, text_lens, x1, x2, h2, q2, c2, kv2, c1, gains, co_w, cq_w, so_w):
+def turn(
+    count, third, ffn_part, in_g, out_g, out_grad, lens, text_lens,
+    x1, x2, h2, q2, c2, kv2, c1, gains, biases, co_w, cq_w, so_w,
+):
     rows, cols = c1.shape
     own, width = x1.shape
     chunk = own // STEPS
@@ -963,44 +1016,48 @@
     far = [pltpu.VMEM((own, width), bf)] * 2 + hop
     return pl.pallas_call(
         functools.partial(turn_kernel, count=count),
-        in_specs=[hbm] * 4 + [pl.BlockSpec(memory_space=pltpu.SMEM)] * 2 + [vmem] * 11,
-        out_specs=[hbm] * 4 + [vmem] * 5,
+        in_specs=[hbm] * 5 + [pl.BlockSpec(memory_space=pltpu.SMEM)] * 2 + [hbm] * 7 + [vmem] * 2 + [hbm] * 3,
+        out_specs=[hbm] * 4 + [vmem] * 6,
         out_shape=[
             pltpu.HBM(in_g.shape, bf),
             pltpu.HBM(out_g.shape, bf),
             pltpu.HBM((width, width), bf),
             pltpu.HBM((width, width), bf),
+            shape((own, width), bf),
             shape((own, width), f32),
             shape((rows, cols), bf),
             shape(kv2.shape, bf),
             shape((2, cols), f32),
             shape((8, width), f32),
         ],
-        scratch_shapes=[
-            pltpu.VMEM((cols, width), bf),
+        scratch_shapes=[pltpu.VMEM(a.shape, a.dtype) for a in (x1, x2, h2, q2, c2, kv2, c1, co_w, cq_w, so_w)]
+        + [
+            pltpu.SemaphoreType.DMA((10,)),
             pltpu.VMEM((width, cols), bf),
-            pltpu.VMEM((cols, width), bf),
-            pltpu.SemaphoreType.DMA((3,)),
+            pltpu.SemaphoreType.DMA((2,)),
             pltpu.VMEM((own, width), bf),
             pltpu.SemaphoreType.DMA,
         ]
+        + far
         + far
         + [pltpu.VMEM((rows, width), bf)]
         + hop
         + [pltpu.VMEM((rows, width), bf)] * 2
         + [
-            pltpu.VMEM((own, width), f32),
             pltpu.VMEM((cols, width), f32),
             pltpu.VMEM((width, cols), f32),
             pltpu.VMEM((cols, width), f32),
             pltpu.VMEM(kv2.shape, f32),
-            pltpu.SemaphoreType.DMA((2,)),
+            pltpu.SemaphoreType.DMA((2, 2)),
         ]
         + ring_scratch(count, (width // count, width)),
         compiler_params=pltpu.CompilerParams(collective_id=1, has_side_effects=True, vmem_limit_bytes=60 * MIB),
         cost_estimate=pl.CostEstimate(flops=100 * 10**9, bytes_accessed=24 * MIB, transcendentals=4 * MIB),
         name="turn",
-    )(third, in_g, out_g, out_grad, lens, text_lens, x1, x2, h2, q2, c2, kv2, c1, gains, co_w, cq_w, so_w)
+    )(
+        third, ffn_part, in_g, out_g, out_grad, lens, text_lens,
+        x1, x2, h2, q2, c2, kv2, c1, gains, biases, co_w, cq_w, so_w,
+    )
 
 
 SMALL = 16
@@ -1074,11 +1131,10 @@
 
 
 def last_kernel(
-    ffn_part, g0, g1, all_units, lens, dqkv, dkv, dx1, x2, self_b, cross_b, ffn_b, stats, gains, biases, qkv_w, kv_w,
-    sum0, sum1, y, units_g, text_g, small_sum,
-    units, own_sem, mine4, theirs4, core4, fromx4, sem4,
-    part6, core6, fromx6, sem6, part7, core7, fromx7, sem7,
-    fetch_sem, block, near, far, small_sem, *ring_refs, count,
+    g0, g1, all_units, far_dqkv, far_dkv, far_dx1, far_qkv, far_kv, self_b, cross_b, ffn_b, stats, gains,
+    sum0, sum1, units_g, text_g, small_sum,
+    dqkv, dkv, dx1, qkv_w, kv_w, arrive_sem, units, own_sem, part6, core6, fromx6, sem6, part7, core7, fromx7, sem7,
+    block, near, far, small_sem, *ring_refs, count,
 ):
     steps, chunk, width = fromx6.shape
     text_steps = fromx7.shape[0]
@@ -1093,12 +1149,16 @@
     fetch.start()
     greet(*ring.peers)
     ring.start()
-    four = FarHop(ffn_part, core4, fromx4, None, sem4, chunk)
+    arriving = moves(
+        (far_dqkv, far_dkv, far_dx1, far_qkv, far_kv), (dqkv, dkv, dx1, qkv_w, kv_w), arrive_sem
+    )
+    for copy in arriving:
+        copy.start()
     six = Hop(part6, core6, fromx6, None, sem6, chunk)
     seven = Hop(part7, core7, fromx7, None, sem7, chunk)
-    four.fetch(mine4, theirs4, fetch_sem)
-    four.fetched()
     fetch.wait()
+    for copy in arriving:
+        copy.wait()
     block[...] = jnp.zeros_like(block)
     cols = self_b.shape[1]
     for row in range(2):
@@ -1106,7 +1166,6 @@
         block[0:1, (2 + row) * cols : (3 + row) * cols] = cross_b[row : row + 1, :]
         block[1 + row : 2 + row, :] = ffn_b[:, row * width : (row + 1) * width]
     block[SMALL - NORM_ROWS : SMALL - 2, :] = stats[:7, :]
-    valid_rows = left_here(lens, x2.shape[0], dqkv.shape[0])
     gain = gains[0:1, :]
 
     def project(step):
@@ -1114,7 +1173,6 @@
         total = dot_nt(grads[:, :cols], qkv_w[0]) + dot_nt(grads[:, cols : 2 * cols], qkv_w[1])
         six.put(part6, step, (total + dot_nt(grads[:, 2 * cols :], qkv_w[2])).astype(jnp.bfloat16))
         six.send_core(step)
-        four.send_core(step)
 
     def norm_one(step):
         rows = six.own_rows(step)
@@ -1139,11 +1197,6 @@
     def text_result(step):
         text_g[seven.own_rows(step), :] = seven.result(step)
 
-    def output(step):
-        rows = four.own_rows(step)
-        total = x2[rows, :] + four.result(step) + biases[2:3, :]
-        y[rows, :] = jnp.where(row_of(step, chunk, width) < valid_rows, total, 0.0).astype(jnp.bfloat16)
-
     ready = steps + 1
 
     def extra(tick):
@@ -1160,8 +1213,7 @@
         list(
             enumerate(
                 [
-                    project, six.send_cross, norm_one, four.send_cross, output,
-                    text_only(text_project), text_only(seven.send_cross), text_only(text_result),
+                    project, six.send_cross, norm_one, text_only(text_project), text_only(seven.send_cross), text_only(text_result),
                 ]
             )
         ),
@@ -1171,7 +1223,6 @@
     )
 
     def finish(step, carry):
-        four.finish(step, False)
         six.finish(step, False)
         text_only(lambda s: seven.finish(s, False))(step)
         return carry
@@ -1181,7 +1232,7 @@
     small.finish(small_sum)
 
 
-def last(count, ffn_part, g0, g1, units, lens, dqkv, dkv, dx1, x2, *rest):
+def last(count, g0, g1, units, dqkv, dkv, dx1, qkv_w, kv_w, *rest):
     rows = dqkv.shape[0]
     own, width = dx1.shape
     chunk = own // STEPS
@@ -1191,27 +1242,24 @@
     vmem = pl.BlockSpec(memory_space=pltpu.VMEM)
     hbm = pl.BlockSpec(memory_space=pl.ANY)
     hop = hop_scratch(own, chunk, width)
-    far = [pltpu.VMEM((own, width), bf)] * 2 + hop
     return pl.pallas_call(
         functools.partial(last_kernel, count=count),
-        in_specs=[hbm] * 4 + [pl.BlockSpec(memory_space=pltpu.SMEM)] + [vmem] * (4 + len(rest)),
-        out_specs=[hbm] * 2 + [vmem] * 4,
+        in_specs=[hbm] * 8 + [vmem] * len(rest),
+        out_specs=[hbm] * 2 + [vmem] * 3,
         out_shape=[
             pltpu.HBM(g0.shape, bf),
             pltpu.HBM(g1.shape, bf),
-            shape((own, width), bf),
             shape((own, width), f32),
             shape((text_own, width), f32),
             shape((SMALL, width), f32),
         ],
-        scratch_shapes=[pltpu.VMEM((own, width), bf), pltpu.SemaphoreType.DMA]
-        + far
+        scratch_shapes=[pltpu.VMEM(a.shape, a.dtype) for a in (dqkv, dkv, dx1, qkv_w, kv_w)]
+        + [pltpu.SemaphoreType.DMA((5,)), pltpu.VMEM((own, width), bf), pltpu.SemaphoreType.DMA]
         + [pltpu.VMEM((rows, width), bf)]
         + hop
         + [pltpu.VMEM((dkv.shape[0], width), bf)]
         + hop_scratch(text_own, chunk, width)
         + [
-            pltpu.SemaphoreType.DMA((2,)),
             pltpu.VMEM((SMALL, width), f32),
             pltpu.VMEM((NARROW, SMALL, width), f32),
             pltpu.VMEM((count, SMALL, width), f32),
@@ -1221,47 +1269,76 @@
         compiler_params=pltpu.CompilerParams(collective_id=2, has_side_effects=True, vmem_limit_bytes=58 * MIB),
         cost_estimate=pl.CostEstimate(flops=30 * 10**9, bytes_accessed=16 * MIB, transcendentals=0),
         name="last",
-    )(ffn_part, g0, g1, units, lens, dqkv, dkv, dx1, x2, *rest)
-
-
-def unpack_kernel(sum0, sum1, small, qkv_g, cq_g, co_g, so_g, kv_g, gain_g, shift_g, bias_g, self_b, cross_b, ffn_b):
+    )(g0, g1, units, dqkv, dkv, dx1, qkv_w, kv_w, *rest)
+
+
+def unpack_kernel(
+    sum0, sum1, small, y_in, units_in, text_in,
+    qkv_g, cq_g, co_g, so_g, kv_g, gain_g, shift_g, bias_g, self_b, cross_b, ffn_b, y, units_g, text_g,
+):
     cols = cq_g.shape[1]
+    step = pl.program_id(0)
+    y[...] = y_in[...]
+    units_g[...] = units_in[...]
+    text_g[...] = text_in[...]
     for part in range(3):
         qkv_g[part] = sum0[:, part * cols : (part + 1) * cols].astype(jnp.float32)
     cq_g[...] = sum0[:, 3 * cols :].astype(jnp.float32)
-    co_g[...] = sum1[:cols, :].astype(jnp.float32)
-    so_g[...] = sum1[cols : 2 * cols, :].astype(jnp.float32)
+    for when, ref in enumerate((co_g, so_g)):
+
+        @pl.when(step == when)
+        def _():
+            ref[...] = sum1[...].astype(jnp.float32)
+
     half = kv_g.shape[0] // 2
-    for side in range(2):
-        for part in range(2):
-            first = (2 * side + part) * cols
-            kv_g[side * half : (side + 1) * half, part, :] = sum1[2 * cols :, first : first + cols].astype(jnp.float32)
-    norms = small[SMALL - NORM_ROWS :, :]
-    for ref, order in ((gain_g, (7, 4, 0)), (shift_g, (8, 5, 1)), (bias_g, (6, 3, 2))):
-        for row, source in enumerate(order):
-            ref[row : row + 1, :] = norms[source : source + 1, :]
-    width = small.shape[1]
-    for row in range(2):
-        self_b[row : row + 1, :] = small[0:1, row * cols : (row + 1) * cols]
-        cross_b[row : row + 1, :] = small[0:1, (2 + row) * cols : (3 + row) * cols]
-        ffn_b[:, row * width : (row + 1) * width] = small[1 + row : 2 + row, :]
-
-
-def unpack(sum0, sum1, small, cols, hidden):
+    for when in range(half // cols):
+
+        @pl.when(step == 2 + when)
+        def _():
+            for side in range(2):
+                rows = slice(side * half + when * cols, side * half + (when + 1) * cols)
+                for part in range(2):
+                    first = (2 * side + part) * cols
+                    kv_g[rows, part, :] = sum1[:, first : first + cols].astype(jnp.float32)
+
+    @pl.when(step == 0)
+    def _():
+        norms = small[SMALL - NORM_ROWS :, :]
+        for ref, order in ((gain_g, (7, 4, 0)), (shift_g, (8, 5, 1)), (bias_g, (6, 3, 2))):
+            for row, source in enumerate(order):
+                ref[row : row + 1, :] = norms[source : source + 1, :]
+        width = small.shape[1]
+        for row in range(2):
+            self_b[row : row + 1, :] = small[0:1, row * cols : (row + 1) * cols]
+            cross_b[row : row + 1, :] = small[0:1, (2 + row) * cols : (3 + row) * cols]
+            ffn_b[:, row * width : (row + 1) * width] = small[1 + row : 2 + row, :]
+
+
+def unpack(sum0, sum1, small, cols, hidden, *row_outs):
     width = sum0.shape[0]
-    shape = lambda *dims: jax.ShapeDtypeStruct(dims, jnp.float32)
-    vmem = pl.BlockSpec(memory_space=pltpu.VMEM)
+    steps = width // cols
+    f32 = jnp.float32
+    block = lambda a: pl.BlockSpec((a.shape[0] // steps,) + a.shape[1:], lambda i: (i, 0))
+    whole = lambda a: pl.BlockSpec(a.shape, lambda i: (0,) * len(a.shape))
+    fixed = [
+        jax.ShapeDtypeStruct(dims, f32)
+        for dims in (
+            (cols, width), (cols, width), (width, 2, cols),
+            (3, width), (3, width), (3, width), (2, cols), (2, cols), (1, hidden),
+        )
+    ]
+    moving = [jax.ShapeDtypeStruct((3, width, cols), f32), jax.ShapeDtypeStruct((width, cols), f32)]
     return pl.pallas_call(
         unpack_kernel,
-        in_specs=[vmem] * 3,
-        out_specs=[vmem] * 11,
-        out_shape=[
-            shape(3, width, cols), shape(width, cols), shape(cols, width), shape(cols, width), shape(width, 2, cols),
-            shape(3, width), shape(3, width), shape(3, width), shape(2, cols), shape(2, cols), shape(1, hidden),
-        ],
-        compiler_params=pltpu.CompilerParams(vmem_limit_bytes=40 * MIB),
+        grid=(steps,),
+        in_specs=[block(sum0), block(sum1), whole(small)] + [block(a) for a in row_outs],
+        out_specs=[pl.BlockSpec((3, cols, cols), lambda i: (0, i, 0)), block(moving[1])]
+        + [whole(a) for a in fixed]
+        + [block(a) for a in row_outs],
+        out_shape=moving + fixed + [jax.ShapeDtypeStruct(a.shape, a.dtype) for a in row_outs],
+        compiler_params=pltpu.CompilerParams(vmem_limit_bytes=60 * MIB),
         name="unpack",
-    )(sum0, sum1, small)
+    )(sum0, sum1, small, *row_outs)
 
 
 def local(
@@ -1322,9 +1399,10 @@
         cross_bias,
         ffn_in_bias,
     )
-    in_sum, out_sum, grads_one, grads_two, resid_one_grad, context_grad, text_kv_grad, cross_bias_sum, stats = turn(
+    in_sum, out_sum, grads_one, grads_two, output, resid_one_grad, context_grad, text_kv_grad, cross_bias_sum, stats = turn(
         count,
         third_part,
+        ffn_part,
         ffn_in_grad,
         ffn_out_grad,
         out_grad,
@@ -1338,6 +1416,7 @@
         text_kv,
         self_context,
         norm_gain,
+        out_bias,
         cross_out,
         cross_q,
         self_out,
@@ -1358,25 +1437,21 @@
         grads_one,
         grads_two,
     )
-    summed_one, summed_two, output, units_grad, text_grad, small = last(
+    summed_one, summed_two, units_grad, text_grad, small = last(
         count,
-        ffn_part,
         grads_one,
         grads_two,
         units,
-        lengths,
         qkv_grad,
         text_kv_grad,
         resid_one_grad,
-        resid_two,
+        qkv_weights,
+        kv_weights,
         self_bias_sum,
         cross_bias_sum,
         ffn_bias_sum,
         stats,
         norm_gain,
-        out_bias,
-        qkv_weights,
-        kv_weights,
     )
     (
         self_qkv_grad,
@@ -1390,7 +1465,12 @@
         self_bias_grad,
         cross_bias_grad,
         ffn_in_bias_grad,
-    ) = unpack(summed_one, summed_two, small, queries.shape[1], ffn_in_bias.shape[0])
+        output,
+        units_grad,
+        text_grad,
+    ) = unpack(
+        summed_one, summed_two, small, queries.shape[1], ffn_in_bias.shape[0], output, units_grad, text_grad
+    )
     self_qkv_grad = jnp.transpose(self_qkv_grad, (1, 0, 2))
     ffn_in_bias_grad = ffn_in_bias_grad.reshape(-1)
     return (

time: 504 us -> 487 us (0.966); the launches traced: 501 us -> 478 us
  local copies, waits for them, and re-layouts: 16.1 us -> 2.42 us
  Pallas kernels: 483 us -> 473 us
    pallas_call x1, Pallas kernels: 119 us -> 98 us  [last(): pl.pallas_call(functools.partial(last_kernel, count=count), in_specs=[hbm...]
    unnamed x36 -> x1, local copies, waits for them, and re-layouts: 16.1 us -> 2.42 us
    pallas_call x1, Pallas kernels: 29.6 us -> 39.4 us  [back(): pl.pallas_call(back_kernel, grid_spec=pltpu.PrefetchScalarGridSpec(num_sc...]
    pallas_call x1, Pallas kernels: 184 us -> 174 us  [turn(): pl.pallas_call(functools.partial(turn_kernel, count=count), in_specs=[hbm...]
    pallas_call x1, Pallas kernels: 9.28 us -> 18.2 us  [front(): pl.pallas_call(front_kernel, grid_spec=pltpu.PrefetchScalarGridSpec(num_s...]
where the time goes in v8:
time: 487 us; the launch traced here: 478 us
  Pallas kernels  473 us (97%)
    pallas_call x1, Pallas kernels, turn(): pl.pallas_call(functools.partial(turn_kernel, count=count), in_specs=[hbm...  174 us
    pallas_call x1, Pallas kernels, middle(): pl.pallas_call(middle_kernel, in_specs=[hbm] * 7 + [pl.BlockSpec(memory_s...  134 us
    pallas_call x1, Pallas kernels, last(): pl.pallas_call(functools.partial(last_kernel, count=count), in_specs=[hbm...  98 us
    pallas_call x1, Pallas kernels, back(): pl.pallas_call(back_kernel, grid_spec=pltpu.PrefetchScalarGridSpec(num_sc...  39.4 us
    pallas_call x1, Pallas kernels, front(): pl.pallas_call(front_kernel, grid_spec=pltpu.PrefetchScalarGridSpec(num_s...  18.2 us

profile of v8, /device:TPU:0, one launch (start us, length us, event | category | flops | bytes accessed | tf_op | source)
XLA Modules:
  0.0 477.9 jit_solution(5664132457963399015)
XLA Ops:
  1.3 1.2 compare_select_fusion.lens
  2.5 2.4 copy.37
  4.9 18.2 %front.1 = (bf16[2048,1024]{1,0:T(8,128)(2,1)}, bf16[2048,256]{1,0:T(8,128)(2,1)}, bf16[2048,256]{1,0:T(8,128)(2,1)}, bf16[2048,256]{1,0:T(8,128)(2,1)}, bf16[51...) custom-call(s32[2]{0:T(128)} %compare_select_fusion.lens, bf16[2048,1024]{1,0:T(8,128)(2,1)} %all_units.3, ...), custom_call_target="tpu_custom_call" | custom-call | flops 20000000000 | bytes 16777216 | tf_op jit(solution)/shard_map/front/pallas_call | solution.py:130
  23.1 134.0 %middle.1 = (bf16[2048,1024]{1,0:T(8,128)(2,1)}, bf16[2048,1024]{1,0:T(8,128)(2,1)}, bf16[1024,2048]{1,0:T(8,128)(2,1)}, bf16[2048,1024]{1,0:T(8,128)(2,1)}, bf1...) custom-call(bf16[2048,1024]{1,0:T(8,128)(2,1)} %all_units.3, ...), custom_call_target="tpu_custom_call" | custom-call | flops 99999997952 | bytes 50331648 | tf_op jit(solution)/shard_map/middle/pallas_call | solution.py:736
  157.1 174.3 %turn.1 = (bf16[1024,2048]{1,0:T(8,128)(2,1)}, bf16[2048,1024]{1,0:T(8,128)(2,1)}, bf16[1024,1024]{1,0:T(8,128)(2,1)}, bf16[1024,1024]{1,0:T(8,128)(2,1)}, bf16[...) custom-call(bf16[2048,1024]{1,0:T(8,128)(2,1)} %get-tuple-element.73, ...), custom_call_target="tpu_custom_call" | custom-call | flops 99999997952 | bytes 25165824 | tf_op jit(solution)/shard_map/turn/pallas_call | solution.py:1017
  331.4 39.4 %back.1 = (bf16[2048,768]{1,0:T(8,128)(2,1)}, bf16[1024,1024]{1,0:T(8,128)(2,1)}, bf16[1024,1024]{1,0:T(8,128)(2,1)}, f32[2,256]{1,0:T(2,128)}, f32[1024,2048]{1,0:T(8,128)}, /*index=5*/f32[2048,1024]{1,0:T(8,128)}) custom-call(s32[2]{0:T(128)} %compare_select_fusion.lens, ...), custom_call_target="tpu_custom_call", output_to_operand_aliasing={{1}: (12, {}), {2}: (13, {})} | custom-call | flops 30000001024 | bytes 41943040 | tf_op jit(solution)/shard_map/back/pallas_call | solution.py:237
  370.8 98.0 %last.1 = (bf16[1024,1024]{1,0:T(8,128)(2,1)}, bf16[1024,1024]{1,0:T(8,128)(2,1)}, f32[512,1024]{1,0:T(8,128)}, f32[128,1024]{1,0:T(8,128)}, f32[16,1024]{1,0:T(8,128)}) custom-call(bf16[1024,1024]{1,0:T(8,128)(2,1)} %get-tuple-element.90.g0, bf16[1024,1024]{1,0:T(8,128)(2,1)} %get-tuple-element.91.g1, bf16[2048,1024]{1,0:T(8,128)(2,1)} %all_units.3, ...), custom_call_target="tpu_custom_call" | custom-call | flops 30000001024 | bytes 16777216 | tf_op jit(solution)/shard_map/last/pallas_call | solution.py:1245
  468.9 8.7 %unpack.1 = (f32[3,1024,256]{2,1,0:T(8,128)}, f32[1024,256]{1,0:T(8,128)}, f32[256,1024]{1,0:T(8,128)}, f32[256,1024]{1,0:T(8,128)}, f32[1024,2,256]{2,1,0:T(2,1...) custom-call(bf16[1024,1024]{1,0:T(8,128)(2,1)} %get-tuple-element.98, ...), custom_call_target="tpu_custom_call" | custom-call | tf_op jit(solution)/shard_map/unpack/pallas_call | solution.py:1331

commit v9 on v8

--- a/solution.py
+++ b/solution.py
@@ -525,8 +525,8 @@
                     ring.serve(tick, unit)
                 else:
                     lax.fori_loop(0, per_tick, lambda i, c: (ring.serve(tick * per_tick + i, unit), c)[1], 0)
-        if extra is not None:
-            extra(tick)
+            if extra is not None and number in (len(work) // 2, len(work) - 1):
+                extra(2 * tick + (number == len(work) - 1))
         return carry
 
     lax.fori_loop(0, ticks, body, 0)
@@ -556,17 +556,16 @@
         pltpu.make_async_copy(far_in, w_in, weight_sem.at[0]),
         pltpu.make_async_copy(far_out, w_out, weight_sem.at[1]),
     ]
-    for fetch in fetches:
-        fetch.start()
+    fetches[0].start()
     greet()
     one = Hop(part, core1, fromx1, h2, sem1, chunk)
     two = Hop(part, core2, fromx2, h3, sem2, chunk)
     scale = jnp.bfloat16(HEAD_DIM**-0.5)
-    in_acc[...] = jnp.zeros_like(in_acc)
-    out_acc[...] = jnp.zeros_like(out_acc)
     in_bias_g[...] = jnp.zeros_like(in_bias_g)
     for fetch in near:
         fetch.wait()
+
+    leaving = moves((h2, q2, c2, x1, x2), (far_h2, far_q2, far_c2, far_x1, far_x2), leave_sem)
 
     def grad_copies(step):
         slot = step % 2
@@ -593,6 +592,12 @@
     def project(step):
         one.put(part, step, dot_nn(one.take(c1, step), so_w[...]).astype(jnp.bfloat16))
         one.send_core(step)
+        for when, ref in ((1, in_acc), (2, out_acc)):
+
+            @pl.when(step == when)
+            def _():
+                fetches[when].start()
+                ref[...] = jnp.zeros_like(ref)
 
     def norm_one(step):
         @pl.when(step == 0)
@@ -649,6 +654,11 @@
             fetches[1].wait()
             fetches[2].wait()
 
+        @pl.when(step == steps - 3)
+        def _():
+            for copy in leaving:
+                copy.start()
+
         two.gathered(step)
         for copy in grad_copies(step):
             copy.wait()
@@ -703,9 +713,6 @@
         return carry
 
     lax.fori_loop(0, steps, finish, 0)
-    leaving = moves((h2, q2, c2, x1, x2), (far_h2, far_q2, far_c2, far_x1, far_x2), leave_sem)
-    for copy in leaving:
-        copy.start()
     part[...] = out_acc[...].astype(jnp.bfloat16)
     results = [pltpu.make_async_copy(part, out_g, weight_sem.at[0])]
     results[0].start()
@@ -954,12 +961,13 @@
     half = steps // 2
     late = steps + 2
 
-    def side(tick):
+    def side(half_tick):
+        tick = half_tick // 2
         for begin, first in ((0, 0), (late, half)):
             for ahead, work in ((1, output), (0, four.send_cross)):
                 step = tick - begin - ahead
 
-                @pl.when((step >= 0) & (step < half))
+                @pl.when((step >= 0) & (step < half) & (half_tick % 2 == 1))
                 def _():
                     work(first + step)
 
@@ -1197,12 +1205,12 @@
     def text_result(step):
         text_g[seven.own_rows(step), :] = seven.result(step)
 
-    ready = steps + 1
-
-    def extra(tick):
+    ready = 2 * (steps + 1)
+
+    def extra(half_tick):
         for when, work in enumerate((small.begin, small.forward, small.launch)):
-            pl.when(tick == ready + when)(work)
-        step = tick - ready - 3
+            pl.when(half_tick == ready + when)(work)
+        step = half_tick - ready - 3
 
         @pl.when((step >= 0) & (step < count // 2))
         def _():
@@ -1219,7 +1227,7 @@
         ),
         ring,
         extra,
-        ready + 3 + count // 2,
+        max((ready + 4 + count // 2) // 2, 2 * (count - 1)),
     )
 
     def finish(step, carry):

time: 487 us -> 481 us (0.988)
    pallas_call x1, Pallas kernels: 39.4 us -> 24.4 us  [back(): pl.pallas_call(back_kernel, grid_spec=pltpu.PrefetchScalarGridSpec(num_sc...]
    pallas_call x1, Pallas kernels: 98 us -> 109 us  [last(): pl.pallas_call(functools.partial(last_kernel, count=count), in_specs=[hbm...]
    pallas_call x1, Pallas kernels: 174 us -> 185 us  [turn(): pl.pallas_call(functools.partial(turn_kernel, count=count), in_specs=[hbm...]
where the time goes in v9:
time: 481 us; the launch traced here: 476 us
  Pallas kernels  471 us (98%)
    pallas_call x1, Pallas kernels, turn(): pl.pallas_call(functools.partial(turn_kernel, count=count), in_specs=[hbm...  185 us
    pallas_call x1, Pallas kernels, middle(): pl.pallas_call(middle_kernel, in_specs=[hbm] * 7 + [pl.BlockSpec(memory_s...  130 us
    pallas_call x1, Pallas kernels, last(): pl.pallas_call(functools.partial(last_kernel, count=count), in_specs=[hbm...  109 us
    pallas_call x1, Pallas kernels, back(): pl.pallas_call(back_kernel, grid_spec=pltpu.PrefetchScalarGridSpec(num_sc...  24.4 us
    pallas_call x1, Pallas kernels, front(): pl.pallas_call(front_kernel, grid_spec=pltpu.PrefetchScalarGridSpec(num_s...  13.6 us

profile of v9, /device:TPU:0, one launch (start us, length us, event | category | flops | bytes accessed | tf_op | source)
XLA Modules:
  0.0 476.2 jit_solution(5118175020472577946)
XLA Ops:
  1.3 1.2 compare_select_fusion.lens
  2.5 2.4 copy.37
  4.9 13.6 %front.1 = (bf16[2048,1024]{1,0:T(8,128)(2,1)}, bf16[2048,256]{1,0:T(8,128)(2,1)}, bf16[2048,256]{1,0:T(8,128)(2,1)}, bf16[2048,256]{1,0:T(8,128)(2,1)}, bf16[51...) custom-call(s32[2]{0:T(128)} %compare_select_fusion.lens, bf16[2048,1024]{1,0:T(8,128)(2,1)} %all_units.3, ...), custom_call_target="tpu_custom_call" | custom-call | flops 20000000000 | bytes 16777216 | tf_op jit(solution)/shard_map/front/pallas_call | solution.py:130
  18.5 130.0 %middle.1 = (bf16[2048,1024]{1,0:T(8,128)(2,1)}, bf16[2048,1024]{1,0:T(8,128)(2,1)}, bf16[1024,2048]{1,0:T(8,128)(2,1)}, bf16[2048,1024]{1,0:T(8,128)(2,1)}, bf1...) custom-call(bf16[2048,1024]{1,0:T(8,128)(2,1)} %all_units.3, ...), custom_call_target="tpu_custom_call" | custom-call | flops 99999997952 | bytes 50331648 | tf_op jit(solution)/shard_map/middle/pallas_call | solution.py:743
  148.5 185.2 %turn.1 = (bf16[1024,2048]{1,0:T(8,128)(2,1)}, bf16[2048,1024]{1,0:T(8,128)(2,1)}, bf16[1024,1024]{1,0:T(8,128)(2,1)}, bf16[1024,1024]{1,0:T(8,128)(2,1)}, bf16[...) custom-call(bf16[2048,1024]{1,0:T(8,128)(2,1)} %get-tuple-element.73, ...), custom_call_target="tpu_custom_call" | custom-call | flops 99999997952 | bytes 25165824 | tf_op jit(solution)/shard_map/turn/pallas_call | solution.py:1025
  333.6 24.4 %back.1 = (bf16[2048,768]{1,0:T(8,128)(2,1)}, bf16[1024,1024]{1,0:T(8,128)(2,1)}, bf16[1024,1024]{1,0:T(8,128)(2,1)}, f32[2,256]{1,0:T(2,128)}, f32[1024,2048]{1,0:T(8,128)}, /*index=5*/f32[2048,1024]{1,0:T(8,128)}) custom-call(s32[2]{0:T(128)} %compare_select_fusion.lens, ...), custom_call_target="tpu_custom_call", output_to_operand_aliasing={{1}: (12, {}), {2}: (13, {})} | custom-call | flops 30000001024 | bytes 41943040 | tf_op jit(solution)/shard_map/back/pallas_call | solution.py:237
  358.1 109.1 %last.1 = (bf16[1024,1024]{1,0:T(8,128)(2,1)}, bf16[1024,1024]{1,0:T(8,128)(2,1)}, f32[512,1024]{1,0:T(8,128)}, f32[128,1024]{1,0:T(8,128)}, f32[16,1024]{1,0:T(8,128)}) custom-call(bf16[1024,1024]{1,0:T(8,128)(2,1)} %get-tuple-element.90.g0, bf16[1024,1024]{1,0:T(8,128)(2,1)} %get-tuple-element.91.g1, bf16[2048,1024]{1,0:T(8,128)(2,1)} %all_units.3, ...), custom_call_target="tpu_custom_call" | custom-call | flops 30000001024 | bytes 16777216 | tf_op jit(solution)/shard_map/last/pallas_call | solution.py:1253
  467.2 8.7 %unpack.1 = (f32[3,1024,256]{2,1,0:T(8,128)}, f32[1024,256]{1,0:T(8,128)}, f32[256,1024]{1,0:T(8,128)}, f32[256,1024]{1,0:T(8,128)}, f32[1024,2,256]{2,1,0:T(2,1...) custom-call(bf16[1024,1024]{1,0:T(8,128)(2,1)} %get-tuple-element.98, ...), custom_call_target="tpu_custom_call" | custom-call | tf_op jit(solution)/shard_map/unpack/pallas_call | solution.py:1339

commit v10 on v9

--- a/solution.py
+++ b/solution.py
@@ -67,8 +67,8 @@
 def mask_diagonal(scores, axis):
     count = scores.shape[axis]
     parts = [scores] if count == BLOCK else jnp.split(scores, [count - BLOCK], axis=axis)
-    keys = lax.broadcasted_iota(jnp.int32, (BLOCK, BLOCK), axis)
-    queries = lax.broadcasted_iota(jnp.int32, (BLOCK, BLOCK), 1 - axis)
+    keys = lax.broadcasted_iota(jnp.int32, parts[-1].shape, axis)
+    queries = lax.broadcasted_iota(jnp.int32, keys.shape, 1 - axis) & (BLOCK - 1)
     parts[-1] = jnp.where(keys <= queries, parts[-1], MASKED_SCORE)
     return jnp.concatenate(parts, axis=axis)
 
@@ -157,8 +157,11 @@
 ):
     in_f32[...] = in_ref[...].astype(jnp.float32)
     out_f32[...] = out_ref[...].astype(jnp.float32)
-
-    @pl.when(pl.program_id(0) == 0)
+    slot, turn_now = pl.program_id(0), pl.program_id(1)
+    slot_rows, width = q_ref.shape
+    heads = range(width // HEAD_DIM)
+
+    @pl.when((slot == 0) & (turn_now == 0))
     def _():
         w_acc[...] = jnp.zeros_like(w_acc)
         b_ref[...] = jnp.zeros_like(b_ref)
@@ -167,61 +170,59 @@
         g1_ref[:, :both] = kv_grad[:half]
         g1_ref[:, both:] = kv_grad[half:]
 
-    length = lens[pl.program_id(0)]
-    slot_rows, width = q_ref.shape
-    dk_acc[...] = jnp.zeros_like(dk_acc)
-    dv_acc[...] = jnp.zeros_like(dv_acc)
+    @pl.when(turn_now == 0)
+    def _():
+        dk_acc[...] = jnp.zeros_like(dk_acc)
+        dv_acc[...] = jnp.zeros_like(dv_acc)
+        o_ref[:, :width] = jnp.zeros((slot_rows, width), jnp.bfloat16)
+
+    def stack(values):
+        return jnp.concatenate([pick_head(values, head) for head in heads], axis=0)
+
+    def side_by_side(values):
+        return jnp.concatenate([values[head : head + 1, :] for head in heads], axis=1)
+
     for i in range(slot_rows // BLOCK):
         rows = pl.ds(i * BLOCK, BLOCK)
 
-        @pl.when(i * BLOCK < length)
+        @pl.when((turn_now == i) & (i * BLOCK < lens[slot]))
         def _():
             count = (i + 1) * BLOCK
             keys, values = k_ref[:count, :], v_ref[:count, :]
-            scaled = q_ref[rows, :] * jnp.bfloat16(HEAD_DIM**-0.5)
             grads = dc_ref[rows, :]
-            total = jnp.zeros((BLOCK, width), jnp.float32)
-            heads = lax.broadcasted_iota(jnp.int32, (8, width), 0)
+            q_heads, g_heads = stack(q_ref[rows, :] * jnp.bfloat16(HEAD_DIM**-0.5)), stack(grads)
+            owners = lax.broadcasted_iota(jnp.int32, (8, width), 0)
             lanes = lax.broadcasted_iota(jnp.int32, (8, width), 1)
             inner = lax.dot_general(
-                jnp.where((lanes >= heads * HEAD_DIM) & (lanes < (heads + 1) * HEAD_DIM), 1.0, 0.0),
+                jnp.where((lanes >= owners * HEAD_DIM) & (lanes < (owners + 1) * HEAD_DIM), 1.0, 0.0),
                 grads.astype(jnp.float32) * c_ref[rows, :].astype(jnp.float32),
                 (((1,), (1,)), ((), ())),
                 precision=EXACT,
                 preferred_element_type=jnp.float32,
             )
-            for head in range(width // HEAD_DIM):
-                q_head, g_head = pick_head(scaled, head), pick_head(grads, head)
-                scores = mask_diagonal(dot_nt(keys, q_head), 0)
-                weights = jnp.exp(scores - log_ref[head : head + 1, rows])
-                dv_acc[:count, :] += dot_nn(weights.astype(jnp.bfloat16), g_head)
-                weight_grad = dot_nt(values, g_head)
-                score_grad = (weights * (weight_grad - inner[head : head + 1, :])).astype(jnp.bfloat16)
-                dk_acc[:count, :] += dot_nn(score_grad, q_head)
-                total += dot_tn(score_grad, pick_head(keys, head))
-            o_ref[rows, :width] = (total * HEAD_DIM**-0.5).astype(jnp.bfloat16)
-
-        @pl.when(i * BLOCK >= length)
+            weights = jnp.exp(mask_diagonal(dot_nt(keys, q_heads), 0) - side_by_side(log_ref[:, rows]))
+            dv_acc[:count, :] += dot_nn(weights.astype(jnp.bfloat16), g_heads)
+            score_grad = (weights * (dot_nt(values, g_heads) - side_by_side(inner))).astype(jnp.bfloat16)
+            dk_acc[:count, :] += dot_nn(score_grad, q_heads)
+            total = jnp.zeros((BLOCK, width), jnp.float32)
+            for head in heads:
+                total += dot_tn(score_grad[:, head * BLOCK : (head + 1) * BLOCK], pick_head(keys, head))
+            q_grad = (total * HEAD_DIM**-0.5).astype(jnp.bfloat16)
+            o_ref[rows, :width] = q_grad
+            b_ref[0:1, :] += column_sum(q_grad.astype(jnp.float32))
+
+    @pl.when(turn_now == pl.num_programs(1) - 1)
+    def _():
+        v_grad = dv_acc[...].astype(jnp.bfloat16)
+        o_ref[:, width : 2 * width] = dk_acc[...].astype(jnp.bfloat16)
+        o_ref[:, 2 * width :] = v_grad
+        b_ref[1:2, :] += column_sum(v_grad.astype(jnp.float32))
+        for first in range(0, h_ref.shape[1], BLOCK):
+            w_acc[first : first + BLOCK, :] += dot_tn(h_ref[:, first : first + BLOCK], o_ref[...])
+
+        @pl.when(slot == pl.num_programs(0) - 1)
         def _():
-            o_ref[rows, :width] = jnp.zeros((BLOCK, width), jnp.bfloat16)
-
-    o_ref[:, width : 2 * width] = dk_acc[...].astype(jnp.bfloat16)
-    o_ref[:, 2 * width :] = dv_acc[...].astype(jnp.bfloat16)
-    for i in range(slot_rows // BLOCK):
-        rows = pl.ds(i * BLOCK, BLOCK)
-
-        @pl.when(i * BLOCK < length)
-        def _():
-            sums = column_sum(o_ref[rows, :].astype(jnp.float32))
-            b_ref[0:1, :] += sums[:, :width]
-            b_ref[1:2, :] += sums[:, 2 * width :]
-
-    for first in range(0, h_ref.shape[1], BLOCK):
-        w_acc[first : first + BLOCK, :] += dot_tn(h_ref[:, first : first + BLOCK], o_ref[...])
-
-    @pl.when(pl.program_id(0) == pl.num_programs(0) - 1)
-    def _():
-        g0_ref[...] = w_acc[...].astype(jnp.bfloat16)
+            g0_ref[...] = w_acc[...].astype(jnp.bfloat16)
 
 
 def back(lengths, queries, keys, values, grads, context, logs, rows_in, text, dkv, in_sum, out_sum, g0, g1):
@@ -230,25 +231,27 @@
     slots = lengths.shape[0]
     bf, f32 = jnp.bfloat16, jnp.float32
     shape = jax.ShapeDtypeStruct
-    slot = lambda a: pl.BlockSpec((a.shape[0] // slots, a.shape[1]), lambda s, *_: (s, 0))
-    whole = lambda a: pl.BlockSpec(a.shape, lambda s, *_: (0, 0))
+    slot = lambda a: pl.BlockSpec((a.shape[0] // slots, a.shape[1]), lambda s, i, *_: (s, 0))
+    blocks = rows // slots // BLOCK
+    piece = lambda a: pl.BlockSpec((a.shape[0] // (slots * blocks), a.shape[1]), lambda s, i, *_: (s * blocks + i, 0))
+    whole = lambda a: pl.BlockSpec(a.shape, lambda s, i, *_: (0, 0))
     hbm = pl.BlockSpec(memory_space=pl.ANY)
     half = text.shape[1] // 2
     return pl.pallas_call(
         back_kernel,
         grid_spec=pltpu.PrefetchScalarGridSpec(
             num_scalar_prefetch=1,
-            grid=(slots,),
+            grid=(slots, blocks),
             in_specs=[slot(queries)] * 5
-            + [pl.BlockSpec((8, rows // slots), lambda s, *_: (0, s))]
-            + [slot(rows_in), whole(text), whole(dkv), slot(in_sum), slot(out_sum), hbm, hbm],
+            + [pl.BlockSpec((8, rows // slots), lambda s, i, *_: (0, s))]
+            + [slot(rows_in), whole(text), whole(dkv), piece(in_sum), piece(out_sum), hbm, hbm],
             out_specs=[
-                pl.BlockSpec((rows // slots, 3 * cols), lambda s, *_: (s, 0)),
-                pl.BlockSpec((width, 3 * cols), lambda s, *_: (0, 0)),
-                pl.BlockSpec((half, width), lambda s, *_: (1, 0)),
-                pl.BlockSpec((2, cols), lambda s, *_: (0, 0)),
-                slot(in_sum),
-                slot(out_sum),
+                pl.BlockSpec((rows // slots, 3 * cols), lambda s, i, *_: (s, 0)),
+                pl.BlockSpec((width, 3 * cols), lambda s, i, *_: (0, 0)),
+                pl.BlockSpec((half, width), lambda s, i, *_: (1, 0)),
+                pl.BlockSpec((2, cols), lambda s, i, *_: (0, 0)),
+                piece(in_sum),
+                piece(out_sum),
             ],
             scratch_shapes=[pltpu.VMEM((rows // slots, cols), f32)] * 2 + [pltpu.VMEM((width, 3 * cols), f32)],
         ),

time: 481 us -> 474 us (0.985)
  Pallas kernels: 471 us -> 462 us
    pallas_call x1, Pallas kernels: 109 us -> 102 us  [last(): pl.pallas_call(functools.partial(last_kernel, count=count), in_specs=[hbm...]
where the time goes in v10:
time: 474 us; the launch traced here: 467 us
  Pallas kernels  462 us (97%)
    pallas_call x1, Pallas kernels, turn(): pl.pallas_call(functools.partial(turn_kernel, count=count), in_specs=[hbm...  188 us
    pallas_call x1, Pallas kernels, middle(): pl.pallas_call(middle_kernel, in_specs=[hbm] * 7 + [pl.BlockSpec(memory_s...  130 us
    pallas_call x1, Pallas kernels, last(): pl.pallas_call(functools.partial(last_kernel, count=count), in_specs=[hbm...  102 us
    pallas_call x1, Pallas kernels, back(): pl.pallas_call(back_kernel, grid_spec=pltpu.PrefetchScalarGridSpec(num_sc...  22.1 us
    pallas_call x1, Pallas kernels, front(): pl.pallas_call(front_kernel, grid_spec=pltpu.PrefetchScalarGridSpec(num_s...  10.8 us

profile of v10, /device:TPU:0, one launch (start us, length us, event | category | flops | bytes accessed | tf_op | source)
XLA Modules:
  0.0 467.0 jit_solution(6157839613154736192)
XLA Ops:
  1.3 1.2 compare_select_fusion.lens
  2.5 2.4 copy.37
  4.9 10.8 %front.1 = (bf16[2048,1024]{1,0:T(8,128)(2,1)}, bf16[2048,256]{1,0:T(8,128)(2,1)}, bf16[2048,256]{1,0:T(8,128)(2,1)}, bf16[2048,256]{1,0:T(8,128)(2,1)}, bf16[51...) custom-call(s32[2]{0:T(128)} %compare_select_fusion.lens, bf16[2048,1024]{1,0:T(8,128)(2,1)} %all_units.3, ...), custom_call_target="tpu_custom_call" | custom-call | flops 20000000000 | bytes 16777216 | tf_op jit(solution)/shard_map/front/pallas_call | solution.py:130
  15.7 130.0 %middle.1 = (bf16[2048,1024]{1,0:T(8,128)(2,1)}, bf16[2048,1024]{1,0:T(8,128)(2,1)}, bf16[1024,2048]{1,0:T(8,128)(2,1)}, bf16[2048,1024]{1,0:T(8,128)(2,1)}, bf1...) custom-call(bf16[2048,1024]{1,0:T(8,128)(2,1)} %all_units.3, ...), custom_call_target="tpu_custom_call" | custom-call | flops 99999997952 | bytes 50331648 | tf_op jit(solution)/shard_map/middle/pallas_call | solution.py:746
  145.7 188.0 %turn.1 = (bf16[1024,2048]{1,0:T(8,128)(2,1)}, bf16[2048,1024]{1,0:T(8,128)(2,1)}, bf16[1024,1024]{1,0:T(8,128)(2,1)}, bf16[1024,1024]{1,0:T(8,128)(2,1)}, bf16[...) custom-call(bf16[2048,1024]{1,0:T(8,128)(2,1)} %get-tuple-element.73, ...), custom_call_target="tpu_custom_call" | custom-call | flops 99999997952 | bytes 25165824 | tf_op jit(solution)/shard_map/turn/pallas_call | solution.py:1028
  333.7 22.1 %back.1 = (bf16[2048,768]{1,0:T(8,128)(2,1)}, bf16[1024,1024]{1,0:T(8,128)(2,1)}, bf16[1024,1024]{1,0:T(8,128)(2,1)}, f32[2,256]{1,0:T(2,128)}, f32[1024,2048]{1,0:T(8,128)}, /*index=5*/f32[2048,1024]{1,0:T(8,128)}) custom-call(s32[2]{0:T(128)} %compare_select_fusion.lens, ...), custom_call_target="tpu_custom_call", output_to_operand_aliasing={{1}: (12, {}), {2}: (13, {})} | custom-call | flops 30000001024 | bytes 41943040 | tf_op jit(solution)/shard_map/back/pallas_call | solution.py:240
  355.8 102.3 %last.1 = (bf16[1024,1024]{1,0:T(8,128)(2,1)}, bf16[1024,1024]{1,0:T(8,128)(2,1)}, f32[512,1024]{1,0:T(8,128)}, f32[128,1024]{1,0:T(8,128)}, f32[16,1024]{1,0:T(8,128)}) custom-call(bf16[1024,1024]{1,0:T(8,128)(2,1)} %get-tuple-element.90.g0, bf16[1024,1024]{1,0:T(8,128)(2,1)} %get-tuple-element.91.g1, bf16[2048,1024]{1,0:T(8,128)(2,1)} %all_units.3, ...), custom_call_target="tpu_custom_call" | custom-call | flops 30000001024 | bytes 16777216 | tf_op jit(solution)/shard_map/last/pallas_call | solution.py:1256
  458.0 8.7 %unpack.1 = (f32[3,1024,256]{2,1,0:T(8,128)}, f32[1024,256]{1,0:T(8,128)}, f32[256,1024]{1,0:T(8,128)}, f32[256,1024]{1,0:T(8,128)}, f32[1024,2,256]{2,1,0:T(2,1...) custom-call(bf16[1024,1024]{1,0:T(8,128)(2,1)} %get-tuple-element.98, ...), custom_call_target="tpu_custom_call" | custom-call | tf_op jit(solution)/shard_map/unpack/pallas_call | solution.py:1342

commit v11 on v10

--- a/solution.py
+++ b/solution.py
@@ -78,17 +78,22 @@
 ):
     length = lens[pl.program_id(0)]
     width = q_ref.shape[1]
-    both = dot_nn(t_ref[...], kvw_ref[...])
-    kv_ref[:, :width] = both[:, :width].astype(jnp.bfloat16)
-    kv_ref[:, width:] = (both[:, width:] + vb_ref[1:2, :]).astype(jnp.bfloat16)
-    for i in range(x_ref.shape[0] // BLOCK):
+    turn_now = pl.program_id(1)
+
+    @pl.when(turn_now == 0)
+    def _():
+        both = dot_nn(t_ref[...], kvw_ref[...])
+        kv_ref[:, :width] = both[:, :width].astype(jnp.bfloat16)
+        kv_ref[:, width:] = (both[:, width:] + vb_ref[1:2, :]).astype(jnp.bfloat16)
+
+    for i in range(q_ref.shape[0] // BLOCK):
         rows = pl.ds(i * BLOCK, BLOCK)
 
-        @pl.when(i * BLOCK < length)
+        @pl.when((turn_now == i) & (i * BLOCK < length))
         def _():
-            normed, _, _ = norm_forward(x_ref[rows, :].astype(jnp.float32), g_ref[0:1, :], s_ref[0:1, :])
+            normed, _, _ = norm_forward(x_ref[...].astype(jnp.float32), g_ref[0:1, :], s_ref[0:1, :])
             h1 = normed.astype(jnp.bfloat16)
-            h_ref[rows, :] = h1
+            h_ref[...] = h1
             queries = (dot_nn(h1, w_ref[0]) + b_ref[0:1, :]).astype(jnp.bfloat16)
             q_ref[rows, :] = queries
             k_ref[rows, :] = dot_nn(h1, w_ref[1]).astype(jnp.bfloat16)
@@ -109,9 +114,10 @@
             log_ref[:, rows] = logs.T[: log_ref.shape[0], :]
             c_ref[rows, :] = total.astype(jnp.bfloat16)
 
-        @pl.when(i * BLOCK >= length)
+        @pl.when((turn_now == i) & (i * BLOCK >= length))
         def _():
-            for ref in (h_ref, q_ref, k_ref, v_ref, c_ref):
+            h_ref[...] = jnp.zeros_like(h_ref)
+            for ref in (q_ref, k_ref, v_ref, c_ref):
                 ref[rows, :] = jnp.zeros((BLOCK, ref.shape[1]), ref.dtype)
             log_ref[:, rows] = jnp.zeros((log_ref.shape[0], BLOCK), jnp.float32)
 
@@ -121,20 +127,22 @@
     slots = lengths.shape[0]
     slot_rows = rows // slots
     cols = weights.shape[2]
-    whole = lambda a: pl.BlockSpec(a.shape, lambda s, *_: (0,) * a.ndim)
-    slot = lambda w: pl.BlockSpec((slot_rows, w), lambda s, *_: (s, 0))
-    texts = lambda w: pl.BlockSpec((text.shape[0] // slots, w), lambda s, *_: (s, 0))
-    logs = pl.BlockSpec((8, slot_rows), lambda s, *_: (0, s))
+    whole = lambda a: pl.BlockSpec(a.shape, lambda s, i, *_: (0,) * a.ndim)
+    slot = lambda w: pl.BlockSpec((slot_rows, w), lambda s, i, *_: (s, 0))
+    texts = lambda w: pl.BlockSpec((text.shape[0] // slots, w), lambda s, i, *_: (s, 0))
+    logs = pl.BlockSpec((8, slot_rows), lambda s, i, *_: (0, s))
+    blocks = slot_rows // BLOCK
+    piece = pl.BlockSpec((BLOCK, width), lambda s, i, *_: (s * blocks + i, 0))
     shape = lambda w: jax.ShapeDtypeStruct((rows, w), jnp.bfloat16)
     far = lambda w: pltpu.HBM((rows, w), jnp.bfloat16)
     return pl.pallas_call(
         front_kernel,
         grid_spec=pltpu.PrefetchScalarGridSpec(
             num_scalar_prefetch=1,
-            grid=(slots,),
-            in_specs=[slot(width), texts(width)]
+            grid=(slots, blocks),
+            in_specs=[piece, texts(width)]
             + [whole(a) for a in (gains, shifts, weights, bias, kv_w, cross_bias)],
-            out_specs=[slot(width), slot(cols), slot(cols), slot(cols), texts(2 * cols), slot(cols), logs],
+            out_specs=[piece, slot(cols), slot(cols), slot(cols), texts(2 * cols), slot(cols), logs],
         ),
         out_shape=[
             far(width),

time: 474 us -> 477 us (level); the launches traced: 467 us -> 476 us
  Pallas kernels: 462 us -> 471 us
    pallas_call x1, Pallas kernels: 102 us -> 109 us  [last(): pl.pallas_call(functools.partial(last_kernel, count=count), in_specs=[hbm...]
where the time goes in v11:
time: 477 us; the launch traced here: 476 us
  Pallas kernels  471 us (99%)
    pallas_call x1, Pallas kernels, turn(): pl.pallas_call(functools.partial(turn_kernel, count=count), in_specs=[hbm...  188 us
    pallas_call x1, Pallas kernels, middle(): pl.pallas_call(middle_kernel, in_specs=[hbm] * 7 + [pl.BlockSpec(memory_s...  130 us
    pallas_call x1, Pallas kernels, last(): pl.pallas_call(functools.partial(last_kernel, count=count), in_specs=[hbm...  109 us
    pallas_call x1, Pallas kernels, back(): pl.pallas_call(back_kernel, grid_spec=pltpu.PrefetchScalarGridSpec(num_sc...  22.1 us
    pallas_call x1, Pallas kernels, front(): pl.pallas_call(front_kernel, grid_spec=pltpu.PrefetchScalarGridSpec(num_s...  13 us

profile of v11, /device:TPU:0, one launch (start us, length us, event | category | flops | bytes accessed | tf_op | source)
XLA Modules:
  0.0 476.4 jit_solution(17023880224636497478)
XLA Ops:
  1.3 1.2 compare_select_fusion.lens
  2.5 2.4 copy.37
  4.9 13.0 %front.1 = (bf16[2048,1024]{1,0:T(8,128)(2,1)}, bf16[2048,256]{1,0:T(8,128)(2,1)}, bf16[2048,256]{1,0:T(8,128)(2,1)}, bf16[2048,256]{1,0:T(8,128)(2,1)}, bf16[51...) custom-call(s32[2]{0:T(128)} %compare_select_fusion.lens, bf16[2048,1024]{1,0:T(8,128)(2,1)} %all_units.3, ...), custom_call_target="tpu_custom_call" | custom-call | flops 20000000000 | bytes 16777216 | tf_op jit(solution)/shard_map/front/pallas_call | solution.py:138
  17.9 130.0 %middle.1 = (bf16[2048,1024]{1,0:T(8,128)(2,1)}, bf16[2048,1024]{1,0:T(8,128)(2,1)}, bf16[1024,2048]{1,0:T(8,128)(2,1)}, bf16[2048,1024]{1,0:T(8,128)(2,1)}, bf1...) custom-call(bf16[2048,1024]{1,0:T(8,128)(2,1)} %all_units.3, ...), custom_call_target="tpu_custom_call" | custom-call | flops 99999997952 | bytes 50331648 | tf_op jit(solution)/shard_map/middle/pallas_call | solution.py:754
  147.9 188.2 %turn.1 = (bf16[1024,2048]{1,0:T(8,128)(2,1)}, bf16[2048,1024]{1,0:T(8,128)(2,1)}, bf16[1024,1024]{1,0:T(8,128)(2,1)}, bf16[1024,1024]{1,0:T(8,128)(2,1)}, bf16[...) custom-call(bf16[2048,1024]{1,0:T(8,128)(2,1)} %get-tuple-element.73, ...), custom_call_target="tpu_custom_call" | custom-call | flops 99999997952 | bytes 25165824 | tf_op jit(solution)/shard_map/turn/pallas_call | solution.py:1036
  336.1 22.1 %back.1 = (bf16[2048,768]{1,0:T(8,128)(2,1)}, bf16[1024,1024]{1,0:T(8,128)(2,1)}, bf16[1024,1024]{1,0:T(8,128)(2,1)}, f32[2,256]{1,0:T(2,128)}, f32[1024,2048]{1,0:T(8,128)}, /*index=5*/f32[2048,1024]{1,0:T(8,128)}) custom-call(s32[2]{0:T(128)} %compare_select_fusion.lens, ...), custom_call_target="tpu_custom_call", output_to_operand_aliasing={{1}: (12, {}), {2}: (13, {})} | custom-call | flops 30000001024 | bytes 41943040 | tf_op jit(solution)/shard_map/back/pallas_call | solution.py:248
  358.1 109.3 %last.1 = (bf16[1024,1024]{1,0:T(8,128)(2,1)}, bf16[1024,1024]{1,0:T(8,128)(2,1)}, f32[512,1024]{1,0:T(8,128)}, f32[128,1024]{1,0:T(8,128)}, f32[16,1024]{1,0:T(8,128)}) custom-call(bf16[1024,1024]{1,0:T(8,128)(2,1)} %get-tuple-element.90.g0, bf16[1024,1024]{1,0:T(8,128)(2,1)} %get-tuple-element.91.g1, bf16[2048,1024]{1,0:T(8,128)(2,1)} %all_units.3, ...), custom_call_target="tpu_custom_call" | custom-call | flops 30000001024 | bytes 16777216 | tf_op jit(solution)/shard_map/last/pallas_call | solution.py:1264
  467.4 8.7 %unpack.1 = (f32[3,1024,256]{2,1,0:T(8,128)}, f32[1024,256]{1,0:T(8,128)}, f32[256,1024]{1,0:T(8,128)}, f32[256,1024]{1,0:T(8,128)}, f32[1024,2,256]{2,1,0:T(2,1...) custom-call(bf16[1024,1024]{1,0:T(8,128)(2,1)} %get-tuple-element.98, ...), custom_call_target="tpu_custom_call" | custom-call | tf_op jit(solution)/shard_map/unpack/pallas_call | solution.py:1350

commit v12 on v10

--- a/solution.py
+++ b/solution.py
@@ -719,9 +719,9 @@
     part[...] = out_acc[...].astype(jnp.bfloat16)
     results = [pltpu.make_async_copy(part, out_g, weight_sem.at[0])]
     results[0].start()
-    h3[...] = in_acc[...].astype(jnp.bfloat16)
     for side in range(hidden_count // width):
         here = pl.ds(side * width, width)
+        h3[here, :] = in_acc[here, :].astype(jnp.bfloat16)
         results.append(pltpu.make_async_copy(h3.at[here, :], in_g.at[:, here], weight_sem.at[1 + side]))
         results[-1].start()
     for step in (steps - 2, steps - 1):

time: 474 us -> 479 us (1.011)
  Pallas kernels: 462 us -> 469 us
where the time goes in v12:
time: 479 us; the launch traced here: 474 us
  Pallas kernels  469 us (98%)
    pallas_call x1, Pallas kernels, turn(): pl.pallas_call(functools.partial(turn_kernel, count=count), in_specs=[hbm...  187 us
    pallas_call x1, Pallas kernels, middle(): pl.pallas_call(middle_kernel, in_specs=[hbm] * 7 + [pl.BlockSpec(memory_s...  130 us
    pallas_call x1, Pallas kernels, last(): pl.pallas_call(functools.partial(last_kernel, count=count), in_specs=[hbm...  106 us
    pallas_call x1, Pallas kernels, back(): pl.pallas_call(back_kernel, grid_spec=pltpu.PrefetchScalarGridSpec(num_sc...  23.7 us
    pallas_call x1, Pallas kernels, front(): pl.pallas_call(front_kernel, grid_spec=pltpu.PrefetchScalarGridSpec(num_s...  13.6 us

profile of v12, /device:TPU:0, one launch (start us, length us, event | category | flops | bytes accessed | tf_op | source)
XLA Modules:
  0.0 473.7 jit_solution(10679810540774783985)
XLA Ops:
  1.3 1.2 compare_select_fusion.lens
  2.5 2.4 copy.37
  4.9 13.6 %front.1 = (bf16[2048,1024]{1,0:T(8,128)(2,1)}, bf16[2048,256]{1,0:T(8,128)(2,1)}, bf16[2048,256]{1,0:T(8,128)(2,1)}, bf16[2048,256]{1,0:T(8,128)(2,1)}, bf16[51...) custom-call(s32[2]{0:T(128)} %compare_select_fusion.lens, bf16[2048,1024]{1,0:T(8,128)(2,1)} %all_units.3, ...), custom_call_target="tpu_custom_call" | custom-call | flops 20000000000 | bytes 16777216 | tf_op jit(solution)/shard_map/front/pallas_call | solution.py:130
  18.5 130.0 %middle.1 = (bf16[2048,1024]{1,0:T(8,128)(2,1)}, bf16[2048,1024]{1,0:T(8,128)(2,1)}, bf16[1024,2048]{1,0:T(8,128)(2,1)}, bf16[2048,1024]{1,0:T(8,128)(2,1)}, bf1...) custom-call(bf16[2048,1024]{1,0:T(8,128)(2,1)} %all_units.3, ...), custom_call_target="tpu_custom_call" | custom-call | flops 99999997952 | bytes 50331648 | tf_op jit(solution)/shard_map/middle/pallas_call | solution.py:746
  148.5 186.6 %turn.1 = (bf16[1024,2048]{1,0:T(8,128)(2,1)}, bf16[2048,1024]{1,0:T(8,128)(2,1)}, bf16[1024,1024]{1,0:T(8,128)(2,1)}, bf16[1024,1024]{1,0:T(8,128)(2,1)}, bf16[...) custom-call(bf16[2048,1024]{1,0:T(8,128)(2,1)} %get-tuple-element.73, ...), custom_call_target="tpu_custom_call" | custom-call | flops 99999997952 | bytes 25165824 | tf_op jit(solution)/shard_map/turn/pallas_call | solution.py:1028
  335.0 23.7 %back.1 = (bf16[2048,768]{1,0:T(8,128)(2,1)}, bf16[1024,1024]{1,0:T(8,128)(2,1)}, bf16[1024,1024]{1,0:T(8,128)(2,1)}, f32[2,256]{1,0:T(2,128)}, f32[1024,2048]{1,0:T(8,128)}, /*index=5*/f32[2048,1024]{1,0:T(8,128)}) custom-call(s32[2]{0:T(128)} %compare_select_fusion.lens, ...), custom_call_target="tpu_custom_call", output_to_operand_aliasing={{1}: (12, {}), {2}: (13, {})} | custom-call | flops 30000001024 | bytes 41943040 | tf_op jit(solution)/shard_map/back/pallas_call | solution.py:240
  358.7 106.0 %last.1 = (bf16[1024,1024]{1,0:T(8,128)(2,1)}, bf16[1024,1024]{1,0:T(8,128)(2,1)}, f32[512,1024]{1,0:T(8,128)}, f32[128,1024]{1,0:T(8,128)}, f32[16,1024]{1,0:T(8,128)}) custom-call(bf16[1024,1024]{1,0:T(8,128)(2,1)} %get-tuple-element.90.g0, bf16[1024,1024]{1,0:T(8,128)(2,1)} %get-tuple-element.91.g1, bf16[2048,1024]{1,0:T(8,128)(2,1)} %all_units.3, ...), custom_call_target="tpu_custom_call" | custom-call | flops 30000001024 | bytes 16777216 | tf_op jit(solution)/shard_map/last/pallas_call | solution.py:1256
  464.7 8.7 %unpack.1 = (f32[3,1024,256]{2,1,0:T(8,128)}, f32[1024,256]{1,0:T(8,128)}, f32[256,1024]{1,0:T(8,128)}, f32[256,1024]{1,0:T(8,128)}, f32[1024,2,256]{2,1,0:T(2,1...) custom-call(bf16[1024,1024]{1,0:T(8,128)(2,1)} %get-tuple-element.98, ...), custom_call_target="tpu_custom_call" | custom-call | tf_op jit(solution)/shard_map/unpack/pallas_call | solution.py:1342
